TPU v7x, 256 devices: a whole 4x4x8 slice. The times are simulated.
256 devices in a mesh: batch: 2 (over z_hi), resp: 32 (over z_lo, x, core), head: 4 (over y).
Axes of the slice: x: 4, y: 4, z: 8 (z_hi: 2, z_lo: 4; z = z_hi * 4 + z_lo), core: 2. Of those that a mesh axis runs over, the one named last changes fastest.
Arguments:
- prompt_q: bfloat16 [4096, 8192], P(('batch', 'resp'), 'head'), parts along dimension 0, may hold values from -40 to 40
- prompt_kv: bfloat16 [4096, 2048], P(('batch', 'resp'), 'head'), parts along dimension 0, may hold values from -4 to 4
- resp_q: bfloat16 [64, 64, 8192], P(('batch', 'resp'), None, 'head'), parts along dimension 0, may hold values from -40 to 40
- resp_kv: bfloat16 [64, 64, 2048], P(('batch', 'resp'), None, 'head'), parts along dimension 0, may hold values from -4 to 4
- prompt_grad: bfloat16 [4096, 8192], P(('batch', 'resp'), 'head'), parts along dimension 0, may hold values from -6 to 6
- resp_grad: bfloat16 [64, 64, 8192], P(('batch', 'resp'), None, 'head'), parts along dimension 0, may hold values from -6 to 6
- resp_len: int32 [64], P(('batch', 'resp')), parts along dimension 0, may hold values from 1 to 64, 1536 in all
- logratio: float32 [64], P(('batch', 'resp')), parts along dimension 0, may hold values from -60 to 60
- partner: int32 [64], P(('batch', 'resp')), parts along dimension 0, may hold values from 0 to 31, as said below
- chosen: int32 [64], P(('batch', 'resp')), parts along dimension 0, may hold values from 0 to 1, as said below
Outputs:
- prompt_out: bfloat16 [4096, 8192], P(('batch', 'resp'), 'head'), parts along dimension 0
- resp_out: bfloat16 [64, 64, 8192], P(('batch', 'resp'), None, 'head'), parts along dimension 0
- prompt_dq: bfloat16 [4096, 8192], P(('batch', 'resp'), 'head'), parts along dimension 0
- resp_dq: bfloat16 [64, 64, 8192], P(('batch', 'resp'), None, 'head'), parts along dimension 0
- prompt_dkv: bfloat16 [4096, 2048], P(('batch', 'resp'), 'head'), parts along dimension 0
- resp_dkv: bfloat16 [64, 64, 2048], P(('batch', 'resp'), None, 'head'), parts along dimension 0
There are 2 independent parts, one for each index of `batch`. A program takes and returns all parts, laid end to end along the dimension named above; each array names one. Nothing has to cross between parts.
Inputs may be any that keep to these rules, and one draw needn't show every extreme that they name: The responses of one prompt form pairs: partner[partner[j]] = j and partner[j] != j. `chosen`: exactly one response of each pair has 1.
All inputs are finite; a program needn't handle non-finite values. No bound on the sum of `resp_len` on one device may be relied on, other than what follows from the above.
Results may differ from a plain program's by a relative error of at most 0.035.
Values may be sent and summed in bfloat16 or wider, within the bound.
No kernel may reach another device: no remote copies, remote signals or barrier semaphores. Data moves between devices by JAX's collectives and lax.ppermute only.
A program may use at most 128 MiB of HBM per device.

v0:
```python
import jax
import jax.numpy as jnp
from jax import lax
from jax.sharding import PartitionSpec as P

HEAD_DIM = 128


pair_beta = 0.1
masked_score = -1e30


def head_pass(queries, key_rows, value_rows, cotangent, allowed):
    score_scale = HEAD_DIM ** (-0.5)
    scores = (
        jnp.einsum("ngd,md->gnm", queries, key_rows, preferred_element_type=jnp.float32)
        * score_scale
    )
    scores = jnp.where(allowed[None], scores, masked_score)
    row_max = jnp.max(scores, axis=-1, keepdims=True)
    raised = jnp.exp(scores - row_max)
    normed = raised / jnp.sum(raised, axis=-1, keepdims=True)
    weights = normed.astype(jnp.bfloat16)
    output = jnp.einsum(
        "gnm,md->ngd", weights, value_rows, preferred_element_type=jnp.float32
    ).astype(jnp.bfloat16)
    row_dot = jnp.sum(cotangent.astype(jnp.float32) * output.astype(jnp.float32), axis=-1)
    dweights = jnp.einsum("ngd,md->gnm", cotangent, value_rows, preferred_element_type=jnp.float32)
    dscores = (score_scale * normed * (dweights - jnp.transpose(row_dot)[:, :, None])).astype(
        jnp.bfloat16
    )
    dqueries = jnp.einsum(
        "gnm,md->ngd", dscores, key_rows, preferred_element_type=jnp.float32
    ).astype(jnp.bfloat16)
    return (output, dqueries, dscores, weights)


def key_grads(dscores, weights, queries, cotangent, first_row, row_count):
    score_block = lax.dynamic_slice_in_dim(dscores, first_row, row_count, 2)
    weight_block = lax.dynamic_slice_in_dim(weights, first_row, row_count, 2)
    key_grad = jnp.einsum("gnm,ngd->md", score_block, queries, preferred_element_type=jnp.float32)
    value_grad = jnp.einsum(
        "gnm,ngd->md", weight_block, cotangent, preferred_element_type=jnp.float32
    )
    return (key_grad, value_grad)


def shards(
    prompt_q,
    prompt_kv,
    resp_q,
    resp_kv,
    prompt_grad,
    resp_grad,
    resp_len,
    logratio,
    partner,
    chosen,
):
    resp_count = lax.axis_size("resp")
    own_index = lax.axis_index("resp")
    prompt_rows = prompt_q.shape[0]
    length = resp_q.shape[1]
    head_pairs = resp_kv.shape[2] // (2 * HEAD_DIM)
    group_size = prompt_q.shape[1] // (head_pairs * HEAD_DIM)
    whole_kv = lax.all_gather(prompt_kv, "resp", axis=0, tiled=True)
    prompt_len = whole_kv.shape[0]
    ratios = lax.all_gather(logratio, "resp", axis=0, tiled=True)
    slot_ids = jnp.arange(resp_count, dtype=jnp.int32)
    mate_ratio = jnp.sum(jnp.where(slot_ids == partner[0], ratios, 0.0))
    pair_sign = 2.0 * chosen[0].astype(jnp.float32) - 1.0
    margin = pair_sign * (logratio[0] - mate_ratio)
    pair_weight = pair_sign * jax.nn.sigmoid(-pair_beta * margin)
    positions = jnp.arange(length, dtype=jnp.int32)
    live_rows = (positions < resp_len[0]).astype(jnp.float32)
    resp_cot = (pair_weight * live_rows[:, None] * resp_grad[0].astype(jnp.float32)).astype(
        jnp.bfloat16
    )
    columns = jnp.arange(prompt_len, dtype=jnp.int32)
    prompt_pos = own_index * prompt_rows + jnp.arange(prompt_rows, dtype=jnp.int32)
    prompt_allowed = columns[None, :] <= prompt_pos[:, None]
    resp_allowed = jnp.concatenate(
        [jnp.ones((length, prompt_len), bool), positions[None, :] <= positions[:, None]], axis=1
    )
    prompt_query = prompt_q.reshape(prompt_rows, head_pairs, group_size, HEAD_DIM)
    prompt_cot = prompt_grad.reshape(prompt_rows, head_pairs, group_size, HEAD_DIM)
    resp_query = resp_q[0].reshape(length, head_pairs, group_size, HEAD_DIM)
    resp_cots = resp_cot.reshape(length, head_pairs, group_size, HEAD_DIM)
    shared_rows = whole_kv.reshape(prompt_len, head_pairs, 2, HEAD_DIM)
    own_rows = resp_kv[0].reshape(length, head_pairs, 2, HEAD_DIM)
    stored = []
    own_grads = []
    for head_slot in range(head_pairs):
        key_rows = jnp.concatenate(
            [shared_rows[:, head_slot, 0], own_rows[:, head_slot, 0]], axis=0
        )
        value_rows = jnp.concatenate(
            [shared_rows[:, head_slot, 1], own_rows[:, head_slot, 1]], axis=0
        )
        prompt_pass = head_pass(
            prompt_query[:, head_slot],
            shared_rows[:, head_slot, 0],
            shared_rows[:, head_slot, 1],
            prompt_cot[:, head_slot],
            prompt_allowed,
        )
        resp_pass = head_pass(
            resp_query[:, head_slot], key_rows, value_rows, resp_cots[:, head_slot], resp_allowed
        )
        own_key, own_value = key_grads(
            resp_pass[2],
            resp_pass[3],
            resp_query[:, head_slot],
            resp_cots[:, head_slot],
            prompt_len,
            length,
        )
        stored.append((prompt_pass, resp_pass))
        own_grads.append(jnp.stack([own_key, own_value], axis=1))
    pieces = []
    for prompt_head_slot in range(head_pairs):
        prompt_pass, resp_pass = stored[prompt_head_slot]
        from_prompt = key_grads(
            prompt_pass[2],
            prompt_pass[3],
            prompt_query[:, prompt_head_slot],
            prompt_cot[:, prompt_head_slot],
            0,
            prompt_len,
        )
        from_resp = key_grads(
            resp_pass[2],
            resp_pass[3],
            resp_query[:, prompt_head_slot],
            resp_cots[:, prompt_head_slot],
            0,
            prompt_len,
        )
        pieces.append(
            jnp.stack([from_prompt[0] + from_resp[0], from_prompt[1] + from_resp[1]], axis=1)
        )
    received = lax.all_to_all(
        jnp.stack(pieces, axis=1)
        .reshape(prompt_len, head_pairs * 2 * HEAD_DIM)
        .astype(jnp.bfloat16),
        "resp",
        split_axis=0,
        concat_axis=0,
        tiled=True,
    )
    summed = jnp.sum(received.reshape(resp_count, prompt_rows, -1), axis=0, dtype=jnp.float32)
    prompt_out = jnp.stack(
        [stored[head_slot][0][0] for head_slot in range(head_pairs)], axis=1
    ).reshape(prompt_rows, -1)
    prompt_dq = jnp.stack(
        [stored[head_slot][0][1] for head_slot in range(head_pairs)], axis=1
    ).reshape(prompt_rows, -1)
    resp_out = jnp.stack(
        [stored[head_slot][1][0] for head_slot in range(head_pairs)], axis=1
    ).reshape(1, length, -1)
    resp_dq = jnp.stack(
        [stored[head_slot][1][1] for head_slot in range(head_pairs)], axis=1
    ).reshape(1, length, -1)
    prompt_dkv = summed.astype(jnp.bfloat16)
    resp_dkv = jnp.stack(own_grads, axis=1).reshape(1, length, -1).astype(jnp.bfloat16)
    return (prompt_out, resp_out, prompt_dq, resp_dq, prompt_dkv, resp_dkv)


def solution(mesh):
    return jax.shard_map(
        shards,
        mesh=mesh,
        in_specs=(
            P(("batch", "resp"), "head"),
            P(("batch", "resp"), "head"),
            P(("batch", "resp"), None, "head"),
            P(("batch", "resp"), None, "head"),
            P(("batch", "resp"), "head"),
            P(("batch", "resp"), None, "head"),
            P(("batch", "resp")),
            P(("batch", "resp")),
            P(("batch", "resp")),
            P(("batch", "resp")),
        ),
        out_specs=(
            P(("batch", "resp"), "head"),
            P(("batch", "resp"), None, "head"),
            P(("batch", "resp"), "head"),
            P(("batch", "resp"), None, "head"),
            P(("batch", "resp"), "head"),
            P(("batch", "resp"), None, "head"),
        ),
        check_vma=False,
    )
```

profile of v0, /device:TPU:1, one launch (start us, length us, event | category | flops | bytes accessed | tf_op | source)
XLA Modules:
  0.0 243.7 jit_solution(4372324529891981260)
XLA Ops:
  7.9 0.9 reshape_squeeze.6
  8.8 1.0 copy.92
  11.7 1.3 dynamic-slice
  13.8 70.4 %all-reduce.1 = f32[32]{0:T(128)S(1)} all-reduce(f32[32]{0:T(128)S(1)} %dynamic-update-slice), channel_id=1, replica_groups=mesh['batch'=2,'resp'=32,'head'=4] {'resp'}, use_global_device_ids=true, to_apply=%add.1 | all-reduce | flops 32 | bytes 256
  86.2 1.0 convert_bitcast_fusion
  91.2 0.8 iota_compare_fusion
  92.0 2.9 %copy.46 = bf16[2048,512]{0,1:T(8,128)(2,1)S(1)} copy(bf16[2048,512]{1,0:T(8,128)(2,1)} %all-gather.2.cloned.1.call-done) | data formatting | bytes 4194304 | tf_op jit(solution)/shard_map/all_gather | solution.py:66
  94.9 1.2 fusion.124
  96.1 2.0 copy.79
  98.1 2.1 copy.81
  100.2 1.0 copy.76
  101.2 1.0 copy.78
  102.2 4.9 %fusion.135 = (f32[8,64]{1,0:T(8,128)S(1)}, f32[8,64,2112]{2,1,0:T(8,128)}) fusion(pred[64,2112]{1,0:T(8,128)(4,1)S(1)} %concatenate.16, bf16[64,128]{1,0:T(8,128)(2,1)} %get-tuple-element.35, bf16[2048,128]{1,0:T(8,128)(2,1)} %bitcast.405, bf16[64,1,8,128]{3,2,1,0:T(8,128)(2,1)} %get-tuple-element.15), kind=kOutput, calls=%fused_computation.192 | convolution fusion | flops 282232896 | bytes 5134336 | tf_op jit(solution)/shard_map/sub | solution.py:21
  107.1 4.2 %fusion.47 = bf16[8,64,2112]{2,1,0:T(8,128)(2,1)} fusion(f32[8,64,2112]{2,1,0:T(8,128)} %get-tuple-element.27, f32[8,64]{1,0:T(8,128)S(1)} %get-tuple-element.26), kind=kLoop, calls=%fused_computation.70 | loop fusion | flops 2162688 | bytes 6490112 | tf_op jit(solution)/shard_map/convert_element_type | solution.py:23
  111.4 3.9 %fusion.136 = (f32[8,64]{1,0:T(8,128)S(1)}, f32[8,64,2112]{2,1,0:T(8,128)}) fusion(pred[64,2112]{1,0:T(8,128)(4,1)S(1)} %concatenate.16, bf16[64,128]{1,0:T(8,128)(2,1)S(1)} %copy-done.27, bf16[2048,128]{1,0:T(8,128)(2,1)S(1)} %bitcast.407, bf16[64,1,8,128]{3,2,1,0:T(8,128)(2,1)S(1)} %copy-done.13), kind=kOutput, calls=%fused_computation.193 | convolution fusion | flops 282232896 | bytes 5134336 | tf_op jit(solution)/shard_map/sub | solution.py:21
  115.2 2.9 %fusion.46 = bf16[8,64,2112]{2,1,0:T(8,128)(2,1)S(1)} fusion(f32[8,64,2112]{2,1,0:T(8,128)} %get-tuple-element.29, f32[8,64]{1,0:T(8,128)S(1)} %get-tuple-element.28), kind=kLoop, calls=%fused_computation.69 | loop fusion | flops 2162688 | bytes 6490112 | tf_op jit(solution)/shard_map/convert_element_type | solution.py:23
  118.2 1.7 convolution_bitcast_fusion.6
  119.9 1.7 convolution_bitcast_fusion.2
  122.7 1.4 multiply_reduce_fusion.1
  124.2 1.0 fusion.16
  125.3 2.4 %fusion.17 = bf16[8,64,2112]{2,1,0:T(8,128)(2,1)} fusion(f32[8,64]{1,0:T(8,128)S(1)} %bitcast.420, f32[8,64,2112]{2,1,0:T(8,128)S(1)} %bitcast.396, f32[8,64]{1,0:T(8,128)S(1)} %get-tuple-element.26, bf16[64,128]{1,0:T(8,128)(2,1)S(1)} %copy-done.28, bf16[2048,128]{1,0:T(8,128)(2,1)S(1)} %bitcast.410, bf16[64,2,8,128]{3,0,2,1:T(8,128)(2,1)S(1)} %fusion.84), kind=kOutput, calls=%fused_computation.21 | convolution fusion | flops 283312128 | bytes 7299072 | tf_op jit(solution)/shard_map/ngd,md->gnm/dot_general | solution.py:28
  127.8 1.8 convolution_bitcast_fusion.8
  129.6 3.7 %fusion.132 = (f32[8,64]{1,0:T(8,128)S(1)}, f32[8,64,2048]{2,1,0:T(8,128)}) fusion(pred[64,2048]{1,0:T(8,128)(4,1)S(1)} %copy-done.10, bf16[64,1,8,128]{3,2,1,0:T(8,128)(2,1)S(1)} %copy-done.21, bf16[2048,2,2,128]{0,3,2,1:T(8,128)(2,1)S(1)} %bitcast.387), kind=kOutput, calls=%fused_computation.191 | convolution fusion | flops 272631808 | bytes 4982784 | tf_op jit(solution)/shard_map/sub | solution.py:21
  133.2 2.9 %fusion.48 = bf16[8,64,2048]{2,1,0:T(8,128)(2,1)S(1)} fusion(f32[8,64,2048]{2,1,0:T(8,128)} %get-tuple-element.25, f32[8,64]{1,0:T(8,128)S(1)} %get-tuple-element.24), kind=kLoop, calls=%fused_computation.71 | loop fusion | flops 2097152 | bytes 6293504 | tf_op jit(solution)/shard_map/convert_element_type | solution.py:23
  136.2 1.4 multiply_reduce_fusion.3
  137.6 2.1 fusion.21
  139.7 0.8 fusion.33
  140.6 0.8 copy-done.31
  141.4 1.7 convolution_bitcast_fusion.4
  143.1 4.4 %fusion.129 = (f32[8,64]{1,0:T(8,128)S(1)}, f32[8,64,2048]{2,1,0:T(8,128)}) fusion(pred[64,2048]{1,0:T(8,128)(4,1)S(1)} %copy-done.10, bf16[64,1,8,128]{3,2,1,0:T(8,128)(2,1)} %get-tuple-element.17, bf16[2048,2,2,128]{0,3,2,1:T(8,128)(2,1)S(1)} %bitcast.390), kind=kOutput, calls=%fused_computation.190 | convolution fusion | flops 272631808 | bytes 4982784 | tf_op jit(solution)/shard_map/sub | solution.py:21
  147.5 2.9 %fusion.49 = bf16[8,64,2048]{2,1,0:T(8,128)(2,1)S(1)} fusion(f32[8,64,2048]{2,1,0:T(8,128)} %get-tuple-element.23, f32[8,64]{1,0:T(8,128)S(1)} %get-tuple-element.22), kind=kLoop, calls=%fused_computation.72 | loop fusion | flops 2097152 | bytes 6293504 | tf_op jit(solution)/shard_map/convert_element_type | solution.py:23
  150.5 1.4 multiply_reduce_fusion.2
  151.9 0.8 fusion.19
  154.1 1.4 copy-done.33
  158.2 14.2 %copy.66 = bf16[2048,2,2,128]{3,2,1,0:T(2,128)(2,1)} copy(bf16[2048,2,2,128]{3,0,2,1:T(8,128)(2,1)S(1)} %pad_maximum_fusion) | data formatting | bytes 4194304 | tf_op jit(solution)/shard_map/stack | solution.py:143
  172.4 4.1 %convert_element_type.168 = bf16[32,64,512]{2,1,0:T(8,128)(2,1)} reshape(bf16[2048,2,2,128]{3,2,1,0:T(2,128)(2,1)} %copy.66) | data formatting | bytes 4194304 | tf_op jit(solution)/shard_map/convert_element_type | solution.py:145
  176.5 9.5 %all-to-all-start = ((bf16[32,64,512]{2,1,0:T(8,128)(2,1)}), bf16[32,64,512]{2,1,0:T(8,128)(2,1)}, u32[]{:S(2)}, u32[]{:S(2)}) async-start(bf16[32,64,512]{2,1,0:T(8,128)(2,1)} %convert_element_type.168), calls=%async_computation | async-start | bytes 4194304 | tf_op jit(solution)/shard_map/all_to_all | solution.py:142
  186.0 1.1 fusion.61
  187.1 1.2 fusion.60
  188.3 1.1 fusion.59
  189.4 1.1 fusion.58
  191.3 2.5 %fusion.52 = bf16[64,1,8,128]{3,0,2,1:T(8,128)(2,1)S(1)} fusion(bf16[8,64,2112]{2,1,0:T(8,128)(2,1)} %copy-done.30, bf16[64,128]{1,0:T(8,128)(2,1)} %get-tuple-element.37, bf16[2048,128]{1,0:T(8,128)(2,1)S(1)} %bitcast.408), kind=kOutput, calls=%fused_computation.83 | convolution fusion | flops 277970944 | bytes 2834432 | tf_op jit(solution)/shard_map/gnm,md->ngd/dot_general | solution.py:32
  194.9 0.8 reshape.116
  195.9 0.8 reshape.113
  196.8 2.5 %fusion.50 = bf16[64,1,8,128]{3,0,2,1:T(8,128)(2,1)S(1)} fusion(bf16[8,64,2048]{2,1,0:T(8,128)(2,1)} %fusion.21, bf16[2048,2,2,128]{0,3,2,1:T(8,128)(2,1)S(1)} %bitcast.393), kind=kOutput, calls=%fused_computation.81 | convolution fusion | flops 268500992 | bytes 2752512 | tf_op jit(solution)/shard_map/gnm,md->ngd/dot_general | solution.py:32
  200.4 0.9 copy_bitcast_fusion
  201.3 33.0 %all-to-all-done = bf16[32,64,512]{2,1,0:T(8,128)(2,1)} async-done(((bf16[32,64,512]{2,1,0:T(8,128)(2,1)}), bf16[32,64,512]{2,1,0:T(8,128)(2,1)}, u32[]{:S(2)}, u32[]{:S(2)}) %all-to-all-start) | async-done | bytes 2097184 | tf_op jit(solution)/shard_map/all_to_all | solution.py:142
  234.3 2.5 %reduce_sum.102 = bf16[64,512]{1,0:T(8,128)(2,1)} reduce(bf16[32,64,512]{2,1,0:T(8,128)(2,1)} %all-to-all-done, bf16[]{:T(256)} %constant.31.clone.1), dimensions={0}, to_apply=%region_13.14 | reduce | flops 1015808 | bytes 2162690 | tf_op jit(solution)/shard_map/reduce_sum | solution.py:151
  (130 shorter events, 14.4 us)
Async XLA Ops:
  7.2 80.1 %copy-start.8 = (bf16[64,2048]{1,0:T(8,128)(2,1)S(1)}, bf16[64,2048]{1,0:T(8,128)(2,1)}, u32[]{:S(2)}) copy-start(bf16[64,2048]{1,0:T(8,128)(2,1)} %param.10) | copy-start | bytes 786436
  7.2 80.2 %copy-start.9 = (bf16[64,2048]{1,0:T(8,128)(2,1)S(1)}, bf16[64,2048]{1,0:T(8,128)(2,1)}, u32[]{:S(2)}) copy-start(bf16[64,2048]{1,0:T(8,128)(2,1)} %param.14) | copy-start | bytes 786436
  7.2 84.8 %all-gather.2.cloned.1.call-start = ((), (), s32[]{:S(2)}) async-start(), calls=%async_computation.1 | async-start | bytes 2162688 | tf_op jit(solution)/shard_map/all_gather | solution.py:66
  107.1 4.2 %copy-start.5 = (bf16[2048,1,1,128]{3,0,2,1:T(8,128)(2,1)S(1)}, bf16[2048,1,1,128]{3,0,2,1:T(8,128)(2,1)}, u32[]{:S(2)}) copy-start(bf16[2048,1,1,128]{3,0,2,1:T(8,128)(2,1)} %copy.76) | copy-start | bytes 1572868
  107.1 4.2 %copy-start.13 = (bf16[64,1,8,128]{3,2,1,0:T(8,128)(2,1)S(1)}, bf16[64,1,8,128]{3,2,1,0:T(8,128)(2,1)}, u32[]{:S(2)}) copy-start(bf16[64,1,8,128]{3,2,1,0:T(8,128)(2,1)} %get-tuple-element.14) | copy-start | bytes 393220
  107.1 4.2 %copy-start.27 = (bf16[64,128]{1,0:T(8,128)(2,1)S(1)}, bf16[64,128]{1,0:T(8,128)(2,1)}, u32[]{:S(2)}) copy-start(bf16[64,128]{1,0:T(8,128)(2,1)} %get-tuple-element.37) | copy-start | bytes 49156
  115.2 4.7 %copy-start.2 = (bf16[8,64,2112]{2,1,0:T(8,128)(2,1)S(1)}, bf16[8,64,2112]{2,1,0:T(8,128)(2,1)}, u32[]{:S(2)}) copy-start(bf16[8,64,2112]{2,1,0:T(8,128)(2,1)} %fusion.47) | copy-start | bytes 6488068
  118.2 4.3 %copy-start.3 = (bf16[8,64,2112]{2,1,0:T(8,128)(2,1)}, bf16[8,64,2112]{2,1,0:T(8,128)(2,1)S(1)}, u32[]{:S(2)}) copy-start(bf16[8,64,2112]{2,1,0:T(8,128)(2,1)S(1)} %fusion.46) | copy-start | bytes 6488068
  118.2 5.9 %slice-start.2 = ((s8[4456448]{0:T(1024)(128)(4,1)}), s8[4194304]{0:T(1024)(128)(4,1)S(1)}, s32[]{:S(2)}) async-start(s8[4456448]{0:T(1024)(128)(4,1)} %bitcast.397), calls=%async_computation.4 | async-start | bytes 8388608
  119.9 1.8 copy-start.6
  119.9 1.8 copy-start.28
  119.9 4.2 %slice-start.3 = ((s8[4456448]{0:T(1024)(128)(4,1)}), s8[262144]{0:T(1024)(128)(4,1)S(1)}, s32[]{:S(2)}) async-start(s8[4456448]{0:T(1024)(128)(4,1)} %bitcast.397), calls=%async_computation.5 | async-start | bytes 524288
  121.7 1.0 copy-start.7
  121.7 1.0 copy-start.29
  122.5 1.7 copy-start.16
  122.7 2.5 %slice-start = ((s8[4456448]{0:T(1024)(128)(4,1)}), s8[4194304]{0:T(1024)(128)(4,1)S(1)}, s32[]{:S(2)}) async-start(s8[4456448]{0:T(1024)(128)(4,1)} %bitcast.395), calls=%async_computation.2 | async-start | bytes 8388608
  124.1 1.2 slice-start.1
  125.2 2.5 %copy-start.30 = (bf16[8,64,2112]{2,1,0:T(8,128)(2,1)}, bf16[8,64,2112]{2,1,0:T(8,128)(2,1)S(1)}, u32[]{:S(2)}) copy-start(bf16[8,64,2112]{2,1,0:T(8,128)(2,1)S(1)} %fusion.16) | copy-start | bytes 6488068
  125.3 2.5 %copy-start.14 = (bf16[64,1,8,128]{3,2,1,0:T(8,128)(2,1)S(1)}, bf16[64,1,8,128]{3,2,1,0:T(8,128)(2,1)}, u32[]{:S(2)}) copy-start(bf16[64,1,8,128]{3,2,1,0:T(8,128)(2,1)} %get-tuple-element.14) | copy-start | bytes 393220
  127.8 1.8 copy-start.10
  127.8 1.8 copy-start.21
  133.2 3.0 %copy-start.25 = (bf16[64,1,8,128]{3,2,1,0:T(8,128)(2,1)S(1)}, bf16[64,1,8,128]{3,2,1,0:T(8,128)(2,1)}, u32[]{:S(2)}) copy-start(bf16[64,1,8,128]{3,2,1,0:T(8,128)(2,1)} %get-tuple-element.12) | copy-start | bytes 393220
  133.2 4.3 %copy-start.1 = (f32[8,64,2048]{2,1,0:T(8,128)S(1)}, f32[8,64,2048]{2,1,0:T(8,128)}, u32[]{:S(2)}) copy-start(f32[8,64,2048]{2,1,0:T(8,128)} %get-tuple-element.25) | copy-start | bytes 12582916
  137.6 2.1 copy-start.38
  139.7 0.9 copy-start.11
  139.7 1.7 copy-start.31
  147.5 3.0 %copy-start.23 = (bf16[64,1,8,128]{3,2,1,0:T(8,128)(2,1)S(1)}, bf16[64,1,8,128]{3,2,1,0:T(8,128)(2,1)}, u32[]{:S(2)}) copy-start(bf16[64,1,8,128]{3,2,1,0:T(8,128)(2,1)} %get-tuple-element.13) | copy-start | bytes 393220
  147.5 4.3 %copy-start = (f32[8,64,2048]{2,1,0:T(8,128)S(1)}, f32[8,64,2048]{2,1,0:T(8,128)}, u32[]{:S(2)}) copy-start(f32[8,64,2048]{2,1,0:T(8,128)} %get-tuple-element.23) | copy-start | bytes 12582916
  151.9 1.2 copy-start.36
  153.1 3.6 %copy-start.34 = (bf16[8,64,2048]{2,1,0:T(8,128)(2,1)}, bf16[8,64,2048]{2,1,0:T(8,128)(2,1)S(1)}, u32[]{:S(2)}) copy-start(bf16[8,64,2048]{2,1,0:T(8,128)(2,1)S(1)} %fusion.19) | copy-start | bytes 6291460
  153.1 1.0 copy-start.22
  153.1 2.4 copy-start.33
  153.1 2.7 %copy-start.37 = (f32[2048,128]{1,0:T(8,128)S(1)}, f32[2048,128]{1,0:T(8,128)}, u32[]{:S(2)}) copy-start(f32[2048,128]{1,0:T(8,128)} %convolution_bitcast_fusion.8) | copy-start | bytes 3145732
  155.8 0.9 copy-start.20
  155.8 1.3 copy-start.39
  176.5 9.6 %copy-start.15 = (bf16[64,1,8,128]{3,2,1,0:T(8,128)(2,1)S(1)}, bf16[64,1,8,128]{3,2,1,0:T(8,128)(2,1)}, u32[]{:S(2)}) copy-start(bf16[64,1,8,128]{3,2,1,0:T(8,128)(2,1)} %get-tuple-element.14) | copy-start | bytes 393220
  176.5 11.9 %copy-start.12 = (bf16[64,1,8,128]{3,2,1,0:T(8,128)(2,1)S(1)}, bf16[64,1,8,128]{3,2,1,0:T(8,128)(2,1)}, u32[]{:S(2)}) copy-start(bf16[64,1,8,128]{3,2,1,0:T(8,128)(2,1)} %get-tuple-element.15) | copy-start | bytes 393220
  176.5 57.8 %all-to-all-start = ((bf16[32,64,512]{2,1,0:T(8,128)(2,1)}), bf16[32,64,512]{2,1,0:T(8,128)(2,1)}, u32[]{:S(2)}, u32[]{:S(2)}) async-start(bf16[32,64,512]{2,1,0:T(8,128)(2,1)} %convert_element_type.168), calls=%async_computation | async-start | bytes 4194304 | tf_op jit(solution)/shard_map/all_to_all | solution.py:142
  187.1 6.8 %copy-start.4 = (bf16[2048,1,1,128]{3,0,2,1:T(8,128)(2,1)S(1)}, bf16[2048,1,1,128]{3,0,2,1:T(8,128)(2,1)}, u32[]{:S(2)}) copy-start(bf16[2048,1,1,128]{3,0,2,1:T(8,128)(2,1)} %copy.79) | copy-start | bytes 1572868
  187.1 6.8 %copy-start.26 = (bf16[64,128]{1,0:T(8,128)(2,1)S(1)}, bf16[64,128]{1,0:T(8,128)(2,1)}, u32[]{:S(2)}) copy-start(bf16[64,128]{1,0:T(8,128)(2,1)} %get-tuple-element.35) | copy-start | bytes 49156
  191.3 2.6 %copy-start.32 = (bf16[8,64,2112]{2,1,0:T(8,128)(2,1)S(1)}, bf16[8,64,2112]{2,1,0:T(8,128)(2,1)}, u32[]{:S(2)}) copy-start(bf16[8,64,2112]{2,1,0:T(8,128)(2,1)} %fusion.17) | copy-start | bytes 6488068
  193.9 1.8 copy-start.17
  193.9 1.8 copy-start.18
  196.8 2.5 %copy-start.35 = (bf16[8,64,2048]{2,1,0:T(8,128)(2,1)S(1)}, bf16[8,64,2048]{2,1,0:T(8,128)(2,1)}, u32[]{:S(2)}) copy-start(bf16[8,64,2048]{2,1,0:T(8,128)(2,1)} %copy-done.34) | copy-start | bytes 6291460
  199.2 1.0 copy-start.19
  199.2 1.0 copy-start.24
Sparse Core Ops, SparseCore 0:
  9.9 64.3 all-gather.1
where the time goes:
time: 245 us; the launch traced here: 244 us
  blocking collectives  70.4 us (29%)
  matrix products  49.2 us (20%)
  local copies, waits for them, and re-layouts  44.1 us (18%)
  waiting for transfers between devices  33.6 us (14%)
  other arithmetic  18.7 us (8%)
  between operations  18 us (7%)
  starting transfers between devices  9.58 us (4%)
    unnamed x1, blocking collectives  70.4 us
    all_to_all x1, waiting for transfers between devices, shards(): lax.all_to_all(jnp.stack(pieces, axis=1).reshape(prompt_len, head_pairs *...  33 us
    sub x4, matrix products, head_pass(): raised = jnp.exp(scores - row_max)  16.9 us
    another operation x1, local copies, waits for them, and re-layouts, shards(): jnp.stack(pieces, axis=1).reshape(prompt_len, head_pairs * 2 * HEAD_DIM)  14.2 us
    unnamed x99, local copies, waits for them, and re-layouts  13.4 us
    convert_element_type x4, other arithmetic, head_pass(): weights = normed.astype(jnp.bfloat16)  13 us
    all_to_all x1, starting transfers between devices, shards(): lax.all_to_all(jnp.stack(pieces, axis=1).reshape(prompt_len, head_pairs *...  9.54 us
    dot_general x6, matrix products, key_grads(): jnp.einsum('gnm,ngd->md', weight_block, cotangent, preferred_element_type...  7.31 us
  transfers between devices with their start and end apart: 2, of which 1 were waited for; matrix products, arithmetic and copies ran while one was open for 10% of the time, Pallas kernels for 0%

commit v1 on v0

v1 whole, which is shorter than its diff:
```python
import functools

import jax
import jax.numpy as jnp
from jax import lax
from jax.experimental import pallas as pl
from jax.experimental.pallas import tpu as pltpu
from jax.sharding import PartitionSpec as P

HEAD_DIM = 128
GROUP = 8
TOKENS = 64
KV_COLS = 2 * HEAD_DIM
Q_COLS = GROUP * HEAD_DIM
BLOCK = 2 * TOKENS
CHUNK = 4 * BLOCK
TILE = GROUP * TOKENS
LANES = 4 * TILE
SUB = 256

score_scale = HEAD_DIM ** (-0.5)
exp2_scale = score_scale * 1.4426950408889634
pair_beta = 0.1
blocked_score = -(2.0**30)
no_max = -(2.0**31)

bf16 = jnp.bfloat16
f32 = jnp.float32


def params(**kw):
    return pltpu.CompilerParams(vmem_limit_bytes=40 * 2**20, **kw)


def dot(left, right, left_dim=1, right_dim=0):
    return lax.dot_general(
        left, right, (((left_dim,), (right_dim,)), ((), ())), preferred_element_type=f32
    )


def iota(shape, dim):
    return lax.broadcasted_iota(jnp.int32, shape, dim)


def swap_core(value):
    return lax.ppermute(value, "resp", [(r, r ^ 1) for r in range(32)])


def shift_z(value, step):
    pairs = [(r, ((r // 8 + step) % 4) * 8 + r % 8) for r in range(32)]
    return lax.ppermute(value, "resp", pairs)


def shift_x(value, step):
    pairs = [(r, (r // 8) * 8 + (r % 8 // 2 + step) % 4 * 2 + r % 2) for r in range(32)]
    return lax.ppermute(value, "resp", pairs)


def pack_kv_kernel(info, p_own, r_own, p_sib, r_sib, own, send):
    own[:TOKENS] = p_own[...]
    own[TOKENS:] = r_own[0]
    send[:TOKENS] = p_sib[...]
    send[TOKENS:] = r_sib[0]


def pack_kv(info, prompt_kv, resp_kv):
    two = (TOKENS, KV_COLS)
    three = (1, TOKENS, KV_COLS)
    return pl.pallas_call(
        pack_kv_kernel,
        grid_spec=pltpu.PrefetchScalarGridSpec(
            num_scalar_prefetch=1,
            grid=(1,),
            in_specs=[
                pl.BlockSpec(two, lambda i, s: (0, s[0])),
                pl.BlockSpec(three, lambda i, s: (0, 0, s[0])),
                pl.BlockSpec(two, lambda i, s: (0, 1 - s[0])),
                pl.BlockSpec(three, lambda i, s: (0, 0, 1 - s[0])),
            ],
            out_specs=[pl.BlockSpec((BLOCK, KV_COLS), lambda i, s: (0, 0))] * 2,
        ),
        out_shape=[jax.ShapeDtypeStruct((BLOCK, KV_COLS), bf16)] * 2,
        compiler_params=params(),
        name="pack_kv",
    )(info, prompt_kv, resp_kv, prompt_kv, resp_kv)


def pack_q_kernel(info, pq, rq, pg, rg, send):
    send[0] = pq[...]
    send[1] = rq[0]
    send[2] = pg[...]
    send[3] = rg[0]


def pack_q(info, prompt_q, resp_q, prompt_grad, resp_grad):
    two = pl.BlockSpec((TOKENS, Q_COLS), lambda i, s: (0, 1 - s[0]))
    three = pl.BlockSpec((1, TOKENS, Q_COLS), lambda i, s: (0, 0, 1 - s[0]))
    return pl.pallas_call(
        pack_q_kernel,
        grid_spec=pltpu.PrefetchScalarGridSpec(
            num_scalar_prefetch=1,
            grid=(1,),
            in_specs=[two, three, two, three],
            out_specs=pl.BlockSpec((4, TOKENS, Q_COLS), lambda i, s: (0, 0, 0)),
        ),
        out_shape=jax.ShapeDtypeStruct((4, TOKENS, Q_COLS), bf16),
        compiler_params=params(),
        name="pack_q",
    )(info, prompt_q, resp_q, prompt_grad, resp_grad)


def turned(block):
    rows = jnp.concatenate(
        [block[:, g * HEAD_DIM : (g + 1) * HEAD_DIM] for g in range(GROUP)], axis=0
    )
    return rows.T


def softmax_part(scores, value_rows):
    top = jnp.max(scores, axis=0, keepdims=True)
    raised = jnp.exp2((scores - top) * exp2_scale).astype(bf16)
    total = dot(value_rows, raised)
    packed = jnp.concatenate(
        [total[: HEAD_DIM + 8], jnp.broadcast_to(top, (8, top.shape[1]))], axis=0
    )
    return raised, packed


def with_ones(value_rows):
    return jnp.concatenate([value_rows.T, jnp.ones((16, value_rows.shape[0]), bf16)], axis=0)


def prep_kernel(info, pq, rq, pg, rg, recv, kv_own, kv_recv, q_aug, grads, raised, packed):
    core = info[0]
    none = jnp.concatenate(
        [jnp.zeros((HEAD_DIM + 8, TILE), f32), jnp.full((8, TILE), no_max, f32)], axis=0
    )
    for j in range(4):
        lanes = slice(j * TILE, (j + 1) * TILE)
        sib, resp = j // 2, j % 2
        if sib:
            block, grad = recv[resp], recv[2 + resp]
        else:
            block, grad = (rq[0], rg[0]) if resp else (pq[...], pg[...])
        turned_q = turned(block)
        q_aug[:HEAD_DIM, lanes] = turned_q
        grads[:, lanes] = turned(grad)
        if resp:
            q_aug[HEAD_DIM:, lanes] = jnp.zeros((HEAD_DIM, TILE), bf16)
            rows = (kv_recv if sib else kv_own)[TOKENS:]
            scores = dot(rows[:, :HEAD_DIM], turned_q)
            token = iota(scores.shape, 1) % TOKENS
            scores = jnp.where(iota(scores.shape, 0) <= token, scores, blocked_score)
            part, info_rows = softmax_part(scores, with_ones(rows[:, HEAD_DIM:]))
            raised[:, sib * TILE : (sib + 1) * TILE] = part
            packed[:, lanes] = info_rows
        else:
            own_core = 1 - core if sib else core
            token = iota((HEAD_DIM, TILE), 1) % TOKENS + own_core * TOKENS
            row = iota((HEAD_DIM, TILE), 0)
            hidden = jnp.logical_or(row == 0, row > token)
            q_aug[HEAD_DIM:, lanes] = jnp.where(hidden, blocked_score, 0.0).astype(bf16)
            packed[:, lanes] = none


def prep(info, prompt_q, resp_q, prompt_grad, resp_grad, recv, kv_own, kv_recv):
    two = pl.BlockSpec((TOKENS, Q_COLS), lambda i, s: (0, s[0]))
    three = pl.BlockSpec((1, TOKENS, Q_COLS), lambda i, s: (0, 0, s[0]))

    def whole(*shape):
        return pl.BlockSpec(shape, lambda i, s: (0,) * len(shape))

    return pl.pallas_call(
        prep_kernel,
        grid_spec=pltpu.PrefetchScalarGridSpec(
            num_scalar_prefetch=1,
            grid=(1,),
            in_specs=[
                two,
                three,
                two,
                three,
                whole(4, TOKENS, Q_COLS),
                whole(BLOCK, KV_COLS),
                whole(BLOCK, KV_COLS),
            ],
            out_specs=[
                whole(2 * HEAD_DIM, LANES),
                whole(HEAD_DIM, LANES),
                whole(TOKENS, 2 * TILE),
                whole(HEAD_DIM + 16, LANES),
            ],
        ),
        out_shape=[
            jax.ShapeDtypeStruct((2 * HEAD_DIM, LANES), bf16),
            jax.ShapeDtypeStruct((HEAD_DIM, LANES), bf16),
            jax.ShapeDtypeStruct((TOKENS, 2 * TILE), bf16),
            jax.ShapeDtypeStruct((HEAD_DIM + 16, LANES), f32),
        ],
        compiler_params=params(),
        name="prep",
    )(info, prompt_q, resp_q, prompt_grad, resp_grad, recv, kv_own, kv_recv)


def forward_kernel(offset, info, kv, q_aug, raised, packed, key_aug, value_rows):
    @pl.when(pl.program_id(0) == 0)
    def _():
        core, z_own, x_own = info[0], info[1], info[2]
        x_here = (x_own + offset) % 4
        row = iota((BLOCK, HEAD_DIM), 1)
        token = (iota((BLOCK, HEAD_DIM), 0) + core * TOKENS) % BLOCK
        first = (row == 0).astype(f32)
        same = jnp.logical_and(row == token, row > 0).astype(f32)
        for p in range(4):
            rows = slice(p * BLOCK, (p + 1) * BLOCK)
            z_here = (z_own + 4 - p) % 4
            later = jnp.logical_or(
                z_here > z_own, jnp.logical_and(z_here == z_own, x_here > x_own)
            )
            diagonal = jnp.logical_and(z_here == z_own, x_here == x_own)
            key_aug[rows, :HEAD_DIM] = kv[rows, :HEAD_DIM]
            key_aug[rows, HEAD_DIM:] = (
                first * later.astype(f32) + same * diagonal.astype(f32)
            ).astype(bf16)
        value_rows[...] = with_ones(kv[:, HEAD_DIM:])

    for s in range(TILE // SUB):
        lanes = slice(s * SUB, (s + 1) * SUB)
        part, info_rows = softmax_part(dot(key_aug[...], q_aug[:, lanes]), value_rows[...])
        raised[:, lanes] = part
        packed[:, lanes] = info_rows


def forward(info, kv, q_aug, offset):
    return pl.pallas_call(
        functools.partial(forward_kernel, offset),
        grid_spec=pltpu.PrefetchScalarGridSpec(
            num_scalar_prefetch=1,
            grid=(4,),
            in_specs=[
                pl.BlockSpec((CHUNK, KV_COLS), lambda j, s: (0, 0)),
                pl.BlockSpec((2 * HEAD_DIM, TILE), lambda j, s: (0, j)),
            ],
            out_specs=[
                pl.BlockSpec((CHUNK, TILE), lambda j, s: (0, j)),
                pl.BlockSpec((HEAD_DIM + 16, TILE), lambda j, s: (0, j)),
            ],
            scratch_shapes=[
                pltpu.VMEM((CHUNK, 2 * HEAD_DIM), bf16),
                pltpu.VMEM((HEAD_DIM + 16, CHUNK), bf16),
            ],
        ),
        out_shape=[
            jax.ShapeDtypeStruct((CHUNK, LANES), bf16),
            jax.ShapeDtypeStruct((HEAD_DIM + 16, LANES), f32),
        ],
        compiler_params=params(),
        cost_estimate=pl.CostEstimate(
            flops=4 * CHUNK * LANES * HEAD_DIM, bytes_accessed=5 * 2**20, transcendentals=0
        ),
        name="forward",
    )(info, kv, q_aug)


def combine_kernel(info, table, grads, part_0, part_1, part_2, part_3, part_own, out, cot_aug, gains):
    j = pl.program_id(0)
    parts = (part_0, part_1, part_2, part_3, part_own)
    tops = [part[HEAD_DIM + 8 : HEAD_DIM + 9, :] for part in parts]
    top = functools.reduce(jnp.maximum, tops)
    factors = [jnp.exp2((one - top) * exp2_scale) for one in tops]
    length = sum(f * part[HEAD_DIM : HEAD_DIM + 1, :] for f, part in zip(factors, parts))
    total = sum(f * part[:HEAD_DIM, :] for f, part in zip(factors, parts))
    inverse = 1.0 / length
    rounded = (total * inverse).astype(bf16)
    out[...] = rounded
    gains[...] = jnp.concatenate(
        [f * inverse for f in factors] + [jnp.zeros((3, TILE), f32)], axis=0
    )
    own = info[1] * 8 + info[2] * 2 + jnp.where(j < 2, info[0], 1 - info[0])
    ids = iota((32, 1), 0)
    here = ids == own

    def pick(column, mask):
        return jnp.sum(
            jnp.where(mask, table[:, column : column + 1], 0.0), axis=0, keepdims=True
        )

    ratio, partner, chosen, count = [pick(column, here) for column in range(4)]
    mate = pick(0, ids.astype(f32) == partner)
    sign = 2.0 * chosen - 1.0
    pair_weight = sign * jax.nn.sigmoid(-pair_beta * (sign * (ratio - mate)))
    token = (iota((1, TILE), 1) % TOKENS).astype(f32)
    weight = jnp.where(token < count, pair_weight, 0.0)
    weight = jnp.where(j % 2 == 1, weight, 1.0)
    cot = (weight * grads[...].astype(f32)).astype(bf16)
    cot_aug[:HEAD_DIM] = cot
    row_dot = -jnp.sum(cot.astype(f32) * rounded.astype(f32), axis=0, keepdims=True)
    high = row_dot.astype(bf16).astype(f32)
    middle = (row_dot - high).astype(bf16).astype(f32)
    low = row_dot - high - middle
    row = iota((HEAD_DIM, TILE), 0)
    cot_aug[HEAD_DIM:] = jnp.where(
        row == 0, high, jnp.where(row == 1, middle, jnp.where(row == 2, low, 0.0))
    ).astype(bf16)


def combine(info, table, grads, parts):
    def tile(rows):
        return pl.BlockSpec((rows, TILE), lambda j, s: (0, j))

    return pl.pallas_call(
        combine_kernel,
        grid_spec=pltpu.PrefetchScalarGridSpec(
            num_scalar_prefetch=1,
            grid=(4,),
            in_specs=[pl.BlockSpec((32, 128), lambda j, s: (0, 0)), tile(HEAD_DIM)]
            + [tile(HEAD_DIM + 16)] * 5,
            out_specs=[tile(HEAD_DIM), tile(2 * HEAD_DIM), tile(8)],
        ),
        out_shape=[
            jax.ShapeDtypeStruct((HEAD_DIM, LANES), bf16),
            jax.ShapeDtypeStruct((2 * HEAD_DIM, LANES), bf16),
            jax.ShapeDtypeStruct((8, LANES), f32),
        ],
        compiler_params=params(),
        name="combine",
    )(info, table, grads, *parts)


def value_aug_of(value_rows):
    column = iota(value_rows.shape, 1)
    return jnp.concatenate([value_rows, (column < 3).astype(f32).astype(bf16)], axis=1)


def backward_kernel(chunk, kv, raised, q_aug, cot_aug, gains, slopes, grad, value_aug, dkey, dvalue):
    j = pl.program_id(0)

    @pl.when(j == 0)
    def _():
        value_aug[...] = value_aug_of(kv[:, HEAD_DIM:])
        dkey[...] = jnp.zeros_like(dkey)
        dvalue[...] = jnp.zeros_like(dvalue)

    gain = gains[chunk : chunk + 1, :]
    scaled_q = (q_aug[...].astype(f32) * (gain * score_scale)).astype(bf16)
    scaled_cot = (cot_aug[:HEAD_DIM].astype(f32) * gain).astype(bf16)
    for s in range(TILE // SUB):
        lanes = slice(s * SUB, (s + 1) * SUB)
        moved = dot(value_aug[...], cot_aug[:, lanes])
        slopes[:, lanes] = (raised[:, lanes].astype(f32) * moved).astype(bf16)
    dkey[...] += dot(slopes[...], scaled_q, 1, 1)
    dvalue[...] += dot(raised[...], scaled_cot, 1, 1)

    @pl.when(j == 3)
    def _():
        grad[:, :HEAD_DIM] = dkey[...].astype(grad.dtype)
        grad[:, HEAD_DIM:] = dvalue[...].astype(grad.dtype)


def backward(kv, raised, q_aug, cot_aug, gains, chunk, kind):
    def tile(rows):
        return pl.BlockSpec((rows, TILE), lambda j: (0, j))

    return pl.pallas_call(
        functools.partial(backward_kernel, chunk),
        grid=(4,),
        in_specs=[
            pl.BlockSpec((CHUNK, KV_COLS), lambda j: (0, 0)),
            tile(CHUNK),
            tile(HEAD_DIM),
            tile(2 * HEAD_DIM),
            tile(8),
        ],
        out_specs=[tile(CHUNK), pl.BlockSpec((CHUNK, KV_COLS), lambda j: (0, 0))],
        scratch_shapes=[
            pltpu.VMEM((CHUNK, 2 * HEAD_DIM), bf16),
            pltpu.VMEM((CHUNK, HEAD_DIM), f32),
            pltpu.VMEM((CHUNK, HEAD_DIM), f32),
        ],
        out_shape=[
            jax.ShapeDtypeStruct((CHUNK, LANES), bf16),
            jax.ShapeDtypeStruct((CHUNK, KV_COLS), kind),
        ],
        compiler_params=params(),
        cost_estimate=pl.CostEstimate(
            flops=6 * CHUNK * LANES * HEAD_DIM, bytes_accessed=6 * 2**20, transcendentals=0
        ),
        name="backward",
    )(kv, raised, q_aug, cot_aug, gains)


def rows_of(turned_rows):
    rows = turned_rows.T
    return jnp.concatenate(
        [rows[g * TOKENS : (g + 1) * TOKENS] for g in range(GROUP)], axis=1
    )


def finish_kernel(
    kv_0, kv_1, kv_2, kv_3, slopes_0, slopes_1, slopes_2, slopes_3,
    kv_own, raised, q_aug, cot_aug, gains, out, result, own_grad, keys, total,
):
    j = pl.program_id(0)

    @pl.when(j == 0)
    def _():
        for chunk, kv in enumerate((kv_0, kv_1, kv_2, kv_3)):
            keys[:, chunk * CHUNK : (chunk + 1) * CHUNK] = kv[:, :HEAD_DIM].T

    acc = None
    for chunk, slopes in enumerate((slopes_0, slopes_1, slopes_2, slopes_3)):
        part = dot(keys[:, chunk * CHUNK : (chunk + 1) * CHUNK], slopes[...])
        part = part * (gains[chunk : chunk + 1, :] * score_scale)
        acc = part if acc is None else acc + part
    total[...] = acc

    @pl.when(j == 1)
    def _():
        gain = gains[4:5, :]
        rows = kv_own[TOKENS:]
        moved = dot(value_aug_of(rows[:, HEAD_DIM:]), cot_aug[...])
        slopes = (raised[...].astype(f32) * moved).astype(bf16)
        total[...] += dot(rows[:, :HEAD_DIM].T, slopes) * (gain * score_scale)
        scaled_q = (q_aug[...].astype(f32) * (gain * score_scale)).astype(bf16)
        scaled_cot = (cot_aug[:HEAD_DIM].astype(f32) * gain).astype(bf16)
        own_grad[:, :HEAD_DIM] = dot(slopes, scaled_q, 1, 1).astype(bf16)
        own_grad[:, HEAD_DIM:] = dot(raised[...], scaled_cot, 1, 1).astype(bf16)

    result[0, 0] = rows_of(out[...].astype(f32)).astype(bf16)
    result[0, 1] = rows_of(total[...]).astype(bf16)


def finish(kvs, slopes, kv_own, raised, q_aug, cot_aug, gains, out, sib):
    def whole(*shape):
        return pl.BlockSpec(shape, lambda j: (0,) * len(shape))

    def tile(rows):
        return pl.BlockSpec((rows, TILE), lambda j: (0, 2 * sib + j))

    return pl.pallas_call(
        finish_kernel,
        grid=(2,),
        in_specs=[whole(CHUNK, KV_COLS)] * 4
        + [tile(CHUNK)] * 4
        + [
            whole(BLOCK, KV_COLS),
            pl.BlockSpec((TOKENS, TILE), lambda j: (0, sib)),
            tile(HEAD_DIM),
            tile(2 * HEAD_DIM),
            tile(8),
            tile(HEAD_DIM),
        ],
        out_specs=[
            pl.BlockSpec((1, 2, TOKENS, Q_COLS), lambda j: (j, 0, 0, 0)),
            whole(TOKENS, KV_COLS),
        ],
        scratch_shapes=[
            pltpu.VMEM((HEAD_DIM, 4 * CHUNK), bf16),
            pltpu.VMEM((HEAD_DIM, TILE), f32),
        ],
        out_shape=[
            jax.ShapeDtypeStruct((2, 2, TOKENS, Q_COLS), bf16),
            jax.ShapeDtypeStruct((TOKENS, KV_COLS), bf16),
        ],
        compiler_params=params(),
        cost_estimate=pl.CostEstimate(
            flops=4 * CHUNK * LANES * HEAD_DIM, bytes_accessed=5 * 2**20, transcendentals=0
        ),
        name="finish",
    )(*kvs, *slopes, kv_own, raised, q_aug, cot_aug, gains, out)


def place_kernel(info, own, recv, own_dkv, recv_dkv, prompt_out, resp_out, prompt_dq, resp_dq, resp_dkv):
    def write(source, dkv):
        prompt_out[...] = source[0, 0]
        prompt_dq[...] = source[0, 1]
        resp_out[0] = source[1, 0]
        resp_dq[0] = source[1, 1]
        resp_dkv[0] = dkv[...]

    @pl.when(pl.program_id(0) == 0)
    def _():
        write(own, own_dkv)

    @pl.when(pl.program_id(0) == 1)
    def _():
        write(recv, recv_dkv)


def place(info, own, recv, own_dkv, recv_dkv):
    def whole(*shape):
        return pl.BlockSpec(shape, lambda i, s: (0,) * len(shape))

    def column(i, s):
        return s[0] + i - 2 * s[0] * i

    two = pl.BlockSpec((TOKENS, Q_COLS), lambda i, s: (0, column(i, s)))
    three = pl.BlockSpec((1, TOKENS, Q_COLS), lambda i, s: (0, 0, column(i, s)))
    prompt = jax.ShapeDtypeStruct((TOKENS, 2 * Q_COLS), bf16)
    resp = jax.ShapeDtypeStruct((1, TOKENS, 2 * Q_COLS), bf16)
    return pl.pallas_call(
        place_kernel,
        grid_spec=pltpu.PrefetchScalarGridSpec(
            num_scalar_prefetch=1,
            grid=(2,),
            in_specs=[whole(2, 2, TOKENS, Q_COLS)] * 2 + [whole(TOKENS, KV_COLS)] * 2,
            out_specs=[
                two,
                three,
                two,
                three,
                pl.BlockSpec((1, TOKENS, KV_COLS), lambda i, s: (0, 0, column(i, s))),
            ],
        ),
        out_shape=[
            prompt,
            resp,
            prompt,
            resp,
            jax.ShapeDtypeStruct((1, TOKENS, 2 * KV_COLS), bf16),
        ],
        compiler_params=params(),
        name="place",
    )(info, own, recv, own_dkv, recv_dkv)


def sum_x_kernel(own, recv_1, recv_2, recv_3, first, second, third, fourth):
    for p, out in enumerate((first, second, third, fourth)):
        rows = slice(p * BLOCK, (p + 1) * BLOCK)
        total = own[rows]
        for recv in (recv_1, recv_2, recv_3):
            total = total + recv[rows].astype(f32)
        out[...] = total.astype(out.dtype)


def sum_x(own, recvs):
    return pl.pallas_call(
        sum_x_kernel,
        out_shape=[
            jax.ShapeDtypeStruct((BLOCK, KV_COLS), f32 if p == 0 else bf16) for p in range(4)
        ],
        compiler_params=params(),
        name="sum_x",
    )(own, *recvs)


def sum_z_kernel(own, recv_1, recv_2, recv_3, kept, sent):
    total = own[...]
    for recv in (recv_1, recv_2, recv_3):
        total = total + recv[...].astype(f32)
    kept[...] = total[:TOKENS].astype(bf16)
    sent[...] = total[TOKENS:].astype(bf16)


def sum_z(own, recvs):
    return pl.pallas_call(
        sum_z_kernel,
        out_shape=[jax.ShapeDtypeStruct((TOKENS, KV_COLS), bf16)] * 2,
        compiler_params=params(),
        name="sum_z",
    )(own, *recvs)


def shards(
    prompt_q,
    prompt_kv,
    resp_q,
    resp_kv,
    prompt_grad,
    resp_grad,
    resp_len,
    logratio,
    partner,
    chosen,
):
    own_index = lax.axis_index("resp")
    core = own_index % 2
    info = jnp.stack([core, own_index // 8, own_index // 2 % 4]).astype(jnp.int32)

    kv_own, kv_send = pack_kv(info, prompt_kv, resp_kv)
    kv_recv = swap_core(kv_send)
    q_send = pack_q(info, prompt_q, resp_q, prompt_grad, resp_grad)
    q_recv = swap_core(q_send)

    scalars = jnp.concatenate(
        [
            logratio,
            partner.astype(f32),
            chosen.astype(f32),
            resp_len.astype(f32),
            jnp.zeros((124,), f32),
        ]
    )
    table = lax.all_to_all(
        jnp.broadcast_to(scalars[None, :], (32, 128)), "resp", split_axis=0, concat_axis=0, tiled=True
    )

    block = jnp.concatenate([kv_own[:TOKENS], kv_recv[:TOKENS]], axis=0)
    chunk_own = jnp.concatenate([block] + [shift_z(block, step) for step in (1, 2, 3)], axis=0)
    offsets = (0, 3, 1, 2)
    kvs = [chunk_own] + [shift_x(chunk_own, 4 - offset) for offset in offsets[1:]]

    q_aug, grads, raised_own, part_own = prep(
        info, prompt_q, resp_q, prompt_grad, resp_grad, q_recv, kv_own, kv_recv
    )
    raised, parts = [], []
    for kv, offset in zip(kvs, offsets):
        one, part = forward(info, kv, q_aug, offset)
        raised.append(one)
        parts.append(part)
    out, cot_aug, gains = combine(info, table, grads, parts + [part_own])

    slopes = [None] * 4
    returned = []
    for chunk in (3, 2, 1, 0):
        kind = bf16 if chunk else f32
        slopes[chunk], grad = backward(
            kvs[chunk], raised[chunk], q_aug, cot_aug, gains, chunk, kind
        )
        returned.append(shift_x(grad, offsets[chunk]) if chunk else grad)

    blocks = sum_x(returned[3], returned[:3])
    recvs = [shift_z(blocks[p], 4 - p) for p in (1, 2, 3)]

    sib_result, sib_dkv = finish(
        kvs, slopes, kv_recv, raised_own, q_aug, cot_aug, gains, out, 1
    )
    recv_result = swap_core(sib_result)
    recv_dkv = swap_core(sib_dkv)
    own_result, own_dkv = finish(
        kvs, slopes, kv_own, raised_own, q_aug, cot_aug, gains, out, 0
    )
    prompt_out, resp_out, prompt_dq, resp_dq, resp_dkv = place(
        info, own_result, recv_result, own_dkv, recv_dkv
    )

    kept, sent = sum_z(blocks[0], recvs)
    other = swap_core(sent)
    prompt_dkv = jnp.where(
        core == 0,
        jnp.concatenate([kept, other], axis=1),
        jnp.concatenate([other, kept], axis=1),
    )
    return (prompt_out, resp_out, prompt_dq, resp_dq, prompt_dkv, resp_dkv)


def solution(mesh):
    return jax.shard_map(
        shards,
        mesh=mesh,
        in_specs=(
            P(("batch", "resp"), "head"),
            P(("batch", "resp"), "head"),
            P(("batch", "resp"), None, "head"),
            P(("batch", "resp"), None, "head"),
            P(("batch", "resp"), "head"),
            P(("batch", "resp"), None, "head"),
            P(("batch", "resp")),
            P(("batch", "resp")),
            P(("batch", "resp")),
            P(("batch", "resp")),
        ),
        out_specs=(
            P(("batch", "resp"), "head"),
            P(("batch", "resp"), None, "head"),
            P(("batch", "resp"), "head"),
            P(("batch", "resp"), None, "head"),
            P(("batch", "resp"), "head"),
            P(("batch", "resp"), None, "head"),
        ),
        check_vma=False,
    )
```

time: 245 us -> 138 us (0.56)
  blocking collectives: 70.4 us -> 0 us
  matrix products: 49.2 us -> 0 us
  Pallas kernels: 0 us -> 45.5 us
  starting transfers between devices: 9.58 us -> 32.7 us
  other arithmetic: 18.7 us -> 0.73 us
  between operations: 18 us -> 3.74 us
  waiting for transfers between devices: 33.6 us -> 20.7 us
  local copies, waits for them, and re-layouts: 44.1 us -> 33.3 us
    unnamed x1 -> x0, blocking collectives: 70.4 us -> none
    pallas_call x0 -> x17, Pallas kernels: none -> 45.5 us  [the longest x4 18.8 us: forward(): pl.pallas_call(functools.partial(forward_kernel, offset), grid_spec=pltpu...]
    all_to_all x1, waiting for transfers between devices: 33 us -> 0.01 us  [shards(): lax.all_to_all(jnp.broadcast_to(scalars[None, :], (32, 128)), 'resp', spl...]
    dot_general x24 -> x0, matrix products: 32.3 us -> none  [the longest x6 7.31 us: key_grads(): jnp.einsum('gnm,ngd->md', weight_block, cotangent, preferred_element_type...]
    ppermute x0 -> x17, starting transfers between devices: none -> 24.2 us  [the longest x5 10.4 us: swap_core(): return lax.ppermute(value, 'resp', [(r, r ^ 1) for r in range(32)])]
    ppermute x0 -> x17, waiting for transfers between devices: none -> 20.7 us  [the longest x6 11.6 us: shift_x(): return lax.ppermute(value, 'resp', pairs)]
    unnamed x99 -> x88, local copies, waits for them, and re-layouts: 13.4 us -> 32.6 us
    sub x4 -> x0, matrix products: 16.9 us -> none  [head_pass(): raised = jnp.exp(scores - row_max)]
  transfers between devices with their start and end apart: 2 -> 18, of which waited for: 1 -> 6; matrix products, arithmetic and copies ran while one was open for 10% -> 1% of each run, Pallas kernels for 0% -> 18%
where the time goes in v1:
time: 138 us; the launch traced here: 137 us
  Pallas kernels  45.5 us (33%)
  local copies, waits for them, and re-layouts  33.3 us (24%)
  starting transfers between devices  32.7 us (24%)
  waiting for transfers between devices  20.7 us (15%)
  between operations  3.74 us (3%)
    unnamed x88, local copies, waits for them, and re-layouts  32.6 us
    pallas_call x4, Pallas kernels, forward(): pl.pallas_call(functools.partial(forward_kernel, offset), grid_spec=pltpu...  18.8 us
    pallas_call x4, Pallas kernels, backward(): pl.pallas_call(functools.partial(backward_kernel, chunk), grid=(4,), in_s...  11.8 us
    ppermute x6, waiting for transfers between devices, shift_x(): return lax.ppermute(value, 'resp', pairs)  11.6 us
    ppermute x5, starting transfers between devices, swap_core(): return lax.ppermute(value, 'resp', [(r, r ^ 1) for r in range(32)])  10.4 us
    all_to_all x1, starting transfers between devices, shards(): lax.all_to_all(jnp.broadcast_to(scalars[None, :], (32, 128)), 'resp', spl...  8.56 us
    ppermute x6, waiting for transfers between devices, shift_z(): return lax.ppermute(value, 'resp', pairs)  8.16 us
    ppermute x6, starting transfers between devices, shift_z(): return lax.ppermute(value, 'resp', pairs)  7.03 us
  transfers between devices with their start and end apart: 18, of which 6 were waited for; matrix products, arithmetic and copies ran while one was open for 1% of the time, Pallas kernels for 18%

profile of v1, /device:TPU:1, one launch (start us, length us, event | category | flops | bytes accessed | tf_op | source)
XLA Modules:
  0.0 136.7 jit_solution(2005103616877532625)
XLA Ops:
  3.0 3.3 %collective-permute-start = (bf16[128,256]{1,0:T(8,128)(2,1)S(1)}, bf16[128,256]{1,0:T(8,128)(2,1)S(1)}, u32[]{:S(2)}, u32[]{:S(2)}) collective-permute-start(bf16[128,256]{1,0:T(8,128)(2,1)S(1)} %get-tuple-element.47), channel_id=1, source_target_pairs={{0,4},{4,0},{8,12},{12,8},{16,20},{20,16},{24,28},{28,24},{32,36},... | collective-permute-start | bytes 196616 | tf_op jit(solution)/shard_map/ppermute | solution.py:46
  8.3 0.9 copy-done.30
  9.3 0.9 copy-done.32
  12.4 3.4 %collective-permute-start.3 = (bf16[128,256]{1,0:T(8,128)(2,1)S(1)}, bf16[128,256]{1,0:T(8,128)(2,1)S(1)}, u32[]{:S(2)}, u32[]{:S(2)}) collective-permute-start(bf16[128,256]{1,0:T(8,128)(2,1)S(1)} %pad_maximum_fusion), channel_id=1, source_target_pairs={{0,96},{4,100},{8,104},{12,108},{16,112},{20,116},{24,120},{28,124... | collective-permute-start | bytes 196616 | tf_op jit(solution)/shard_map/ppermute | solution.py:51
  15.8 5.8 %collective-permute-done.2 = bf16[128,256]{1,0:T(8,128)(2,1)S(1)} collective-permute-done((bf16[128,256]{1,0:T(8,128)(2,1)S(1)}, bf16[128,256]{1,0:T(8,128)(2,1)S(1)}, u32[]{:S(2)}, u32[]{:S(2)}) %collective-permute-start.2) | collective-permute-done | bytes 65568 | tf_op jit(solution)/shard_map/ppermute | solution.py:51
  27.4 8.6 %all-to-all-start = ((f32[32,1,128]{2,1,0:T(1,128)}), f32[32,1,128]{2,1,0:T(1,128)S(1)}, u32[]{:S(2)}, u32[]{:S(2)}) async-start(f32[32,1,128]{2,1,0:T(1,128)} %broadcast_in_dim.10), calls=%async_computation | async-start | bytes 32768 | tf_op jit(solution)/shard_map/all_to_all | solution.py:594
  36.8 1.0 copy-done.39
  37.8 1.2 prep.1
  39.0 1.0 copy-done.18
  40.9 4.7 %forward.4 = (bf16[512,2048]{1,0:T(8,128)(2,1)S(1)}, f32[144,2048]{1,0:T(8,128)S(1)}) custom-call(s32[3]{0:T(128)S(1)} %pad_add_fusion.info, bf16[512,256]{1,0:T(8,128)(2,1)S(1)} %constant_dynamic-update-slice_fusion.kv.kv_0, bf16[256,2048]{1,0:T(8,128)(2,1)S(1)} %get-tuple-element.48.q_aug), custom_call_target="tpu_custom_call" | custom-call | flops 536870912 | bytes 5242880 | tf_op jit(solution)/shard_map/forward/pallas_call | solution.py:235
  45.6 1.3 copy-done.10
  46.9 4.7 %forward.7 = (bf16[512,2048]{1,0:T(8,128)(2,1)S(1)}, f32[144,2048]{1,0:T(8,128)S(1)}) custom-call(s32[3]{0:T(128)S(1)} %pad_add_fusion.info, bf16[512,256]{1,0:T(8,128)(2,1)S(1)} %collective-permute-done.6.kv.kv_3, bf16[256,2048]{1,0:T(8,128)(2,1)S(1)} %get-tuple-element.48.q_aug), custom_call_target="tpu_custom_call" | custom-call | flops 536870912 | bytes 5242880 | tf_op jit(solution)/shard_map/forward/pallas_call | solution.py:235
  51.6 1.4 %copy-done.12 = bf16[512,2048]{1,0:T(8,128)(2,1)} copy-done((bf16[512,2048]{1,0:T(8,128)(2,1)}, bf16[512,2048]{1,0:T(8,128)(2,1)S(1)}, u32[]{:S(2)}) %copy-start.12) | copy-done | bytes 2097176
  53.0 1.1 copy-done.22
  54.1 4.7 %forward.6 = (bf16[512,2048]{1,0:T(8,128)(2,1)S(1)}, f32[144,2048]{1,0:T(8,128)S(1)}) custom-call(s32[3]{0:T(128)S(1)} %pad_add_fusion.info, bf16[512,256]{1,0:T(8,128)(2,1)S(1)} %collective-permute-done.5.kv.kv_2, bf16[256,2048]{1,0:T(8,128)(2,1)S(1)} %get-tuple-element.48.q_aug), custom_call_target="tpu_custom_call" | custom-call | flops 536870912 | bytes 5242880 | tf_op jit(solution)/shard_map/forward/pallas_call | solution.py:235
  58.8 1.3 copy-done.14
  60.1 1.0 copy-done.24
  61.1 4.7 %forward.5 = (bf16[512,2048]{1,0:T(8,128)(2,1)S(1)}, f32[144,2048]{1,0:T(8,128)S(1)}) custom-call(s32[3]{0:T(128)S(1)} %pad_add_fusion.info, bf16[512,256]{1,0:T(8,128)(2,1)S(1)} %collective-permute-done.4.kv.kv_1, bf16[256,2048]{1,0:T(8,128)(2,1)S(1)} %get-tuple-element.48.q_aug), custom_call_target="tpu_custom_call" | custom-call | flops 536870912 | bytes 5242880 | tf_op jit(solution)/shard_map/forward/pallas_call | solution.py:235
  65.9 1.4 copy-done.16
  67.2 1.0 copy-done.26
  68.2 1.3 copy-done.19
  69.5 1.3 copy-done.21
  70.8 1.3 copy-done.23
  72.0 1.3 copy-done.25
  73.3 1.3 copy-done.27
  74.6 1.0 copy-done.37
  75.6 3.0 %combine.1 = (bf16[128,2048]{1,0:T(8,128)(2,1)S(1)}, bf16[256,2048]{1,0:T(8,128)(2,1)S(1)}, f32[8,2048]{1,0:T(8,128)S(1)}) custom-call(s32[3]{0:T(128)S(1)} %pad_add_fusion.info, f32[32,128]{1,0:T(8,128)S(1)} %bitcast.4, bf16[128,2048]{1,0:T(8,128)(2,1)S(1)} %copy-done.37, f32[144,2048]{1,0:T(8,128)S(1)} %copy-done.21, f32[144,2048]{1,0:T(8,128)S(1)} %copy-done.27, ...), custom_call_target="tpu_custom_call" | custom-call | tf_op jit(solution)/shard_map/combine/pallas_call | solution.py:311
  78.7 2.9 %backward.4 = (bf16[512,2048]{1,0:T(8,128)(2,1)S(1)}, f32[512,256]{1,0:T(8,128)S(1)}) custom-call(bf16[512,256]{1,0:T(8,128)(2,1)S(1)} %constant_dynamic-update-slice_fusion.kv.kv_0, bf16[512,2048]{1,0:T(8,128)(2,1)S(1)} %copy-done.11, bf16[256,2048]{1,0:T(8,128)(2,1)S(1)} %get-tuple-element.48.q_aug, bf16[256,2048]{1,0:T(8,128)(2,1)S(1)} %get-tuple-element.56.cot_aug, ...), custom_call_target="tpu_custom_call" | custom-call | flops 805306368 | bytes 6291456 | tf_op jit(solution)/shard_map/backward/pallas_call | solution.py:364
  81.7 2.9 %backward.7 = (bf16[512,2048]{1,0:T(8,128)(2,1)S(1)}, bf16[512,256]{1,0:T(8,128)(2,1)S(1)}) custom-call(bf16[512,256]{1,0:T(8,128)(2,1)S(1)} %collective-permute-done.6.kv.kv_3, bf16[512,2048]{1,0:T(8,128)(2,1)S(1)} %copy-done.13, bf16[256,2048]{1,0:T(8,128)(2,1)S(1)} %get-tuple-element.48.q_aug, bf16[256,2048]{1,0:T(8,128)(2,1)S(1)} %get-tuple-element.56.cot_aug, ...), custom_call_target="tpu_custom_call" | custom-call | flops 805306368 | bytes 6291456 | tf_op jit(solution)/shard_map/backward/pallas_call | solution.py:364
  84.6 2.9 %backward.6 = (bf16[512,2048]{1,0:T(8,128)(2,1)S(1)}, bf16[512,256]{1,0:T(8,128)(2,1)S(1)}) custom-call(bf16[512,256]{1,0:T(8,128)(2,1)S(1)} %collective-permute-done.5.kv.kv_2, bf16[512,2048]{1,0:T(8,128)(2,1)S(1)} %copy-done.15, bf16[256,2048]{1,0:T(8,128)(2,1)S(1)} %get-tuple-element.48.q_aug, bf16[256,2048]{1,0:T(8,128)(2,1)S(1)} %get-tuple-element.56.cot_aug, ...), custom_call_target="tpu_custom_call" | custom-call | flops 805306368 | bytes 6291456 | tf_op jit(solution)/shard_map/backward/pallas_call | solution.py:364
  87.6 2.9 %backward.5 = (bf16[512,2048]{1,0:T(8,128)(2,1)S(1)}, bf16[512,256]{1,0:T(8,128)(2,1)S(1)}) custom-call(bf16[512,256]{1,0:T(8,128)(2,1)S(1)} %collective-permute-done.4.kv.kv_1, bf16[512,2048]{1,0:T(8,128)(2,1)S(1)} %copy-done.17, bf16[256,2048]{1,0:T(8,128)(2,1)S(1)} %get-tuple-element.48.q_aug, bf16[256,2048]{1,0:T(8,128)(2,1)S(1)} %get-tuple-element.56.cot_aug, ...), custom_call_target="tpu_custom_call" | custom-call | flops 805306368 | bytes 6291456 | tf_op jit(solution)/shard_map/backward/pallas_call | solution.py:364
  90.6 3.0 %finish.3 = (bf16[2,2,64,1024]{3,2,1,0:T(8,128)(2,1)}, bf16[64,256]{1,0:T(8,128)(2,1)S(1)}) custom-call(bf16[512,256]{1,0:T(8,128)(2,1)S(1)} %constant_dynamic-update-slice_fusion.kv.kv_0, bf16[512,256]{1,0:T(8,128)(2,1)S(1)} %collective-permute-done.4.kv.kv_1, bf16[512,256]{1,0:T(8,128)(2,1)S(1)} %collective-permute-done.5.kv.kv_2, ...), custom_call_target="tpu_custom_call" | custom-call | flops 536870912 | bytes 5242880 | tf_op jit(solution)/shard_map/finish/pallas_call | solution.py:440
  94.0 2.5 %collective-permute-start.12 = (bf16[512,256]{1,0:T(8,128)(2,1)S(1)}, bf16[512,256]{1,0:T(8,128)(2,1)S(1)}, u32[]{:S(2)}, u32[]{:S(2)}) collective-permute-start(bf16[512,256]{1,0:T(8,128)(2,1)S(1)} %get-tuple-element.78), channel_id=1, source_target_pairs={{0,24},{4,28},{8,0},{12,4},{16,8},{20,12},{24,16},{28,20},{32,56},... | collective-permute-start | bytes 786440 | tf_op jit(solution)/shard_map/ppermute | solution.py:56
  96.6 1.8 %collective-permute-start.10 = (bf16[512,256]{1,0:T(8,128)(2,1)S(1)}, bf16[512,256]{1,0:T(8,128)(2,1)S(1)}, u32[]{:S(2)}, u32[]{:S(2)}) collective-permute-start(bf16[512,256]{1,0:T(8,128)(2,1)S(1)} %get-tuple-element.76), channel_id=1, source_target_pairs={{0,16},{4,20},{8,24},{12,28},{16,0},{20,4},{24,8},{28,12},{32,48},... | collective-permute-start | bytes 786440 | tf_op jit(solution)/shard_map/ppermute | solution.py:56
  98.3 9.3 %collective-permute-done.12.recv_3 = bf16[512,256]{1,0:T(8,128)(2,1)S(1)} collective-permute-done((bf16[512,256]{1,0:T(8,128)(2,1)S(1)}, bf16[512,256]{1,0:T(8,128)(2,1)S(1)}, u32[]{:S(2)}, u32[]{:S(2)}) %collective-permute-start.12) | collective-permute-done | bytes 262176 | tf_op jit(solution)/shard_map/ppermute | solution.py:56
  107.6 2.4 %collective-permute-done.10.recv_1 = bf16[512,256]{1,0:T(8,128)(2,1)S(1)} collective-permute-done((bf16[512,256]{1,0:T(8,128)(2,1)S(1)}, bf16[512,256]{1,0:T(8,128)(2,1)S(1)}, u32[]{:S(2)}, u32[]{:S(2)}) %collective-permute-start.10) | collective-permute-done | bytes 262176 | tf_op jit(solution)/shard_map/ppermute | solution.py:56
  110.7 3.1 %collective-permute-start.13 = (bf16[128,256]{1,0:T(8,128)(2,1)}, bf16[128,256]{1,0:T(8,128)(2,1)}, u32[]{:S(2)}, u32[]{:S(2)}) collective-permute-start(bf16[128,256]{1,0:T(8,128)(2,1)} %get-tuple-element.80), channel_id=1, source_target_pairs={{0,96},{4,100},{8,104},{12,108},{16,112},{20,116},{24,120},{28,124... | collective-permute-start | bytes 196616 | tf_op jit(solution)/shard_map/ppermute | solution.py:51
  114.3 3.0 %collective-permute-start.9 = (bf16[64,256]{1,0:T(8,128)(2,1)}, bf16[64,256]{1,0:T(8,128)(2,1)S(1)}, u32[]{:S(2)}, u32[]{:S(2)}) collective-permute-start(bf16[64,256]{1,0:T(8,128)(2,1)} %copy-done.42), channel_id=1, source_target_pairs={{0,4},{4,0},{8,12},{12,8},{16,20},{20,16},{24,28},{28,24},{32,36},... | collective-permute-start | bytes 98312 | tf_op jit(solution)/shard_map/ppermute | solution.py:46
  117.3 1.1 collective-permute-done.14.recv_2
  118.4 1.2 collective-permute-done.15.recv_3
  120.5 3.1 %collective-permute-start.16 = (bf16[64,256]{1,0:T(8,128)(2,1)S(1)}, bf16[64,256]{1,0:T(8,128)(2,1)S(1)}, u32[]{:S(2)}, u32[]{:S(2)}) collective-permute-start(bf16[64,256]{1,0:T(8,128)(2,1)S(1)} %get-tuple-element.84), channel_id=1, source_target_pairs={{0,4},{4,0},{8,12},{12,8},{16,20},{20,16},{24,28},{28,24},{32,36},... | collective-permute-start | bytes 98312 | tf_op jit(solution)/shard_map/ppermute | solution.py:46
  123.6 1.6 %copy-done.1 = bf16[512,2048]{1,0:T(8,128)(2,1)S(1)} copy-done((bf16[512,2048]{1,0:T(8,128)(2,1)S(1)}, bf16[512,2048]{1,0:T(8,128)(2,1)}, u32[]{:S(2)}) %copy-start.1) | copy-done | bytes 2097176
  125.2 1.6 %copy-done.3 = bf16[512,2048]{1,0:T(8,128)(2,1)S(1)} copy-done((bf16[512,2048]{1,0:T(8,128)(2,1)S(1)}, bf16[512,2048]{1,0:T(8,128)(2,1)}, u32[]{:S(2)}) %copy-start.3) | copy-done | bytes 2097176
  126.8 1.6 %copy-done.5 = bf16[512,2048]{1,0:T(8,128)(2,1)S(1)} copy-done((bf16[512,2048]{1,0:T(8,128)(2,1)S(1)}, bf16[512,2048]{1,0:T(8,128)(2,1)}, u32[]{:S(2)}) %copy-start.5) | copy-done | bytes 2097176
  128.4 1.6 %copy-done.7 = bf16[512,2048]{1,0:T(8,128)(2,1)S(1)} copy-done((bf16[512,2048]{1,0:T(8,128)(2,1)S(1)}, bf16[512,2048]{1,0:T(8,128)(2,1)}, u32[]{:S(2)}) %copy-start.7) | copy-done | bytes 2097176
  130.0 1.0 copy-done.9
  131.0 2.3 %finish.2 = (bf16[2,2,64,1024]{3,2,1,0:T(8,128)(2,1)S(1)}, bf16[64,256]{1,0:T(8,128)(2,1)S(1)}) custom-call(bf16[512,256]{1,0:T(8,128)(2,1)S(1)} %constant_dynamic-update-slice_fusion.kv.kv_0, bf16[512,256]{1,0:T(8,128)(2,1)S(1)} %collective-permute-done.4.kv.kv_1, bf16[512,256]{1,0:T(8,128)(2,1)S(1)} %collective-permute-done.5.kv.kv_2, ...), custom_call_target="tpu_custom_call" | custom-call | flops 536870912 | bytes 5242880 | tf_op jit(solution)/shard_map/finish/pallas_call | solution.py:440
  134.0 2.7 %place.1 = (bf16[64,2048]{1,0:T(8,128)(2,1)}, bf16[1,64,2048]{2,1,0:T(8,128)(2,1)}, bf16[64,2048]{1,0:T(8,128)(2,1)}, bf16[1,64,2048]{2,1,0:T(8,128)(2,1)}, bf16[1,64,512]{2,1,0:T(8,128)(2,1)}) custom-call(s32[3]{0:T(128)S(1)} %pad_add_fusion.info, bf16[2,2,64,1024]{3,2,1,0:T(8,128)(2,1)S(1)} %get-tuple-element.67.own, ...), custom_call_target="tpu_custom_call" | custom-call | tf_op jit(solution)/shard_map/place/pallas_call | solution.py:501
  (102 shorter events, 14.5 us)
Async XLA Ops:
  0.6 36.1 %copy-start.31 = (bf16[1,64,2048]{2,1,0:T(8,128)(2,1)S(1)}, bf16[1,64,2048]{2,1,0:T(8,128)(2,1)}, u32[]{:S(2)}) copy-start(bf16[1,64,2048]{2,1,0:T(8,128)(2,1)} %rq.3) | copy-start | bytes 786436
  0.6 36.1 %copy-start.29 = (bf16[64,2048]{1,0:T(8,128)(2,1)S(1)}, bf16[64,2048]{1,0:T(8,128)(2,1)}, u32[]{:S(2)}) copy-start(bf16[64,2048]{1,0:T(8,128)(2,1)} %pq.3) | copy-start | bytes 786436
  3.0 4.2 %collective-permute-start = (bf16[128,256]{1,0:T(8,128)(2,1)S(1)}, bf16[128,256]{1,0:T(8,128)(2,1)S(1)}, u32[]{:S(2)}, u32[]{:S(2)}) collective-permute-start(bf16[128,256]{1,0:T(8,128)(2,1)S(1)} %get-tuple-element.47), channel_id=1, source_target_pairs={{0,4},{4,0},{8,12},{12,8},{16,20},{20,16},{24,28},{28,24},{32,36},... | collective-permute-start | bytes 196616 | tf_op jit(solution)/shard_map/ppermute | solution.py:46
  7.3 8.5 %collective-permute-start.1 = (bf16[128,256]{1,0:T(8,128)(2,1)S(1)}, bf16[128,256]{1,0:T(8,128)(2,1)S(1)}, u32[]{:S(2)}, u32[]{:S(2)}) collective-permute-start(bf16[128,256]{1,0:T(8,128)(2,1)S(1)} %pad_maximum_fusion), channel_id=1, source_target_pairs={{0,32},{4,36},{8,40},{12,44},{16,48},{20,52},{24,56},{28,60},{32,6... | collective-permute-start | bytes 196616 | tf_op jit(solution)/shard_map/ppermute | solution.py:51
  11.2 25.6 %copy-start.33 = (bf16[64,2048]{1,0:T(8,128)(2,1)S(1)}, bf16[64,2048]{1,0:T(8,128)(2,1)}, u32[]{:S(2)}) copy-start(bf16[64,2048]{1,0:T(8,128)(2,1)} %pg.3) | copy-start | bytes 786436
  11.2 25.6 %copy-start.35 = (bf16[1,64,2048]{2,1,0:T(8,128)(2,1)S(1)}, bf16[1,64,2048]{2,1,0:T(8,128)(2,1)}, u32[]{:S(2)}) copy-start(bf16[1,64,2048]{2,1,0:T(8,128)(2,1)} %rg.3) | copy-start | bytes 786436
  11.8 24.2 %collective-permute-start.7 = (bf16[4,64,1024]{2,1,0:T(8,128)(2,1)S(1)}, bf16[4,64,1024]{2,1,0:T(8,128)(2,1)S(1)}, u32[]{:S(2)}, u32[]{:S(2)}) collective-permute-start(bf16[4,64,1024]{2,1,0:T(8,128)(2,1)S(1)} %pack_q.1), channel_id=1, source_target_pairs={{0,4},{4,0},{8,12},{12,8},{16,20},{20,16},{24,28},{28,24},{32,36},... | collective-permute-start | bytes 1572872 | tf_op jit(solution)/shard_map/ppermute | solution.py:46
  12.4 9.2 %collective-permute-start.3 = (bf16[128,256]{1,0:T(8,128)(2,1)S(1)}, bf16[128,256]{1,0:T(8,128)(2,1)S(1)}, u32[]{:S(2)}, u32[]{:S(2)}) collective-permute-start(bf16[128,256]{1,0:T(8,128)(2,1)S(1)} %pad_maximum_fusion), channel_id=1, source_target_pairs={{0,96},{4,100},{8,104},{12,108},{16,112},{20,116},{24,120},{28,124... | collective-permute-start | bytes 196616 | tf_op jit(solution)/shard_map/ppermute | solution.py:51
  15.8 5.8 %collective-permute-start.2 = (bf16[128,256]{1,0:T(8,128)(2,1)S(1)}, bf16[128,256]{1,0:T(8,128)(2,1)S(1)}, u32[]{:S(2)}, u32[]{:S(2)}) collective-permute-start(bf16[128,256]{1,0:T(8,128)(2,1)S(1)} %pad_maximum_fusion), channel_id=1, source_target_pairs={{0,64},{4,68},{8,72},{12,76},{16,80},{20,84},{24,88},{28,92},{32,9... | collective-permute-start | bytes 196616 | tf_op jit(solution)/shard_map/ppermute | solution.py:51
  21.6 25.3 %collective-permute-start.6 = (bf16[512,256]{1,0:T(8,128)(2,1)S(1)}, bf16[512,256]{1,0:T(8,128)(2,1)S(1)}, u32[]{:S(2)}, u32[]{:S(2)}) collective-permute-start(bf16[512,256]{1,0:T(8,128)(2,1)S(1)} %constant_dynamic-update-slice_fusion.kv.kv_0), channel_id=1, source_target_pairs={{0,16},{4,20},{8,24},{12,28},{16,0},{20,4},{24,8},{28,12},{32,48},... | collective-permute-start | bytes 786440 | tf_op jit(solution)/shard_map/ppermute | solution.py:56
  22.6 31.5 %collective-permute-start.5 = (bf16[512,256]{1,0:T(8,128)(2,1)S(1)}, bf16[512,256]{1,0:T(8,128)(2,1)S(1)}, u32[]{:S(2)}, u32[]{:S(2)}) collective-permute-start(bf16[512,256]{1,0:T(8,128)(2,1)S(1)} %constant_dynamic-update-slice_fusion.kv.kv_0), channel_id=1, source_target_pairs={{0,24},{4,28},{8,0},{12,4},{16,8},{20,12},{24,16},{28,20},{32,56},... | collective-permute-start | bytes 786440 | tf_op jit(solution)/shard_map/ppermute | solution.py:56
  23.4 37.7 %collective-permute-start.4 = (bf16[512,256]{1,0:T(8,128)(2,1)S(1)}, bf16[512,256]{1,0:T(8,128)(2,1)S(1)}, u32[]{:S(2)}, u32[]{:S(2)}) collective-permute-start(bf16[512,256]{1,0:T(8,128)(2,1)S(1)} %constant_dynamic-update-slice_fusion.kv.kv_0), channel_id=1, source_target_pairs={{0,8},{4,12},{8,16},{12,20},{16,24},{20,28},{24,0},{28,4},{32,40},... | collective-permute-start | bytes 786440 | tf_op jit(solution)/shard_map/ppermute | solution.py:56
  27.4 40.9 %all-to-all-start = ((f32[32,1,128]{2,1,0:T(1,128)}), f32[32,1,128]{2,1,0:T(1,128)S(1)}, u32[]{:S(2)}, u32[]{:S(2)}) async-start(f32[32,1,128]{2,1,0:T(1,128)} %broadcast_in_dim.10), calls=%async_computation | async-start | bytes 32768 | tf_op jit(solution)/shard_map/all_to_all | solution.py:594
  39.0 1.0 copy-start.18
  45.6 1.3 copy-start.10
  46.9 14.3 %copy-start.20 = (f32[144,2048]{1,0:T(8,128)}, f32[144,2048]{1,0:T(8,128)S(1)}, u32[]{:S(2)}) copy-start(f32[144,2048]{1,0:T(8,128)S(1)} %get-tuple-element.51.part_0) | copy-start | bytes 3538948
  51.6 1.4 %copy-start.12 = (bf16[512,2048]{1,0:T(8,128)(2,1)}, bf16[512,2048]{1,0:T(8,128)(2,1)S(1)}, u32[]{:S(2)}) copy-start(bf16[512,2048]{1,0:T(8,128)(2,1)S(1)} %get-tuple-element.63.raised) | copy-start | bytes 6291460
  53.0 1.1 copy-start.22
  58.8 1.4 copy-start.14
  65.8 1.4 copy-start.16
  68.2 1.3 copy-start.19
  69.5 1.3 copy-start.21
  70.8 1.3 copy-start.23
  72.0 1.3 copy-start.25
  73.3 1.3 copy-start.27
  75.6 3.0 %copy-start.11 = (bf16[512,2048]{1,0:T(8,128)(2,1)S(1)}, bf16[512,2048]{1,0:T(8,128)(2,1)}, u32[]{:S(2)}) copy-start(bf16[512,2048]{1,0:T(8,128)(2,1)} %copy-done.10) | copy-start | bytes 6291460
  78.7 11.9 %copy-start.8 = (bf16[128,2048]{1,0:T(8,128)(2,1)}, bf16[128,2048]{1,0:T(8,128)(2,1)S(1)}, u32[]{:S(2)}) copy-start(bf16[128,2048]{1,0:T(8,128)(2,1)S(1)} %get-tuple-element.66.out) | copy-start | bytes 1572868
  78.7 3.0 %copy-start.13 = (bf16[512,2048]{1,0:T(8,128)(2,1)S(1)}, bf16[512,2048]{1,0:T(8,128)(2,1)}, u32[]{:S(2)}) copy-start(bf16[512,2048]{1,0:T(8,128)(2,1)} %copy-done.12) | copy-start | bytes 6291460
  81.6 8.9 %copy-start = (bf16[512,2048]{1,0:T(8,128)(2,1)}, bf16[512,2048]{1,0:T(8,128)(2,1)S(1)}, u32[]{:S(2)}) copy-start(bf16[512,2048]{1,0:T(8,128)(2,1)S(1)} %get-tuple-element.58.slopes_0) | copy-start | bytes 6291460
  81.7 3.0 %copy-start.15 = (bf16[512,2048]{1,0:T(8,128)(2,1)S(1)}, bf16[512,2048]{1,0:T(8,128)(2,1)}, u32[]{:S(2)}) copy-start(bf16[512,2048]{1,0:T(8,128)(2,1)} %copy-done.14) | copy-start | bytes 6291460
  84.6 6.0 %copy-start.2 = (bf16[512,2048]{1,0:T(8,128)(2,1)}, bf16[512,2048]{1,0:T(8,128)(2,1)S(1)}, u32[]{:S(2)}) copy-start(bf16[512,2048]{1,0:T(8,128)(2,1)S(1)} %get-tuple-element.64.slopes_3) | copy-start | bytes 6291460
  84.6 3.0 %copy-start.17 = (bf16[512,2048]{1,0:T(8,128)(2,1)S(1)}, bf16[512,2048]{1,0:T(8,128)(2,1)}, u32[]{:S(2)}) copy-start(bf16[512,2048]{1,0:T(8,128)(2,1)} %copy-done.16) | copy-start | bytes 6291460
  87.6 3.0 %copy-start.4 = (bf16[512,2048]{1,0:T(8,128)(2,1)}, bf16[512,2048]{1,0:T(8,128)(2,1)S(1)}, u32[]{:S(2)}) copy-start(bf16[512,2048]{1,0:T(8,128)(2,1)S(1)} %get-tuple-element.62.slopes_2) | copy-start | bytes 6291460
  90.6 3.1 %copy-start.6 = (bf16[512,2048]{1,0:T(8,128)(2,1)}, bf16[512,2048]{1,0:T(8,128)(2,1)S(1)}, u32[]{:S(2)}) copy-start(bf16[512,2048]{1,0:T(8,128)(2,1)S(1)} %get-tuple-element.60.slopes_1) | copy-start | bytes 6291460
  93.6 17.1 %copy-start.42 = (bf16[64,256]{1,0:T(8,128)(2,1)}, bf16[64,256]{1,0:T(8,128)(2,1)S(1)}, u32[]{:S(2)}) copy-start(bf16[64,256]{1,0:T(8,128)(2,1)S(1)} %get-tuple-element.70) | copy-start | bytes 98308
  93.6 40.3 %collective-permute-start.8 = (bf16[2,2,64,1024]{3,2,1,0:T(8,128)(2,1)}, bf16[2,2,64,1024]{3,2,1,0:T(8,128)(2,1)}, u32[]{:S(2)}, u32[]{:S(2)}) collective-permute-start(bf16[2,2,64,1024]{3,2,1,0:T(8,128)(2,1)} %get-tuple-element.68), channel_id=1, source_target_pairs={{0,4},{4,0},{8,12},{12,8},{16,20},{20,16},{24,28},{28,24},{32,36},... | collective-permute-start | bytes 1572872 | tf_op jit(solution)/shard_map/ppermute | solution.py:46
  94.0 13.6 %collective-permute-start.12 = (bf16[512,256]{1,0:T(8,128)(2,1)S(1)}, bf16[512,256]{1,0:T(8,128)(2,1)S(1)}, u32[]{:S(2)}, u32[]{:S(2)}) collective-permute-start(bf16[512,256]{1,0:T(8,128)(2,1)S(1)} %get-tuple-element.78), channel_id=1, source_target_pairs={{0,24},{4,28},{8,0},{12,4},{16,8},{20,12},{24,16},{28,20},{32,56},... | collective-permute-start | bytes 786440 | tf_op jit(solution)/shard_map/ppermute | solution.py:56
  96.6 11.0 %collective-permute-start.11 = (bf16[512,256]{1,0:T(8,128)(2,1)S(1)}, bf16[512,256]{1,0:T(8,128)(2,1)S(1)}, u32[]{:S(2)}, u32[]{:S(2)}) collective-permute-start(bf16[512,256]{1,0:T(8,128)(2,1)S(1)} %get-tuple-element.77), channel_id=1, source_target_pairs={{0,8},{4,12},{8,16},{12,20},{16,24},{20,28},{24,0},{28,4},{32,40},... | collective-permute-start | bytes 786440 | tf_op jit(solution)/shard_map/ppermute | solution.py:56
  96.6 13.4 %collective-permute-start.10 = (bf16[512,256]{1,0:T(8,128)(2,1)S(1)}, bf16[512,256]{1,0:T(8,128)(2,1)S(1)}, u32[]{:S(2)}, u32[]{:S(2)}) collective-permute-start(bf16[512,256]{1,0:T(8,128)(2,1)S(1)} %get-tuple-element.76), channel_id=1, source_target_pairs={{0,16},{4,20},{8,24},{12,28},{16,0},{20,4},{24,8},{28,12},{32,48},... | collective-permute-start | bytes 786440 | tf_op jit(solution)/shard_map/ppermute | solution.py:56
  110.7 6.6 %collective-permute-start.13 = (bf16[128,256]{1,0:T(8,128)(2,1)}, bf16[128,256]{1,0:T(8,128)(2,1)}, u32[]{:S(2)}, u32[]{:S(2)}) collective-permute-start(bf16[128,256]{1,0:T(8,128)(2,1)} %get-tuple-element.80), channel_id=1, source_target_pairs={{0,96},{4,100},{8,104},{12,108},{16,112},{20,116},{24,120},{28,124... | collective-permute-start | bytes 196616 | tf_op jit(solution)/shard_map/ppermute | solution.py:51
  113.7 4.6 %collective-permute-start.14 = (bf16[128,256]{1,0:T(8,128)(2,1)}, bf16[128,256]{1,0:T(8,128)(2,1)}, u32[]{:S(2)}, u32[]{:S(2)}) collective-permute-start(bf16[128,256]{1,0:T(8,128)(2,1)} %get-tuple-element.81), channel_id=1, source_target_pairs={{0,64},{4,68},{8,72},{12,76},{16,80},{20,84},{24,88},{28,92},{32,9... | collective-permute-start | bytes 196616 | tf_op jit(solution)/shard_map/ppermute | solution.py:51
  113.8 5.8 %collective-permute-start.15 = (bf16[128,256]{1,0:T(8,128)(2,1)}, bf16[128,256]{1,0:T(8,128)(2,1)}, u32[]{:S(2)}, u32[]{:S(2)}) collective-permute-start(bf16[128,256]{1,0:T(8,128)(2,1)} %get-tuple-element.82), channel_id=1, source_target_pairs={{0,32},{4,36},{8,40},{12,44},{16,48},{20,52},{24,56},{28,60},{32,6... | collective-permute-start | bytes 196616 | tf_op jit(solution)/shard_map/ppermute | solution.py:51
  114.3 19.7 %collective-permute-start.9 = (bf16[64,256]{1,0:T(8,128)(2,1)}, bf16[64,256]{1,0:T(8,128)(2,1)S(1)}, u32[]{:S(2)}, u32[]{:S(2)}) collective-permute-start(bf16[64,256]{1,0:T(8,128)(2,1)} %copy-done.42), channel_id=1, source_target_pairs={{0,4},{4,0},{8,12},{12,8},{16,20},{20,16},{24,28},{28,24},{32,36},... | collective-permute-start | bytes 98312 | tf_op jit(solution)/shard_map/ppermute | solution.py:46
  120.5 12.8 %collective-permute-start.16 = (bf16[64,256]{1,0:T(8,128)(2,1)S(1)}, bf16[64,256]{1,0:T(8,128)(2,1)S(1)}, u32[]{:S(2)}, u32[]{:S(2)}) collective-permute-start(bf16[64,256]{1,0:T(8,128)(2,1)S(1)} %get-tuple-element.84), channel_id=1, source_target_pairs={{0,4},{4,0},{8,12},{12,8},{16,20},{20,16},{24,28},{28,24},{32,36},... | collective-permute-start | bytes 98312 | tf_op jit(solution)/shard_map/ppermute | solution.py:46
  123.6 1.6 %copy-start.1 = (bf16[512,2048]{1,0:T(8,128)(2,1)S(1)}, bf16[512,2048]{1,0:T(8,128)(2,1)}, u32[]{:S(2)}) copy-start(bf16[512,2048]{1,0:T(8,128)(2,1)} %copy-done) | copy-start | bytes 6291460
  125.2 1.6 %copy-start.3 = (bf16[512,2048]{1,0:T(8,128)(2,1)S(1)}, bf16[512,2048]{1,0:T(8,128)(2,1)}, u32[]{:S(2)}) copy-start(bf16[512,2048]{1,0:T(8,128)(2,1)} %copy-done.2) | copy-start | bytes 6291460
  126.8 1.6 %copy-start.5 = (bf16[512,2048]{1,0:T(8,128)(2,1)S(1)}, bf16[512,2048]{1,0:T(8,128)(2,1)}, u32[]{:S(2)}) copy-start(bf16[512,2048]{1,0:T(8,128)(2,1)} %copy-done.4) | copy-start | bytes 6291460
  128.4 1.6 %copy-start.7 = (bf16[512,2048]{1,0:T(8,128)(2,1)S(1)}, bf16[512,2048]{1,0:T(8,128)(2,1)}, u32[]{:S(2)}) copy-start(bf16[512,2048]{1,0:T(8,128)(2,1)} %copy-done.6) | copy-start | bytes 6291460
  (13 other events, 12.3 us)

commit v2 on v1

--- a/solution.py
+++ b/solution.py
@@ -13,6 +13,8 @@
 KV_COLS = 2 * HEAD_DIM
 Q_COLS = GROUP * HEAD_DIM
 BLOCK = 2 * TOKENS
+NOTE = 16
+PIECE = BLOCK + NOTE
 CHUNK = 4 * BLOCK
 TILE = GROUP * TOKENS
 LANES = 4 * TILE
@@ -29,7 +31,7 @@
 
 
 def params(**kw):
-    return pltpu.CompilerParams(vmem_limit_bytes=40 * 2**20, **kw)
+    return pltpu.CompilerParams(vmem_limit_bytes=16 * 2**20, **kw)
 
 
 def dot(left, right, left_dim=1, right_dim=0):
@@ -56,54 +58,75 @@
     return lax.ppermute(value, "resp", pairs)
 
 
-def pack_kv_kernel(info, p_own, r_own, p_sib, r_sib, own, send):
-    own[:TOKENS] = p_own[...]
-    own[TOKENS:] = r_own[0]
-    send[:TOKENS] = p_sib[...]
-    send[TOKENS:] = r_sib[0]
-
-
-def pack_kv(info, prompt_kv, resp_kv):
-    two = (TOKENS, KV_COLS)
-    three = (1, TOKENS, KV_COLS)
+def columns(core, width):
+    return pl.ds(pl.multiple_of(core * width, width), width)
+
+
+def run_copies(pairs, sems):
+    copies = [pltpu.make_async_copy(a, b, sems.at[i]) for i, (a, b) in enumerate(pairs)]
+    for copy in copies:
+        copy.start()
+    for copy in copies:
+        copy.wait()
+
+
+def pack_kv_kernel(info, facts, prompt_kv, resp_kv, own, send, sems):
+    core = info[0]
+    pairs = []
+    for side, out in ((core, own), (1 - core, send)):
+        cols = columns(side, KV_COLS)
+        pairs.append((prompt_kv.at[:, cols], out.at[pl.ds(0, TOKENS)]))
+        pairs.append((resp_kv.at[0, :, cols], out.at[pl.ds(TOKENS, TOKENS)]))
+    copies = [pltpu.make_async_copy(a, b, sems.at[i]) for i, (a, b) in enumerate(pairs)]
+    for copy in copies:
+        copy.start()
+    row, lane = iota((NOTE, KV_COLS), 0), iota((NOTE, KV_COLS), 1)
+    ratio = jnp.full((NOTE, KV_COLS), facts[0], f32)
+    high = ratio.astype(bf16).astype(f32)
+    middle = (ratio - high).astype(bf16).astype(f32)
+    low = ratio - high - middle
+    note = jnp.zeros((NOTE, KV_COLS), f32)
+    for field, value in enumerate((high, middle, low, facts[1], facts[2], facts[3])):
+        note = jnp.where(lane == core * 8 + field, value, note)
+    note = jnp.where(row == 0, note, 0.0).astype(bf16)
+    own[BLOCK:] = note
+    send[BLOCK:] = note
+    for copy in copies:
+        copy.wait()
+
+
+def pack_kv(info, facts, prompt_kv, resp_kv):
     return pl.pallas_call(
         pack_kv_kernel,
-        grid_spec=pltpu.PrefetchScalarGridSpec(
-            num_scalar_prefetch=1,
-            grid=(1,),
-            in_specs=[
-                pl.BlockSpec(two, lambda i, s: (0, s[0])),
-                pl.BlockSpec(three, lambda i, s: (0, 0, s[0])),
-                pl.BlockSpec(two, lambda i, s: (0, 1 - s[0])),
-                pl.BlockSpec(three, lambda i, s: (0, 0, 1 - s[0])),
-            ],
-            out_specs=[pl.BlockSpec((BLOCK, KV_COLS), lambda i, s: (0, 0))] * 2,
-        ),
-        out_shape=[jax.ShapeDtypeStruct((BLOCK, KV_COLS), bf16)] * 2,
+        in_specs=[pl.BlockSpec(memory_space=pltpu.SMEM)] * 2
+        + [pl.BlockSpec(memory_space=pltpu.HBM)] * 2,
+        out_shape=[jax.ShapeDtypeStruct((PIECE, KV_COLS), bf16)] * 2,
+        scratch_shapes=[pltpu.SemaphoreType.DMA((4,))],
         compiler_params=params(),
         name="pack_kv",
-    )(info, prompt_kv, resp_kv, prompt_kv, resp_kv)
-
-
-def pack_q_kernel(info, pq, rq, pg, rg, send):
-    send[0] = pq[...]
-    send[1] = rq[0]
-    send[2] = pg[...]
-    send[3] = rg[0]
+    )(info, facts, prompt_kv, resp_kv)
+
+
+def pack_q_kernel(info, pq, rq, pg, rg, send, sems):
+    cols = columns(1 - info[0], Q_COLS)
+    run_copies(
+        [
+            (pq.at[:, cols], send.at[0]),
+            (rq.at[0, :, cols], send.at[1]),
+            (pg.at[:, cols], send.at[2]),
+            (rg.at[0, :, cols], send.at[3]),
+        ],
+        sems,
+    )
 
 
 def pack_q(info, prompt_q, resp_q, prompt_grad, resp_grad):
-    two = pl.BlockSpec((TOKENS, Q_COLS), lambda i, s: (0, 1 - s[0]))
-    three = pl.BlockSpec((1, TOKENS, Q_COLS), lambda i, s: (0, 0, 1 - s[0]))
     return pl.pallas_call(
         pack_q_kernel,
-        grid_spec=pltpu.PrefetchScalarGridSpec(
-            num_scalar_prefetch=1,
-            grid=(1,),
-            in_specs=[two, three, two, three],
-            out_specs=pl.BlockSpec((4, TOKENS, Q_COLS), lambda i, s: (0, 0, 0)),
-        ),
+        in_specs=[pl.BlockSpec(memory_space=pltpu.SMEM)]
+        + [pl.BlockSpec(memory_space=pltpu.HBM)] * 4,
         out_shape=jax.ShapeDtypeStruct((4, TOKENS, Q_COLS), bf16),
+        scratch_shapes=[pltpu.SemaphoreType.DMA((4,))],
         compiler_params=params(),
         name="pack_q",
     )(info, prompt_q, resp_q, prompt_grad, resp_grad)
@@ -130,24 +153,33 @@
     return jnp.concatenate([value_rows.T, jnp.ones((16, value_rows.shape[0]), bf16)], axis=0)
 
 
-def prep_kernel(info, pq, rq, pg, rg, recv, kv_own, kv_recv, q_aug, grads, raised, packed):
+def prep_kernel(
+    info, pq, rq, pg, rg, recv, kv_own, kv_recv, q_aug, grads, raised, packed, local, sems
+):
     core = info[0]
+    cols = columns(core, Q_COLS)
+    run_copies(
+        [
+            (pq.at[:, cols], local.at[0]),
+            (rq.at[0, :, cols], local.at[1]),
+            (pg.at[:, cols], local.at[2]),
+            (rg.at[0, :, cols], local.at[3]),
+        ],
+        sems,
+    )
     none = jnp.concatenate(
         [jnp.zeros((HEAD_DIM + 8, TILE), f32), jnp.full((8, TILE), no_max, f32)], axis=0
     )
     for j in range(4):
         lanes = slice(j * TILE, (j + 1) * TILE)
         sib, resp = j // 2, j % 2
-        if sib:
-            block, grad = recv[resp], recv[2 + resp]
-        else:
-            block, grad = (rq[0], rg[0]) if resp else (pq[...], pg[...])
-        turned_q = turned(block)
+        source = recv if sib else local
+        turned_q = turned(source[resp])
         q_aug[:HEAD_DIM, lanes] = turned_q
-        grads[:, lanes] = turned(grad)
+        grads[:, lanes] = turned(source[2 + resp])
         if resp:
             q_aug[HEAD_DIM:, lanes] = jnp.zeros((HEAD_DIM, TILE), bf16)
-            rows = (kv_recv if sib else kv_own)[TOKENS:]
+            rows = (kv_recv if sib else kv_own)[TOKENS:BLOCK]
             scores = dot(rows[:, :HEAD_DIM], turned_q)
             token = iota(scores.shape, 1) % TOKENS
             scores = jnp.where(iota(scores.shape, 0) <= token, scores, blocked_score)
@@ -164,45 +196,35 @@
 
 
 def prep(info, prompt_q, resp_q, prompt_grad, resp_grad, recv, kv_own, kv_recv):
-    two = pl.BlockSpec((TOKENS, Q_COLS), lambda i, s: (0, s[0]))
-    three = pl.BlockSpec((1, TOKENS, Q_COLS), lambda i, s: (0, 0, s[0]))
-
-    def whole(*shape):
-        return pl.BlockSpec(shape, lambda i, s: (0,) * len(shape))
-
     return pl.pallas_call(
         prep_kernel,
-        grid_spec=pltpu.PrefetchScalarGridSpec(
-            num_scalar_prefetch=1,
-            grid=(1,),
-            in_specs=[
-                two,
-                three,
-                two,
-                three,
-                whole(4, TOKENS, Q_COLS),
-                whole(BLOCK, KV_COLS),
-                whole(BLOCK, KV_COLS),
-            ],
-            out_specs=[
-                whole(2 * HEAD_DIM, LANES),
-                whole(HEAD_DIM, LANES),
-                whole(TOKENS, 2 * TILE),
-                whole(HEAD_DIM + 16, LANES),
-            ],
-        ),
+        in_specs=[pl.BlockSpec(memory_space=pltpu.SMEM)]
+        + [pl.BlockSpec(memory_space=pltpu.HBM)] * 4
+        + [pl.BlockSpec(memory_space=pltpu.VMEM)] * 3,
         out_shape=[
             jax.ShapeDtypeStruct((2 * HEAD_DIM, LANES), bf16),
             jax.ShapeDtypeStruct((HEAD_DIM, LANES), bf16),
             jax.ShapeDtypeStruct((TOKENS, 2 * TILE), bf16),
             jax.ShapeDtypeStruct((HEAD_DIM + 16, LANES), f32),
         ],
+        scratch_shapes=[
+            pltpu.VMEM((4, TOKENS, Q_COLS), bf16),
+            pltpu.SemaphoreType.DMA((4,)),
+        ],
         compiler_params=params(),
         name="prep",
     )(info, prompt_q, resp_q, prompt_grad, resp_grad, recv, kv_own, kv_recv)
 
 
-def forward_kernel(offset, info, kv, q_aug, raised, packed, key_aug, value_rows):
+def chunk_rows(kv, cols):
+    return jnp.concatenate([kv[p * PIECE : p * PIECE + BLOCK, cols] for p in range(4)], axis=0)
+
+
+key_cols = slice(0, HEAD_DIM)
+value_cols = slice(HEAD_DIM, KV_COLS)
+
+
+def forward_kernel(offset, info, kv, q_aug, raised, packed, notes, key_aug, value_rows):
     @pl.when(pl.program_id(0) == 0)
     def _():
         core, z_own, x_own = info[0], info[1], info[2]
@@ -218,11 +240,12 @@
                 z_here > z_own, jnp.logical_and(z_here == z_own, x_here > x_own)
             )
             diagonal = jnp.logical_and(z_here == z_own, x_here == x_own)
-            key_aug[rows, :HEAD_DIM] = kv[rows, :HEAD_DIM]
+            key_aug[rows, :HEAD_DIM] = kv[p * PIECE : p * PIECE + BLOCK, key_cols]
+            notes[p * NOTE : (p + 1) * NOTE] = kv[p * PIECE + BLOCK : (p + 1) * PIECE]
             key_aug[rows, HEAD_DIM:] = (
                 first * later.astype(f32) + same * diagonal.astype(f32)
             ).astype(bf16)
-        value_rows[...] = with_ones(kv[:, HEAD_DIM:])
+        value_rows[...] = with_ones(chunk_rows(kv, value_cols))
 
     for s in range(TILE // SUB):
         lanes = slice(s * SUB, (s + 1) * SUB)
@@ -238,12 +261,13 @@
             num_scalar_prefetch=1,
             grid=(4,),
             in_specs=[
-                pl.BlockSpec((CHUNK, KV_COLS), lambda j, s: (0, 0)),
+                pl.BlockSpec((4 * PIECE, KV_COLS), lambda j, s: (0, 0)),
                 pl.BlockSpec((2 * HEAD_DIM, TILE), lambda j, s: (0, j)),
             ],
             out_specs=[
                 pl.BlockSpec((CHUNK, TILE), lambda j, s: (0, j)),
                 pl.BlockSpec((HEAD_DIM + 16, TILE), lambda j, s: (0, j)),
+                pl.BlockSpec((4 * NOTE, KV_COLS), lambda j, s: (0, 0)),
             ],
             scratch_shapes=[
                 pltpu.VMEM((CHUNK, 2 * HEAD_DIM), bf16),
@@ -253,6 +277,7 @@
         out_shape=[
             jax.ShapeDtypeStruct((CHUNK, LANES), bf16),
             jax.ShapeDtypeStruct((HEAD_DIM + 16, LANES), f32),
+            jax.ShapeDtypeStruct((4 * NOTE, KV_COLS), bf16),
         ],
         compiler_params=params(),
         cost_estimate=pl.CostEstimate(
@@ -262,7 +287,7 @@
     )(info, kv, q_aug)
 
 
-def combine_kernel(info, table, grads, part_0, part_1, part_2, part_3, part_own, out, cot_aug, gains):
+def combine_kernel(info, note_0, note_1, note_2, note_3, grads, part_0, part_1, part_2, part_3, part_own, out, cot_aug, gains):
     j = pl.program_id(0)
     parts = (part_0, part_1, part_2, part_3, part_own)
     tops = [part[HEAD_DIM + 8 : HEAD_DIM + 9, :] for part in parts]
@@ -276,17 +301,28 @@
     gains[...] = jnp.concatenate(
         [f * inverse for f in factors] + [jnp.zeros((3, TILE), f32)], axis=0
     )
-    own = info[1] * 8 + info[2] * 2 + jnp.where(j < 2, info[0], 1 - info[0])
-    ids = iota((32, 1), 0)
-    here = ids == own
-
-    def pick(column, mask):
-        return jnp.sum(
-            jnp.where(mask, table[:, column : column + 1], 0.0), axis=0, keepdims=True
-        )
-
-    ratio, partner, chosen, count = [pick(column, here) for column in range(4)]
-    mate = pick(0, ids.astype(f32) == partner)
+    own_core = jnp.where(j < 2, info[0], 1 - info[0])
+    own_row = note_0[0:1, :].astype(f32)
+    lane = iota(own_row.shape, 1)
+
+    def field(number):
+        mask = lane == own_core * 8 + number
+        return jnp.sum(jnp.where(mask, own_row, 0.0), axis=1, keepdims=True)
+
+    ratio = field(0) + field(1) + field(2)
+    partner, chosen, count = field(3), field(4), field(5)
+    mate = jnp.zeros((1, 1), f32)
+    row = iota((4 * NOTE, 1), 0)
+    z_here = (info[1] + 4 - row // NOTE) % 4
+    for offset, note in zip(offsets, (note_0, note_1, note_2, note_3)):
+        seat = z_here * 8 + (info[2] + offset) % 4 * 2
+        for side in range(2):
+            lanes = [note[:, side * 8 + k : side * 8 + k + 1].astype(f32) for k in range(3)]
+            found = jnp.logical_and(
+                row % NOTE == 0, (seat + side).astype(f32) == partner
+            )
+            ratios = lanes[0] + lanes[1] + lanes[2]
+            mate = mate + jnp.sum(jnp.where(found, ratios, 0.0), axis=0, keepdims=True)
     sign = 2.0 * chosen - 1.0
     pair_weight = sign * jax.nn.sigmoid(-pair_beta * (sign * (ratio - mate)))
     token = (iota((1, TILE), 1) % TOKENS).astype(f32)
@@ -304,7 +340,7 @@
     ).astype(bf16)
 
 
-def combine(info, table, grads, parts):
+def combine(info, notes, grads, parts):
     def tile(rows):
         return pl.BlockSpec((rows, TILE), lambda j, s: (0, j))
 
@@ -313,7 +349,8 @@
         grid_spec=pltpu.PrefetchScalarGridSpec(
             num_scalar_prefetch=1,
             grid=(4,),
-            in_specs=[pl.BlockSpec((32, 128), lambda j, s: (0, 0)), tile(HEAD_DIM)]
+            in_specs=[pl.BlockSpec((4 * NOTE, KV_COLS), lambda j, s: (0, 0))] * 4
+            + [tile(HEAD_DIM)]
             + [tile(HEAD_DIM + 16)] * 5,
             out_specs=[tile(HEAD_DIM), tile(2 * HEAD_DIM), tile(8)],
         ),
@@ -324,7 +361,10 @@
         ],
         compiler_params=params(),
         name="combine",
-    )(info, table, grads, *parts)
+    )(info, *notes, grads, *parts)
+
+
+offsets = (0, 3, 1, 2)
 
 
 def value_aug_of(value_rows):
@@ -337,7 +377,7 @@
 
     @pl.when(j == 0)
     def _():
-        value_aug[...] = value_aug_of(kv[:, HEAD_DIM:])
+        value_aug[...] = value_aug_of(chunk_rows(kv, value_cols))
         dkey[...] = jnp.zeros_like(dkey)
         dvalue[...] = jnp.zeros_like(dvalue)
 
@@ -365,7 +405,7 @@
         functools.partial(backward_kernel, chunk),
         grid=(4,),
         in_specs=[
-            pl.BlockSpec((CHUNK, KV_COLS), lambda j: (0, 0)),
+            pl.BlockSpec((4 * PIECE, KV_COLS), lambda j: (0, 0)),
             tile(CHUNK),
             tile(HEAD_DIM),
             tile(2 * HEAD_DIM),
@@ -398,14 +438,14 @@
 
 def finish_kernel(
     kv_0, kv_1, kv_2, kv_3, slopes_0, slopes_1, slopes_2, slopes_3,
-    kv_own, raised, q_aug, cot_aug, gains, out, result, own_grad, keys, total,
+    kv_own, raised, q_aug, cot_aug, gains, out, after, result, own_grad, keys, total,
 ):
     j = pl.program_id(0)
 
     @pl.when(j == 0)
     def _():
         for chunk, kv in enumerate((kv_0, kv_1, kv_2, kv_3)):
-            keys[:, chunk * CHUNK : (chunk + 1) * CHUNK] = kv[:, :HEAD_DIM].T
+            keys[:, chunk * CHUNK : (chunk + 1) * CHUNK] = chunk_rows(kv, key_cols).T
 
     acc = None
     for chunk, slopes in enumerate((slopes_0, slopes_1, slopes_2, slopes_3)):
@@ -417,7 +457,7 @@
     @pl.when(j == 1)
     def _():
         gain = gains[4:5, :]
-        rows = kv_own[TOKENS:]
+        rows = kv_own[TOKENS:BLOCK]
         moved = dot(value_aug_of(rows[:, HEAD_DIM:]), cot_aug[...])
         slopes = (raised[...].astype(f32) * moved).astype(bf16)
         total[...] += dot(rows[:, :HEAD_DIM].T, slopes) * (gain * score_scale)
@@ -430,7 +470,7 @@
     result[0, 1] = rows_of(total[...]).astype(bf16)
 
 
-def finish(kvs, slopes, kv_own, raised, q_aug, cot_aug, gains, out, sib):
+def finish(kvs, slopes, kv_own, raised, q_aug, cot_aug, gains, out, after, sib):
     def whole(*shape):
         return pl.BlockSpec(shape, lambda j: (0,) * len(shape))
 
@@ -440,15 +480,16 @@
     return pl.pallas_call(
         finish_kernel,
         grid=(2,),
-        in_specs=[whole(CHUNK, KV_COLS)] * 4
+        in_specs=[whole(4 * PIECE, KV_COLS)] * 4
         + [tile(CHUNK)] * 4
         + [
-            whole(BLOCK, KV_COLS),
+            whole(PIECE, KV_COLS),
             pl.BlockSpec((TOKENS, TILE), lambda j: (0, sib)),
             tile(HEAD_DIM),
             tile(2 * HEAD_DIM),
             tile(8),
             tile(HEAD_DIM),
+            pl.BlockSpec(memory_space=pl.ANY),
         ],
         out_specs=[
             pl.BlockSpec((1, 2, TOKENS, Q_COLS), lambda j: (j, 0, 0, 0)),
@@ -467,7 +508,7 @@
             flops=4 * CHUNK * LANES * HEAD_DIM, bytes_accessed=5 * 2**20, transcendentals=0
         ),
         name="finish",
-    )(*kvs, *slopes, kv_own, raised, q_aug, cot_aug, gains, out)
+    )(*kvs, *slopes, kv_own, raised, q_aug, cot_aug, gains, out, after)
 
 
 def place_kernel(info, own, recv, own_dkv, recv_dkv, prompt_out, resp_out, prompt_dq, resp_dq, resp_dkv):
@@ -544,7 +585,7 @@
     )(own, *recvs)
 
 
-def sum_z_kernel(own, recv_1, recv_2, recv_3, kept, sent):
+def sum_z_kernel(own, recv_1, recv_2, recv_3, after, kept, sent):
     total = own[...]
     for recv in (recv_1, recv_2, recv_3):
         total = total + recv[...].astype(f32)
@@ -552,13 +593,15 @@
     sent[...] = total[TOKENS:].astype(bf16)
 
 
-def sum_z(own, recvs):
+def sum_z(own, recvs, after):
     return pl.pallas_call(
         sum_z_kernel,
+        in_specs=[pl.BlockSpec(memory_space=pltpu.VMEM)] * 4
+        + [pl.BlockSpec(memory_space=pl.ANY)],
         out_shape=[jax.ShapeDtypeStruct((TOKENS, KV_COLS), bf16)] * 2,
         compiler_params=params(),
         name="sum_z",
-    )(own, *recvs)
+    )(own, *recvs, after)
 
 
 def shards(
@@ -577,38 +620,34 @@
     core = own_index % 2
     info = jnp.stack([core, own_index // 8, own_index // 2 % 4]).astype(jnp.int32)
 
-    kv_own, kv_send = pack_kv(info, prompt_kv, resp_kv)
+    prompt_q, prompt_kv, resp_q, resp_kv, prompt_grad, resp_grad = [
+        pltpu.with_memory_space_constraint(array, pltpu.HBM)
+        for array in (prompt_q, prompt_kv, resp_q, resp_kv, prompt_grad, resp_grad)
+    ]
+    facts = jnp.concatenate(
+        [logratio, partner.astype(f32), chosen.astype(f32), resp_len.astype(f32)]
+    )
+
+    kv_own, kv_send = pack_kv(info, facts, prompt_kv, resp_kv)
     kv_recv = swap_core(kv_send)
-    q_send = pack_q(info, prompt_q, resp_q, prompt_grad, resp_grad)
-    q_recv = swap_core(q_send)
-
-    scalars = jnp.concatenate(
-        [
-            logratio,
-            partner.astype(f32),
-            chosen.astype(f32),
-            resp_len.astype(f32),
-            jnp.zeros((124,), f32),
-        ]
-    )
-    table = lax.all_to_all(
-        jnp.broadcast_to(scalars[None, :], (32, 128)), "resp", split_axis=0, concat_axis=0, tiled=True
-    )
-
-    block = jnp.concatenate([kv_own[:TOKENS], kv_recv[:TOKENS]], axis=0)
+    q_recv = swap_core(pack_q(info, prompt_q, resp_q, prompt_grad, resp_grad))
+
+    block = jnp.concatenate(
+        [kv_own[:TOKENS], kv_recv[:TOKENS], kv_own[BLOCK:] + kv_recv[BLOCK:]], axis=0
+    )
     chunk_own = jnp.concatenate([block] + [shift_z(block, step) for step in (1, 2, 3)], axis=0)
-    offsets = (0, 3, 1, 2)
     kvs = [chunk_own] + [shift_x(chunk_own, 4 - offset) for offset in offsets[1:]]
 
     q_aug, grads, raised_own, part_own = prep(
         info, prompt_q, resp_q, prompt_grad, resp_grad, q_recv, kv_own, kv_recv
     )
-    raised, parts = [], []
+    raised, parts, notes = [], [], []
     for kv, offset in zip(kvs, offsets):
-        one, part = forward(info, kv, q_aug, offset)
+        one, part, note = forward(info, kv, q_aug, offset)
         raised.append(one)
         parts.append(part)
-    out, cot_aug, gains = combine(info, table, grads, parts + [part_own])
+        notes.append(note)
+    out, cot_aug, gains = combine(info, notes, grads, parts + [part_own])
 
     slopes = [None] * 4
     returned = []
@@ -623,18 +662,18 @@
     recvs = [shift_z(blocks[p], 4 - p) for p in (1, 2, 3)]
 
     sib_result, sib_dkv = finish(
-        kvs, slopes, kv_recv, raised_own, q_aug, cot_aug, gains, out, 1
+        kvs, slopes, kv_recv, raised_own, q_aug, cot_aug, gains, out, blocks[3], 1
     )
     recv_result = swap_core(sib_result)
     recv_dkv = swap_core(sib_dkv)
     own_result, own_dkv = finish(
-        kvs, slopes, kv_own, raised_own, q_aug, cot_aug, gains, out, 0
+        kvs, slopes, kv_own, raised_own, q_aug, cot_aug, gains, out, sib_dkv, 0
     )
     prompt_out, resp_out, prompt_dq, resp_dq, resp_dkv = place(
         info, own_result, recv_result, own_dkv, recv_dkv
     )
 
-    kept, sent = sum_z(blocks[0], recvs)
+    kept, sent = sum_z(blocks[0], recvs, own_dkv)
     other = swap_core(sent)
     prompt_dkv = jnp.where(
         core == 0,

time: 138 us -> 90 us (0.65)
  local copies, waits for them, and re-layouts: 33.3 us -> 0.03 us
  starting transfers between devices: 32.7 us -> 23 us
  waiting for transfers between devices: 20.7 us -> 17 us
    unnamed x88 -> x2, local copies, waits for them, and re-layouts: 32.6 us -> 0.01 us
    all_to_all x1 -> x0, starting transfers between devices: 8.56 us -> none  [shards(): lax.all_to_all(jnp.broadcast_to(scalars[None, :], (32, 128)), 'resp', spl...]
    ppermute x6, waiting for transfers between devices: 11.6 us -> 5.26 us  [shift_x(): return lax.ppermute(value, 'resp', pairs)]
    ppermute x5, starting transfers between devices: 10.4 us -> 8.38 us  [swap_core(): return lax.ppermute(value, 'resp', [(r, r ^ 1) for r in range(32)])]
    ppermute x6, waiting for transfers between devices: 8.16 us -> 10.1 us  [shift_z(): return lax.ppermute(value, 'resp', pairs)]
    pallas_call x6, Pallas kernels: 8.54 us -> 10 us  [the longest x2 4.58 us: finish(): pl.pallas_call(finish_kernel, grid=(2,), in_specs=[whole(4 * PIECE, KV_CO...]
  transfers between devices with their start and end apart: 18 -> 17, of which waited for: 6 -> 6; matrix products, arithmetic and copies ran while one was open for 1% -> 1% of each run, Pallas kernels for 18% -> 33%
where the time goes in v2:
time: 90 us; the launch traced here: 89.7 us
  Pallas kernels  45.3 us (50%)
  starting transfers between devices  23 us (26%)
  waiting for transfers between devices  17 us (19%)
  between operations  3.48 us (4%)
    pallas_call x4, Pallas kernels, forward(): pl.pallas_call(functools.partial(forward_kernel, offset), grid_spec=pltpu...  18.8 us
    pallas_call x4, Pallas kernels, backward(): pl.pallas_call(functools.partial(backward_kernel, chunk), grid=(4,), in_s...  11.7 us
    ppermute x6, waiting for transfers between devices, shift_z(): return lax.ppermute(value, 'resp', pairs)  10.1 us
    ppermute x5, starting transfers between devices, swap_core(): return lax.ppermute(value, 'resp', [(r, r ^ 1) for r in range(32)])  8.38 us
    ppermute x6, starting transfers between devices, shift_z(): return lax.ppermute(value, 'resp', pairs)  8.05 us
    ppermute x6, starting transfers between devices, shift_x(): return lax.ppermute(value, 'resp', pairs)  6.59 us
    ppermute x6, waiting for transfers between devices, shift_x(): return lax.ppermute(value, 'resp', pairs)  5.26 us
    pallas_call x2, Pallas kernels, finish(): pl.pallas_call(finish_kernel, grid=(2,), in_specs=[whole(4 * PIECE, KV_CO...  4.58 us
  transfers between devices with their start and end apart: 17, of which 6 were waited for; matrix products, arithmetic and copies ran while one was open for 1% of the time, Pallas kernels for 33%

profile of v2, /device:TPU:1, one launch (start us, length us, event | category | flops | bytes accessed | tf_op | source)
XLA Modules:
  0.0 89.7 jit_solution(28674164427130024)
XLA Ops:
  3.3 0.1 pad_add_fusion.info
  3.3 0.1 pad_maximum_fusion.1.facts
  3.4 1.4 %pack_kv.1 = (bf16[144,256]{1,0:T(8,128)(2,1)S(1)}, bf16[144,256]{1,0:T(8,128)(2,1)S(1)}) custom-call(s32[3]{0:T(128)S(1)} %pad_add_fusion.info, f32[4]{0:T(128)S(1)} %pad_maximum_fusion.1.facts, bf16[64,512]{1,0:T(8,128)(2,1)} %prompt_kv.1, bf16[1,64,512]{2,1,0:T(8,128)(2,1)} %resp_kv.1), custom_call_target="tpu_custom_call" | custom-call | tf_op jit(solution)/shard_map/pack_kv/pallas_call | solution.py:99
  4.8 3.3 %collective-permute-start = (bf16[144,256]{1,0:T(8,128)(2,1)S(1)}, bf16[144,256]{1,0:T(8,128)(2,1)S(1)}, u32[]{:S(2)}, u32[]{:S(2)}) collective-permute-start(bf16[144,256]{1,0:T(8,128)(2,1)S(1)} %get-tuple-element.51), channel_id=1, source_target_pairs={{0,4},{4,0},{8,12},{12,8},{16,20},{20,16},{24,28},{28,24},{32,36},... | collective-permute-start | bytes 221192 | tf_op jit(solution)/shard_map/ppermute | solution.py:48
  8.1 0.9 %collective-permute-done.kv_recv.kv_own = bf16[144,256]{1,0:T(8,128)(2,1)S(1)} collective-permute-done((bf16[144,256]{1,0:T(8,128)(2,1)S(1)}, bf16[144,256]{1,0:T(8,128)(2,1)S(1)}, u32[]{:S(2)}, u32[]{:S(2)}) %collective-permute-start) | collective-permute-done | bytes 73760 | tf_op jit(solution)/shard_map/ppermute | solution.py:48
  9.1 0.1 collective-permute-start.1
  9.2 1.7 %pack_q.1 = bf16[4,64,1024]{2,1,0:T(8,128)(2,1)S(1)} custom-call(s32[3]{0:T(128)S(1)} %pad_add_fusion.info, bf16[64,2048]{1,0:T(8,128)(2,1)} %pq.3, bf16[1,64,2048]{2,1,0:T(8,128)(2,1)} %rq.3, bf16[64,2048]{1,0:T(8,128)(2,1)} %pg.3, bf16[1,64,2048]{2,1,0:T(8,128)(2,1)} %rg.3), custom_call_target="tpu_custom_call" | custom-call | tf_op jit(solution)/shard_map/pack_q/pallas_call | solution.py:124
  10.9 0.6 collective-permute-start.7
  11.5 3.4 %collective-permute-start.3 = (bf16[144,256]{1,0:T(8,128)(2,1)S(1)}, bf16[144,256]{1,0:T(8,128)(2,1)S(1)}, u32[]{:S(2)}, u32[]{:S(2)}) collective-permute-start(bf16[144,256]{1,0:T(8,128)(2,1)S(1)} %pad_maximum_fusion), channel_id=1, source_target_pairs={{0,96},{4,100},{8,104},{12,108},{16,112},{20,116},{24,120},{28,124... | collective-permute-start | bytes 221192 | tf_op jit(solution)/shard_map/ppermute | solution.py:53
  14.8 0.0 collective-permute-done.1
  14.8 6.2 %collective-permute-done.2 = bf16[144,256]{1,0:T(8,128)(2,1)S(1)} collective-permute-done((bf16[144,256]{1,0:T(8,128)(2,1)S(1)}, bf16[144,256]{1,0:T(8,128)(2,1)S(1)}, u32[]{:S(2)}, u32[]{:S(2)}) %collective-permute-start.2) | collective-permute-done | bytes 73760 | tf_op jit(solution)/shard_map/ppermute | solution.py:53
  21.0 0.0 collective-permute-done.3
  21.1 0.6 collective-permute-start.6
  21.7 0.9 collective-permute-start.5
  22.5 0.6 collective-permute-start.4
  23.1 2.3 %prep.1 = (bf16[256,2048]{1,0:T(8,128)(2,1)S(1)}, bf16[128,2048]{1,0:T(8,128)(2,1)S(1)}, bf16[64,1024]{1,0:T(8,128)(2,1)S(1)}, f32[144,2048]{1,0:T(8,128)S(1)}) custom-call(s32[3]{0:T(128)S(1)} %pad_add_fusion.info, bf16[64,2048]{1,0:T(8,128)(2,1)} %pq.3, bf16[1,64,2048]{2,1,0:T(8,128)(2,1)} %rq.3, bf16[64,2048]{1,0:T(8,128)(2,1)} %pg.3, ...), custom_call_target="tpu_custom_call" | custom-call | tf_op jit(solution)/shard_map/prep/pallas_call | solution.py:199
  25.5 4.7 %forward.4 = (bf16[512,2048]{1,0:T(8,128)(2,1)S(1)}, f32[144,2048]{1,0:T(8,128)S(1)}, bf16[64,256]{1,0:T(8,128)(2,1)S(1)}) custom-call(s32[3]{0:T(128)S(1)} %pad_add_fusion.info, bf16[576,256]{1,0:T(8,128)(2,1)S(1)} %constant_dynamic-update-slice_fusion.kv.kv_0, bf16[256,2048]{1,0:T(8,128)(2,1)S(1)} %get-tuple-element.52.q_aug), custom_call_target="tpu_custom_call" | custom-call | flops 536870912 | bytes 5242880 | tf_op jit(solution)/shard_map/forward/pallas_call | solution.py:258
  30.2 0.3 collective-permute-done.6.kv.kv_3
  30.5 4.7 %forward.7 = (bf16[512,2048]{1,0:T(8,128)(2,1)S(1)}, f32[144,2048]{1,0:T(8,128)S(1)}, bf16[64,256]{1,0:T(8,128)(2,1)S(1)}) custom-call(s32[3]{0:T(128)S(1)} %pad_add_fusion.info, bf16[576,256]{1,0:T(8,128)(2,1)S(1)} %collective-permute-done.6.kv.kv_3, bf16[256,2048]{1,0:T(8,128)(2,1)S(1)} %get-tuple-element.52.q_aug), custom_call_target="tpu_custom_call" | custom-call | flops 536870912 | bytes 5242880 | tf_op jit(solution)/shard_map/forward/pallas_call | solution.py:258
  35.2 4.7 %forward.6 = (bf16[512,2048]{1,0:T(8,128)(2,1)S(1)}, f32[144,2048]{1,0:T(8,128)S(1)}, bf16[64,256]{1,0:T(8,128)(2,1)S(1)}) custom-call(s32[3]{0:T(128)S(1)} %pad_add_fusion.info, bf16[576,256]{1,0:T(8,128)(2,1)S(1)} %collective-permute-done.5.kv.kv_2, bf16[256,2048]{1,0:T(8,128)(2,1)S(1)} %get-tuple-element.52.q_aug), custom_call_target="tpu_custom_call" | custom-call | flops 536870912 | bytes 5242880 | tf_op jit(solution)/shard_map/forward/pallas_call | solution.py:258
  39.9 0.0 collective-permute-done.4.kv.kv_1
  39.9 4.7 %forward.5 = (bf16[512,2048]{1,0:T(8,128)(2,1)S(1)}, f32[144,2048]{1,0:T(8,128)S(1)}, bf16[64,256]{1,0:T(8,128)(2,1)S(1)}) custom-call(s32[3]{0:T(128)S(1)} %pad_add_fusion.info, bf16[576,256]{1,0:T(8,128)(2,1)S(1)} %collective-permute-done.4.kv.kv_1, bf16[256,2048]{1,0:T(8,128)(2,1)S(1)} %get-tuple-element.52.q_aug), custom_call_target="tpu_custom_call" | custom-call | flops 536870912 | bytes 5242880 | tf_op jit(solution)/shard_map/forward/pallas_call | solution.py:258
  44.6 3.1 %combine.1 = (bf16[128,2048]{1,0:T(8,128)(2,1)S(1)}, bf16[256,2048]{1,0:T(8,128)(2,1)S(1)}, f32[8,2048]{1,0:T(8,128)S(1)}) custom-call(s32[3]{0:T(128)S(1)} %pad_add_fusion.info, bf16[64,256]{1,0:T(8,128)(2,1)S(1)} %get-tuple-element.54.note_0, bf16[64,256]{1,0:T(8,128)(2,1)S(1)} %get-tuple-element.55.note_1, bf16[64,256]{1,0:T(8,128)(2,1)S(1)} %get-tuple-element.56.note_2, ...), custom_call_target="tpu_custom_call" | custom-call | tf_op jit(solution)/shard_map/combine/pallas_call | solution.py:347
  47.7 2.9 %backward.5 = (bf16[512,2048]{1,0:T(8,128)(2,1)S(1)}, bf16[512,256]{1,0:T(8,128)(2,1)S(1)}) custom-call(bf16[576,256]{1,0:T(8,128)(2,1)S(1)} %collective-permute-done.4.kv.kv_1, bf16[512,2048]{1,0:T(8,128)(2,1)S(1)} %get-tuple-element.67.raised, bf16[256,2048]{1,0:T(8,128)(2,1)S(1)} %get-tuple-element.52.q_aug, ...), custom_call_target="tpu_custom_call" | custom-call | flops 805306368 | bytes 6291456 | tf_op jit(solution)/shard_map/backward/pallas_call | solution.py:404
  50.6 3.0 %collective-permute-start.10 = (bf16[512,256]{1,0:T(8,128)(2,1)S(1)}, bf16[512,256]{1,0:T(8,128)(2,1)S(1)}, u32[]{:S(2)}, u32[]{:S(2)}) collective-permute-start(bf16[512,256]{1,0:T(8,128)(2,1)S(1)} %get-tuple-element.78), channel_id=1, source_target_pairs={{0,24},{4,28},{8,0},{12,4},{16,8},{20,12},{24,16},{28,20},{32,56},... | collective-permute-start | bytes 786440 | tf_op jit(solution)/shard_map/ppermute | solution.py:58
  53.6 2.9 %backward.6 = (bf16[512,2048]{1,0:T(8,128)(2,1)S(1)}, bf16[512,256]{1,0:T(8,128)(2,1)S(1)}) custom-call(bf16[576,256]{1,0:T(8,128)(2,1)S(1)} %collective-permute-done.5.kv.kv_2, bf16[512,2048]{1,0:T(8,128)(2,1)S(1)} %get-tuple-element.69.raised, bf16[256,2048]{1,0:T(8,128)(2,1)S(1)} %get-tuple-element.52.q_aug, ...), custom_call_target="tpu_custom_call" | custom-call | flops 805306368 | bytes 6291456 | tf_op jit(solution)/shard_map/backward/pallas_call | solution.py:404
  56.6 0.3 collective-permute-start.9
  56.8 2.9 %backward.7 = (bf16[512,2048]{1,0:T(8,128)(2,1)S(1)}, bf16[512,256]{1,0:T(8,128)(2,1)S(1)}) custom-call(bf16[576,256]{1,0:T(8,128)(2,1)S(1)} %collective-permute-done.6.kv.kv_3, bf16[512,2048]{1,0:T(8,128)(2,1)S(1)} %get-tuple-element.71.raised, bf16[256,2048]{1,0:T(8,128)(2,1)S(1)} %get-tuple-element.52.q_aug, ...), custom_call_target="tpu_custom_call" | custom-call | flops 805306368 | bytes 6291456 | tf_op jit(solution)/shard_map/backward/pallas_call | solution.py:404
  59.8 1.3 %collective-permute-start.8 = (bf16[512,256]{1,0:T(8,128)(2,1)S(1)}, bf16[512,256]{1,0:T(8,128)(2,1)S(1)}, u32[]{:S(2)}, u32[]{:S(2)}) collective-permute-start(bf16[512,256]{1,0:T(8,128)(2,1)S(1)} %get-tuple-element.76), channel_id=1, source_target_pairs={{0,16},{4,20},{8,24},{12,28},{16,0},{20,4},{24,8},{28,12},{32,48},... | collective-permute-start | bytes 786440 | tf_op jit(solution)/shard_map/ppermute | solution.py:58
  61.1 2.9 %backward.4 = (bf16[512,2048]{1,0:T(8,128)(2,1)S(1)}, f32[512,256]{1,0:T(8,128)S(1)}) custom-call(bf16[576,256]{1,0:T(8,128)(2,1)S(1)} %constant_dynamic-update-slice_fusion.kv.kv_0, bf16[512,2048]{1,0:T(8,128)(2,1)S(1)} %get-tuple-element.53.raised, bf16[256,2048]{1,0:T(8,128)(2,1)S(1)} %get-tuple-element.52.q_aug, ...), custom_call_target="tpu_custom_call" | custom-call | flops 805306368 | bytes 6291456 | tf_op jit(solution)/shard_map/backward/pallas_call | solution.py:404
  64.0 0.0 collective-permute-done.10.recv_3
  64.0 0.0 collective-permute-done.9.recv_2
  64.0 4.9 %collective-permute-done.8.recv_1 = bf16[512,256]{1,0:T(8,128)(2,1)S(1)} collective-permute-done((bf16[512,256]{1,0:T(8,128)(2,1)S(1)}, bf16[512,256]{1,0:T(8,128)(2,1)S(1)}, u32[]{:S(2)}, u32[]{:S(2)}) %collective-permute-start.8) | collective-permute-done | bytes 262176 | tf_op jit(solution)/shard_map/ppermute | solution.py:58
  69.0 0.1 sum_x.1
  69.1 2.3 %finish.2 = (bf16[2,2,64,1024]{3,2,1,0:T(8,128)(2,1)S(1)}, bf16[64,256]{1,0:T(8,128)(2,1)S(1)}) custom-call(bf16[576,256]{1,0:T(8,128)(2,1)S(1)} %constant_dynamic-update-slice_fusion.kv.kv_0, bf16[576,256]{1,0:T(8,128)(2,1)S(1)} %collective-permute-done.4.kv.kv_1, bf16[576,256]{1,0:T(8,128)(2,1)S(1)} %collective-permute-done.5.kv.kv_2, ...), custom_call_target="tpu_custom_call" | custom-call | flops 536870912 | bytes 5242880 | tf_op jit(solution)/shard_map/finish/pallas_call | solution.py:480
  71.4 3.5 %collective-permute-start.11 = (bf16[2,2,64,1024]{3,2,1,0:T(8,128)(2,1)S(1)}, bf16[2,2,64,1024]{3,2,1,0:T(8,128)(2,1)S(1)}, u32[]{:S(2)}, u32[]{:S(2)}) collective-permute-start(bf16[2,2,64,1024]{3,2,1,0:T(8,128)(2,1)S(1)} %get-tuple-element.82), channel_id=1, source_target_pairs={{0,4},{4,0},{8,12},{12,8},{16,20},{20,16},{24,28},{28,24},{32,36},... | collective-permute-start | bytes 1572872 | tf_op jit(solution)/shard_map/ppermute | solution.py:48
  74.9 4.3 %collective-permute-start.13 = (bf16[128,256]{1,0:T(8,128)(2,1)S(1)}, bf16[128,256]{1,0:T(8,128)(2,1)S(1)}, u32[]{:S(2)}, u32[]{:S(2)}) collective-permute-start(bf16[128,256]{1,0:T(8,128)(2,1)S(1)} %get-tuple-element.89), channel_id=1, source_target_pairs={{0,96},{4,100},{8,104},{12,108},{16,112},{20,116},{24,120},{28,124... | collective-permute-start | bytes 196616 | tf_op jit(solution)/shard_map/ppermute | solution.py:53
  79.2 0.0 collective-permute-start.14
  79.2 0.3 collective-permute-start.15
  79.5 2.3 %finish.3 = (bf16[2,2,64,1024]{3,2,1,0:T(8,128)(2,1)S(1)}, bf16[64,256]{1,0:T(8,128)(2,1)S(1)}) custom-call(bf16[576,256]{1,0:T(8,128)(2,1)S(1)} %constant_dynamic-update-slice_fusion.kv.kv_0, bf16[576,256]{1,0:T(8,128)(2,1)S(1)} %collective-permute-done.4.kv.kv_1, bf16[576,256]{1,0:T(8,128)(2,1)S(1)} %collective-permute-done.5.kv.kv_2, ...), custom_call_target="tpu_custom_call" | custom-call | flops 536870912 | bytes 5242880 | tf_op jit(solution)/shard_map/finish/pallas_call | solution.py:480
  81.8 0.0 collective-permute-done.13.recv_1
  81.8 3.9 %collective-permute-done.14.recv_2 = bf16[128,256]{1,0:T(8,128)(2,1)S(1)} collective-permute-done((bf16[128,256]{1,0:T(8,128)(2,1)S(1)}, bf16[128,256]{1,0:T(8,128)(2,1)S(1)}, u32[]{:S(2)}, u32[]{:S(2)}) %collective-permute-start.14) | collective-permute-done | bytes 65568 | tf_op jit(solution)/shard_map/ppermute | solution.py:53
  85.7 0.8 collective-permute-start.16
  86.6 0.1 collective-permute-start.12
  86.7 0.8 collective-permute-done.16
  87.4 0.6 maximum_select_fusion
  88.1 0.0 collective-permute-done.11.recv
  88.1 1.6 %place.1 = (bf16[64,2048]{1,0:T(8,128)(2,1)}, bf16[1,64,2048]{2,1,0:T(8,128)(2,1)}, bf16[64,2048]{1,0:T(8,128)(2,1)}, bf16[1,64,2048]{2,1,0:T(8,128)(2,1)}, bf16[1,64,512]{2,1,0:T(8,128)(2,1)}) custom-call(s32[3]{0:T(128)S(1)} %pad_add_fusion.info, bf16[2,2,64,1024]{3,2,1,0:T(8,128)(2,1)S(1)} %get-tuple-element.81.own, ...), custom_call_target="tpu_custom_call" | custom-call | tf_op jit(solution)/shard_map/place/pallas_call | solution.py:542
  (13 shorter events, 0.1 us)
Async XLA Ops:
  4.8 4.2 %collective-permute-start = (bf16[144,256]{1,0:T(8,128)(2,1)S(1)}, bf16[144,256]{1,0:T(8,128)(2,1)S(1)}, u32[]{:S(2)}, u32[]{:S(2)}) collective-permute-start(bf16[144,256]{1,0:T(8,128)(2,1)S(1)} %get-tuple-element.51), channel_id=1, source_target_pairs={{0,4},{4,0},{8,12},{12,8},{16,20},{20,16},{24,28},{28,24},{32,36},... | collective-permute-start | bytes 221192 | tf_op jit(solution)/shard_map/ppermute | solution.py:48
  9.1 5.8 %collective-permute-start.1 = (bf16[144,256]{1,0:T(8,128)(2,1)S(1)}, bf16[144,256]{1,0:T(8,128)(2,1)S(1)}, u32[]{:S(2)}, u32[]{:S(2)}) collective-permute-start(bf16[144,256]{1,0:T(8,128)(2,1)S(1)} %pad_maximum_fusion), channel_id=1, source_target_pairs={{0,32},{4,36},{8,40},{12,44},{16,48},{20,52},{24,56},{28,60},{32,6... | collective-permute-start | bytes 221192 | tf_op jit(solution)/shard_map/ppermute | solution.py:53
  10.9 12.3 %collective-permute-start.7 = (bf16[4,64,1024]{2,1,0:T(8,128)(2,1)S(1)}, bf16[4,64,1024]{2,1,0:T(8,128)(2,1)S(1)}, u32[]{:S(2)}, u32[]{:S(2)}) collective-permute-start(bf16[4,64,1024]{2,1,0:T(8,128)(2,1)S(1)} %pack_q.1), channel_id=1, source_target_pairs={{0,4},{4,0},{8,12},{12,8},{16,20},{20,16},{24,28},{28,24},{32,36},... | collective-permute-start | bytes 1572872 | tf_op jit(solution)/shard_map/ppermute | solution.py:48
  11.5 9.6 %collective-permute-start.3 = (bf16[144,256]{1,0:T(8,128)(2,1)S(1)}, bf16[144,256]{1,0:T(8,128)(2,1)S(1)}, u32[]{:S(2)}, u32[]{:S(2)}) collective-permute-start(bf16[144,256]{1,0:T(8,128)(2,1)S(1)} %pad_maximum_fusion), channel_id=1, source_target_pairs={{0,96},{4,100},{8,104},{12,108},{16,112},{20,116},{24,120},{28,124... | collective-permute-start | bytes 221192 | tf_op jit(solution)/shard_map/ppermute | solution.py:53
  14.8 6.2 %collective-permute-start.2 = (bf16[144,256]{1,0:T(8,128)(2,1)S(1)}, bf16[144,256]{1,0:T(8,128)(2,1)S(1)}, u32[]{:S(2)}, u32[]{:S(2)}) collective-permute-start(bf16[144,256]{1,0:T(8,128)(2,1)S(1)} %pad_maximum_fusion), channel_id=1, source_target_pairs={{0,64},{4,68},{8,72},{12,76},{16,80},{20,84},{24,88},{28,92},{32,9... | collective-permute-start | bytes 221192 | tf_op jit(solution)/shard_map/ppermute | solution.py:53
  21.1 9.4 %collective-permute-start.6 = (bf16[576,256]{1,0:T(8,128)(2,1)S(1)}, bf16[576,256]{1,0:T(8,128)(2,1)S(1)}, u32[]{:S(2)}, u32[]{:S(2)}) collective-permute-start(bf16[576,256]{1,0:T(8,128)(2,1)S(1)} %constant_dynamic-update-slice_fusion.kv.kv_0), channel_id=1, source_target_pairs={{0,16},{4,20},{8,24},{12,28},{16,0},{20,4},{24,8},{28,12},{32,48},... | collective-permute-start | bytes 884744 | tf_op jit(solution)/shard_map/ppermute | solution.py:58
  21.7 13.5 %collective-permute-start.5 = (bf16[576,256]{1,0:T(8,128)(2,1)S(1)}, bf16[576,256]{1,0:T(8,128)(2,1)S(1)}, u32[]{:S(2)}, u32[]{:S(2)}) collective-permute-start(bf16[576,256]{1,0:T(8,128)(2,1)S(1)} %constant_dynamic-update-slice_fusion.kv.kv_0), channel_id=1, source_target_pairs={{0,24},{4,28},{8,0},{12,4},{16,8},{20,12},{24,16},{28,20},{32,56},... | collective-permute-start | bytes 884744 | tf_op jit(solution)/shard_map/ppermute | solution.py:58
  22.5 17.4 %collective-permute-start.4 = (bf16[576,256]{1,0:T(8,128)(2,1)S(1)}, bf16[576,256]{1,0:T(8,128)(2,1)S(1)}, u32[]{:S(2)}, u32[]{:S(2)}) collective-permute-start(bf16[576,256]{1,0:T(8,128)(2,1)S(1)} %constant_dynamic-update-slice_fusion.kv.kv_0), channel_id=1, source_target_pairs={{0,8},{4,12},{8,16},{12,20},{16,24},{20,28},{24,0},{28,4},{32,40},... | collective-permute-start | bytes 884744 | tf_op jit(solution)/shard_map/ppermute | solution.py:58
  50.6 13.3 %collective-permute-start.10 = (bf16[512,256]{1,0:T(8,128)(2,1)S(1)}, bf16[512,256]{1,0:T(8,128)(2,1)S(1)}, u32[]{:S(2)}, u32[]{:S(2)}) collective-permute-start(bf16[512,256]{1,0:T(8,128)(2,1)S(1)} %get-tuple-element.78), channel_id=1, source_target_pairs={{0,24},{4,28},{8,0},{12,4},{16,8},{20,12},{24,16},{28,20},{32,56},... | collective-permute-start | bytes 786440 | tf_op jit(solution)/shard_map/ppermute | solution.py:58
  56.6 7.4 %collective-permute-start.9 = (bf16[512,256]{1,0:T(8,128)(2,1)S(1)}, bf16[512,256]{1,0:T(8,128)(2,1)S(1)}, u32[]{:S(2)}, u32[]{:S(2)}) collective-permute-start(bf16[512,256]{1,0:T(8,128)(2,1)S(1)} %get-tuple-element.77), channel_id=1, source_target_pairs={{0,8},{4,12},{8,16},{12,20},{16,24},{20,28},{24,0},{28,4},{32,40},... | collective-permute-start | bytes 786440 | tf_op jit(solution)/shard_map/ppermute | solution.py:58
  59.8 9.2 %collective-permute-start.8 = (bf16[512,256]{1,0:T(8,128)(2,1)S(1)}, bf16[512,256]{1,0:T(8,128)(2,1)S(1)}, u32[]{:S(2)}, u32[]{:S(2)}) collective-permute-start(bf16[512,256]{1,0:T(8,128)(2,1)S(1)} %get-tuple-element.76), channel_id=1, source_target_pairs={{0,16},{4,20},{8,24},{12,28},{16,0},{20,4},{24,8},{28,12},{32,48},... | collective-permute-start | bytes 786440 | tf_op jit(solution)/shard_map/ppermute | solution.py:58
  71.4 16.7 %collective-permute-start.11 = (bf16[2,2,64,1024]{3,2,1,0:T(8,128)(2,1)S(1)}, bf16[2,2,64,1024]{3,2,1,0:T(8,128)(2,1)S(1)}, u32[]{:S(2)}, u32[]{:S(2)}) collective-permute-start(bf16[2,2,64,1024]{3,2,1,0:T(8,128)(2,1)S(1)} %get-tuple-element.82), channel_id=1, source_target_pairs={{0,4},{4,0},{8,12},{12,8},{16,20},{20,16},{24,28},{28,24},{32,36},... | collective-permute-start | bytes 1572872 | tf_op jit(solution)/shard_map/ppermute | solution.py:48
  74.9 6.9 %collective-permute-start.13 = (bf16[128,256]{1,0:T(8,128)(2,1)S(1)}, bf16[128,256]{1,0:T(8,128)(2,1)S(1)}, u32[]{:S(2)}, u32[]{:S(2)}) collective-permute-start(bf16[128,256]{1,0:T(8,128)(2,1)S(1)} %get-tuple-element.89), channel_id=1, source_target_pairs={{0,96},{4,100},{8,104},{12,108},{16,112},{20,116},{24,120},{28,124... | collective-permute-start | bytes 196616 | tf_op jit(solution)/shard_map/ppermute | solution.py:53
  79.2 6.5 %collective-permute-start.14 = (bf16[128,256]{1,0:T(8,128)(2,1)S(1)}, bf16[128,256]{1,0:T(8,128)(2,1)S(1)}, u32[]{:S(2)}, u32[]{:S(2)}) collective-permute-start(bf16[128,256]{1,0:T(8,128)(2,1)S(1)} %get-tuple-element.90), channel_id=1, source_target_pairs={{0,64},{4,68},{8,72},{12,76},{16,80},{20,84},{24,88},{28,92},{32,9... | collective-permute-start | bytes 196616 | tf_op jit(solution)/shard_map/ppermute | solution.py:53
  79.2 6.5 %collective-permute-start.15 = (bf16[128,256]{1,0:T(8,128)(2,1)S(1)}, bf16[128,256]{1,0:T(8,128)(2,1)S(1)}, u32[]{:S(2)}, u32[]{:S(2)}) collective-permute-start(bf16[128,256]{1,0:T(8,128)(2,1)S(1)} %get-tuple-element.79.after), channel_id=1, source_target_pairs={{0,32},{4,36},{8,40},{12,44},{16,48},{20,52},{24,56},{28,60},{32,6... | collective-permute-start | bytes 196616 | tf_op jit(solution)/shard_map/ppermute | solution.py:53
  85.7 1.7 %collective-permute-start.16 = (bf16[64,256]{1,0:T(8,128)(2,1)S(1)}, bf16[64,256]{1,0:T(8,128)(2,1)S(1)}, u32[]{:S(2)}, u32[]{:S(2)}) collective-permute-start(bf16[64,256]{1,0:T(8,128)(2,1)S(1)} %get-tuple-element.92), channel_id=1, source_target_pairs={{0,4},{4,0},{8,12},{12,8},{16,20},{20,16},{24,28},{28,24},{32,36},... | collective-permute-start | bytes 98312 | tf_op jit(solution)/shard_map/ppermute | solution.py:48
  86.6 1.5 %collective-permute-start.12 = (bf16[64,256]{1,0:T(8,128)(2,1)S(1)}, bf16[64,256]{1,0:T(8,128)(2,1)S(1)}, u32[]{:S(2)}, u32[]{:S(2)}) collective-permute-start(bf16[64,256]{1,0:T(8,128)(2,1)S(1)} %get-tuple-element.80.after), channel_id=1, source_target_pairs={{0,4},{4,0},{8,12},{12,8},{16,20},{20,16},{24,28},{28,24},{32,36},... | collective-permute-start | bytes 98312 | tf_op jit(solution)/shard_map/ppermute | solution.py:48

commit v3 on v0

v3 whole, which is shorter than its diff:
```python
import functools

import jax
import jax.numpy as jnp
from jax import lax
from jax.experimental import pallas as pl
from jax.experimental.pallas import tpu as pltpu
from jax.sharding import PartitionSpec as P

HEAD_DIM = 128
GROUP = 8
TOKENS = 64
KV_COLS = 2 * HEAD_DIM
Q_COLS = GROUP * HEAD_DIM
BLOCK = 2 * TOKENS
NOTE = 16
PIECE = BLOCK + NOTE
CHUNK = 4 * BLOCK
TILE = GROUP * TOKENS
LANES = 4 * TILE
SUBS = LANES // TILE

score_scale = HEAD_DIM ** (-0.5)
exp2_scale = score_scale * 1.4426950408889634
pair_beta = 0.1
blocked_score = -(2.0**30)
no_max = -(2.0**31)

bf16 = jnp.bfloat16
f32 = jnp.float32


def params(**kw):
    return pltpu.CompilerParams(vmem_limit_bytes=16 * 2**20, **kw)


def dot(left, right, left_dim=1, right_dim=0):
    return lax.dot_general(
        left, right, (((left_dim,), (right_dim,)), ((), ())), preferred_element_type=f32
    )


def iota(shape, dim):
    return lax.broadcasted_iota(jnp.int32, shape, dim)


VMEM = pl.BlockSpec(memory_space=pltpu.VMEM)
SMEM = pl.BlockSpec(memory_space=pltpu.SMEM)
HBM = pl.BlockSpec(memory_space=pltpu.HBM)
AFTER = pl.BlockSpec(memory_space=pl.ANY)


def shape(*dims, dtype=bf16):
    return jax.ShapeDtypeStruct(dims, dtype)


def call(kernel, name, in_specs, out_shape, scratch=(), out_specs=None, flops=0):
    extra = {} if out_specs is None else {"out_specs": out_specs}
    cost = pl.CostEstimate(flops=flops, bytes_accessed=2**20, transcendentals=0)
    return pl.pallas_call(
        kernel,
        in_specs=in_specs,
        out_shape=out_shape,
        scratch_shapes=list(scratch),
        compiler_params=params(),
        cost_estimate=cost,
        name=name,
        **extra,
    )


def lanes_of(j):
    return slice(j * TILE, (j + 1) * TILE)


def swap_core(value):
    return lax.ppermute(value, "resp", [(r, r ^ 1) for r in range(32)])


def shift_z(value, step):
    pairs = [(r, ((r // 8 + step) % 4) * 8 + r % 8) for r in range(32)]
    return lax.ppermute(value, "resp", pairs)


def shift_x(value, step):
    pairs = [(r, (r // 8) * 8 + (r % 8 // 2 + step) % 4 * 2 + r % 2) for r in range(32)]
    return lax.ppermute(value, "resp", pairs)


def columns(core, width):
    return pl.ds(pl.multiple_of(core * width, width), width)


def run_copies(pairs, sems):
    copies = [pltpu.make_async_copy(a, b, sems.at[i]) for i, (a, b) in enumerate(pairs)]
    for copy in copies:
        copy.start()
    for copy in copies:
        copy.wait()


def columns(core, width):
    return pl.ds(pl.multiple_of(core * width, width), width)


def started(pairs, sems):
    copies = [pltpu.make_async_copy(a, b, sems.at[i]) for i, (a, b) in enumerate(pairs)]
    for copy in copies:
        copy.start()
    return copies


def waited(copies):
    for copy in copies:
        copy.wait()


def half_copies(side, pq, rq, pg, rg, target):
    cols = columns(side, Q_COLS)
    return [
        (pq.at[:, cols], target.at[0]),
        (rq.at[0, :, cols], target.at[1]),
        (pg.at[:, cols], target.at[2]),
        (rg.at[0, :, cols], target.at[3]),
    ]


def pack_kernel(
    info, logratio, partner, chosen, resp_len, prompt_kv, resp_kv, pq, rq, pg, rg,
    own, send, send_q, sems,
):
    core = info[0]
    pairs = []
    for side, out in ((core, own), (1 - core, send)):
        cols = columns(side, KV_COLS)
        pairs.append((prompt_kv.at[:, cols], out.at[pl.ds(0, TOKENS)]))
        pairs.append((resp_kv.at[0, :, cols], out.at[pl.ds(TOKENS, TOKENS)]))
    pairs += half_copies(1 - core, pq, rq, pg, rg, send_q)
    copies = started(pairs, sems)
    row, lane = iota((NOTE, KV_COLS), 0), iota((NOTE, KV_COLS), 1)
    ratio = jnp.full((NOTE, KV_COLS), logratio[0], f32)
    high = ratio.astype(bf16).astype(f32)
    middle = (ratio - high).astype(bf16).astype(f32)
    low = ratio - high - middle
    note = jnp.zeros((NOTE, KV_COLS), f32)
    fields = (
        high,
        middle,
        low,
        partner[0].astype(f32),
        chosen[0].astype(f32),
        resp_len[0].astype(f32),
    )
    for number, value in enumerate(fields):
        note = jnp.where(lane == core * 8 + number, value, note)
    note = jnp.where(row == 0, note, 0.0).astype(bf16)
    own[BLOCK:] = note
    send[BLOCK:] = note
    waited(copies)


def pack(*operands):
    return call(
        pack_kernel,
        "pack",
        [SMEM] * 5 + [HBM] * 6,
        [shape(PIECE, KV_COLS)] * 2 + [shape(4, TOKENS, Q_COLS)],
        [pltpu.SemaphoreType.DMA((8,))],
    )(*operands)


def join_cores_kernel(own, recv, block):
    block[:TOKENS] = own[:TOKENS]
    block[TOKENS:BLOCK] = recv[:TOKENS]
    block[BLOCK:] = own[BLOCK:] + recv[BLOCK:]


def join_cores(own, recv):
    return call(join_cores_kernel, "join_cores", [VMEM] * 2, shape(PIECE, KV_COLS))(own, recv)


def join_z_kernel(piece_0, piece_1, piece_2, piece_3, after, chunk):
    for p, piece in enumerate((piece_0, piece_1, piece_2, piece_3)):
        chunk[p * PIECE : (p + 1) * PIECE] = piece[...]


def join_z(pieces, after):
    return call(join_z_kernel, "join_z", [VMEM] * 4 + [AFTER], shape(4 * PIECE, KV_COLS))(
        *pieces, after
    )


def turned(block):
    rows = jnp.concatenate(
        [block[:, g * HEAD_DIM : (g + 1) * HEAD_DIM] for g in range(GROUP)], axis=0
    )
    return rows.T


def softmax_part(scores, value_rows):
    top = jnp.max(scores, axis=0, keepdims=True)
    raised = jnp.exp2((scores - top) * exp2_scale).astype(bf16)
    total = dot(value_rows, raised)
    packed = jnp.concatenate(
        [total[: HEAD_DIM + 8], jnp.broadcast_to(top, (8, top.shape[1]))], axis=0
    )
    return raised, packed


def with_ones(value_rows):
    return jnp.concatenate([value_rows.T, jnp.ones((16, value_rows.shape[0]), bf16)], axis=0)


def prep_kernel(
    info, pq, rq, pg, rg, recv, kv_own, kv_recv, q_aug, grads, raised, packed, local, sems
):
    core = info[0]
    copies = started(half_copies(core, pq, rq, pg, rg, local), sems)
    none = jnp.concatenate(
        [jnp.zeros((HEAD_DIM + 8, TILE), f32), jnp.full((8, TILE), no_max, f32)], axis=0
    )
    for j in (2, 3, 0, 1):
        lanes = lanes_of(j)
        sib, resp = j // 2, j % 2
        if j == 0:
            waited(copies)
        source = recv if sib else local
        turned_q = turned(source[resp])
        q_aug[:HEAD_DIM, lanes] = turned_q
        grads[:, lanes] = turned(source[2 + resp])
        if resp:
            q_aug[HEAD_DIM:, lanes] = jnp.zeros((HEAD_DIM, TILE), bf16)
            rows = (kv_recv if sib else kv_own)[TOKENS:BLOCK]
            scores = dot(rows[:, :HEAD_DIM], turned_q)
            token = iota(scores.shape, 1) % TOKENS
            scores = jnp.where(iota(scores.shape, 0) <= token, scores, blocked_score)
            part, info_rows = softmax_part(scores, with_ones(rows[:, HEAD_DIM:]))
            raised[:, lanes_of(sib)] = part
            packed[:, lanes] = info_rows
        else:
            own_core = 1 - core if sib else core
            token = iota((HEAD_DIM, TILE), 1) % TOKENS + own_core * TOKENS
            row = iota((HEAD_DIM, TILE), 0)
            hidden = jnp.logical_or(row == 0, row > token)
            q_aug[HEAD_DIM:, lanes] = jnp.where(hidden, blocked_score, 0.0).astype(bf16)
            packed[:, lanes] = none


def prep(info, prompt_q, resp_q, prompt_grad, resp_grad, recv, kv_own, kv_recv):
    return call(
        prep_kernel,
        "prep",
        [SMEM] + [HBM] * 4 + [VMEM] * 3,
        [
            shape(2 * HEAD_DIM, LANES),
            shape(HEAD_DIM, LANES),
            shape(TOKENS, 2 * TILE),
            shape(HEAD_DIM + 16, LANES, dtype=f32),
        ],
        [pltpu.VMEM((4, TOKENS, Q_COLS), bf16), pltpu.SemaphoreType.DMA((4,))],
    )(info, prompt_q, resp_q, prompt_grad, resp_grad, recv, kv_own, kv_recv)


offsets = (0, 3, 1, 2)
key_cols = slice(0, HEAD_DIM)
value_cols = slice(HEAD_DIM, KV_COLS)


def chunk_rows(kv, cols):
    return jnp.concatenate([kv[p * PIECE : p * PIECE + BLOCK, cols] for p in range(4)], axis=0)


def forward_kernel(offset, info, kv, q_aug, raised, packed, notes, key_aug, value_rows, scores):
    core, z_own, x_own = info[0], info[1], info[2]
    x_here = (x_own + offset) % 4
    row = iota((BLOCK, HEAD_DIM), 1)
    token = (iota((BLOCK, HEAD_DIM), 0) + core * TOKENS) % BLOCK
    first = (row == 0).astype(f32)
    same = jnp.logical_and(row == token, row > 0).astype(f32)
    for p in range(4):
        rows = slice(p * BLOCK, (p + 1) * BLOCK)
        z_here = (z_own + 4 - p) % 4
        later = jnp.logical_or(
            z_here > z_own, jnp.logical_and(z_here == z_own, x_here > x_own)
        )
        diagonal = jnp.logical_and(z_here == z_own, x_here == x_own)
        key_aug[rows, :HEAD_DIM] = kv[p * PIECE : p * PIECE + BLOCK, key_cols]
        notes[p * NOTE : (p + 1) * NOTE] = kv[p * PIECE + BLOCK : (p + 1) * PIECE]
        key_aug[rows, HEAD_DIM:] = (
            first * later.astype(f32) + same * diagonal.astype(f32)
        ).astype(bf16)
    value_rows[...] = with_ones(chunk_rows(kv, value_cols))
    scores[0] = dot(key_aug[...], q_aug[:, lanes_of(0)])
    for j in range(SUBS):
        if j + 1 < SUBS:
            scores[(j + 1) % 2] = dot(key_aug[...], q_aug[:, lanes_of(j + 1)])
        part, info_rows = softmax_part(scores[j % 2], value_rows[...])
        raised[:, lanes_of(j)] = part
        packed[:, lanes_of(j)] = info_rows


def forward(info, kv, q_aug, offset):
    return call(
        functools.partial(forward_kernel, offset),
        "forward",
        [SMEM] + [VMEM] * 2,
        [
            shape(CHUNK, LANES),
            shape(HEAD_DIM + 16, LANES, dtype=f32),
            shape(4 * NOTE, KV_COLS),
        ],
        [
            pltpu.VMEM((CHUNK, 2 * HEAD_DIM), bf16),
            pltpu.VMEM((HEAD_DIM + 16, CHUNK), bf16),
            pltpu.VMEM((2, CHUNK, TILE), f32),
        ],
        flops=4 * CHUNK * LANES * HEAD_DIM,
    )(info, kv, q_aug)


def combine_kernel(
    info, note_0, note_1, note_2, note_3, grads, part_0, part_1, part_2, part_3, part_own,
    out, cot_aug, gains,
):
    notes = (note_0, note_1, note_2, note_3)
    weights = []
    for sib in range(2):
        own_core = 1 - info[0] if sib else info[0]
        own_row = note_0[0:1, :].astype(f32)
        lane = iota(own_row.shape, 1)

        def field(number):
            mask = lane == own_core * 8 + number
            return jnp.sum(jnp.where(mask, own_row, 0.0), axis=1, keepdims=True)

        ratio = field(0) + field(1) + field(2)
        partner, chosen, count = field(3), field(4), field(5)
        mate = jnp.zeros((1, 1), f32)
        row = iota((4 * NOTE, 1), 0)
        z_here = (info[1] + 4 - row // NOTE) % 4
        for offset, note in zip(offsets, notes):
            seat = z_here * 8 + (info[2] + offset) % 4 * 2
            for side in range(2):
                lanes = [note[:, side * 8 + k : side * 8 + k + 1].astype(f32) for k in range(3)]
                found = jnp.logical_and(
                    row % NOTE == 0, (seat + side).astype(f32) == partner
                )
                ratios = lanes[0] + lanes[1] + lanes[2]
                mate = mate + jnp.sum(jnp.where(found, ratios, 0.0), axis=0, keepdims=True)
        sign = 2.0 * chosen - 1.0
        pair_weight = sign * jax.nn.sigmoid(-pair_beta * (sign * (ratio - mate)))
        token = (iota((1, TILE), 1) % TOKENS).astype(f32)
        weights.append(jnp.where(token < count, pair_weight, 0.0))

    for j in range(SUBS):
        lanes = lanes_of(j)
        parts = (part_0, part_1, part_2, part_3) + ((part_own,) if j % 2 else ())
        tops = [part[HEAD_DIM + 8 : HEAD_DIM + 9, lanes] for part in parts]
        top = functools.reduce(jnp.maximum, tops)
        factors = [jnp.exp2((one - top) * exp2_scale) for one in tops]
        length = sum(f * part[HEAD_DIM : HEAD_DIM + 1, lanes] for f, part in zip(factors, parts))
        inverse = 1.0 / length
        factors = [f * inverse for f in factors]
        rounded = sum(f * part[:HEAD_DIM, lanes] for f, part in zip(factors, parts)).astype(bf16)
        out[:, lanes] = rounded
        gains[:, lanes] = jnp.concatenate(
            factors + [jnp.zeros((8 - len(factors), TILE), f32)], axis=0
        )
        if j % 2:
            cot = (weights[j // 2] * grads[:, lanes].astype(f32)).astype(bf16)
        else:
            cot = grads[:, lanes]
        cot_aug[:HEAD_DIM, lanes] = cot
        row_dot = -jnp.sum(cot.astype(f32) * rounded.astype(f32), axis=0, keepdims=True)
        high = row_dot.astype(bf16).astype(f32)
        middle = (row_dot - high).astype(bf16).astype(f32)
        low = row_dot - high - middle
        row = iota((16, TILE), 0)
        split = jnp.where(
            row == 0, high, jnp.where(row == 1, middle, jnp.where(row == 2, low, 0.0))
        )
        cot_aug[HEAD_DIM : HEAD_DIM + 16, lanes] = split.astype(bf16)
        cot_aug[HEAD_DIM + 16 :, lanes] = jnp.zeros((HEAD_DIM - 16, TILE), bf16)


def combine(info, notes, grads, parts):
    return call(
        combine_kernel,
        "combine",
        [SMEM] + [VMEM] * 10,
        [shape(HEAD_DIM, LANES), shape(2 * HEAD_DIM, LANES), shape(8, LANES, dtype=f32)],
    )(info, *notes, grads, *parts)


def value_aug_of(value_rows):
    column = iota(value_rows.shape, 1)
    return jnp.concatenate([value_rows, (column < 3).astype(f32).astype(bf16)], axis=1)


def backward_kernel(
    chunk, kv, raised, q_aug, cot_aug, gains, slopes, grad, value_aug, moved, scaled_q, scaled_cot
):
    value_aug[...] = value_aug_of(chunk_rows(kv, value_cols))
    moved[0] = dot(value_aug[...], cot_aug[:, lanes_of(0)])
    for j in range(SUBS):
        lanes = lanes_of(j)
        if j + 1 < SUBS:
            moved[(j + 1) % 2] = dot(value_aug[...], cot_aug[:, lanes_of(j + 1)])
        gain = gains[chunk : chunk + 1, lanes]
        scaled_cot[:, lanes] = (cot_aug[:HEAD_DIM, lanes].astype(f32) * gain).astype(bf16)
        scaled_q[:, lanes] = (
            q_aug[:HEAD_DIM, lanes].astype(f32) * (gain * score_scale)
        ).astype(bf16)
        slopes[:, lanes] = (raised[:, lanes].astype(f32) * moved[j % 2]).astype(bf16)
    grad[:, HEAD_DIM:] = dot(raised[...], scaled_cot[...], 1, 1).astype(grad.dtype)
    grad[:, :HEAD_DIM] = dot(slopes[...], scaled_q[...], 1, 1).astype(grad.dtype)


def backward(kv, raised, q_aug, cot_aug, gains, chunk, kind):
    return call(
        functools.partial(backward_kernel, chunk),
        "backward",
        [VMEM] * 5,
        [shape(CHUNK, LANES), shape(CHUNK, KV_COLS, dtype=kind)],
        [
            pltpu.VMEM((CHUNK, 2 * HEAD_DIM), bf16),
            pltpu.VMEM((2, CHUNK, TILE), f32),
            pltpu.VMEM((HEAD_DIM, LANES), bf16),
            pltpu.VMEM((HEAD_DIM, LANES), bf16),
        ],
        flops=6 * CHUNK * LANES * HEAD_DIM,
    )(kv, raised, q_aug, cot_aug, gains)


def rows_of(turned_rows):
    rows = turned_rows.T
    return jnp.concatenate(
        [rows[g * TOKENS : (g + 1) * TOKENS] for g in range(GROUP)], axis=1
    )


def finish_kernel(
    kv_0, kv_1, kv_2, kv_3, slopes_0, slopes_1, slopes_2, slopes_3,
    kv_own, kv_recv, raised, q_aug, cot_aug, gains, out,
    own_result, sib_result, own_grad, sib_grad, keys,
):
    for chunk, kv in enumerate((kv_0, kv_1, kv_2, kv_3)):
        keys[:, chunk * CHUNK : (chunk + 1) * CHUNK] = chunk_rows(kv, key_cols).T
    for j in (2, 3, 0, 1):
        lanes = lanes_of(j)
        sib, resp = j // 2, j % 2
        result = sib_result if sib else own_result
        total = None
        for chunk, slopes in enumerate((slopes_0, slopes_1, slopes_2, slopes_3)):
            part = dot(keys[:, chunk * CHUNK : (chunk + 1) * CHUNK], slopes[:, lanes])
            part = part * (gains[chunk : chunk + 1, lanes] * score_scale)
            total = part if total is None else total + part
        if resp:
            gain = gains[4:5, lanes]
            rows = (kv_recv if sib else kv_own)[TOKENS:BLOCK]
            own_raised = raised[:, lanes_of(sib)]
            grad = sib_grad if sib else own_grad
            moved = dot(value_aug_of(rows[:, HEAD_DIM:]), cot_aug[:, lanes])
            own_slopes = (own_raised.astype(f32) * moved).astype(bf16)
            total = total + dot(rows[:, :HEAD_DIM].T, own_slopes) * (gain * score_scale)
            scaled_q = (q_aug[:HEAD_DIM, lanes].astype(f32) * (gain * score_scale)).astype(bf16)
            scaled_cot = (cot_aug[:HEAD_DIM, lanes].astype(f32) * gain).astype(bf16)
            grad[:, :HEAD_DIM] = dot(own_slopes, scaled_q, 1, 1).astype(bf16)
            grad[:, HEAD_DIM:] = dot(own_raised, scaled_cot, 1, 1).astype(bf16)
        result[resp] = rows_of(out[:, lanes].astype(f32)).astype(bf16)
        result[2 + resp] = rows_of(total).astype(bf16)


def finish(kvs, slopes, kv_own, kv_recv, raised, q_aug, cot_aug, gains, out):
    return call(
        finish_kernel,
        "finish",
        [VMEM] * 15,
        [shape(4, TOKENS, Q_COLS)] * 2 + [shape(TOKENS, KV_COLS)] * 2,
        [pltpu.VMEM((HEAD_DIM, 4 * CHUNK), bf16)],
        flops=6 * CHUNK * LANES * HEAD_DIM,
    )(*kvs, *slopes, kv_own, kv_recv, raised, q_aug, cot_aug, gains, out)


def gate_kernel(result, grad, after, result_out, grad_out):
    result_out[...] = result[...]
    grad_out[...] = grad[...]


def gate(result, grad, after):
    return call(
        gate_kernel,
        "gate",
        [VMEM] * 2 + [AFTER],
        [shape(4, TOKENS, Q_COLS), shape(TOKENS, KV_COLS)],
    )(result, grad, after)


def place_kernel(
    info, own, recv, own_grad, recv_grad, prompt_out, resp_out, prompt_dq, resp_dq, resp_dkv, done, sems
):
    pairs = []
    for side, source, grad in ((info[0], own, own_grad), (1 - info[0], recv, recv_grad)):
        pairs += [
            (b, a) for a, b in half_copies(side, prompt_out, resp_out, prompt_dq, resp_dq, source)
        ]
        pairs.append((grad, resp_dkv.at[0, :, columns(side, KV_COLS)]))
    copies = started(pairs, sems)
    done[...] = jnp.zeros_like(done)
    waited(copies)


def place(info, own, recv, own_grad, recv_grad):
    prompt = shape(TOKENS, 2 * Q_COLS)
    resp = shape(1, TOKENS, 2 * Q_COLS)
    return call(
        place_kernel,
        "place",
        [SMEM] + [VMEM] * 4,
        [prompt, resp, prompt, resp, shape(1, TOKENS, 2 * KV_COLS), shape(8, 128, dtype=f32)],
        [pltpu.SemaphoreType.DMA((10,))],
        out_specs=[HBM] * 5 + [VMEM],
    )(info, own, recv, own_grad, recv_grad)


def sum_x_kernel(own, recv_1, recv_2, recv_3, after, kept, sent):
    for p in range(4):
        rows = slice(p * BLOCK, (p + 1) * BLOCK)
        total = own[rows]
        for recv in (recv_1, recv_2, recv_3):
            total = total + recv[rows].astype(f32)
        kept[p * TOKENS : (p + 1) * TOKENS] = total[:TOKENS]
        sent[p * TOKENS : (p + 1) * TOKENS] = total[TOKENS:].astype(bf16)


def sum_x(own, recvs, after):
    return call(
        sum_x_kernel,
        "sum_x",
        [VMEM] * 4 + [AFTER],
        [shape(4 * TOKENS, KV_COLS, dtype=f32), shape(4 * TOKENS, KV_COLS)],
    )(own, *recvs, after)


def mix_kernel(kept, recv, first, second, third, fourth):
    for p, out in enumerate((first, second, third, fourth)):
        rows = slice(p * TOKENS, (p + 1) * TOKENS)
        out[:, :KV_COLS] = kept[rows].astype(out.dtype)
        out[:, KV_COLS:] = recv[rows].astype(out.dtype)


def mix(kept, recv):
    return call(
        mix_kernel,
        "mix",
        [VMEM] * 2,
        [shape(TOKENS, 2 * KV_COLS, dtype=bf16 if p else f32) for p in range(4)],
    )(kept, recv)


def sum_z_kernel(info, own, recv_1, recv_2, recv_3, after, out):
    total = own[...]
    for recv in (recv_1, recv_2, recv_3):
        total = total + recv[...].astype(f32)
    total = total.astype(bf16)
    core = info[0]

    @pl.when(core == 0)
    def _():
        out[...] = total

    @pl.when(core == 1)
    def _():
        out[:, :KV_COLS] = total[:, KV_COLS:]
        out[:, KV_COLS:] = total[:, :KV_COLS]


def sum_z(info, own, recvs, after):
    return call(
        sum_z_kernel,
        "sum_z",
        [SMEM] + [VMEM] * 4 + [AFTER],
        shape(TOKENS, 2 * KV_COLS),
    )(info, own, *recvs, after)


def shards(
    prompt_q,
    prompt_kv,
    resp_q,
    resp_kv,
    prompt_grad,
    resp_grad,
    resp_len,
    logratio,
    partner,
    chosen,
):
    own_index = lax.axis_index("resp")
    core = own_index % 2
    info = jnp.stack([core, own_index // 8, own_index // 2 % 4]).astype(jnp.int32)
    prompt_q, prompt_kv, resp_q, resp_kv, prompt_grad, resp_grad = [
        pltpu.with_memory_space_constraint(array, pltpu.HBM)
        for array in (prompt_q, prompt_kv, resp_q, resp_kv, prompt_grad, resp_grad)
    ]

    kv_own, kv_send, q_send = pack(
        info,
        logratio,
        partner,
        chosen,
        resp_len,
        prompt_kv,
        resp_kv,
        prompt_q,
        resp_q,
        prompt_grad,
        resp_grad,
    )
    kv_recv = swap_core(kv_send)
    q_recv = swap_core(q_send)
    block = join_cores(kv_own, kv_recv)
    pieces = [block] + [shift_z(block, step) for step in (1, 2, 3)]
    q_aug, grads, raised_own, part_own = prep(
        info, prompt_q, resp_q, prompt_grad, resp_grad, q_recv, kv_own, kv_recv
    )
    chunk_own = join_z(pieces, part_own)
    kvs = [chunk_own] + [shift_x(chunk_own, 4 - offset) for offset in offsets[1:]]

    raised, parts, notes = [], [], []
    for kv, offset in zip(kvs, offsets):
        one, part, note = forward(info, kv, q_aug, offset)
        raised.append(one)
        parts.append(part)
        notes.append(note)
    out, cot_aug, gains = combine(info, notes, grads, parts + [part_own])

    slopes = [None] * 4
    returned = []
    for chunk in (3, 2, 1, 0):
        kind = bf16 if chunk else f32
        slopes[chunk], grad = backward(
            kvs[chunk], raised[chunk], q_aug, cot_aug, gains, chunk, kind
        )
        returned.append(shift_x(grad, offsets[chunk]) if chunk else grad)

    own_result, sib_result, own_grad, sib_grad = finish(
        kvs, slopes, kv_own, kv_recv, raised_own, q_aug, cot_aug, gains, out
    )
    kept, sent = sum_x(returned[3], returned[:3], own_grad)
    recv_sent = swap_core(sent)
    blocks = mix(kept, recv_sent)
    sib_result, sib_grad = gate(sib_result, sib_grad, blocks[3])
    recv_result = swap_core(sib_result)
    recv_grad = swap_core(sib_grad)
    recvs = [shift_z(blocks[p], 4 - p) for p in (1, 2, 3)]
    prompt_out, resp_out, prompt_dq, resp_dq, resp_dkv, placed = place(
        info, own_result, recv_result, own_grad, recv_grad
    )
    prompt_dkv = sum_z(info, blocks[0], recvs, placed)
    return (prompt_out, resp_out, prompt_dq, resp_dq, prompt_dkv, resp_dkv)


def solution(mesh):
    return jax.shard_map(
        shards,
        mesh=mesh,
        in_specs=(
            P(("batch", "resp"), "head"),
            P(("batch", "resp"), "head"),
            P(("batch", "resp"), None, "head"),
            P(("batch", "resp"), None, "head"),
            P(("batch", "resp"), "head"),
            P(("batch", "resp"), None, "head"),
            P(("batch", "resp")),
            P(("batch", "resp")),
            P(("batch", "resp")),
            P(("batch", "resp")),
        ),
        out_specs=(
            P(("batch", "resp"), "head"),
            P(("batch", "resp"), None, "head"),
            P(("batch", "resp"), "head"),
            P(("batch", "resp"), None, "head"),
            P(("batch", "resp"), "head"),
            P(("batch", "resp"), None, "head"),
        ),
        check_vma=False,
    )
```

time: 245 us -> 72.1 us (0.29)
  blocking collectives: 70.4 us -> 0 us
  matrix products: 49.2 us -> 0 us
  local copies, waits for them, and re-layouts: 44.1 us -> 0 us
  Pallas kernels: 0 us -> 27.5 us
  other arithmetic: 18.7 us -> 0.08 us
  waiting for transfers between devices: 33.6 us -> 18.8 us
  between operations: 18 us -> 3.43 us
  starting transfers between devices: 9.58 us -> 21.9 us
    unnamed x1 -> x0, blocking collectives: 70.4 us -> none
    all_to_all x1 -> x0, waiting for transfers between devices: 33 us -> none  [shards(): lax.all_to_all(jnp.stack(pieces, axis=1).reshape(prompt_len, head_pairs *...]
    dot_general x24 -> x0, matrix products: 32.3 us -> none  [the longest x6 7.31 us: key_grads(): jnp.einsum('gnm,ngd->md', weight_block, cotangent, preferred_element_type...]
    pallas_call x0 -> x19, Pallas kernels: none -> 27.5 us  [the longest x4 9.28 us: forward(): call(functools.partial(forward_kernel, offset), 'forward', [SMEM] + [VMEM...]
    ppermute x0 -> x17, starting transfers between devices: none -> 21.9 us  [the longest x5 9.99 us: swap_core(): return lax.ppermute(value, 'resp', [(r, r ^ 1) for r in range(32)])]
    ppermute x0 -> x17, waiting for transfers between devices: none -> 18.8 us  [the longest x6 9.56 us: shift_x(): return lax.ppermute(value, 'resp', pairs)]
    sub x4 -> x0, matrix products: 16.9 us -> none  [head_pass(): raised = jnp.exp(scores - row_max)]
    another operation x7 -> x0, local copies, waits for them, and re-layouts: 15.8 us -> none  [the longest x1 14.2 us: shards(): jnp.stack(pieces, axis=1).reshape(prompt_len, head_pairs * 2 * HEAD_DIM)]
  transfers between devices with their start and end apart: 2 -> 17, of which waited for: 1 -> 9; matrix products, arithmetic and copies ran while one was open for 10% -> 0% of each run, Pallas kernels for 0% -> 26%
where the time goes in v3:
time: 72.1 us; the launch traced here: 71.7 us
  Pallas kernels  27.5 us (38%)
  starting transfers between devices  21.9 us (30%)
  waiting for transfers between devices  18.8 us (26%)
  between operations  3.43 us (5%)
    ppermute x5, starting transfers between devices, swap_core(): return lax.ppermute(value, 'resp', [(r, r ^ 1) for r in range(32)])  9.99 us
    ppermute x6, waiting for transfers between devices, shift_x(): return lax.ppermute(value, 'resp', pairs)  9.56 us
    pallas_call x4, Pallas kernels, forward(): call(functools.partial(forward_kernel, offset), 'forward', [SMEM] + [VMEM...  9.28 us
    pallas_call x4, Pallas kernels, backward(): call(functools.partial(backward_kernel, chunk), 'backward', [VMEM] * 5, [...  7.28 us
    ppermute x6, starting transfers between devices, shift_x(): return lax.ppermute(value, 'resp', pairs)  7.1 us
    ppermute x6, waiting for transfers between devices, shift_z(): return lax.ppermute(value, 'resp', pairs)  5.85 us
    ppermute x6, starting transfers between devices, shift_z(): return lax.ppermute(value, 'resp', pairs)  4.81 us
    ppermute x5, waiting for transfers between devices, swap_core(): return lax.ppermute(value, 'resp', [(r, r ^ 1) for r in range(32)])  3.39 us
  transfers between devices with their start and end apart: 17, of which 9 were waited for; matrix products, arithmetic and copies ran while one was open for 0% of the time, Pallas kernels for 26%

profile of v3, /device:TPU:1, one launch (start us, length us, event | category | flops | bytes accessed | tf_op | source)
XLA Modules:
  0.0 71.7 jit_solution(3578329922735883291)
XLA Ops:
  3.3 0.1 pad_add_fusion.info
  3.3 1.8 %pack.1 = (bf16[144,256]{1,0:T(8,128)(2,1)S(1)}, bf16[144,256]{1,0:T(8,128)(2,1)S(1)}, bf16[4,64,1024]{2,1,0:T(8,128)(2,1)S(1)}) custom-call(s32[3]{0:T(128)S(1)} %pad_add_fusion.info, f32[1]{0:T(128)S(6)} %copy.17.logratio, s32[1]{0:T(128)S(6)} %copy.18.partner, s32[1]{0:T(128)S(6)} %copy.19.chosen, s32[1]{0:T(128)S(6)} %copy.16.resp_len, ...), custom_call_target="tpu_custom_call" | custom-call | bytes 1048576 | tf_op jit(solution)/shard_map/pack/pallas_call | solution.py:163
  5.1 3.3 %collective-permute-start.4 = (bf16[4,64,1024]{2,1,0:T(8,128)(2,1)S(1)}, bf16[4,64,1024]{2,1,0:T(8,128)(2,1)S(1)}, u32[]{:S(2)}, u32[]{:S(2)}) collective-permute-start(bf16[4,64,1024]{2,1,0:T(8,128)(2,1)S(1)} %get-tuple-element.56), channel_id=1, source_target_pairs={{0,4},{4,0},{8,12},{12,8},{16,20},{20,16},{24,28},{28,24},{32,36},... | collective-permute-start | bytes 1572872 | tf_op jit(solution)/shard_map/ppermute | solution.py:77
  8.5 0.1 collective-permute-start
  8.6 1.5 %collective-permute-done.recv.kv_recv = bf16[144,256]{1,0:T(8,128)(2,1)S(1)} collective-permute-done((bf16[144,256]{1,0:T(8,128)(2,1)S(1)}, bf16[144,256]{1,0:T(8,128)(2,1)S(1)}, u32[]{:S(2)}, u32[]{:S(2)}) %collective-permute-start) | collective-permute-done | bytes 73760 | tf_op jit(solution)/shard_map/ppermute | solution.py:77
  10.1 2.6 %collective-permute-start.3 = (bf16[144,256]{1,0:T(8,128)(2,1)S(1)}, bf16[144,256]{1,0:T(8,128)(2,1)S(1)}, u32[]{:S(2)}, u32[]{:S(2)}) collective-permute-start(bf16[144,256]{1,0:T(8,128)(2,1)S(1)} %join_cores.1.piece_0), channel_id=1, source_target_pairs={{0,96},{4,100},{8,104},{12,108},{16,112},{20,116},{24,120},{28,124... | collective-permute-start | bytes 221192 | tf_op jit(solution)/shard_map/ppermute | solution.py:82
  12.8 0.0 collective-permute-start.2
  12.8 0.4 collective-permute-start.1
  13.1 0.0 collective-permute-done.4.recv
  13.1 2.5 %prep.1 = (bf16[256,2048]{1,0:T(8,128)(2,1)S(1)}, bf16[128,2048]{1,0:T(8,128)(2,1)S(1)}, bf16[64,1024]{1,0:T(8,128)(2,1)S(1)}, f32[144,2048]{1,0:T(8,128)S(1)}) custom-call(s32[3]{0:T(128)S(1)} %pad_add_fusion.info, bf16[64,2048]{1,0:T(8,128)(2,1)} %pq.3, bf16[1,64,2048]{2,1,0:T(8,128)(2,1)} %rq.3, bf16[64,2048]{1,0:T(8,128)(2,1)} %pg.3, ...), custom_call_target="tpu_custom_call" | custom-call | bytes 1048576 | tf_op jit(solution)/shard_map/prep/pallas_call | solution.py:250
  15.6 0.0 collective-permute-done.3.piece_3
  15.6 4.6 %collective-permute-done.2.piece_2 = bf16[144,256]{1,0:T(8,128)(2,1)S(1)} collective-permute-done((bf16[144,256]{1,0:T(8,128)(2,1)S(1)}, bf16[144,256]{1,0:T(8,128)(2,1)S(1)}, u32[]{:S(2)}, u32[]{:S(2)}) %collective-permute-start.2) | collective-permute-done | bytes 73760 | tf_op jit(solution)/shard_map/ppermute | solution.py:82
  20.2 0.0 collective-permute-done.1.piece_1
  20.2 1.3 %collective-permute-start.5 = (bf16[576,256]{1,0:T(8,128)(2,1)S(1)}, bf16[576,256]{1,0:T(8,128)(2,1)S(1)}, u32[]{:S(2)}, u32[]{:S(2)}) collective-permute-start(bf16[576,256]{1,0:T(8,128)(2,1)S(1)} %join_z.1.kv.kv_0), channel_id=1, source_target_pairs={{0,8},{4,12},{8,16},{12,20},{16,24},{20,28},{24,0},{28,4},{32,40},... | collective-permute-start | bytes 884744 | tf_op jit(solution)/shard_map/ppermute | solution.py:87
  21.5 1.5 %collective-permute-start.6 = (bf16[576,256]{1,0:T(8,128)(2,1)S(1)}, bf16[576,256]{1,0:T(8,128)(2,1)S(1)}, u32[]{:S(2)}, u32[]{:S(2)}) collective-permute-start(bf16[576,256]{1,0:T(8,128)(2,1)S(1)} %join_z.1.kv.kv_0), channel_id=1, source_target_pairs={{0,24},{4,28},{8,0},{12,4},{16,8},{20,12},{24,16},{28,20},{32,56},... | collective-permute-start | bytes 884744 | tf_op jit(solution)/shard_map/ppermute | solution.py:87
  23.0 1.5 %collective-permute-start.7 = (bf16[576,256]{1,0:T(8,128)(2,1)S(1)}, bf16[576,256]{1,0:T(8,128)(2,1)S(1)}, u32[]{:S(2)}, u32[]{:S(2)}) collective-permute-start(bf16[576,256]{1,0:T(8,128)(2,1)S(1)} %join_z.1.kv.kv_0), channel_id=1, source_target_pairs={{0,16},{4,20},{8,24},{12,28},{16,0},{20,4},{24,8},{28,12},{32,48},... | collective-permute-start | bytes 884744 | tf_op jit(solution)/shard_map/ppermute | solution.py:87
  24.5 2.3 %forward.4 = (bf16[512,2048]{1,0:T(8,128)(2,1)S(1)}, f32[144,2048]{1,0:T(8,128)S(1)}, bf16[64,256]{1,0:T(8,128)(2,1)S(1)}) custom-call(s32[3]{0:T(128)S(1)} %pad_add_fusion.info, bf16[576,256]{1,0:T(8,128)(2,1)S(1)} %join_z.1.kv.kv_0, bf16[256,2048]{1,0:T(8,128)(2,1)S(1)} %get-tuple-element.58.q_aug), custom_call_target="tpu_custom_call" | custom-call | flops 536870912 | bytes 1048576 | tf_op jit(solution)/shard_map/forward/pallas_call | solution.py:303
  26.9 2.7 %collective-permute-done.5.kv.kv_1 = bf16[576,256]{1,0:T(8,128)(2,1)S(1)} collective-permute-done((bf16[576,256]{1,0:T(8,128)(2,1)S(1)}, bf16[576,256]{1,0:T(8,128)(2,1)S(1)}, u32[]{:S(2)}, u32[]{:S(2)}) %collective-permute-start.5) | collective-permute-done | bytes 294944 | tf_op jit(solution)/shard_map/ppermute | solution.py:87
  29.6 2.3 %forward.5 = (bf16[512,2048]{1,0:T(8,128)(2,1)S(1)}, f32[144,2048]{1,0:T(8,128)S(1)}, bf16[64,256]{1,0:T(8,128)(2,1)S(1)}) custom-call(s32[3]{0:T(128)S(1)} %pad_add_fusion.info, bf16[576,256]{1,0:T(8,128)(2,1)S(1)} %collective-permute-done.5.kv.kv_1, bf16[256,2048]{1,0:T(8,128)(2,1)S(1)} %get-tuple-element.58.q_aug), custom_call_target="tpu_custom_call" | custom-call | flops 536870912 | bytes 1048576 | tf_op jit(solution)/shard_map/forward/pallas_call | solution.py:303
  31.9 0.0 collective-permute-done.6.kv.kv_2
  31.9 2.3 %forward.6 = (bf16[512,2048]{1,0:T(8,128)(2,1)S(1)}, f32[144,2048]{1,0:T(8,128)S(1)}, bf16[64,256]{1,0:T(8,128)(2,1)S(1)}) custom-call(s32[3]{0:T(128)S(1)} %pad_add_fusion.info, bf16[576,256]{1,0:T(8,128)(2,1)S(1)} %collective-permute-done.6.kv.kv_2, bf16[256,2048]{1,0:T(8,128)(2,1)S(1)} %get-tuple-element.58.q_aug), custom_call_target="tpu_custom_call" | custom-call | flops 536870912 | bytes 1048576 | tf_op jit(solution)/shard_map/forward/pallas_call | solution.py:303
  34.3 2.7 %collective-permute-done.7.kv.kv_3 = bf16[576,256]{1,0:T(8,128)(2,1)S(1)} collective-permute-done((bf16[576,256]{1,0:T(8,128)(2,1)S(1)}, bf16[576,256]{1,0:T(8,128)(2,1)S(1)}, u32[]{:S(2)}, u32[]{:S(2)}) %collective-permute-start.7) | collective-permute-done | bytes 294944 | tf_op jit(solution)/shard_map/ppermute | solution.py:87
  36.9 2.3 %forward.7 = (bf16[512,2048]{1,0:T(8,128)(2,1)S(1)}, f32[144,2048]{1,0:T(8,128)S(1)}, bf16[64,256]{1,0:T(8,128)(2,1)S(1)}) custom-call(s32[3]{0:T(128)S(1)} %pad_add_fusion.info, bf16[576,256]{1,0:T(8,128)(2,1)S(1)} %collective-permute-done.7.kv.kv_3, bf16[256,2048]{1,0:T(8,128)(2,1)S(1)} %get-tuple-element.58.q_aug), custom_call_target="tpu_custom_call" | custom-call | flops 536870912 | bytes 1048576 | tf_op jit(solution)/shard_map/forward/pallas_call | solution.py:303
  39.2 1.6 %combine.1 = (bf16[128,2048]{1,0:T(8,128)(2,1)S(1)}, bf16[256,2048]{1,0:T(8,128)(2,1)S(1)}, f32[8,2048]{1,0:T(8,128)S(1)}) custom-call(s32[3]{0:T(128)S(1)} %pad_add_fusion.info, bf16[64,256]{1,0:T(8,128)(2,1)S(1)} %get-tuple-element.60.note_0, bf16[64,256]{1,0:T(8,128)(2,1)S(1)} %get-tuple-element.61.note_1, bf16[64,256]{1,0:T(8,128)(2,1)S(1)} %get-tuple-element.62.note_2, ...), custom_call_target="tpu_custom_call" | custom-call | bytes 1048576 | tf_op jit(solution)/shard_map/combine/pallas_call | solution.py:387
  40.9 1.8 %backward.5 = (bf16[512,2048]{1,0:T(8,128)(2,1)S(1)}, bf16[512,256]{1,0:T(8,128)(2,1)S(1)}) custom-call(bf16[576,256]{1,0:T(8,128)(2,1)S(1)} %collective-permute-done.5.kv.kv_1, bf16[512,2048]{1,0:T(8,128)(2,1)S(1)} %get-tuple-element.72.raised, bf16[256,2048]{1,0:T(8,128)(2,1)S(1)} %get-tuple-element.58.q_aug, ...), custom_call_target="tpu_custom_call" | custom-call | flops 805306368 | bytes 1048576 | tf_op jit(solution)/shard_map/backward/pallas_call | solution.py:420
  42.7 1.2 %collective-permute-start.10 = (bf16[512,256]{1,0:T(8,128)(2,1)S(1)}, bf16[512,256]{1,0:T(8,128)(2,1)S(1)}, u32[]{:S(2)}, u32[]{:S(2)}) collective-permute-start(bf16[512,256]{1,0:T(8,128)(2,1)S(1)} %get-tuple-element.86), channel_id=1, source_target_pairs={{0,24},{4,28},{8,0},{12,4},{16,8},{20,12},{24,16},{28,20},{32,56},... | collective-permute-start | bytes 786440 | tf_op jit(solution)/shard_map/ppermute | solution.py:87
  43.9 1.8 %backward.6 = (bf16[512,2048]{1,0:T(8,128)(2,1)S(1)}, bf16[512,256]{1,0:T(8,128)(2,1)S(1)}) custom-call(bf16[576,256]{1,0:T(8,128)(2,1)S(1)} %collective-permute-done.6.kv.kv_2, bf16[512,2048]{1,0:T(8,128)(2,1)S(1)} %get-tuple-element.74.raised, bf16[256,2048]{1,0:T(8,128)(2,1)S(1)} %get-tuple-element.58.q_aug, ...), custom_call_target="tpu_custom_call" | custom-call | flops 805306368 | bytes 1048576 | tf_op jit(solution)/shard_map/backward/pallas_call | solution.py:420
  45.8 0.6 collective-permute-start.9
  46.4 1.8 %backward.7 = (bf16[512,2048]{1,0:T(8,128)(2,1)S(1)}, bf16[512,256]{1,0:T(8,128)(2,1)S(1)}) custom-call(bf16[576,256]{1,0:T(8,128)(2,1)S(1)} %collective-permute-done.7.kv.kv_3, bf16[512,2048]{1,0:T(8,128)(2,1)S(1)} %get-tuple-element.76.raised, bf16[256,2048]{1,0:T(8,128)(2,1)S(1)} %get-tuple-element.58.q_aug, ...), custom_call_target="tpu_custom_call" | custom-call | flops 805306368 | bytes 1048576 | tf_op jit(solution)/shard_map/backward/pallas_call | solution.py:420
  48.2 1.0 %collective-permute-start.8 = (bf16[512,256]{1,0:T(8,128)(2,1)S(1)}, bf16[512,256]{1,0:T(8,128)(2,1)S(1)}, u32[]{:S(2)}, u32[]{:S(2)}) collective-permute-start(bf16[512,256]{1,0:T(8,128)(2,1)S(1)} %get-tuple-element.84), channel_id=1, source_target_pairs={{0,16},{4,20},{8,24},{12,28},{16,0},{20,4},{24,8},{28,12},{32,48},... | collective-permute-start | bytes 786440 | tf_op jit(solution)/shard_map/ppermute | solution.py:87
  49.2 1.8 %backward.4 = (bf16[512,2048]{1,0:T(8,128)(2,1)S(1)}, f32[512,256]{1,0:T(8,128)S(1)}) custom-call(bf16[576,256]{1,0:T(8,128)(2,1)S(1)} %join_z.1.kv.kv_0, bf16[512,2048]{1,0:T(8,128)(2,1)S(1)} %get-tuple-element.59.raised, bf16[256,2048]{1,0:T(8,128)(2,1)S(1)} %get-tuple-element.58.q_aug, bf16[256,2048]{1,0:T(8,128)(2,1)S(1)} %get-tuple-element.69.cot_aug, ...), custom_call_target="tpu_custom_call" | custom-call | flops 805306368 | bytes 1048576 | tf_op jit(solution)/shard_map/backward/pallas_call | solution.py:420
  51.0 2.0 %finish.1 = (bf16[4,64,1024]{2,1,0:T(8,128)(2,1)S(1)}, bf16[4,64,1024]{2,1,0:T(8,128)(2,1)S(1)}, bf16[64,256]{1,0:T(8,128)(2,1)S(1)}, bf16[64,256]{1,0:T(8,128)(2,1)S(1)}) custom-call(bf16[576,256]{1,0:T(8,128)(2,1)S(1)} %join_z.1.kv.kv_0, bf16[576,256]{1,0:T(8,128)(2,1)S(1)} %collective-permute-done.5.kv.kv_1, ...), custom_call_target="tpu_custom_call" | custom-call | flops 805306368 | bytes 1048576 | tf_op jit(solution)/shard_map/finish/pallas_call | solution.py:475
  53.0 0.0 collective-permute-done.10.recv_3
  53.0 0.3 collective-permute-done.9.recv_2
  53.4 3.8 %collective-permute-done.8.recv_1 = bf16[512,256]{1,0:T(8,128)(2,1)S(1)} collective-permute-done((bf16[512,256]{1,0:T(8,128)(2,1)S(1)}, bf16[512,256]{1,0:T(8,128)(2,1)S(1)}, u32[]{:S(2)}, u32[]{:S(2)}) %collective-permute-start.8) | collective-permute-done | bytes 262176 | tf_op jit(solution)/shard_map/ppermute | solution.py:87
  57.2 0.1 sum_x.1
  57.3 5.1 %collective-permute-start.11 = (bf16[256,256]{1,0:T(8,128)(2,1)S(1)}, bf16[256,256]{1,0:T(8,128)(2,1)S(1)}, u32[]{:S(2)}, u32[]{:S(2)}) collective-permute-start(bf16[256,256]{1,0:T(8,128)(2,1)S(1)} %get-tuple-element.89), channel_id=1, source_target_pairs={{0,4},{4,0},{8,12},{12,8},{16,20},{20,16},{24,28},{28,24},{32,36},... | collective-permute-start | bytes 393224 | tf_op jit(solution)/shard_map/ppermute | solution.py:77
  62.4 1.0 %collective-permute-done.11.recv = bf16[256,256]{1,0:T(8,128)(2,1)S(1)} collective-permute-done((bf16[256,256]{1,0:T(8,128)(2,1)S(1)}, bf16[256,256]{1,0:T(8,128)(2,1)S(1)}, u32[]{:S(2)}, u32[]{:S(2)}) %collective-permute-start.11) | collective-permute-done | bytes 131104 | tf_op jit(solution)/shard_map/ppermute | solution.py:77
  63.5 0.4 collective-permute-start.12
  64.0 0.0 collective-permute-start.14
  64.0 0.3 collective-permute-start.15
  64.3 1.5 %collective-permute-start.16 = (bf16[64,512]{1,0:T(8,128)(2,1)S(1)}, bf16[64,512]{1,0:T(8,128)(2,1)S(1)}, u32[]{:S(2)}, u32[]{:S(2)}) collective-permute-start(bf16[64,512]{1,0:T(8,128)(2,1)S(1)} %get-tuple-element.90.after), channel_id=1, source_target_pairs={{0,32},{4,36},{8,40},{12,44},{16,48},{20,52},{24,56},{28,60},{32,6... | collective-permute-start | bytes 196616 | tf_op jit(solution)/shard_map/ppermute | solution.py:82
  65.7 1.0 %collective-permute-start.13 = (bf16[64,256]{1,0:T(8,128)(2,1)S(1)}, bf16[64,256]{1,0:T(8,128)(2,1)S(1)}, u32[]{:S(2)}, u32[]{:S(2)}) collective-permute-start(bf16[64,256]{1,0:T(8,128)(2,1)S(1)} %get-tuple-element.92), channel_id=1, source_target_pairs={{0,4},{4,0},{8,12},{12,8},{16,20},{20,16},{24,28},{28,24},{32,36},... | collective-permute-start | bytes 98312 | tf_op jit(solution)/shard_map/ppermute | solution.py:77
  66.7 0.9 %collective-permute-done.13.recv_grad = bf16[64,256]{1,0:T(8,128)(2,1)S(1)} collective-permute-done((bf16[64,256]{1,0:T(8,128)(2,1)S(1)}, bf16[64,256]{1,0:T(8,128)(2,1)S(1)}, u32[]{:S(2)}, u32[]{:S(2)}) %collective-permute-start.13) | collective-permute-done | bytes 32800 | tf_op jit(solution)/shard_map/ppermute | solution.py:77
  67.6 0.0 collective-permute-done.12.recv
  67.6 1.6 %place.1 = (bf16[64,2048]{1,0:T(8,128)(2,1)}, bf16[1,64,2048]{2,1,0:T(8,128)(2,1)}, bf16[64,2048]{1,0:T(8,128)(2,1)}, bf16[1,64,2048]{2,1,0:T(8,128)(2,1)}, bf16...) custom-call(s32[3]{0:T(128)S(1)} %pad_add_fusion.info, bf16[4,64,1024]{2,1,0:T(8,128)(2,1)S(1)} %get-tuple-element.80.own, ...), custom_call_target="tpu_custom_call" | custom-call | bytes 1048576 | tf_op jit(solution)/shard_map/place/pallas_call | solution.py:516
  69.2 1.2 %collective-permute-done.16.recv_3 = bf16[64,512]{1,0:T(8,128)(2,1)S(1)} collective-permute-done((bf16[64,512]{1,0:T(8,128)(2,1)S(1)}, bf16[64,512]{1,0:T(8,128)(2,1)S(1)}, u32[]{:S(2)}, u32[]{:S(2)}) %collective-permute-start.16) | collective-permute-done | bytes 65568 | tf_op jit(solution)/shard_map/ppermute | solution.py:82
  70.5 1.2 %sum_z.1 = bf16[64,512]{1,0:T(8,128)(2,1)} custom-call(s32[3]{0:T(128)S(1)} %pad_add_fusion.info, f32[64,512]{1,0:T(8,128)S(1)} %get-tuple-element.97.own, bf16[64,512]{1,0:T(8,128)(2,1)S(1)} %collective-permute-done.14.recv_1, bf16[64,512]{1,0:T(8,128)(2,1)S(1)} %collective-permute-done.15.recv_2, bf16[64,512]{1,0:T(8,128)(2,1)S(1)} %collective-permute-done.16.recv_3, ...), custom_call_target="tpu_custom_call" | custom-call | bytes 1048576 | tf_op jit(solution)/shard_map/sum_z/pallas_call | solution.py:579
  (6 shorter events, 0.1 us)
Async XLA Ops:
  5.1 8.0 %collective-permute-start.4 = (bf16[4,64,1024]{2,1,0:T(8,128)(2,1)S(1)}, bf16[4,64,1024]{2,1,0:T(8,128)(2,1)S(1)}, u32[]{:S(2)}, u32[]{:S(2)}) collective-permute-start(bf16[4,64,1024]{2,1,0:T(8,128)(2,1)S(1)} %get-tuple-element.56), channel_id=1, source_target_pairs={{0,4},{4,0},{8,12},{12,8},{16,20},{20,16},{24,28},{28,24},{32,36},... | collective-permute-start | bytes 1572872 | tf_op jit(solution)/shard_map/ppermute | solution.py:77
  8.5 1.6 %collective-permute-start = (bf16[144,256]{1,0:T(8,128)(2,1)S(1)}, bf16[144,256]{1,0:T(8,128)(2,1)S(1)}, u32[]{:S(2)}, u32[]{:S(2)}) collective-permute-start(bf16[144,256]{1,0:T(8,128)(2,1)S(1)} %get-tuple-element.55), channel_id=1, source_target_pairs={{0,4},{4,0},{8,12},{12,8},{16,20},{20,16},{24,28},{28,24},{32,36},... | collective-permute-start | bytes 221192 | tf_op jit(solution)/shard_map/ppermute | solution.py:77
  10.1 5.5 %collective-permute-start.3 = (bf16[144,256]{1,0:T(8,128)(2,1)S(1)}, bf16[144,256]{1,0:T(8,128)(2,1)S(1)}, u32[]{:S(2)}, u32[]{:S(2)}) collective-permute-start(bf16[144,256]{1,0:T(8,128)(2,1)S(1)} %join_cores.1.piece_0), channel_id=1, source_target_pairs={{0,96},{4,100},{8,104},{12,108},{16,112},{20,116},{24,120},{28,124... | collective-permute-start | bytes 221192 | tf_op jit(solution)/shard_map/ppermute | solution.py:82
  12.8 7.5 %collective-permute-start.2 = (bf16[144,256]{1,0:T(8,128)(2,1)S(1)}, bf16[144,256]{1,0:T(8,128)(2,1)S(1)}, u32[]{:S(2)}, u32[]{:S(2)}) collective-permute-start(bf16[144,256]{1,0:T(8,128)(2,1)S(1)} %join_cores.1.piece_0), channel_id=1, source_target_pairs={{0,64},{4,68},{8,72},{12,76},{16,80},{20,84},{24,88},{28,92},{32,9... | collective-permute-start | bytes 221192 | tf_op jit(solution)/shard_map/ppermute | solution.py:82
  12.8 7.5 %collective-permute-start.1 = (bf16[144,256]{1,0:T(8,128)(2,1)S(1)}, bf16[144,256]{1,0:T(8,128)(2,1)S(1)}, u32[]{:S(2)}, u32[]{:S(2)}) collective-permute-start(bf16[144,256]{1,0:T(8,128)(2,1)S(1)} %join_cores.1.piece_0), channel_id=1, source_target_pairs={{0,32},{4,36},{8,40},{12,44},{16,48},{20,52},{24,56},{28,60},{32,6... | collective-permute-start | bytes 221192 | tf_op jit(solution)/shard_map/ppermute | solution.py:82
  20.2 9.4 %collective-permute-start.5 = (bf16[576,256]{1,0:T(8,128)(2,1)S(1)}, bf16[576,256]{1,0:T(8,128)(2,1)S(1)}, u32[]{:S(2)}, u32[]{:S(2)}) collective-permute-start(bf16[576,256]{1,0:T(8,128)(2,1)S(1)} %join_z.1.kv.kv_0), channel_id=1, source_target_pairs={{0,8},{4,12},{8,16},{12,20},{16,24},{20,28},{24,0},{28,4},{32,40},... | collective-permute-start | bytes 884744 | tf_op jit(solution)/shard_map/ppermute | solution.py:87
  21.5 10.4 %collective-permute-start.6 = (bf16[576,256]{1,0:T(8,128)(2,1)S(1)}, bf16[576,256]{1,0:T(8,128)(2,1)S(1)}, u32[]{:S(2)}, u32[]{:S(2)}) collective-permute-start(bf16[576,256]{1,0:T(8,128)(2,1)S(1)} %join_z.1.kv.kv_0), channel_id=1, source_target_pairs={{0,24},{4,28},{8,0},{12,4},{16,8},{20,12},{24,16},{28,20},{32,56},... | collective-permute-start | bytes 884744 | tf_op jit(solution)/shard_map/ppermute | solution.py:87
  23.0 13.9 %collective-permute-start.7 = (bf16[576,256]{1,0:T(8,128)(2,1)S(1)}, bf16[576,256]{1,0:T(8,128)(2,1)S(1)}, u32[]{:S(2)}, u32[]{:S(2)}) collective-permute-start(bf16[576,256]{1,0:T(8,128)(2,1)S(1)} %join_z.1.kv.kv_0), channel_id=1, source_target_pairs={{0,16},{4,20},{8,24},{12,28},{16,0},{20,4},{24,8},{28,12},{32,48},... | collective-permute-start | bytes 884744 | tf_op jit(solution)/shard_map/ppermute | solution.py:87
  42.7 10.3 %collective-permute-start.10 = (bf16[512,256]{1,0:T(8,128)(2,1)S(1)}, bf16[512,256]{1,0:T(8,128)(2,1)S(1)}, u32[]{:S(2)}, u32[]{:S(2)}) collective-permute-start(bf16[512,256]{1,0:T(8,128)(2,1)S(1)} %get-tuple-element.86), channel_id=1, source_target_pairs={{0,24},{4,28},{8,0},{12,4},{16,8},{20,12},{24,16},{28,20},{32,56},... | collective-permute-start | bytes 786440 | tf_op jit(solution)/shard_map/ppermute | solution.py:87
  45.8 7.6 %collective-permute-start.9 = (bf16[512,256]{1,0:T(8,128)(2,1)S(1)}, bf16[512,256]{1,0:T(8,128)(2,1)S(1)}, u32[]{:S(2)}, u32[]{:S(2)}) collective-permute-start(bf16[512,256]{1,0:T(8,128)(2,1)S(1)} %get-tuple-element.85), channel_id=1, source_target_pairs={{0,8},{4,12},{8,16},{12,20},{16,24},{20,28},{24,0},{28,4},{32,40},... | collective-permute-start | bytes 786440 | tf_op jit(solution)/shard_map/ppermute | solution.py:87
  48.2 9.0 %collective-permute-start.8 = (bf16[512,256]{1,0:T(8,128)(2,1)S(1)}, bf16[512,256]{1,0:T(8,128)(2,1)S(1)}, u32[]{:S(2)}, u32[]{:S(2)}) collective-permute-start(bf16[512,256]{1,0:T(8,128)(2,1)S(1)} %get-tuple-element.84), channel_id=1, source_target_pairs={{0,16},{4,20},{8,24},{12,28},{16,0},{20,4},{24,8},{28,12},{32,48},... | collective-permute-start | bytes 786440 | tf_op jit(solution)/shard_map/ppermute | solution.py:87
  57.3 6.1 %collective-permute-start.11 = (bf16[256,256]{1,0:T(8,128)(2,1)S(1)}, bf16[256,256]{1,0:T(8,128)(2,1)S(1)}, u32[]{:S(2)}, u32[]{:S(2)}) collective-permute-start(bf16[256,256]{1,0:T(8,128)(2,1)S(1)} %get-tuple-element.89), channel_id=1, source_target_pairs={{0,4},{4,0},{8,12},{12,8},{16,20},{20,16},{24,28},{28,24},{32,36},... | collective-permute-start | bytes 393224 | tf_op jit(solution)/shard_map/ppermute | solution.py:77
  63.5 4.1 %collective-permute-start.12 = (bf16[4,64,1024]{2,1,0:T(8,128)(2,1)S(1)}, bf16[4,64,1024]{2,1,0:T(8,128)(2,1)S(1)}, u32[]{:S(2)}, u32[]{:S(2)}) collective-permute-start(bf16[4,64,1024]{2,1,0:T(8,128)(2,1)S(1)} %get-tuple-element.91), channel_id=1, source_target_pairs={{0,4},{4,0},{8,12},{12,8},{16,20},{20,16},{24,28},{28,24},{32,36},... | collective-permute-start | bytes 1572872 | tf_op jit(solution)/shard_map/ppermute | solution.py:77
  64.0 5.3 %collective-permute-start.14 = (bf16[64,512]{1,0:T(8,128)(2,1)S(1)}, bf16[64,512]{1,0:T(8,128)(2,1)S(1)}, u32[]{:S(2)}, u32[]{:S(2)}) collective-permute-start(bf16[64,512]{1,0:T(8,128)(2,1)S(1)} %get-tuple-element.98), channel_id=1, source_target_pairs={{0,96},{4,100},{8,104},{12,108},{16,112},{20,116},{24,120},{28,124... | collective-permute-start | bytes 196616 | tf_op jit(solution)/shard_map/ppermute | solution.py:82
  64.0 5.3 %collective-permute-start.15 = (bf16[64,512]{1,0:T(8,128)(2,1)S(1)}, bf16[64,512]{1,0:T(8,128)(2,1)S(1)}, u32[]{:S(2)}, u32[]{:S(2)}) collective-permute-start(bf16[64,512]{1,0:T(8,128)(2,1)S(1)} %get-tuple-element.99), channel_id=1, source_target_pairs={{0,64},{4,68},{8,72},{12,76},{16,80},{20,84},{24,88},{28,92},{32,9... | collective-permute-start | bytes 196616 | tf_op jit(solution)/shard_map/ppermute | solution.py:82
  64.3 6.2 %collective-permute-start.16 = (bf16[64,512]{1,0:T(8,128)(2,1)S(1)}, bf16[64,512]{1,0:T(8,128)(2,1)S(1)}, u32[]{:S(2)}, u32[]{:S(2)}) collective-permute-start(bf16[64,512]{1,0:T(8,128)(2,1)S(1)} %get-tuple-element.90.after), channel_id=1, source_target_pairs={{0,32},{4,36},{8,40},{12,44},{16,48},{20,52},{24,56},{28,60},{32,6... | collective-permute-start | bytes 196616 | tf_op jit(solution)/shard_map/ppermute | solution.py:82
  65.7 1.9 %collective-permute-start.13 = (bf16[64,256]{1,0:T(8,128)(2,1)S(1)}, bf16[64,256]{1,0:T(8,128)(2,1)S(1)}, u32[]{:S(2)}, u32[]{:S(2)}) collective-permute-start(bf16[64,256]{1,0:T(8,128)(2,1)S(1)} %get-tuple-element.92), channel_id=1, source_target_pairs={{0,4},{4,0},{8,12},{12,8},{16,20},{20,16},{24,28},{28,24},{32,36},... | collective-permute-start | bytes 98312 | tf_op jit(solution)/shard_map/ppermute | solution.py:77

commit v4 on v3

v4 whole, which is shorter than its diff:
```python
import functools

import jax
import jax.numpy as jnp
from jax import lax
from jax.experimental import pallas as pl
from jax.experimental.pallas import tpu as pltpu
from jax.sharding import PartitionSpec as P

HEAD_DIM = 128
GROUP = 8
TOKENS = 64
KV_COLS = 2 * HEAD_DIM
Q_COLS = GROUP * HEAD_DIM
BLOCK = 2 * TOKENS
NOTE = 16
PIECE = BLOCK + NOTE
TILE = GROUP * TOKENS
LANES = 4 * TILE
SUBS = LANES // TILE

score_scale = HEAD_DIM ** (-0.5)
exp2_scale = score_scale * 1.4426950408889634
pair_beta = 0.1
blocked_score = -(2.0**30)
no_max = -(2.0**31)

bf16 = jnp.bfloat16
f32 = jnp.float32


def params(**kw):
    return pltpu.CompilerParams(vmem_limit_bytes=16 * 2**20, **kw)


def dot(left, right, left_dim=1, right_dim=0):
    return lax.dot_general(
        left, right, (((left_dim,), (right_dim,)), ((), ())), preferred_element_type=f32
    )


def iota(shape, dim):
    return lax.broadcasted_iota(jnp.int32, shape, dim)


VMEM = pl.BlockSpec(memory_space=pltpu.VMEM)
SMEM = pl.BlockSpec(memory_space=pltpu.SMEM)
HBM = pl.BlockSpec(memory_space=pltpu.HBM)
AFTER = pl.BlockSpec(memory_space=pl.ANY)


def shape(*dims, dtype=bf16):
    return jax.ShapeDtypeStruct(dims, dtype)


def call(kernel, name, in_specs, out_shape, scratch=(), out_specs=None, flops=0):
    extra = {} if out_specs is None else {"out_specs": out_specs}
    cost = pl.CostEstimate(flops=flops, bytes_accessed=2**20, transcendentals=0)
    return pl.pallas_call(
        kernel,
        in_specs=in_specs,
        out_shape=out_shape,
        scratch_shapes=list(scratch),
        compiler_params=params(),
        cost_estimate=cost,
        name=name,
        **extra,
    )


def lanes_of(j):
    return slice(j * TILE, (j + 1) * TILE)


def swap_core(value):
    return lax.ppermute(value, "resp", [(r, r ^ 1) for r in range(32)])


def shift_z(value, step):
    pairs = [(r, ((r // 8 + step) % 4) * 8 + r % 8) for r in range(32)]
    return lax.ppermute(value, "resp", pairs)


def shift_x(value, step):
    pairs = [(r, (r // 8) * 8 + (r % 8 // 2 + step) % 4 * 2 + r % 2) for r in range(32)]
    return lax.ppermute(value, "resp", pairs)


def here():
    index = lax.axis_index("resp")
    return lax.rem(index, 2), lax.div(index, 8), lax.rem(lax.div(index, 2), 4)


def columns(core, width):
    return pl.ds(pl.multiple_of(core * width, width), width)


def run_copies(pairs, sems):
    copies = [pltpu.make_async_copy(a, b, sems.at[i]) for i, (a, b) in enumerate(pairs)]
    for copy in copies:
        copy.start()
    for copy in copies:
        copy.wait()


def columns(core, width):
    return pl.ds(pl.multiple_of(core * width, width), width)


def started(pairs, sems):
    copies = [pltpu.make_async_copy(a, b, sems.at[i]) for i, (a, b) in enumerate(pairs)]
    for copy in copies:
        copy.start()
    return copies


def waited(copies):
    for copy in copies:
        copy.wait()


def half_copies(side, pq, rq, pg, rg, target):
    cols = columns(side, Q_COLS)
    return [
        (pq.at[:, cols], target.at[0]),
        (rq.at[0, :, cols], target.at[1]),
        (pg.at[:, cols], target.at[2]),
        (rg.at[0, :, cols], target.at[3]),
    ]


def pack_kernel(prompt_kv, resp_kv, pq, rq, pg, rg, own, send, send_q, sems):
    core = here()[0]
    pairs = []
    for side, out in ((core, own), (1 - core, send)):
        cols = columns(side, KV_COLS)
        pairs.append((prompt_kv.at[:, cols], out.at[pl.ds(0, TOKENS)]))
        pairs.append((resp_kv.at[0, :, cols], out.at[pl.ds(TOKENS, TOKENS)]))
    pairs += half_copies(1 - core, pq, rq, pg, rg, send_q)
    waited(started(pairs, sems))


def pack(*operands):
    return call(
        pack_kernel,
        "pack",
        [HBM] * 6,
        [shape(BLOCK, KV_COLS)] * 2 + [shape(4, TOKENS, Q_COLS)],
        [pltpu.SemaphoreType.DMA((8,))],
    )(*operands)


def note_of(core, first, values):
    row, lane = iota((NOTE, KV_COLS), 0), iota((NOTE, KV_COLS), 1)
    note = jnp.zeros((NOTE, KV_COLS), f32)
    for number, value in enumerate(values):
        note = jnp.where(lane == core * 8 + first + number, value, note)
    return jnp.where(row == 0, note, 0.0).astype(bf16)


def join_cores_kernel(logratio, own, recv, after, block):
    block[:TOKENS] = own[:TOKENS]
    block[TOKENS:BLOCK] = recv[:TOKENS]
    ratio = jnp.full((NOTE, KV_COLS), logratio[0], f32)
    high = ratio.astype(bf16).astype(f32)
    middle = (ratio - high).astype(bf16).astype(f32)
    block[BLOCK:] = note_of(here()[0], 0, (high, middle, ratio - high - middle))


def join_cores(logratio, own, recv, after):
    return call(
        join_cores_kernel,
        "join_cores",
        [SMEM] + [VMEM] * 2 + [AFTER],
        shape(PIECE, KV_COLS),
    )(logratio, own, recv, after)


def facts_kernel(partner, chosen, resp_len, after, note):
    values = [ref[0].astype(f32) for ref in (partner, chosen, resp_len)]
    note[...] = note_of(here()[0], 3, values)


def facts(partner, chosen, resp_len, after):
    return call(facts_kernel, "facts", [SMEM] * 3 + [AFTER], shape(NOTE, KV_COLS))(
        partner, chosen, resp_len, after
    )


def join_kernel(*refs):
    pieces, chunk = refs[:-2], refs[-1]
    for p, piece in enumerate(pieces):
        chunk[p * PIECE : (p + 1) * PIECE] = piece[...]


def join(pieces, after):
    return call(
        join_kernel,
        "join",
        [VMEM] * len(pieces) + [AFTER],
        shape(len(pieces) * PIECE, KV_COLS),
    )(*pieces, after)


def turned(block):
    rows = jnp.concatenate(
        [block[:, g * HEAD_DIM : (g + 1) * HEAD_DIM] for g in range(GROUP)], axis=0
    )
    return rows.T


def softmax_part(scores, value_rows):
    top = jnp.max(scores, axis=0, keepdims=True)
    raised = jnp.exp2((scores - top) * exp2_scale).astype(bf16)
    total = dot(value_rows, raised)
    packed = jnp.concatenate(
        [total[: HEAD_DIM + 8], jnp.broadcast_to(top, (8, top.shape[1]))], axis=0
    )
    return raised, packed


def with_ones(value_rows):
    return jnp.concatenate([value_rows.T, jnp.ones((16, value_rows.shape[0]), bf16)], axis=0)


def prep_kernel(
    pq, rq, pg, rg, recv, kv_own, kv_recv, q_aug, grads, raised, packed, local, sems
):
    core = here()[0]
    copies = started(half_copies(core, pq, rq, pg, rg, local), sems)
    none = jnp.concatenate(
        [jnp.zeros((HEAD_DIM + 8, TILE), f32), jnp.full((8, TILE), no_max, f32)], axis=0
    )
    for j in (2, 3, 0, 1):
        lanes = lanes_of(j)
        sib, resp = j // 2, j % 2
        if j == 0:
            waited(copies)
        source = recv if sib else local
        turned_q = turned(source[resp])
        q_aug[:HEAD_DIM, lanes] = turned_q
        grads[:, lanes] = turned(source[2 + resp])
        if resp:
            q_aug[HEAD_DIM:, lanes] = jnp.zeros((HEAD_DIM, TILE), bf16)
            rows = (kv_recv if sib else kv_own)[TOKENS:BLOCK]
            scores = dot(rows[:, :HEAD_DIM], turned_q)
            token = iota(scores.shape, 1) % TOKENS
            scores = jnp.where(iota(scores.shape, 0) <= token, scores, blocked_score)
            part, info_rows = softmax_part(scores, with_ones(rows[:, HEAD_DIM:]))
            raised[:, lanes_of(sib)] = part
            packed[:, lanes] = info_rows
        else:
            own_core = 1 - core if sib else core
            token = iota((HEAD_DIM, TILE), 1) % TOKENS + own_core * TOKENS
            row = iota((HEAD_DIM, TILE), 0)
            hidden = jnp.logical_or(row == 0, row > token)
            q_aug[HEAD_DIM:, lanes] = jnp.where(hidden, blocked_score, 0.0).astype(bf16)
            packed[:, lanes] = none


def prep(prompt_q, resp_q, prompt_grad, resp_grad, recv, kv_own, kv_recv):
    return call(
        prep_kernel,
        "prep",
        [HBM] * 4 + [VMEM] * 3,
        [
            shape(2 * HEAD_DIM, LANES),
            shape(HEAD_DIM, LANES),
            shape(TOKENS, 2 * TILE),
            shape(HEAD_DIM + 16, LANES, dtype=f32),
        ],
        [pltpu.VMEM((4, TOKENS, Q_COLS), bf16), pltpu.SemaphoreType.DMA((4,))],
    )(prompt_q, resp_q, prompt_grad, resp_grad, recv, kv_own, kv_recv)


offsets = (0, 3, 1, 2)
early_part = (((0, 0),), ((1, 0),), ((2, 0),), ((3, 0),), ((0, 1), (0, 2)))
side_part = (((1, 1), (1, 2)), ((2, 1), (3, 1)), ((2, 2), (3, 2)))
far_part = (((0, 3), (1, 3), (2, 3), (3, 3)),)
all_parts = (early_part, side_part, far_part)
key_cols = slice(0, HEAD_DIM)
value_cols = slice(HEAD_DIM, KV_COLS)


def blocks_of(part):
    return [block for array in part for block in array]


def keys_in(part):
    return BLOCK * len(blocks_of(part))


def part_rows(kvs, part, cols):
    return jnp.concatenate(
        [
            kv[n * PIECE : n * PIECE + BLOCK, cols]
            for kv, array in zip(kvs, part)
            for n in range(len(array))
        ],
        axis=0,
    )


def place_of(info, block):
    p, i = block
    return (info[1] + 4 - p) % 4, (info[2] + offsets[i]) % 4


def forward_kernel(part, *refs):
    kvs = refs[: len(part)]
    q_aug, after, raised, packed, key_aug, value_rows, scores = refs[len(part) :]
    info = here()
    core, z_own, x_own = info
    row = iota((BLOCK, HEAD_DIM), 1)
    token = (iota((BLOCK, HEAD_DIM), 0) + core * TOKENS) % BLOCK
    first = (row == 0).astype(f32)
    same = jnp.logical_and(row == token, row > 0).astype(f32)
    number = 0
    for kv, array in zip(kvs, part):
        for n, block in enumerate(array):
            rows = slice(number * BLOCK, (number + 1) * BLOCK)
            z_here, x_here = place_of(info, block)
            later = jnp.logical_or(
                z_here > z_own, jnp.logical_and(z_here == z_own, x_here > x_own)
            )
            hidden = first * later.astype(f32)
            if block == (0, 0):
                hidden = same
            key_aug[rows, :HEAD_DIM] = kv[n * PIECE : n * PIECE + BLOCK, key_cols]
            key_aug[rows, HEAD_DIM:] = hidden.astype(bf16)
            number += 1
    value_rows[...] = with_ones(part_rows(kvs, part, value_cols))
    scores[0] = dot(key_aug[...], q_aug[:, lanes_of(0)])
    for j in range(SUBS):
        if j + 1 < SUBS:
            scores[(j + 1) % 2] = dot(key_aug[...], q_aug[:, lanes_of(j + 1)])
        one, info_rows = softmax_part(scores[j % 2], value_rows[...])
        raised[:, lanes_of(j)] = one
        packed[:, lanes_of(j)] = info_rows


def forward(kvs, q_aug, after, part):
    keys = keys_in(part)
    return call(
        functools.partial(forward_kernel, part),
        "forward",
        [VMEM] * (len(part) + 1) + [AFTER],
        [
            shape(keys, LANES),
            shape(HEAD_DIM + 16, LANES, dtype=f32),
        ],
        [
            pltpu.VMEM((keys, 2 * HEAD_DIM), bf16),
            pltpu.VMEM((HEAD_DIM + 16, keys), bf16),
            pltpu.VMEM((2, keys, TILE), f32),
        ],
        flops=4 * keys * LANES * HEAD_DIM,
    )(*kvs, q_aug, after)


def collect_kernel(*refs):
    note, *refs = refs
    refs, notes = list(refs[:-1]), refs[-1]
    rows = []
    for part in all_parts:
        for array in part:
            kv = refs.pop(0)
            for n in range(len(array)):
                rows.append(kv[n * PIECE + BLOCK : (n + 1) * PIECE].astype(f32)[0:1])
    notes[...] = (jnp.concatenate(rows, axis=0) + note[...].astype(f32)).astype(bf16)


def collect(note, kv_lists):
    flat = [kv for kvs in kv_lists for kv in kvs]
    return call(collect_kernel, "collect", [VMEM] * (len(flat) + 1), shape(16, KV_COLS))(
        note, *flat
    )


def combine_kernel(
    own_notes, sib_notes, grads, part_0, part_1, part_2, part_own, out, cot_aug, gains
):
    info = here()
    notes = own_notes[...].astype(f32) + sib_notes[...].astype(f32)
    row = iota((16, 1), 0)
    seat = jnp.zeros_like(row)
    for number, block in enumerate(block for part in all_parts for block in blocks_of(part)):
        z_here, x_here = place_of(info, block)
        seat = jnp.where(row == number, z_here * 8 + x_here * 2, seat)
    ratios = [
        notes[:, side * 8 : side * 8 + 1]
        + notes[:, side * 8 + 1 : side * 8 + 2]
        + notes[:, side * 8 + 2 : side * 8 + 3]
        for side in range(2)
    ]
    weights = []
    for sib in range(2):
        own_core = 1 - info[0] if sib else info[0]
        own_row = notes[0:1, :]
        lane = iota(own_row.shape, 1)

        def field(number):
            mask = lane == own_core * 8 + number
            return jnp.sum(jnp.where(mask, own_row, 0.0), axis=1, keepdims=True)

        ratio = field(0) + field(1) + field(2)
        partner, chosen, count = field(3), field(4), field(5)
        mate = jnp.zeros((1, 1), f32)
        for side in range(2):
            found = (seat + side).astype(f32) == partner
            mate = mate + jnp.sum(jnp.where(found, ratios[side], 0.0), axis=0, keepdims=True)
        sign = 2.0 * chosen - 1.0
        pair_weight = sign * jax.nn.sigmoid(-pair_beta * (sign * (ratio - mate)))
        token = (iota((1, TILE), 1) % TOKENS).astype(f32)
        weights.append(jnp.where(token < count, pair_weight, 0.0))

    for j in range(SUBS):
        lanes = lanes_of(j)
        parts = (part_0, part_1, part_2) + ((part_own,) if j % 2 else ())
        tops = [part[HEAD_DIM + 8 : HEAD_DIM + 9, lanes] for part in parts]
        top = functools.reduce(jnp.maximum, tops)
        factors = [jnp.exp2((one - top) * exp2_scale) for one in tops]
        length = sum(f * part[HEAD_DIM : HEAD_DIM + 1, lanes] for f, part in zip(factors, parts))
        inverse = 1.0 / length
        factors = [f * inverse for f in factors]
        rounded = sum(f * part[:HEAD_DIM, lanes] for f, part in zip(factors, parts)).astype(bf16)
        out[:, lanes] = rounded
        gains[:, lanes] = jnp.concatenate(
            factors + [jnp.zeros((8 - len(factors), TILE), f32)], axis=0
        )
        if j % 2:
            cot = (weights[j // 2] * grads[:, lanes].astype(f32)).astype(bf16)
        else:
            cot = grads[:, lanes]
        cot_aug[:HEAD_DIM, lanes] = cot
        row_dot = -jnp.sum(cot.astype(f32) * rounded.astype(f32), axis=0, keepdims=True)
        high = row_dot.astype(bf16).astype(f32)
        middle = (row_dot - high).astype(bf16).astype(f32)
        low = row_dot - high - middle
        row = iota((16, TILE), 0)
        split = jnp.where(
            row == 0, high, jnp.where(row == 1, middle, jnp.where(row == 2, low, 0.0))
        )
        cot_aug[HEAD_DIM : HEAD_DIM + 16, lanes] = split.astype(bf16)
        cot_aug[HEAD_DIM + 16 :, lanes] = jnp.zeros((HEAD_DIM - 16, TILE), bf16)


def combine(own_notes, sib_notes, grads, parts):
    return call(
        combine_kernel,
        "combine",
        [VMEM] * (3 + len(parts)),
        [shape(HEAD_DIM, LANES), shape(2 * HEAD_DIM, LANES), shape(8, LANES, dtype=f32)],
    )(own_notes, sib_notes, grads, *parts)


def value_aug_of(value_rows):
    column = iota(value_rows.shape, 1)
    return jnp.concatenate([value_rows, (column < 3).astype(f32).astype(bf16)], axis=1)


def backward_kernel(part, splits, chunk, *refs):
    kvs = refs[: len(part)]
    raised, q_aug, cot_aug, gains, after, slopes = refs[len(part) : len(part) + 6]
    grads = refs[len(part) + 6 : len(part) + 6 + len(splits)]
    value_aug, moved, scaled_q, scaled_cot = refs[len(part) + 6 + len(splits) :]
    value_aug[...] = value_aug_of(part_rows(kvs, part, value_cols))
    moved[0] = dot(value_aug[...], cot_aug[:, lanes_of(0)])
    for j in range(SUBS):
        lanes = lanes_of(j)
        if j + 1 < SUBS:
            moved[(j + 1) % 2] = dot(value_aug[...], cot_aug[:, lanes_of(j + 1)])
        gain = gains[chunk : chunk + 1, lanes]
        scaled_cot[:, lanes] = (cot_aug[:HEAD_DIM, lanes].astype(f32) * gain).astype(bf16)
        scaled_q[:, lanes] = (
            q_aug[:HEAD_DIM, lanes].astype(f32) * (gain * score_scale)
        ).astype(bf16)
        slopes[:, lanes] = (raised[:, lanes].astype(f32) * moved[j % 2]).astype(bf16)
    for columns_here, left, right in (
        (value_cols, raised, scaled_cot),
        (key_cols, slopes, scaled_q),
    ):
        total = dot(left[...], right[...], 1, 1)
        for grad, (numbers, _) in zip(grads, splits):
            for n, number in enumerate(numbers):
                grad[n * BLOCK : (n + 1) * BLOCK, columns_here] = total[
                    number * BLOCK : (number + 1) * BLOCK
                ].astype(grad.dtype)


def backward(kvs, raised, q_aug, cot_aug, gains, after, part, chunk, splits):
    keys = keys_in(part)
    return call(
        functools.partial(backward_kernel, part, splits, chunk),
        "backward",
        [VMEM] * (len(part) + 4) + [AFTER],
        [shape(keys, LANES)]
        + [shape(len(numbers) * BLOCK, KV_COLS, dtype=kind) for numbers, kind in splits],
        [
            pltpu.VMEM((keys, 2 * HEAD_DIM), bf16),
            pltpu.VMEM((2, keys, TILE), f32),
            pltpu.VMEM((HEAD_DIM, LANES), bf16),
            pltpu.VMEM((HEAD_DIM, LANES), bf16),
        ],
        flops=6 * keys * LANES * HEAD_DIM,
    )(*kvs, raised, q_aug, cot_aug, gains, after)


def rows_of(turned_rows):
    rows = turned_rows.T
    return jnp.concatenate(
        [rows[g * TOKENS : (g + 1) * TOKENS] for g in range(GROUP)], axis=1
    )


def finish_kernel(*refs):
    refs = list(refs)
    kv_lists = [[refs.pop(0) for _ in part] for part in all_parts]
    all_slopes = [refs.pop(0) for _ in all_parts]
    (kv_own, kv_recv, raised, q_aug, cot_aug, gains, out, after) = refs[:8]
    (own_result, sib_result, keys) = refs[8:]
    spans, start = [], 0
    for kvs, part in zip(kv_lists, all_parts):
        span = slice(start, start + keys_in(part))
        keys[:, span] = part_rows(kvs, part, key_cols).T
        spans.append(span)
        start = span.stop
    for j in (2, 3, 0, 1):
        lanes = lanes_of(j)
        sib, resp = j // 2, j % 2
        result = sib_result if sib else own_result
        total = None
        for chunk, slopes in enumerate(all_slopes):
            part = dot(keys[:, spans[chunk]], slopes[:, lanes])
            part = part * (gains[chunk : chunk + 1, lanes] * score_scale)
            total = part if total is None else total + part
        if resp:
            gain = gains[3:4, lanes]
            rows = (kv_recv if sib else kv_own)[TOKENS:BLOCK]
            own_raised = raised[:, lanes_of(sib)]
            moved = dot(value_aug_of(rows[:, HEAD_DIM:]), cot_aug[:, lanes])
            own_slopes = (own_raised.astype(f32) * moved).astype(bf16)
            total = total + dot(rows[:, :HEAD_DIM].T, own_slopes) * (gain * score_scale)
            scaled_q = (q_aug[:HEAD_DIM, lanes].astype(f32) * (gain * score_scale)).astype(bf16)
            scaled_cot = (cot_aug[:HEAD_DIM, lanes].astype(f32) * gain).astype(bf16)
            key_grad = dot(own_slopes, scaled_q, 1, 1)
            value_grad = dot(own_raised, scaled_cot, 1, 1)
            result[:, 4 * Q_COLS :] = jnp.concatenate([key_grad, value_grad], axis=1).astype(bf16)
        result[:, resp * Q_COLS : (resp + 1) * Q_COLS] = rows_of(
            out[:, lanes].astype(f32)
        ).astype(bf16)
        result[:, (2 + resp) * Q_COLS : (3 + resp) * Q_COLS] = rows_of(total).astype(bf16)


def finish(kv_lists, slopes, kv_own, kv_recv, raised, q_aug, cot_aug, gains, out, after):
    flat = [kv for kvs in kv_lists for kv in kvs]
    return call(
        finish_kernel,
        "finish",
        [VMEM] * (len(flat) + len(slopes) + 7) + [AFTER],
        [shape(TOKENS, 4 * Q_COLS + KV_COLS)] * 2,
        [pltpu.VMEM((HEAD_DIM, 16 * BLOCK), bf16)],
        flops=6 * 4 * BLOCK * LANES * HEAD_DIM,
    )(*flat, *slopes, kv_own, kv_recv, raised, q_aug, cot_aug, gains, out, after)


def place_kernel(own, recv, prompt_out, resp_out, prompt_dq, resp_dq, resp_dkv, done, sems):
    pairs = []
    core = here()[0]
    for side, source in ((core, own), (1 - core, recv)):
        cols = columns(side, Q_COLS)
        targets = (
            prompt_out.at[:, cols],
            resp_out.at[0, :, cols],
            prompt_dq.at[:, cols],
            resp_dq.at[0, :, cols],
        )
        pairs += [
            (source.at[:, pl.ds(n * Q_COLS, Q_COLS)], target) for n, target in enumerate(targets)
        ]
        pairs.append(
            (source.at[:, pl.ds(4 * Q_COLS, KV_COLS)], resp_dkv.at[0, :, columns(side, KV_COLS)])
        )
    copies = started(pairs, sems)
    done[...] = jnp.zeros_like(done)
    waited(copies)


def place(own, recv):
    prompt = shape(TOKENS, 2 * Q_COLS)
    resp = shape(1, TOKENS, 2 * Q_COLS)
    return call(
        place_kernel,
        "place",
        [VMEM] * 2,
        [prompt, resp, prompt, resp, shape(1, TOKENS, 2 * KV_COLS), shape(8, 128, dtype=f32)],
        [pltpu.SemaphoreType.DMA((10,))],
        out_specs=[HBM] * 5 + [VMEM],
    )(own, recv)


def add_split_kernel(count, *refs):
    terms, outs = refs[:count], refs[count + 1 :]
    start = 0
    for out in outs:
        rows = slice(start, start + out.shape[0])
        total = terms[0][rows].astype(f32)
        for term in terms[1:]:
            total = total + term[rows].astype(f32)
        out[...] = total.astype(out.dtype)
        start += out.shape[0]


def add_split(terms, outs, rows, after, flops=0):
    return call(
        functools.partial(add_split_kernel, len(terms)),
        "add_split",
        [VMEM] * len(terms) + [AFTER],
        [shape(rows, KV_COLS)] * outs,
        flops=flops,
    )(*terms, after)


def sum_column_kernel(own, grad_z, back_far, back_1, back_2, own_sum, to_1, to_2, to_3):
    own_sum[...] = own[...] + back_far[:BLOCK].astype(f32)
    for p, out in ((1, to_1), (2, to_2), (3, to_3)):
        rows = slice((p - 1) * BLOCK, p * BLOCK)
        total = grad_z[rows] + back_far[p * BLOCK : (p + 1) * BLOCK].astype(f32)
        total = total + back_1[rows].astype(f32) + back_2[rows].astype(f32)
        out[...] = total.astype(bf16)


def sum_column(own, grad_z, back_far, back_1, back_2):
    own_sum, *to_z = call(
        sum_column_kernel,
        "sum_column",
        [VMEM] * 5,
        [shape(BLOCK, KV_COLS, dtype=f32)] + [shape(BLOCK, KV_COLS)] * 3,
    )(own, grad_z, back_far, back_1, back_2)
    return own_sum, to_z


def last_kernel(kept, recv, after, out):
    core = here()[0]

    @pl.when(core == 0)
    def _():
        out[:, :KV_COLS] = kept[...]
        out[:, KV_COLS:] = recv[...]

    @pl.when(core == 1)
    def _():
        out[:, :KV_COLS] = recv[...]
        out[:, KV_COLS:] = kept[...]


def last(kept, recv, after):
    return call(
        last_kernel, "last", [VMEM] * 2 + [AFTER], shape(TOKENS, 2 * KV_COLS)
    )(kept, recv, after)


def shards(
    prompt_q,
    prompt_kv,
    resp_q,
    resp_kv,
    prompt_grad,
    resp_grad,
    resp_len,
    logratio,
    partner,
    chosen,
):
    prompt_q, prompt_kv, resp_q, resp_kv, prompt_grad, resp_grad = [
        pltpu.with_memory_space_constraint(array, pltpu.HBM)
        for array in (prompt_q, prompt_kv, resp_q, resp_kv, prompt_grad, resp_grad)
    ]
    kv_own, kv_send, q_send = pack(
        prompt_kv, resp_kv, prompt_q, resp_q, prompt_grad, resp_grad
    )
    kv_recv = swap_core(kv_send)
    q_recv = swap_core(q_send)
    block = join_cores(logratio, kv_own, kv_recv, q_recv)

    from_z = [shift_z(block, p) for p in (1, 2, 3)]
    from_x = [shift_x(block, 4 - offset) for offset in offsets[1:3]]
    q_aug, grads, raised_own, part_own = prep(
        prompt_q, resp_q, prompt_grad, resp_grad, q_recv, kv_own, kv_recv
    )
    note = facts(partner, chosen, resp_len, part_own)
    far = join(from_z[1:], note)
    near = join(from_x, note)
    column = join([block] + from_z, near)
    early_kvs = [block] + from_z + [near]
    side_kvs = [shift_z(near, 1)] + [shift_x(far, 4 - offset) for offset in offsets[1:3]]
    far_kvs = [shift_x(column, 2)]
    kv_lists = [early_kvs, side_kvs, far_kvs]

    raised, packs = [], []
    for kvs, part in zip(kv_lists, all_parts):
        one, pack_rows = forward(kvs, q_aug, note, part)
        raised.append(one)
        packs.append(pack_rows)
    own_notes = collect(note, kv_lists)
    out, cot_aug, gains = combine(
        own_notes, swap_core(own_notes), grads, packs + [part_own]
    )

    def backward_of(chunk, splits, after):
        return backward(
            kv_lists[chunk],
            raised[chunk],
            q_aug,
            cot_aug,
            gains,
            after,
            all_parts[chunk],
            chunk,
            splits,
        )

    slopes_far, grad_far = backward_of(2, (((0, 1, 2, 3), bf16),), gains)
    back_far = shift_x(grad_far, 2)
    slopes_side, grad_1, grad_2 = backward_of(
        1, (((0, 2, 3), bf16), ((1, 4, 5), bf16)), grad_far
    )
    back_1, back_2 = shift_x(grad_1, offsets[1]), shift_x(grad_2, offsets[2])
    slopes_early, grad_own, grad_z, *to_x = backward_of(
        0, (((0,), f32), ((1, 2, 3), f32), ((4,), bf16), ((5,), bf16)), grad_1
    )
    slopes = [slopes_early, slopes_side, slopes_far]

    back_x = [shift_x(term, offset) for term, offset in zip(to_x, offsets[1:3])]
    own_sum, to_z = sum_column(grad_own, grad_z, back_far, back_1, back_2)
    back_z = [shift_z(term, 4 - p) for p, term in zip((1, 2, 3), to_z)]
    own_result, sib_result = finish(
        kv_lists, slopes, kv_own, kv_recv, raised_own, q_aug, cot_aug, gains, out, grad_own
    )
    prompt_out, resp_out, prompt_dq, resp_dq, resp_dkv, placed = place(
        own_result, swap_core(sib_result)
    )
    kept, sent = add_split([own_sum] + back_z + back_x, 2, TOKENS, own_sum, 2 * 10**10)
    prompt_dkv = last(kept, swap_core(sent), placed)
    return (prompt_out, resp_out, prompt_dq, resp_dq, prompt_dkv, resp_dkv)


def solution(mesh):
    return jax.shard_map(
        shards,
        mesh=mesh,
        in_specs=(
            P(("batch", "resp"), "head"),
            P(("batch", "resp"), "head"),
            P(("batch", "resp"), None, "head"),
            P(("batch", "resp"), None, "head"),
            P(("batch", "resp"), "head"),
            P(("batch", "resp"), None, "head"),
            P(("batch", "resp")),
            P(("batch", "resp")),
            P(("batch", "resp")),
            P(("batch", "resp")),
        ),
        out_specs=(
            P(("batch", "resp"), "head"),
            P(("batch", "resp"), None, "head"),
            P(("batch", "resp"), "head"),
            P(("batch", "resp"), None, "head"),
            P(("batch", "resp"), "head"),
            P(("batch", "resp"), None, "head"),
        ),
        check_vma=False,
    )
```

time: 72.1 us -> 66.3 us (0.920)
  Pallas kernels: 27.5 us -> 22.1 us
  waiting for transfers between devices: 18.8 us -> 15.2 us
  starting transfers between devices: 21.9 us -> 25.4 us
    pallas_call x19 -> x20, Pallas kernels: 27.5 us -> 22.1 us  [the longest x3 7.06 us: forward(): call(functools.partial(forward_kernel, part), 'forward', [VMEM] * (len(pa...]
    ppermute x6 -> x10, starting transfers between devices: 7.1 us -> 11.1 us  [shift_x(): return lax.ppermute(value, 'resp', pairs)]
    ppermute x5, waiting for transfers between devices: 3.39 us -> 0.89 us  [swap_core(): return lax.ppermute(value, 'resp', [(r, r ^ 1) for r in range(32)])]
    ppermute x5, starting transfers between devices: 9.99 us -> 7.91 us  [swap_core(): return lax.ppermute(value, 'resp', [(r, r ^ 1) for r in range(32)])]
    ppermute x6 -> x7, waiting for transfers between devices: 5.85 us -> 3.98 us  [shift_z(): return lax.ppermute(value, 'resp', pairs)]
    ppermute x6 -> x7, starting transfers between devices: 4.81 us -> 6.43 us  [shift_z(): return lax.ppermute(value, 'resp', pairs)]
    ppermute x6 -> x10, waiting for transfers between devices: 9.56 us -> 10.3 us  [shift_x(): return lax.ppermute(value, 'resp', pairs)]
  transfers between devices with their start and end apart: 17 -> 22, of which waited for: 9 -> 6; matrix products, arithmetic and copies ran while one was open for 0% -> 0% of each run, Pallas kernels for 26% -> 26%
where the time goes in v4:
time: 66.3 us; the launch traced here: 66.2 us
  starting transfers between devices  25.4 us (38%)
  Pallas kernels  22.1 us (33%)
  waiting for transfers between devices  15.2 us (23%)
  between operations  3.44 us (5%)
    ppermute x10, starting transfers between devices, shift_x(): return lax.ppermute(value, 'resp', pairs)  11.1 us
    ppermute x10, waiting for transfers between devices, shift_x(): return lax.ppermute(value, 'resp', pairs)  10.3 us
    ppermute x5, starting transfers between devices, swap_core(): return lax.ppermute(value, 'resp', [(r, r ^ 1) for r in range(32)])  7.91 us
    pallas_call x3, Pallas kernels, forward(): call(functools.partial(forward_kernel, part), 'forward', [VMEM] * (len(pa...  7.06 us
    pallas_call x3, Pallas kernels, backward(): call(functools.partial(backward_kernel, part, splits, chunk), 'backward',...  7 us
    ppermute x7, starting transfers between devices, shift_z(): return lax.ppermute(value, 'resp', pairs)  6.43 us
    ppermute x7, waiting for transfers between devices, shift_z(): return lax.ppermute(value, 'resp', pairs)  3.98 us
    pallas_call x1, Pallas kernels, finish(): call(finish_kernel, 'finish', [VMEM] * (len(flat) + len(slopes) + 7) + [A...  1.97 us
  transfers between devices with their start and end apart: 22, of which 6 were waited for; matrix products, arithmetic and copies ran while one was open for 0% of the time, Pallas kernels for 26%

profile of v4, /device:TPU:1, one launch (start us, length us, event | category | flops | bytes accessed | tf_op | source)
XLA Modules:
  0.0 66.2 jit_solution(9220969055349175628)
XLA Ops:
  0.6 1.3 %pack.1 = (bf16[128,256]{1,0:T(8,128)(2,1)S(1)}, bf16[128,256]{1,0:T(8,128)(2,1)S(1)}, bf16[4,64,1024]{2,1,0:T(8,128)(2,1)S(1)}) custom-call(bf16[64,512]{1,0:T(8,128)(2,1)} %prompt_kv.1, bf16[1,64,512]{2,1,0:T(8,128)(2,1)} %resp_kv.1, bf16[64,2048]{1,0:T(8,128)(2,1)} %pq.3, bf16[1,64,2048]{2,1,0:T(8,128)(2,1)} %rq.3, bf16[64,2048]{1,0:T(8,128)(2,1)} %pg.3, ...), custom_call_target="tpu_custom_call" | custom-call | bytes 1048576 | tf_op jit(solution)/shard_map/pack/pallas_call | solution.py:144
  1.9 3.3 %collective-permute-start.1 = (bf16[4,64,1024]{2,1,0:T(8,128)(2,1)S(1)}, bf16[4,64,1024]{2,1,0:T(8,128)(2,1)S(1)}, u32[]{:S(2)}, u32[]{:S(2)}) collective-permute-start(bf16[4,64,1024]{2,1,0:T(8,128)(2,1)S(1)} %get-tuple-element.48), channel_id=1, source_target_pairs={{0,4},{4,0},{8,12},{12,8},{16,20},{20,16},{24,28},{28,24},{32,36},... | collective-permute-start | bytes 1572872 | tf_op jit(solution)/shard_map/ppermute | solution.py:76
  5.2 0.1 collective-permute-start
  6.0 0.9 %collective-permute-done.recv.kv_recv.refs_13_ = bf16[128,256]{1,0:T(8,128)(2,1)S(1)} collective-permute-done((bf16[128,256]{1,0:T(8,128)(2,1)S(1)}, bf16[128,256]{1,0:T(8,128)(2,1)S(1)}, u32[]{:S(2)}, u32[]{:S(2)}) %collective-permute-start) | collective-permute-done | bytes 65568 | tf_op jit(solution)/shard_map/ppermute | solution.py:76
  6.9 0.0 collective-permute-done.1.after.recv
  6.9 0.8 %collective-permute-start.6 = (bf16[144,256]{1,0:T(8,128)(2,1)S(1)}, bf16[144,256]{1,0:T(8,128)(2,1)S(1)}, u32[]{:S(2)}, u32[]{:S(2)}) collective-permute-start(bf16[144,256]{1,0:T(8,128)(2,1)S(1)} %join_cores.1.refs_0_.refs_1_), channel_id=1, source_target_pairs={{0,24},{4,28},{8,0},{12,4},{16,8},{20,12},{24,16},{28,20},{32,56},... | collective-permute-start | bytes 221192 | tf_op jit(solution)/shard_map/ppermute | solution.py:86
  7.7 0.7 %collective-permute-start.5 = (bf16[144,256]{1,0:T(8,128)(2,1)S(1)}, bf16[144,256]{1,0:T(8,128)(2,1)S(1)}, u32[]{:S(2)}, u32[]{:S(2)}) collective-permute-start(bf16[144,256]{1,0:T(8,128)(2,1)S(1)} %join_cores.1.refs_0_.refs_1_), channel_id=1, source_target_pairs={{0,8},{4,12},{8,16},{12,20},{16,24},{20,28},{24,0},{28,4},{32,40},... | collective-permute-start | bytes 221192 | tf_op jit(solution)/shard_map/ppermute | solution.py:86
  8.4 3.6 %collective-permute-start.4 = (bf16[144,256]{1,0:T(8,128)(2,1)S(1)}, bf16[144,256]{1,0:T(8,128)(2,1)S(1)}, u32[]{:S(2)}, u32[]{:S(2)}) collective-permute-start(bf16[144,256]{1,0:T(8,128)(2,1)S(1)} %join_cores.1.refs_0_.refs_1_), channel_id=1, source_target_pairs={{0,96},{4,100},{8,104},{12,108},{16,112},{20,116},{24,120},{28,124... | collective-permute-start | bytes 221192 | tf_op jit(solution)/shard_map/ppermute | solution.py:81
  12.0 0.0 collective-permute-start.3
  12.1 0.3 collective-permute-start.2
  14.3 1.9 %prep.1 = (bf16[256,2048]{1,0:T(8,128)(2,1)S(1)}, bf16[128,2048]{1,0:T(8,128)(2,1)S(1)}, bf16[64,1024]{1,0:T(8,128)(2,1)S(1)}, f32[144,2048]{1,0:T(8,128)S(1)}) custom-call(bf16[64,2048]{1,0:T(8,128)(2,1)} %pq.3, bf16[1,64,2048]{2,1,0:T(8,128)(2,1)} %rq.3, bf16[64,2048]{1,0:T(8,128)(2,1)} %pg.3, bf16[1,64,2048]{2,1,0:T(8,128)(2,1)} %rg.3, ...), custom_call_target="tpu_custom_call" | custom-call | bytes 1048576 | tf_op jit(solution)/shard_map/prep/pallas_call | solution.py:262
  16.2 0.0 collective-permute-done.6.refs_1_
  16.3 0.0 collective-permute-done.5.refs_0_
  16.3 3.2 %collective-permute-done.3.refs_0_.refs_2_.refs_3_ = bf16[144,256]{1,0:T(8,128)(2,1)S(1)} collective-permute-done((bf16[144,256]{1,0:T(8,128)(2,1)S(1)}, bf16[144,256]{1,0:T(8,128)(2,1)S(1)}, u32[]{:S(2)}, u32[]{:S(2)}) %collective-permute-start.3) | collective-permute-done | bytes 73760 | tf_op jit(solution)/shard_map/ppermute | solution.py:81
  19.5 1.8 %collective-permute-start.10 = (bf16[576,256]{1,0:T(8,128)(2,1)S(1)}, bf16[576,256]{1,0:T(8,128)(2,1)S(1)}, u32[]{:S(2)}, u32[]{:S(2)}) collective-permute-start(bf16[576,256]{1,0:T(8,128)(2,1)S(1)} %join.5), channel_id=1, source_target_pairs={{0,16},{4,20},{8,24},{12,28},{16,0},{20,4},{24,8},{28,12},{32,48},... | collective-permute-start | bytes 884744 | tf_op jit(solution)/shard_map/ppermute | solution.py:86
  21.3 1.0 %collective-permute-start.9 = (bf16[288,256]{1,0:T(8,128)(2,1)S(1)}, bf16[288,256]{1,0:T(8,128)(2,1)S(1)}, u32[]{:S(2)}, u32[]{:S(2)}) collective-permute-start(bf16[288,256]{1,0:T(8,128)(2,1)S(1)} %join.4), channel_id=1, source_target_pairs={{0,24},{4,28},{8,0},{12,4},{16,8},{20,12},{24,16},{28,20},{32,56},... | collective-permute-start | bytes 442376 | tf_op jit(solution)/shard_map/ppermute | solution.py:86
  22.4 0.6 collective-permute-start.8
  23.0 0.0 collective-permute-start.7
  23.0 2.7 %forward.3 = (bf16[768,2048]{1,0:T(8,128)(2,1)S(1)}, f32[144,2048]{1,0:T(8,128)S(1)}) custom-call(bf16[144,256]{1,0:T(8,128)(2,1)S(1)} %join_cores.1.refs_0_.refs_1_, bf16[144,256]{1,0:T(8,128)(2,1)S(1)} %collective-permute-done.2.refs_1_.refs_2_, bf16[144,256]{1,0:T(8,128)(2,1)S(1)} %collective-permute-done.3.refs_0_.refs_2_.refs_3_, ...), custom_call_target="tpu_custom_call" | custom-call | flops 805306368 | bytes 1048576 | tf_op jit(solution)/shard_map/forward/pallas_call | solution.py:344
  25.7 7.0 %collective-permute-done.9.refs_8_.refs_2_.refs_7_ = bf16[288,256]{1,0:T(8,128)(2,1)S(1)} collective-permute-done((bf16[288,256]{1,0:T(8,128)(2,1)S(1)}, bf16[288,256]{1,0:T(8,128)(2,1)S(1)}, u32[]{:S(2)}, u32[]{:S(2)}) %collective-permute-start.9) | collective-permute-done | bytes 147488 | tf_op jit(solution)/shard_map/ppermute | solution.py:86
  32.7 0.5 collective-permute-done.8.refs_7_.refs_1_.refs_6_
  33.2 0.0 collective-permute-done.7.refs_6_.refs_0_.refs_5_
  33.2 2.6 %forward.4 = (bf16[768,2048]{1,0:T(8,128)(2,1)S(1)}, f32[144,2048]{1,0:T(8,128)S(1)}) custom-call(bf16[288,256]{1,0:T(8,128)(2,1)S(1)} %collective-permute-done.7.refs_6_.refs_0_.refs_5_, bf16[288,256]{1,0:T(8,128)(2,1)S(1)} %collective-permute-done.8.refs_7_.refs_1_.refs_6_, bf16[288,256]{1,0:T(8,128)(2,1)S(1)} %collective-permute-done.9.refs_8_.refs_2_.refs_7_, ...), custom_call_target="tpu_custom_call" | custom-call | flops 805306368 | bytes 1048576 | tf_op jit(solution)/shard_map/forward/pallas_call | solution.py:344
  35.9 0.0 collective-permute-done.10.refs_9_.refs_0_.refs_8_
  35.9 0.9 %collective-permute-start.11 = (bf16[16,256]{1,0:T(8,128)(2,1)S(1)}, bf16[16,256]{1,0:T(8,128)(2,1)S(1)}, u32[]{:S(2)}, u32[]{:S(2)}) collective-permute-start(bf16[16,256]{1,0:T(8,128)(2,1)S(1)} %collect.1.own_notes), channel_id=1, source_target_pairs={{0,4},{4,0},{8,12},{12,8},{16,20},{20,16},{24,28},{28,24},{32,36},... | collective-permute-start | bytes 24584 | tf_op jit(solution)/shard_map/ppermute | solution.py:76
  36.8 1.8 %forward.5 = (bf16[512,2048]{1,0:T(8,128)(2,1)S(1)}, f32[144,2048]{1,0:T(8,128)S(1)}) custom-call(bf16[576,256]{1,0:T(8,128)(2,1)S(1)} %collective-permute-done.10.refs_9_.refs_0_.refs_8_, bf16[256,2048]{1,0:T(8,128)(2,1)S(1)} %get-tuple-element.50.refs_5_.refs_3_.refs_1_.refs_2_.refs_4_.refs_6_.refs_15_, ...), custom_call_target="tpu_custom_call" | custom-call | flops 536870912 | bytes 1048576 | tf_op jit(solution)/shard_map/forward/pallas_call | solution.py:344
  38.6 0.0 collective-permute-done.11.sib_notes
  38.6 0.9 %combine.1 = (bf16[128,2048]{1,0:T(8,128)(2,1)S(1)}, bf16[256,2048]{1,0:T(8,128)(2,1)S(1)}, f32[8,2048]{1,0:T(8,128)S(1)}) custom-call(bf16[16,256]{1,0:T(8,128)(2,1)S(1)} %collect.1.own_notes, bf16[16,256]{1,0:T(8,128)(2,1)S(1)} %collective-permute-done.11.sib_notes, bf16[128,2048]{1,0:T(8,128)(2,1)S(1)} %get-tuple-element.52.grads, ...), custom_call_target="tpu_custom_call" | custom-call | bytes 1048576 | tf_op jit(solution)/shard_map/combine/pallas_call | solution.py:449
  39.5 1.8 %backward.3 = (bf16[512,2048]{1,0:T(8,128)(2,1)S(1)}, bf16[512,256]{1,0:T(8,128)(2,1)S(1)}) custom-call(bf16[576,256]{1,0:T(8,128)(2,1)S(1)} %collective-permute-done.10.refs_9_.refs_0_.refs_8_, bf16[512,2048]{1,0:T(8,128)(2,1)S(1)} %get-tuple-element.59.refs_1_, ...), custom_call_target="tpu_custom_call" | custom-call | flops 805306368 | bytes 1048576 | tf_op jit(solution)/shard_map/backward/pallas_call | solution.py:493
  41.3 1.5 %collective-permute-start.13 = (bf16[512,256]{1,0:T(8,128)(2,1)S(1)}, bf16[512,256]{1,0:T(8,128)(2,1)S(1)}, u32[]{:S(2)}, u32[]{:S(2)}) collective-permute-start(bf16[512,256]{1,0:T(8,128)(2,1)S(1)} %get-tuple-element.60.refs_7_), channel_id=1, source_target_pairs={{0,16},{4,20},{8,24},{12,28},{16,0},{20,4},{24,8},{28,12},{32,48},... | collective-permute-start | bytes 786440 | tf_op jit(solution)/shard_map/ppermute | solution.py:86
  42.8 2.6 %backward.4 = (bf16[768,2048]{1,0:T(8,128)(2,1)S(1)}, bf16[384,256]{1,0:T(8,128)(2,1)S(1)}, bf16[384,256]{1,0:T(8,128)(2,1)S(1)}) custom-call(bf16[288,256]{1,0:T(8,128)(2,1)S(1)} %collective-permute-done.7.refs_6_.refs_0_.refs_5_, bf16[288,256]{1,0:T(8,128)(2,1)S(1)} %collective-permute-done.8.refs_7_.refs_1_.refs_6_, ...), custom_call_target="tpu_custom_call" | custom-call | flops 1207959552 | bytes 1048576 | tf_op jit(solution)/shard_map/backward/pallas_call | solution.py:493
  45.4 1.6 %collective-permute-start.15 = (bf16[384,256]{1,0:T(8,128)(2,1)S(1)}, bf16[384,256]{1,0:T(8,128)(2,1)S(1)}, u32[]{:S(2)}, u32[]{:S(2)}) collective-permute-start(bf16[384,256]{1,0:T(8,128)(2,1)S(1)} %get-tuple-element.75), channel_id=1, source_target_pairs={{0,8},{4,12},{8,16},{12,20},{16,24},{20,28},{24,0},{28,4},{32,40},... | collective-permute-start | bytes 589832 | tf_op jit(solution)/shard_map/ppermute | solution.py:86
  47.1 1.3 %collective-permute-start.14 = (bf16[384,256]{1,0:T(8,128)(2,1)S(1)}, bf16[384,256]{1,0:T(8,128)(2,1)S(1)}, u32[]{:S(2)}, u32[]{:S(2)}) collective-permute-start(bf16[384,256]{1,0:T(8,128)(2,1)S(1)} %get-tuple-element.61.refs_9_), channel_id=1, source_target_pairs={{0,24},{4,28},{8,0},{12,4},{16,8},{20,12},{24,16},{28,20},{32,56},... | collective-permute-start | bytes 589832 | tf_op jit(solution)/shard_map/ppermute | solution.py:86
  48.4 2.6 %backward.5 = (bf16[768,2048]{1,0:T(8,128)(2,1)S(1)}, f32[128,256]{1,0:T(8,128)S(1)}, f32[384,256]{1,0:T(8,128)S(1)}, bf16[128,256]{1,0:T(8,128)(2,1)S(1)}, bf16[128,256]{1,0:T(8,128)(2,1)S(1)}) custom-call(bf16[144,256]{1,0:T(8,128)(2,1)S(1)} %join_cores.1.refs_0_.refs_1_, bf16[144,256]{1,0:T(8,128)(2,1)S(1)} %collective-permute-done.2.refs_1_.refs_2_, ...), custom_call_target="tpu_custom_call" | custom-call | flops 1207959552 | bytes 1048576 | tf_op jit(solution)/shard_map/backward/pallas_call | solution.py:493
  51.0 0.1 collective-permute-start.19
  51.1 1.5 %collective-permute-start.20 = (bf16[128,256]{1,0:T(8,128)(2,1)S(1)}, bf16[128,256]{1,0:T(8,128)(2,1)S(1)}, u32[]{:S(2)}, u32[]{:S(2)}) collective-permute-start(bf16[128,256]{1,0:T(8,128)(2,1)S(1)} %get-tuple-element.81), channel_id=1, source_target_pairs={{0,8},{4,12},{8,16},{12,20},{16,24},{20,28},{24,0},{28,4},{32,40},... | collective-permute-start | bytes 196616 | tf_op jit(solution)/shard_map/ppermute | solution.py:86
  52.6 2.8 %collective-permute-done.15.back_2 = bf16[384,256]{1,0:T(8,128)(2,1)S(1)} collective-permute-done((bf16[384,256]{1,0:T(8,128)(2,1)S(1)}, bf16[384,256]{1,0:T(8,128)(2,1)S(1)}, u32[]{:S(2)}, u32[]{:S(2)}) %collective-permute-start.15) | collective-permute-done | bytes 196640 | tf_op jit(solution)/shard_map/ppermute | solution.py:86
  55.4 0.1 sum_column.1
  55.5 0.1 collective-permute-start.16
  55.6 1.1 %collective-permute-start.17 = (bf16[128,256]{1,0:T(8,128)(2,1)S(1)}, bf16[128,256]{1,0:T(8,128)(2,1)S(1)}, u32[]{:S(2)}, u32[]{:S(2)}) collective-permute-start(bf16[128,256]{1,0:T(8,128)(2,1)S(1)} %get-tuple-element.78), channel_id=1, source_target_pairs={{0,64},{4,68},{8,72},{12,76},{16,80},{20,84},{24,88},{28,92},{32,9... | collective-permute-start | bytes 196616 | tf_op jit(solution)/shard_map/ppermute | solution.py:81
  56.7 1.4 %collective-permute-start.18 = (bf16[128,256]{1,0:T(8,128)(2,1)S(1)}, bf16[128,256]{1,0:T(8,128)(2,1)S(1)}, u32[]{:S(2)}, u32[]{:S(2)}) collective-permute-start(bf16[128,256]{1,0:T(8,128)(2,1)S(1)} %get-tuple-element.79), channel_id=1, source_target_pairs={{0,32},{4,36},{8,40},{12,44},{16,48},{20,52},{24,56},{28,60},{32,6... | collective-permute-start | bytes 196616 | tf_op jit(solution)/shard_map/ppermute | solution.py:81
  58.0 2.0 %finish.1 = (bf16[64,4352]{1,0:T(8,128)(2,1)S(1)}, bf16[64,4352]{1,0:T(8,128)(2,1)S(1)}) custom-call(bf16[144,256]{1,0:T(8,128)(2,1)S(1)} %join_cores.1.refs_0_.refs_1_, bf16[144,256]{1,0:T(8,128)(2,1)S(1)} %collective-permute-done.2.refs_1_.refs_2_, bf16[144,256]{1,0:T(8,128)(2,1)S(1)} %collective-permute-done.3.refs_0_.refs_2_.refs_3_, ...), custom_call_target="tpu_custom_call" | custom-call | flops 805306368 | bytes 1048576 | tf_op jit(solution)/shard_map/finish/pallas_call | solution.py:557
  60.0 1.6 %collective-permute-start.12 = (bf16[64,4352]{1,0:T(8,128)(2,1)S(1)}, bf16[64,4352]{1,0:T(8,128)(2,1)S(1)}, u32[]{:S(2)}, u32[]{:S(2)}) collective-permute-start(bf16[64,4352]{1,0:T(8,128)(2,1)S(1)} %get-tuple-element.69), channel_id=1, source_target_pairs={{0,4},{4,0},{8,12},{12,8},{16,20},{20,16},{24,28},{28,24},{32,36},... | collective-permute-start | bytes 1671176 | tf_op jit(solution)/shard_map/ppermute | solution.py:76
  61.6 0.8 %collective-permute-done.18.refs_3_ = bf16[128,256]{1,0:T(8,128)(2,1)S(1)} collective-permute-done((bf16[128,256]{1,0:T(8,128)(2,1)S(1)}, bf16[128,256]{1,0:T(8,128)(2,1)S(1)}, u32[]{:S(2)}, u32[]{:S(2)}) %collective-permute-start.18) | collective-permute-done | bytes 65568 | tf_op jit(solution)/shard_map/ppermute | solution.py:81
  62.4 0.1 add_split.1
  62.4 2.0 %collective-permute-start.21 = (bf16[64,256]{1,0:T(8,128)(2,1)S(1)}, bf16[64,256]{1,0:T(8,128)(2,1)S(1)}, u32[]{:S(2)}, u32[]{:S(2)}) collective-permute-start(bf16[64,256]{1,0:T(8,128)(2,1)S(1)} %get-tuple-element.83), channel_id=1, source_target_pairs={{0,4},{4,0},{8,12},{12,8},{16,20},{20,16},{24,28},{28,24},{32,36},... | collective-permute-start | bytes 98312 | tf_op jit(solution)/shard_map/ppermute | solution.py:76
  64.4 1.1 %place.1 = (bf16[64,2048]{1,0:T(8,128)(2,1)}, bf16[1,64,2048]{2,1,0:T(8,128)(2,1)}, bf16[64,2048]{1,0:T(8,128)(2,1)}, bf16[1,64,2048]{2,1,0:T(8,128)(2,1)}, bf16...) custom-call(bf16[64,4352]{1,0:T(8,128)(2,1)S(1)} %get-tuple-element.68.own, bf16[64,4352]{1,0:T(8,128)(2,1)S(1)} %collective-permute-done.12.recv), custom_call_target="tpu_custom_call" | custom-call | bytes 1048576 | tf_op jit(solution)/shard_map/place/pallas_call | solution.py:592
  65.5 0.7 last.1
  (16 shorter events, 0.1 us)
Async XLA Ops:
  1.9 5.0 %collective-permute-start.1 = (bf16[4,64,1024]{2,1,0:T(8,128)(2,1)S(1)}, bf16[4,64,1024]{2,1,0:T(8,128)(2,1)S(1)}, u32[]{:S(2)}, u32[]{:S(2)}) collective-permute-start(bf16[4,64,1024]{2,1,0:T(8,128)(2,1)S(1)} %get-tuple-element.48), channel_id=1, source_target_pairs={{0,4},{4,0},{8,12},{12,8},{16,20},{20,16},{24,28},{28,24},{32,36},... | collective-permute-start | bytes 1572872 | tf_op jit(solution)/shard_map/ppermute | solution.py:76
  5.2 1.6 %collective-permute-start = (bf16[128,256]{1,0:T(8,128)(2,1)S(1)}, bf16[128,256]{1,0:T(8,128)(2,1)S(1)}, u32[]{:S(2)}, u32[]{:S(2)}) collective-permute-start(bf16[128,256]{1,0:T(8,128)(2,1)S(1)} %get-tuple-element.47), channel_id=1, source_target_pairs={{0,4},{4,0},{8,12},{12,8},{16,20},{20,16},{24,28},{28,24},{32,36},... | collective-permute-start | bytes 196616 | tf_op jit(solution)/shard_map/ppermute | solution.py:76
  6.9 9.4 %collective-permute-start.6 = (bf16[144,256]{1,0:T(8,128)(2,1)S(1)}, bf16[144,256]{1,0:T(8,128)(2,1)S(1)}, u32[]{:S(2)}, u32[]{:S(2)}) collective-permute-start(bf16[144,256]{1,0:T(8,128)(2,1)S(1)} %join_cores.1.refs_0_.refs_1_), channel_id=1, source_target_pairs={{0,24},{4,28},{8,0},{12,4},{16,8},{20,12},{24,16},{28,20},{32,56},... | collective-permute-start | bytes 221192 | tf_op jit(solution)/shard_map/ppermute | solution.py:86
  7.7 8.6 %collective-permute-start.5 = (bf16[144,256]{1,0:T(8,128)(2,1)S(1)}, bf16[144,256]{1,0:T(8,128)(2,1)S(1)}, u32[]{:S(2)}, u32[]{:S(2)}) collective-permute-start(bf16[144,256]{1,0:T(8,128)(2,1)S(1)} %join_cores.1.refs_0_.refs_1_), channel_id=1, source_target_pairs={{0,8},{4,12},{8,16},{12,20},{16,24},{20,28},{24,0},{28,4},{32,40},... | collective-permute-start | bytes 221192 | tf_op jit(solution)/shard_map/ppermute | solution.py:86
  8.4 7.9 %collective-permute-start.4 = (bf16[144,256]{1,0:T(8,128)(2,1)S(1)}, bf16[144,256]{1,0:T(8,128)(2,1)S(1)}, u32[]{:S(2)}, u32[]{:S(2)}) collective-permute-start(bf16[144,256]{1,0:T(8,128)(2,1)S(1)} %join_cores.1.refs_0_.refs_1_), channel_id=1, source_target_pairs={{0,96},{4,100},{8,104},{12,108},{16,112},{20,116},{24,120},{28,124... | collective-permute-start | bytes 221192 | tf_op jit(solution)/shard_map/ppermute | solution.py:81
  12.0 7.4 %collective-permute-start.3 = (bf16[144,256]{1,0:T(8,128)(2,1)S(1)}, bf16[144,256]{1,0:T(8,128)(2,1)S(1)}, u32[]{:S(2)}, u32[]{:S(2)}) collective-permute-start(bf16[144,256]{1,0:T(8,128)(2,1)S(1)} %join_cores.1.refs_0_.refs_1_), channel_id=1, source_target_pairs={{0,64},{4,68},{8,72},{12,76},{16,80},{20,84},{24,88},{28,92},{32,9... | collective-permute-start | bytes 221192 | tf_op jit(solution)/shard_map/ppermute | solution.py:81
  12.1 7.4 %collective-permute-start.2 = (bf16[144,256]{1,0:T(8,128)(2,1)S(1)}, bf16[144,256]{1,0:T(8,128)(2,1)S(1)}, u32[]{:S(2)}, u32[]{:S(2)}) collective-permute-start(bf16[144,256]{1,0:T(8,128)(2,1)S(1)} %join_cores.1.refs_0_.refs_1_), channel_id=1, source_target_pairs={{0,32},{4,36},{8,40},{12,44},{16,48},{20,52},{24,56},{28,60},{32,6... | collective-permute-start | bytes 221192 | tf_op jit(solution)/shard_map/ppermute | solution.py:81
  19.5 16.3 %collective-permute-start.10 = (bf16[576,256]{1,0:T(8,128)(2,1)S(1)}, bf16[576,256]{1,0:T(8,128)(2,1)S(1)}, u32[]{:S(2)}, u32[]{:S(2)}) collective-permute-start(bf16[576,256]{1,0:T(8,128)(2,1)S(1)} %join.5), channel_id=1, source_target_pairs={{0,16},{4,20},{8,24},{12,28},{16,0},{20,4},{24,8},{28,12},{32,48},... | collective-permute-start | bytes 884744 | tf_op jit(solution)/shard_map/ppermute | solution.py:86
  21.3 11.3 %collective-permute-start.9 = (bf16[288,256]{1,0:T(8,128)(2,1)S(1)}, bf16[288,256]{1,0:T(8,128)(2,1)S(1)}, u32[]{:S(2)}, u32[]{:S(2)}) collective-permute-start(bf16[288,256]{1,0:T(8,128)(2,1)S(1)} %join.4), channel_id=1, source_target_pairs={{0,24},{4,28},{8,0},{12,4},{16,8},{20,12},{24,16},{28,20},{32,56},... | collective-permute-start | bytes 442376 | tf_op jit(solution)/shard_map/ppermute | solution.py:86
  22.4 10.8 %collective-permute-start.8 = (bf16[288,256]{1,0:T(8,128)(2,1)S(1)}, bf16[288,256]{1,0:T(8,128)(2,1)S(1)}, u32[]{:S(2)}, u32[]{:S(2)}) collective-permute-start(bf16[288,256]{1,0:T(8,128)(2,1)S(1)} %join.4), channel_id=1, source_target_pairs={{0,8},{4,12},{8,16},{12,20},{16,24},{20,28},{24,0},{28,4},{32,40},... | collective-permute-start | bytes 442376 | tf_op jit(solution)/shard_map/ppermute | solution.py:86
  23.0 10.2 %collective-permute-start.7 = (bf16[288,256]{1,0:T(8,128)(2,1)S(1)}, bf16[288,256]{1,0:T(8,128)(2,1)S(1)}, u32[]{:S(2)}, u32[]{:S(2)}) collective-permute-start(bf16[288,256]{1,0:T(8,128)(2,1)S(1)} %join.3.refs_4_.refs_5_), channel_id=1, source_target_pairs={{0,32},{4,36},{8,40},{12,44},{16,48},{20,52},{24,56},{28,60},{32,6... | collective-permute-start | bytes 442376 | tf_op jit(solution)/shard_map/ppermute | solution.py:81
  35.9 2.7 %collective-permute-start.11 = (bf16[16,256]{1,0:T(8,128)(2,1)S(1)}, bf16[16,256]{1,0:T(8,128)(2,1)S(1)}, u32[]{:S(2)}, u32[]{:S(2)}) collective-permute-start(bf16[16,256]{1,0:T(8,128)(2,1)S(1)} %collect.1.own_notes), channel_id=1, source_target_pairs={{0,4},{4,0},{8,12},{12,8},{16,20},{20,16},{24,28},{28,24},{32,36},... | collective-permute-start | bytes 24584 | tf_op jit(solution)/shard_map/ppermute | solution.py:76
  41.3 14.1 %collective-permute-start.13 = (bf16[512,256]{1,0:T(8,128)(2,1)S(1)}, bf16[512,256]{1,0:T(8,128)(2,1)S(1)}, u32[]{:S(2)}, u32[]{:S(2)}) collective-permute-start(bf16[512,256]{1,0:T(8,128)(2,1)S(1)} %get-tuple-element.60.refs_7_), channel_id=1, source_target_pairs={{0,16},{4,20},{8,24},{12,28},{16,0},{20,4},{24,8},{28,12},{32,48},... | collective-permute-start | bytes 786440 | tf_op jit(solution)/shard_map/ppermute | solution.py:86
  45.4 10.0 %collective-permute-start.15 = (bf16[384,256]{1,0:T(8,128)(2,1)S(1)}, bf16[384,256]{1,0:T(8,128)(2,1)S(1)}, u32[]{:S(2)}, u32[]{:S(2)}) collective-permute-start(bf16[384,256]{1,0:T(8,128)(2,1)S(1)} %get-tuple-element.75), channel_id=1, source_target_pairs={{0,8},{4,12},{8,16},{12,20},{16,24},{20,28},{24,0},{28,4},{32,40},... | collective-permute-start | bytes 589832 | tf_op jit(solution)/shard_map/ppermute | solution.py:86
  47.1 8.3 %collective-permute-start.14 = (bf16[384,256]{1,0:T(8,128)(2,1)S(1)}, bf16[384,256]{1,0:T(8,128)(2,1)S(1)}, u32[]{:S(2)}, u32[]{:S(2)}) collective-permute-start(bf16[384,256]{1,0:T(8,128)(2,1)S(1)} %get-tuple-element.61.refs_9_), channel_id=1, source_target_pairs={{0,24},{4,28},{8,0},{12,4},{16,8},{20,12},{24,16},{28,20},{32,56},... | collective-permute-start | bytes 589832 | tf_op jit(solution)/shard_map/ppermute | solution.py:86
  51.0 9.0 %collective-permute-start.19 = (bf16[128,256]{1,0:T(8,128)(2,1)S(1)}, bf16[128,256]{1,0:T(8,128)(2,1)S(1)}, u32[]{:S(2)}, u32[]{:S(2)}) collective-permute-start(bf16[128,256]{1,0:T(8,128)(2,1)S(1)} %get-tuple-element.80), channel_id=1, source_target_pairs={{0,24},{4,28},{8,0},{12,4},{16,8},{20,12},{24,16},{28,20},{32,56},... | collective-permute-start | bytes 196616 | tf_op jit(solution)/shard_map/ppermute | solution.py:86
  51.1 10.5 %collective-permute-start.20 = (bf16[128,256]{1,0:T(8,128)(2,1)S(1)}, bf16[128,256]{1,0:T(8,128)(2,1)S(1)}, u32[]{:S(2)}, u32[]{:S(2)}) collective-permute-start(bf16[128,256]{1,0:T(8,128)(2,1)S(1)} %get-tuple-element.81), channel_id=1, source_target_pairs={{0,8},{4,12},{8,16},{12,20},{16,24},{20,28},{24,0},{28,4},{32,40},... | collective-permute-start | bytes 196616 | tf_op jit(solution)/shard_map/ppermute | solution.py:86
  55.5 6.1 %collective-permute-start.16 = (bf16[128,256]{1,0:T(8,128)(2,1)S(1)}, bf16[128,256]{1,0:T(8,128)(2,1)S(1)}, u32[]{:S(2)}, u32[]{:S(2)}) collective-permute-start(bf16[128,256]{1,0:T(8,128)(2,1)S(1)} %get-tuple-element.77), channel_id=1, source_target_pairs={{0,96},{4,100},{8,104},{12,108},{16,112},{20,116},{24,120},{28,124... | collective-permute-start | bytes 196616 | tf_op jit(solution)/shard_map/ppermute | solution.py:81
  55.6 6.0 %collective-permute-start.17 = (bf16[128,256]{1,0:T(8,128)(2,1)S(1)}, bf16[128,256]{1,0:T(8,128)(2,1)S(1)}, u32[]{:S(2)}, u32[]{:S(2)}) collective-permute-start(bf16[128,256]{1,0:T(8,128)(2,1)S(1)} %get-tuple-element.78), channel_id=1, source_target_pairs={{0,64},{4,68},{8,72},{12,76},{16,80},{20,84},{24,88},{28,92},{32,9... | collective-permute-start | bytes 196616 | tf_op jit(solution)/shard_map/ppermute | solution.py:81
  56.7 5.7 %collective-permute-start.18 = (bf16[128,256]{1,0:T(8,128)(2,1)S(1)}, bf16[128,256]{1,0:T(8,128)(2,1)S(1)}, u32[]{:S(2)}, u32[]{:S(2)}) collective-permute-start(bf16[128,256]{1,0:T(8,128)(2,1)S(1)} %get-tuple-element.79), channel_id=1, source_target_pairs={{0,32},{4,36},{8,40},{12,44},{16,48},{20,52},{24,56},{28,60},{32,6... | collective-permute-start | bytes 196616 | tf_op jit(solution)/shard_map/ppermute | solution.py:81
  60.0 4.4 %collective-permute-start.12 = (bf16[64,4352]{1,0:T(8,128)(2,1)S(1)}, bf16[64,4352]{1,0:T(8,128)(2,1)S(1)}, u32[]{:S(2)}, u32[]{:S(2)}) collective-permute-start(bf16[64,4352]{1,0:T(8,128)(2,1)S(1)} %get-tuple-element.69), channel_id=1, source_target_pairs={{0,4},{4,0},{8,12},{12,8},{16,20},{20,16},{24,28},{28,24},{32,36},... | collective-permute-start | bytes 1671176 | tf_op jit(solution)/shard_map/ppermute | solution.py:76
  62.4 3.1 %collective-permute-start.21 = (bf16[64,256]{1,0:T(8,128)(2,1)S(1)}, bf16[64,256]{1,0:T(8,128)(2,1)S(1)}, u32[]{:S(2)}, u32[]{:S(2)}) collective-permute-start(bf16[64,256]{1,0:T(8,128)(2,1)S(1)} %get-tuple-element.83), channel_id=1, source_target_pairs={{0,4},{4,0},{8,12},{12,8},{16,20},{20,16},{24,28},{28,24},{32,36},... | collective-permute-start | bytes 98312 | tf_op jit(solution)/shard_map/ppermute | solution.py:76

commit v5 on v4

--- a/solution.py
+++ b/solution.py
@@ -187,19 +187,19 @@
     )
 
 
-def join_kernel(*refs):
-    pieces, chunk = refs[:-2], refs[-1]
+def join_kernel(count, *refs):
+    pieces, chunk = refs[:count], refs[-1]
     for p, piece in enumerate(pieces):
         chunk[p * PIECE : (p + 1) * PIECE] = piece[...]
 
 
-def join(pieces, after):
-    return call(
-        join_kernel,
+def join(pieces, *afters):
+    return call(
+        functools.partial(join_kernel, len(pieces)),
         "join",
-        [VMEM] * len(pieces) + [AFTER],
+        [VMEM] * len(pieces) + [AFTER] * len(afters),
         shape(len(pieces) * PIECE, KV_COLS),
-    )(*pieces, after)
+    )(*pieces, *afters)
 
 
 def turned(block):
@@ -360,7 +360,7 @@
 
 def collect_kernel(*refs):
     note, *refs = refs
-    refs, notes = list(refs[:-1]), refs[-1]
+    refs, notes = list(refs[:-2]), refs[-1]
     rows = []
     for part in all_parts:
         for array in part:
@@ -370,11 +370,11 @@
     notes[...] = (jnp.concatenate(rows, axis=0) + note[...].astype(f32)).astype(bf16)
 
 
-def collect(note, kv_lists):
+def collect(note, kv_lists, after):
     flat = [kv for kvs in kv_lists for kv in kvs]
-    return call(collect_kernel, "collect", [VMEM] * (len(flat) + 1), shape(16, KV_COLS))(
-        note, *flat
-    )
+    return call(
+        collect_kernel, "collect", [VMEM] * (len(flat) + 1) + [AFTER], shape(16, KV_COLS)
+    )(note, *flat, after)
 
 
 def combine_kernel(
@@ -621,23 +621,27 @@
     )(*terms, after)
 
 
-def sum_column_kernel(own, grad_z, back_far, back_1, back_2, own_sum, to_1, to_2, to_3):
-    own_sum[...] = own[...] + back_far[:BLOCK].astype(f32)
+def sum_column_kernel(grad_z, back_far, back_1, back_2, after, to_1, to_2, to_3):
     for p, out in ((1, to_1), (2, to_2), (3, to_3)):
         rows = slice((p - 1) * BLOCK, p * BLOCK)
-        total = grad_z[rows] + back_far[p * BLOCK : (p + 1) * BLOCK].astype(f32)
-        total = total + back_1[rows].astype(f32) + back_2[rows].astype(f32)
+        total = grad_z[rows]
+        for back in (back_far, back_1, back_2):
+            total = total + back[rows].astype(f32)
         out[...] = total.astype(bf16)
 
 
-def sum_column(own, grad_z, back_far, back_1, back_2):
-    own_sum, *to_z = call(
-        sum_column_kernel,
-        "sum_column",
-        [VMEM] * 5,
-        [shape(BLOCK, KV_COLS, dtype=f32)] + [shape(BLOCK, KV_COLS)] * 3,
-    )(own, grad_z, back_far, back_1, back_2)
-    return own_sum, to_z
+def sum_column(*operands):
+    return call(
+        sum_column_kernel, "sum_column", [VMEM] * 4 + [AFTER], [shape(BLOCK, KV_COLS)] * 3
+    )(*operands)
+
+
+def gate_kernel(value, after, out):
+    out[...] = value[...]
+
+
+def gate(value, after):
+    return call(gate_kernel, "gate", [VMEM, AFTER], shape(*value.shape))(value, after)
 
 
 def last_kernel(kept, recv, after, out):
@@ -683,28 +687,27 @@
     q_recv = swap_core(q_send)
     block = join_cores(logratio, kv_own, kv_recv, q_recv)
 
+    from_x = [shift_x(block, 4 - offset) for offset in offsets[1:3]]
     from_z = [shift_z(block, p) for p in (1, 2, 3)]
-    from_x = [shift_x(block, 4 - offset) for offset in offsets[1:3]]
     q_aug, grads, raised_own, part_own = prep(
         prompt_q, resp_q, prompt_grad, resp_grad, q_recv, kv_own, kv_recv
     )
     note = facts(partner, chosen, resp_len, part_own)
-    far = join(from_z[1:], note)
-    near = join(from_x, note)
-    column = join([block] + from_z, near)
+    near = join(from_x, note, *from_z)
+    far = join(from_z[1:], note, from_z[0], near)
+    column = join([block] + from_z, note, near)
     early_kvs = [block] + from_z + [near]
     side_kvs = [shift_z(near, 1)] + [shift_x(far, 4 - offset) for offset in offsets[1:3]]
     far_kvs = [shift_x(column, 2)]
     kv_lists = [early_kvs, side_kvs, far_kvs]
 
-    raised, packs = [], []
-    for kvs, part in zip(kv_lists, all_parts):
-        one, pack_rows = forward(kvs, q_aug, note, part)
-        raised.append(one)
-        packs.append(pack_rows)
-    own_notes = collect(note, kv_lists)
+    early = forward(early_kvs, q_aug, part_own, early_part)
+    far_ones = forward(far_kvs, q_aug, early[0], far_part)
+    side = forward(side_kvs, q_aug, far_ones[0], side_part)
+    raised, packs = zip(early, side, far_ones)
+    own_notes = collect(note, kv_lists, far_ones[0])
     out, cot_aug, gains = combine(
-        own_notes, swap_core(own_notes), grads, packs + [part_own]
+        own_notes, swap_core(own_notes), grads, [*packs, part_own]
     )
 
     def backward_of(chunk, splits, after):
@@ -720,7 +723,9 @@
             splits,
         )
 
-    slopes_far, grad_far = backward_of(2, (((0, 1, 2, 3), bf16),), gains)
+    slopes_far, grad_far, grad_x3 = backward_of(
+        2, (((1, 2, 3), bf16), ((0,), bf16)), gains
+    )
     back_far = shift_x(grad_far, 2)
     slopes_side, grad_1, grad_2 = backward_of(
         1, (((0, 2, 3), bf16), ((1, 4, 5), bf16)), grad_far
@@ -731,8 +736,11 @@
     )
     slopes = [slopes_early, slopes_side, slopes_far]
 
-    back_x = [shift_x(term, offset) for term, offset in zip(to_x, offsets[1:3])]
-    own_sum, to_z = sum_column(grad_own, grad_z, back_far, back_1, back_2)
+    to_x3 = gate(grad_x3, back_far)
+    back_x = [
+        shift_x(term, offset) for term, offset in zip((*to_x, to_x3), offsets[1:])
+    ]
+    to_z = sum_column(grad_z, back_far, back_1, back_2, to_x3)
     back_z = [shift_z(term, 4 - p) for p, term in zip((1, 2, 3), to_z)]
     own_result, sib_result = finish(
         kv_lists, slopes, kv_own, kv_recv, raised_own, q_aug, cot_aug, gains, out, grad_own
@@ -740,7 +748,7 @@
     prompt_out, resp_out, prompt_dq, resp_dq, resp_dkv, placed = place(
         own_result, swap_core(sib_result)
     )
-    kept, sent = add_split([own_sum] + back_z + back_x, 2, TOKENS, own_sum, 2 * 10**10)
+    kept, sent = add_split([grad_own] + back_z + back_x, 2, TOKENS, grad_own, 2 * 10**10)
     prompt_dkv = last(kept, swap_core(sent), placed)
     return (prompt_out, resp_out, prompt_dq, resp_dq, prompt_dkv, resp_dkv)
 

time: 66.3 us -> 63.3 us (0.955)
  waiting for transfers between devices: 15.2 us -> 10.5 us
  starting transfers between devices: 25.4 us -> 27 us
    ppermute x10 -> x11, waiting for transfers between devices: 10.3 us -> 6.27 us  [shift_x(): return lax.ppermute(value, 'resp', pairs)]
    ppermute x5, starting transfers between devices: 7.91 us -> 8.9 us  [swap_core(): return lax.ppermute(value, 'resp', [(r, r ^ 1) for r in range(32)])]
    ppermute x10 -> x11, starting transfers between devices: 11.1 us -> 11.7 us  [shift_x(): return lax.ppermute(value, 'resp', pairs)]
  transfers between devices with their start and end apart: 22 -> 23, of which waited for: 6 -> 7; matrix products, arithmetic and copies ran while one was open for 0% -> 0% of each run, Pallas kernels for 26% -> 28%
where the time goes in v5:
time: 63.3 us; the launch traced here: 63.1 us
  starting transfers between devices  27 us (43%)
  Pallas kernels  22.2 us (35%)
  waiting for transfers between devices  10.5 us (17%)
  between operations  3.44 us (5%)
    ppermute x11, starting transfers between devices, shift_x(): return lax.ppermute(value, 'resp', pairs)  11.7 us
    ppermute x5, starting transfers between devices, swap_core(): return lax.ppermute(value, 'resp', [(r, r ^ 1) for r in range(32)])  8.9 us
    pallas_call x3, Pallas kernels, forward(): call(functools.partial(forward_kernel, part), 'forward', [VMEM] * (len(pa...  7.1 us
    pallas_call x3, Pallas kernels, backward(): call(functools.partial(backward_kernel, part, splits, chunk), 'backward',...  7.01 us
    ppermute x7, starting transfers between devices, shift_z(): return lax.ppermute(value, 'resp', pairs)  6.42 us
    ppermute x11, waiting for transfers between devices, shift_x(): return lax.ppermute(value, 'resp', pairs)  6.27 us
    ppermute x7, waiting for transfers between devices, shift_z(): return lax.ppermute(value, 'resp', pairs)  3.32 us
    pallas_call x1, Pallas kernels, finish(): call(finish_kernel, 'finish', [VMEM] * (len(flat) + len(slopes) + 7) + [A...  1.98 us
  transfers between devices with their start and end apart: 23, of which 7 were waited for; matrix products, arithmetic and copies ran while one was open for 0% of the time, Pallas kernels for 28%

profile of v5, /device:TPU:1, one launch (start us, length us, event | category | flops | bytes accessed | tf_op | source)
XLA Modules:
  0.0 63.1 jit_solution(5939814562986144221)
XLA Ops:
  0.6 1.3 %pack.1 = (bf16[128,256]{1,0:T(8,128)(2,1)S(1)}, bf16[128,256]{1,0:T(8,128)(2,1)S(1)}, bf16[4,64,1024]{2,1,0:T(8,128)(2,1)S(1)}) custom-call(bf16[64,512]{1,0:T(8,128)(2,1)} %prompt_kv.1, bf16[1,64,512]{2,1,0:T(8,128)(2,1)} %resp_kv.1, bf16[64,2048]{1,0:T(8,128)(2,1)} %pq.3, bf16[1,64,2048]{2,1,0:T(8,128)(2,1)} %rq.3, bf16[64,2048]{1,0:T(8,128)(2,1)} %pg.3, ...), custom_call_target="tpu_custom_call" | custom-call | bytes 1048576 | tf_op jit(solution)/shard_map/pack/pallas_call | solution.py:144
  1.9 3.3 %collective-permute-start.1 = (bf16[4,64,1024]{2,1,0:T(8,128)(2,1)S(1)}, bf16[4,64,1024]{2,1,0:T(8,128)(2,1)S(1)}, u32[]{:S(2)}, u32[]{:S(2)}) collective-permute-start(bf16[4,64,1024]{2,1,0:T(8,128)(2,1)S(1)} %get-tuple-element.48), channel_id=1, source_target_pairs={{0,4},{4,0},{8,12},{12,8},{16,20},{20,16},{24,28},{28,24},{32,36},... | collective-permute-start | bytes 1572872 | tf_op jit(solution)/shard_map/ppermute | solution.py:76
  5.2 0.1 collective-permute-start
  6.0 0.9 %collective-permute-done.recv.kv_recv.refs_13_ = bf16[128,256]{1,0:T(8,128)(2,1)S(1)} collective-permute-done((bf16[128,256]{1,0:T(8,128)(2,1)S(1)}, bf16[128,256]{1,0:T(8,128)(2,1)S(1)}, u32[]{:S(2)}, u32[]{:S(2)}) %collective-permute-start) | collective-permute-done | bytes 65568 | tf_op jit(solution)/shard_map/ppermute | solution.py:76
  6.9 0.8 %collective-permute-start.6 = (bf16[144,256]{1,0:T(8,128)(2,1)S(1)}, bf16[144,256]{1,0:T(8,128)(2,1)S(1)}, u32[]{:S(2)}, u32[]{:S(2)}) collective-permute-start(bf16[144,256]{1,0:T(8,128)(2,1)S(1)} %join_cores.1.refs_0_.refs_1_), channel_id=1, source_target_pairs={{0,24},{4,28},{8,0},{12,4},{16,8},{20,12},{24,16},{28,20},{32,56},... | collective-permute-start | bytes 221192 | tf_op jit(solution)/shard_map/ppermute | solution.py:86
  7.7 0.7 %collective-permute-start.5 = (bf16[144,256]{1,0:T(8,128)(2,1)S(1)}, bf16[144,256]{1,0:T(8,128)(2,1)S(1)}, u32[]{:S(2)}, u32[]{:S(2)}) collective-permute-start(bf16[144,256]{1,0:T(8,128)(2,1)S(1)} %join_cores.1.refs_0_.refs_1_), channel_id=1, source_target_pairs={{0,8},{4,12},{8,16},{12,20},{16,24},{20,28},{24,0},{28,4},{32,40},... | collective-permute-start | bytes 221192 | tf_op jit(solution)/shard_map/ppermute | solution.py:86
  8.4 3.6 %collective-permute-start.4 = (bf16[144,256]{1,0:T(8,128)(2,1)S(1)}, bf16[144,256]{1,0:T(8,128)(2,1)S(1)}, u32[]{:S(2)}, u32[]{:S(2)}) collective-permute-start(bf16[144,256]{1,0:T(8,128)(2,1)S(1)} %join_cores.1.refs_0_.refs_1_), channel_id=1, source_target_pairs={{0,96},{4,100},{8,104},{12,108},{16,112},{20,116},{24,120},{28,124... | collective-permute-start | bytes 221192 | tf_op jit(solution)/shard_map/ppermute | solution.py:81
  12.1 0.3 collective-permute-start.2
  14.3 1.9 %prep.1 = (bf16[256,2048]{1,0:T(8,128)(2,1)S(1)}, bf16[128,2048]{1,0:T(8,128)(2,1)S(1)}, bf16[64,1024]{1,0:T(8,128)(2,1)S(1)}, f32[144,2048]{1,0:T(8,128)S(1)}) custom-call(bf16[64,2048]{1,0:T(8,128)(2,1)} %pq.3, bf16[1,64,2048]{2,1,0:T(8,128)(2,1)} %rq.3, bf16[64,2048]{1,0:T(8,128)(2,1)} %pg.3, bf16[1,64,2048]{2,1,0:T(8,128)(2,1)} %rg.3, ...), custom_call_target="tpu_custom_call" | custom-call | bytes 1048576 | tf_op jit(solution)/shard_map/prep/pallas_call | solution.py:262
  16.2 0.0 collective-permute-done.6.refs_1_
  16.3 0.0 collective-permute-done.4.refs_5_.refs_1_.refs_3_.refs_4_
  16.3 3.2 %collective-permute-done.3.refs_4_.refs_0_.refs_2_.refs_3_ = bf16[144,256]{1,0:T(8,128)(2,1)S(1)} collective-permute-done((bf16[144,256]{1,0:T(8,128)(2,1)S(1)}, bf16[144,256]{1,0:T(8,128)(2,1)S(1)}, u32[]{:S(2)}, u32[]{:S(2)}) %collective-permute-start.3) | collective-permute-done | bytes 73760 | tf_op jit(solution)/shard_map/ppermute | solution.py:81
  19.5 0.0 collective-permute-done.2.refs_3_.refs_1_.refs_2_
  19.5 1.8 %collective-permute-start.10 = (bf16[576,256]{1,0:T(8,128)(2,1)S(1)}, bf16[576,256]{1,0:T(8,128)(2,1)S(1)}, u32[]{:S(2)}, u32[]{:S(2)}) collective-permute-start(bf16[576,256]{1,0:T(8,128)(2,1)S(1)} %join.5), channel_id=1, source_target_pairs={{0,16},{4,20},{8,24},{12,28},{16,0},{20,4},{24,8},{28,12},{32,48},... | collective-permute-start | bytes 884744 | tf_op jit(solution)/shard_map/ppermute | solution.py:86
  21.4 1.0 %collective-permute-start.9 = (bf16[288,256]{1,0:T(8,128)(2,1)S(1)}, bf16[288,256]{1,0:T(8,128)(2,1)S(1)}, u32[]{:S(2)}, u32[]{:S(2)}) collective-permute-start(bf16[288,256]{1,0:T(8,128)(2,1)S(1)} %join.4), channel_id=1, source_target_pairs={{0,24},{4,28},{8,0},{12,4},{16,8},{20,12},{24,16},{28,20},{32,56},... | collective-permute-start | bytes 442376 | tf_op jit(solution)/shard_map/ppermute | solution.py:86
  22.4 0.6 %collective-permute-start.8 = (bf16[288,256]{1,0:T(8,128)(2,1)S(1)}, bf16[288,256]{1,0:T(8,128)(2,1)S(1)}, u32[]{:S(2)}, u32[]{:S(2)}) collective-permute-start(bf16[288,256]{1,0:T(8,128)(2,1)S(1)} %join.4), channel_id=1, source_target_pairs={{0,8},{4,12},{8,16},{12,20},{16,24},{20,28},{24,0},{28,4},{32,40},... | collective-permute-start | bytes 442376 | tf_op jit(solution)/shard_map/ppermute | solution.py:86
  23.1 0.0 collective-permute-start.7
  23.1 2.7 %forward.3 = (bf16[768,2048]{1,0:T(8,128)(2,1)S(1)}, f32[144,2048]{1,0:T(8,128)S(1)}) custom-call(bf16[144,256]{1,0:T(8,128)(2,1)S(1)} %join_cores.1.refs_0_.refs_1_, bf16[144,256]{1,0:T(8,128)(2,1)S(1)} %collective-permute-done.2.refs_3_.refs_1_.refs_2_, bf16[144,256]{1,0:T(8,128)(2,1)S(1)} %collective-permute-done.3.refs_4_.refs_0_.refs_2_.refs_3_, ...), custom_call_target="tpu_custom_call" | custom-call | flops 805306368 | bytes 1048576 | tf_op jit(solution)/shard_map/forward/pallas_call | solution.py:344
  25.7 3.5 %collective-permute-done.10.refs_0_.refs_9_.refs_8_ = bf16[576,256]{1,0:T(8,128)(2,1)S(1)} collective-permute-done((bf16[576,256]{1,0:T(8,128)(2,1)S(1)}, bf16[576,256]{1,0:T(8,128)(2,1)S(1)}, u32[]{:S(2)}, u32[]{:S(2)}) %collective-permute-start.10) | collective-permute-done | bytes 294944 | tf_op jit(solution)/shard_map/ppermute | solution.py:86
  29.2 1.8 %forward.4 = (bf16[512,2048]{1,0:T(8,128)(2,1)S(1)}, f32[144,2048]{1,0:T(8,128)S(1)}) custom-call(bf16[576,256]{1,0:T(8,128)(2,1)S(1)} %collective-permute-done.10.refs_0_.refs_9_.refs_8_, bf16[256,2048]{1,0:T(8,128)(2,1)S(1)} %get-tuple-element.50.refs_5_.refs_1_.refs_3_.refs_2_.refs_4_.refs_6_.refs_15_, bf16[768,2048]{1,0:T(8,128)(2,1)S(1)} %get-tuple-element.51.refs_2_.refs_5_), custom_call_target="tpu_custom_call" | custom-call | flops 536870912 | bytes 1048576 | tf_op jit(solution)/shard_map/forward/pallas_call | solution.py:344
  31.0 1.7 %collective-permute-done.9.refs_8_.refs_2_.refs_7_ = bf16[288,256]{1,0:T(8,128)(2,1)S(1)} collective-permute-done((bf16[288,256]{1,0:T(8,128)(2,1)S(1)}, bf16[288,256]{1,0:T(8,128)(2,1)S(1)}, u32[]{:S(2)}, u32[]{:S(2)}) %collective-permute-start.9) | collective-permute-done | bytes 147488 | tf_op jit(solution)/shard_map/ppermute | solution.py:86
  32.7 0.5 collective-permute-done.8.refs_7_.refs_1_.refs_6_
  33.2 0.9 %collective-permute-start.11 = (bf16[16,256]{1,0:T(8,128)(2,1)S(1)}, bf16[16,256]{1,0:T(8,128)(2,1)S(1)}, u32[]{:S(2)}, u32[]{:S(2)}) collective-permute-start(bf16[16,256]{1,0:T(8,128)(2,1)S(1)} %collect.1.own_notes), channel_id=1, source_target_pairs={{0,4},{4,0},{8,12},{12,8},{16,20},{20,16},{24,28},{28,24},{32,36},... | collective-permute-start | bytes 24584 | tf_op jit(solution)/shard_map/ppermute | solution.py:76
  34.2 2.7 %forward.5 = (bf16[768,2048]{1,0:T(8,128)(2,1)S(1)}, f32[144,2048]{1,0:T(8,128)S(1)}) custom-call(bf16[288,256]{1,0:T(8,128)(2,1)S(1)} %collective-permute-done.7.refs_6_.refs_0_.refs_5_, bf16[288,256]{1,0:T(8,128)(2,1)S(1)} %collective-permute-done.8.refs_7_.refs_1_.refs_6_, bf16[288,256]{1,0:T(8,128)(2,1)S(1)} %collective-permute-done.9.refs_8_.refs_2_.refs_7_, ...), custom_call_target="tpu_custom_call" | custom-call | flops 805306368 | bytes 1048576 | tf_op jit(solution)/shard_map/forward/pallas_call | solution.py:344
  36.8 0.0 collective-permute-done.11.sib_notes
  36.9 0.9 %combine.1 = (bf16[128,2048]{1,0:T(8,128)(2,1)S(1)}, bf16[256,2048]{1,0:T(8,128)(2,1)S(1)}, f32[8,2048]{1,0:T(8,128)S(1)}) custom-call(bf16[16,256]{1,0:T(8,128)(2,1)S(1)} %collect.1.own_notes, bf16[16,256]{1,0:T(8,128)(2,1)S(1)} %collective-permute-done.11.sib_notes, bf16[128,2048]{1,0:T(8,128)(2,1)S(1)} %get-tuple-element.53.grads, ...), custom_call_target="tpu_custom_call" | custom-call | bytes 1048576 | tf_op jit(solution)/shard_map/combine/pallas_call | solution.py:449
  37.8 1.8 %backward.3 = (bf16[512,2048]{1,0:T(8,128)(2,1)S(1)}, bf16[384,256]{1,0:T(8,128)(2,1)S(1)}, bf16[128,256]{1,0:T(8,128)(2,1)S(1)}) custom-call(bf16[576,256]{1,0:T(8,128)(2,1)S(1)} %collective-permute-done.10.refs_0_.refs_9_.refs_8_, bf16[512,2048]{1,0:T(8,128)(2,1)S(1)} %get-tuple-element.52.refs_10_.refs_4_.refs_1_, ...), custom_call_target="tpu_custom_call" | custom-call | flops 805306368 | bytes 1048576 | tf_op jit(solution)/shard_map/backward/pallas_call | solution.py:493
  39.6 1.5 %collective-permute-start.13 = (bf16[384,256]{1,0:T(8,128)(2,1)S(1)}, bf16[384,256]{1,0:T(8,128)(2,1)S(1)}, u32[]{:S(2)}, u32[]{:S(2)}) collective-permute-start(bf16[384,256]{1,0:T(8,128)(2,1)S(1)} %get-tuple-element.60.refs_7_), channel_id=1, source_target_pairs={{0,16},{4,20},{8,24},{12,28},{16,0},{20,4},{24,8},{28,12},{32,48},... | collective-permute-start | bytes 589832 | tf_op jit(solution)/shard_map/ppermute | solution.py:86
  41.1 2.6 %backward.4 = (bf16[768,2048]{1,0:T(8,128)(2,1)S(1)}, bf16[384,256]{1,0:T(8,128)(2,1)S(1)}, bf16[384,256]{1,0:T(8,128)(2,1)S(1)}) custom-call(bf16[288,256]{1,0:T(8,128)(2,1)S(1)} %collective-permute-done.7.refs_6_.refs_0_.refs_5_, bf16[288,256]{1,0:T(8,128)(2,1)S(1)} %collective-permute-done.8.refs_7_.refs_1_.refs_6_, ...), custom_call_target="tpu_custom_call" | custom-call | flops 1207959552 | bytes 1048576 | tf_op jit(solution)/shard_map/backward/pallas_call | solution.py:493
  43.7 1.6 %collective-permute-start.15 = (bf16[384,256]{1,0:T(8,128)(2,1)S(1)}, bf16[384,256]{1,0:T(8,128)(2,1)S(1)}, u32[]{:S(2)}, u32[]{:S(2)}) collective-permute-start(bf16[384,256]{1,0:T(8,128)(2,1)S(1)} %get-tuple-element.75), channel_id=1, source_target_pairs={{0,8},{4,12},{8,16},{12,20},{16,24},{20,28},{24,0},{28,4},{32,40},... | collective-permute-start | bytes 589832 | tf_op jit(solution)/shard_map/ppermute | solution.py:86
  45.4 1.3 %collective-permute-start.14 = (bf16[384,256]{1,0:T(8,128)(2,1)S(1)}, bf16[384,256]{1,0:T(8,128)(2,1)S(1)}, u32[]{:S(2)}, u32[]{:S(2)}) collective-permute-start(bf16[384,256]{1,0:T(8,128)(2,1)S(1)} %get-tuple-element.61.refs_9_), channel_id=1, source_target_pairs={{0,24},{4,28},{8,0},{12,4},{16,8},{20,12},{24,16},{28,20},{32,56},... | collective-permute-start | bytes 589832 | tf_op jit(solution)/shard_map/ppermute | solution.py:86
  46.7 2.6 %backward.5 = (bf16[768,2048]{1,0:T(8,128)(2,1)S(1)}, f32[128,256]{1,0:T(8,128)S(1)}, f32[384,256]{1,0:T(8,128)S(1)}, bf16[128,256]{1,0:T(8,128)(2,1)S(1)}, bf16[128,256]{1,0:T(8,128)(2,1)S(1)}) custom-call(bf16[144,256]{1,0:T(8,128)(2,1)S(1)} %join_cores.1.refs_0_.refs_1_, bf16[144,256]{1,0:T(8,128)(2,1)S(1)} %collective-permute-done.2.refs_3_.refs_1_.refs_2_, ...), custom_call_target="tpu_custom_call" | custom-call | flops 1207959552 | bytes 1048576 | tf_op jit(solution)/shard_map/backward/pallas_call | solution.py:493
  49.3 0.1 collective-permute-start.19
  49.4 1.5 %collective-permute-start.20 = (bf16[128,256]{1,0:T(8,128)(2,1)S(1)}, bf16[128,256]{1,0:T(8,128)(2,1)S(1)}, u32[]{:S(2)}, u32[]{:S(2)}) collective-permute-start(bf16[128,256]{1,0:T(8,128)(2,1)S(1)} %get-tuple-element.81), channel_id=1, source_target_pairs={{0,8},{4,12},{8,16},{12,20},{16,24},{20,28},{24,0},{28,4},{32,40},... | collective-permute-start | bytes 196616 | tf_op jit(solution)/shard_map/ppermute | solution.py:86
  50.8 0.6 %collective-permute-start.21 = (bf16[128,256]{1,0:T(8,128)(2,1)S(1)}, bf16[128,256]{1,0:T(8,128)(2,1)S(1)}, u32[]{:S(2)}, u32[]{:S(2)}) collective-permute-start(bf16[128,256]{1,0:T(8,128)(2,1)S(1)} %gate.1.after), channel_id=1, source_target_pairs={{0,16},{4,20},{8,24},{12,28},{16,0},{20,4},{24,8},{28,12},{32,48},... | collective-permute-start | bytes 196616 | tf_op jit(solution)/shard_map/ppermute | solution.py:86
  51.5 0.5 collective-permute-done.15.back_2
  52.0 0.0 collective-permute-done.14.back_1
  52.0 0.1 sum_column.1
  52.1 0.1 collective-permute-start.16
  52.2 1.1 %collective-permute-start.17 = (bf16[128,256]{1,0:T(8,128)(2,1)S(1)}, bf16[128,256]{1,0:T(8,128)(2,1)S(1)}, u32[]{:S(2)}, u32[]{:S(2)}) collective-permute-start(bf16[128,256]{1,0:T(8,128)(2,1)S(1)} %get-tuple-element.78), channel_id=1, source_target_pairs={{0,64},{4,68},{8,72},{12,76},{16,80},{20,84},{24,88},{28,92},{32,9... | collective-permute-start | bytes 196616 | tf_op jit(solution)/shard_map/ppermute | solution.py:81
  53.3 1.4 %collective-permute-start.18 = (bf16[128,256]{1,0:T(8,128)(2,1)S(1)}, bf16[128,256]{1,0:T(8,128)(2,1)S(1)}, u32[]{:S(2)}, u32[]{:S(2)}) collective-permute-start(bf16[128,256]{1,0:T(8,128)(2,1)S(1)} %get-tuple-element.79), channel_id=1, source_target_pairs={{0,32},{4,36},{8,40},{12,44},{16,48},{20,52},{24,56},{28,60},{32,6... | collective-permute-start | bytes 196616 | tf_op jit(solution)/shard_map/ppermute | solution.py:81
  54.6 2.0 %finish.1 = (bf16[64,4352]{1,0:T(8,128)(2,1)S(1)}, bf16[64,4352]{1,0:T(8,128)(2,1)S(1)}) custom-call(bf16[144,256]{1,0:T(8,128)(2,1)S(1)} %join_cores.1.refs_0_.refs_1_, bf16[144,256]{1,0:T(8,128)(2,1)S(1)} %collective-permute-done.2.refs_3_.refs_1_.refs_2_, bf16[144,256]{1,0:T(8,128)(2,1)S(1)} %collective-permute-done.3.refs_4_.refs_0_.refs_2_.refs_3_, ...), custom_call_target="tpu_custom_call" | custom-call | flops 805306368 | bytes 1048576 | tf_op jit(solution)/shard_map/finish/pallas_call | solution.py:557
  56.6 2.3 %collective-permute-start.12 = (bf16[64,4352]{1,0:T(8,128)(2,1)S(1)}, bf16[64,4352]{1,0:T(8,128)(2,1)S(1)}, u32[]{:S(2)}, u32[]{:S(2)}) collective-permute-start(bf16[64,4352]{1,0:T(8,128)(2,1)S(1)} %get-tuple-element.69), channel_id=1, source_target_pairs={{0,4},{4,0},{8,12},{12,8},{16,20},{20,16},{24,28},{28,24},{32,36},... | collective-permute-start | bytes 1671176 | tf_op jit(solution)/shard_map/ppermute | solution.py:76
  59.0 0.1 collective-permute-done.18.refs_3_
  59.1 0.1 add_split.1
  59.1 2.2 %collective-permute-start.22 = (bf16[64,256]{1,0:T(8,128)(2,1)S(1)}, bf16[64,256]{1,0:T(8,128)(2,1)S(1)}, u32[]{:S(2)}, u32[]{:S(2)}) collective-permute-start(bf16[64,256]{1,0:T(8,128)(2,1)S(1)} %get-tuple-element.83), channel_id=1, source_target_pairs={{0,4},{4,0},{8,12},{12,8},{16,20},{20,16},{24,28},{28,24},{32,36},... | collective-permute-start | bytes 98312 | tf_op jit(solution)/shard_map/ppermute | solution.py:76
  61.4 1.1 %place.1 = (bf16[64,2048]{1,0:T(8,128)(2,1)}, bf16[1,64,2048]{2,1,0:T(8,128)(2,1)}, bf16[64,2048]{1,0:T(8,128)(2,1)}, bf16[1,64,2048]{2,1,0:T(8,128)(2,1)}, bf16...) custom-call(bf16[64,4352]{1,0:T(8,128)(2,1)S(1)} %get-tuple-element.68.own, bf16[64,4352]{1,0:T(8,128)(2,1)S(1)} %collective-permute-done.12.recv), custom_call_target="tpu_custom_call" | custom-call | bytes 1048576 | tf_op jit(solution)/shard_map/place/pallas_call | solution.py:592
  62.4 0.7 %last.1 = bf16[64,512]{1,0:T(8,128)(2,1)} custom-call(bf16[64,256]{1,0:T(8,128)(2,1)S(1)} %get-tuple-element.82.kept, bf16[64,256]{1,0:T(8,128)(2,1)S(1)} %collective-permute-done.22.recv, f32[8,128]{1,0:T(8,128)S(1)} %get-tuple-element.84.after), custom_call_target="tpu_custom_call" | custom-call | bytes 1048576 | tf_op jit(solution)/shard_map/last/pallas_call | solution.py:662
  (19 shorter events, 0.1 us)
Async XLA Ops:
  1.9 5.0 %collective-permute-start.1 = (bf16[4,64,1024]{2,1,0:T(8,128)(2,1)S(1)}, bf16[4,64,1024]{2,1,0:T(8,128)(2,1)S(1)}, u32[]{:S(2)}, u32[]{:S(2)}) collective-permute-start(bf16[4,64,1024]{2,1,0:T(8,128)(2,1)S(1)} %get-tuple-element.48), channel_id=1, source_target_pairs={{0,4},{4,0},{8,12},{12,8},{16,20},{20,16},{24,28},{28,24},{32,36},... | collective-permute-start | bytes 1572872 | tf_op jit(solution)/shard_map/ppermute | solution.py:76
  5.2 1.6 %collective-permute-start = (bf16[128,256]{1,0:T(8,128)(2,1)S(1)}, bf16[128,256]{1,0:T(8,128)(2,1)S(1)}, u32[]{:S(2)}, u32[]{:S(2)}) collective-permute-start(bf16[128,256]{1,0:T(8,128)(2,1)S(1)} %get-tuple-element.47), channel_id=1, source_target_pairs={{0,4},{4,0},{8,12},{12,8},{16,20},{20,16},{24,28},{28,24},{32,36},... | collective-permute-start | bytes 196616 | tf_op jit(solution)/shard_map/ppermute | solution.py:76
  6.9 9.4 %collective-permute-start.6 = (bf16[144,256]{1,0:T(8,128)(2,1)S(1)}, bf16[144,256]{1,0:T(8,128)(2,1)S(1)}, u32[]{:S(2)}, u32[]{:S(2)}) collective-permute-start(bf16[144,256]{1,0:T(8,128)(2,1)S(1)} %join_cores.1.refs_0_.refs_1_), channel_id=1, source_target_pairs={{0,24},{4,28},{8,0},{12,4},{16,8},{20,12},{24,16},{28,20},{32,56},... | collective-permute-start | bytes 221192 | tf_op jit(solution)/shard_map/ppermute | solution.py:86
  7.7 8.6 %collective-permute-start.5 = (bf16[144,256]{1,0:T(8,128)(2,1)S(1)}, bf16[144,256]{1,0:T(8,128)(2,1)S(1)}, u32[]{:S(2)}, u32[]{:S(2)}) collective-permute-start(bf16[144,256]{1,0:T(8,128)(2,1)S(1)} %join_cores.1.refs_0_.refs_1_), channel_id=1, source_target_pairs={{0,8},{4,12},{8,16},{12,20},{16,24},{20,28},{24,0},{28,4},{32,40},... | collective-permute-start | bytes 221192 | tf_op jit(solution)/shard_map/ppermute | solution.py:86
  8.4 7.8 %collective-permute-start.4 = (bf16[144,256]{1,0:T(8,128)(2,1)S(1)}, bf16[144,256]{1,0:T(8,128)(2,1)S(1)}, u32[]{:S(2)}, u32[]{:S(2)}) collective-permute-start(bf16[144,256]{1,0:T(8,128)(2,1)S(1)} %join_cores.1.refs_0_.refs_1_), channel_id=1, source_target_pairs={{0,96},{4,100},{8,104},{12,108},{16,112},{20,116},{24,120},{28,124... | collective-permute-start | bytes 221192 | tf_op jit(solution)/shard_map/ppermute | solution.py:81
  12.0 7.4 %collective-permute-start.3 = (bf16[144,256]{1,0:T(8,128)(2,1)S(1)}, bf16[144,256]{1,0:T(8,128)(2,1)S(1)}, u32[]{:S(2)}, u32[]{:S(2)}) collective-permute-start(bf16[144,256]{1,0:T(8,128)(2,1)S(1)} %join_cores.1.refs_0_.refs_1_), channel_id=1, source_target_pairs={{0,64},{4,68},{8,72},{12,76},{16,80},{20,84},{24,88},{28,92},{32,9... | collective-permute-start | bytes 221192 | tf_op jit(solution)/shard_map/ppermute | solution.py:81
  12.1 7.4 %collective-permute-start.2 = (bf16[144,256]{1,0:T(8,128)(2,1)S(1)}, bf16[144,256]{1,0:T(8,128)(2,1)S(1)}, u32[]{:S(2)}, u32[]{:S(2)}) collective-permute-start(bf16[144,256]{1,0:T(8,128)(2,1)S(1)} %join_cores.1.refs_0_.refs_1_), channel_id=1, source_target_pairs={{0,32},{4,36},{8,40},{12,44},{16,48},{20,52},{24,56},{28,60},{32,6... | collective-permute-start | bytes 221192 | tf_op jit(solution)/shard_map/ppermute | solution.py:81
  19.5 9.7 %collective-permute-start.10 = (bf16[576,256]{1,0:T(8,128)(2,1)S(1)}, bf16[576,256]{1,0:T(8,128)(2,1)S(1)}, u32[]{:S(2)}, u32[]{:S(2)}) collective-permute-start(bf16[576,256]{1,0:T(8,128)(2,1)S(1)} %join.5), channel_id=1, source_target_pairs={{0,16},{4,20},{8,24},{12,28},{16,0},{20,4},{24,8},{28,12},{32,48},... | collective-permute-start | bytes 884744 | tf_op jit(solution)/shard_map/ppermute | solution.py:86
  21.4 11.3 %collective-permute-start.9 = (bf16[288,256]{1,0:T(8,128)(2,1)S(1)}, bf16[288,256]{1,0:T(8,128)(2,1)S(1)}, u32[]{:S(2)}, u32[]{:S(2)}) collective-permute-start(bf16[288,256]{1,0:T(8,128)(2,1)S(1)} %join.4), channel_id=1, source_target_pairs={{0,24},{4,28},{8,0},{12,4},{16,8},{20,12},{24,16},{28,20},{32,56},... | collective-permute-start | bytes 442376 | tf_op jit(solution)/shard_map/ppermute | solution.py:86
  22.4 10.8 %collective-permute-start.8 = (bf16[288,256]{1,0:T(8,128)(2,1)S(1)}, bf16[288,256]{1,0:T(8,128)(2,1)S(1)}, u32[]{:S(2)}, u32[]{:S(2)}) collective-permute-start(bf16[288,256]{1,0:T(8,128)(2,1)S(1)} %join.4), channel_id=1, source_target_pairs={{0,8},{4,12},{8,16},{12,20},{16,24},{20,28},{24,0},{28,4},{32,40},... | collective-permute-start | bytes 442376 | tf_op jit(solution)/shard_map/ppermute | solution.py:86
  23.1 10.2 %collective-permute-start.7 = (bf16[288,256]{1,0:T(8,128)(2,1)S(1)}, bf16[288,256]{1,0:T(8,128)(2,1)S(1)}, u32[]{:S(2)}, u32[]{:S(2)}) collective-permute-start(bf16[288,256]{1,0:T(8,128)(2,1)S(1)} %join.3.refs_4_.refs_5_), channel_id=1, source_target_pairs={{0,32},{4,36},{8,40},{12,44},{16,48},{20,52},{24,56},{28,60},{32,6... | collective-permute-start | bytes 442376 | tf_op jit(solution)/shard_map/ppermute | solution.py:81
  33.2 3.6 %collective-permute-start.11 = (bf16[16,256]{1,0:T(8,128)(2,1)S(1)}, bf16[16,256]{1,0:T(8,128)(2,1)S(1)}, u32[]{:S(2)}, u32[]{:S(2)}) collective-permute-start(bf16[16,256]{1,0:T(8,128)(2,1)S(1)} %collect.1.own_notes), channel_id=1, source_target_pairs={{0,4},{4,0},{8,12},{12,8},{16,20},{20,16},{24,28},{28,24},{32,36},... | collective-permute-start | bytes 24584 | tf_op jit(solution)/shard_map/ppermute | solution.py:76
  39.6 11.2 %collective-permute-start.13 = (bf16[384,256]{1,0:T(8,128)(2,1)S(1)}, bf16[384,256]{1,0:T(8,128)(2,1)S(1)}, u32[]{:S(2)}, u32[]{:S(2)}) collective-permute-start(bf16[384,256]{1,0:T(8,128)(2,1)S(1)} %get-tuple-element.60.refs_7_), channel_id=1, source_target_pairs={{0,16},{4,20},{8,24},{12,28},{16,0},{20,4},{24,8},{28,12},{32,48},... | collective-permute-start | bytes 589832 | tf_op jit(solution)/shard_map/ppermute | solution.py:86
  43.7 8.3 %collective-permute-start.15 = (bf16[384,256]{1,0:T(8,128)(2,1)S(1)}, bf16[384,256]{1,0:T(8,128)(2,1)S(1)}, u32[]{:S(2)}, u32[]{:S(2)}) collective-permute-start(bf16[384,256]{1,0:T(8,128)(2,1)S(1)} %get-tuple-element.75), channel_id=1, source_target_pairs={{0,8},{4,12},{8,16},{12,20},{16,24},{20,28},{24,0},{28,4},{32,40},... | collective-permute-start | bytes 589832 | tf_op jit(solution)/shard_map/ppermute | solution.py:86
  45.4 6.7 %collective-permute-start.14 = (bf16[384,256]{1,0:T(8,128)(2,1)S(1)}, bf16[384,256]{1,0:T(8,128)(2,1)S(1)}, u32[]{:S(2)}, u32[]{:S(2)}) collective-permute-start(bf16[384,256]{1,0:T(8,128)(2,1)S(1)} %get-tuple-element.61.refs_9_), channel_id=1, source_target_pairs={{0,24},{4,28},{8,0},{12,4},{16,8},{20,12},{24,16},{28,20},{32,56},... | collective-permute-start | bytes 589832 | tf_op jit(solution)/shard_map/ppermute | solution.py:86
  49.3 4.0 %collective-permute-start.19 = (bf16[128,256]{1,0:T(8,128)(2,1)S(1)}, bf16[128,256]{1,0:T(8,128)(2,1)S(1)}, u32[]{:S(2)}, u32[]{:S(2)}) collective-permute-start(bf16[128,256]{1,0:T(8,128)(2,1)S(1)} %get-tuple-element.80), channel_id=1, source_target_pairs={{0,24},{4,28},{8,0},{12,4},{16,8},{20,12},{24,16},{28,20},{32,56},... | collective-permute-start | bytes 196616 | tf_op jit(solution)/shard_map/ppermute | solution.py:86
  49.4 7.2 %collective-permute-start.20 = (bf16[128,256]{1,0:T(8,128)(2,1)S(1)}, bf16[128,256]{1,0:T(8,128)(2,1)S(1)}, u32[]{:S(2)}, u32[]{:S(2)}) collective-permute-start(bf16[128,256]{1,0:T(8,128)(2,1)S(1)} %get-tuple-element.81), channel_id=1, source_target_pairs={{0,8},{4,12},{8,16},{12,20},{16,24},{20,28},{24,0},{28,4},{32,40},... | collective-permute-start | bytes 196616 | tf_op jit(solution)/shard_map/ppermute | solution.py:86
  50.8 8.1 %collective-permute-start.21 = (bf16[128,256]{1,0:T(8,128)(2,1)S(1)}, bf16[128,256]{1,0:T(8,128)(2,1)S(1)}, u32[]{:S(2)}, u32[]{:S(2)}) collective-permute-start(bf16[128,256]{1,0:T(8,128)(2,1)S(1)} %gate.1.after), channel_id=1, source_target_pairs={{0,16},{4,20},{8,24},{12,28},{16,0},{20,4},{24,8},{28,12},{32,48},... | collective-permute-start | bytes 196616 | tf_op jit(solution)/shard_map/ppermute | solution.py:86
  52.1 6.9 %collective-permute-start.16 = (bf16[128,256]{1,0:T(8,128)(2,1)S(1)}, bf16[128,256]{1,0:T(8,128)(2,1)S(1)}, u32[]{:S(2)}, u32[]{:S(2)}) collective-permute-start(bf16[128,256]{1,0:T(8,128)(2,1)S(1)} %get-tuple-element.77), channel_id=1, source_target_pairs={{0,96},{4,100},{8,104},{12,108},{16,112},{20,116},{24,120},{28,124... | collective-permute-start | bytes 196616 | tf_op jit(solution)/shard_map/ppermute | solution.py:81
  52.2 6.8 %collective-permute-start.17 = (bf16[128,256]{1,0:T(8,128)(2,1)S(1)}, bf16[128,256]{1,0:T(8,128)(2,1)S(1)}, u32[]{:S(2)}, u32[]{:S(2)}) collective-permute-start(bf16[128,256]{1,0:T(8,128)(2,1)S(1)} %get-tuple-element.78), channel_id=1, source_target_pairs={{0,64},{4,68},{8,72},{12,76},{16,80},{20,84},{24,88},{28,92},{32,9... | collective-permute-start | bytes 196616 | tf_op jit(solution)/shard_map/ppermute | solution.py:81
  53.3 5.8 %collective-permute-start.18 = (bf16[128,256]{1,0:T(8,128)(2,1)S(1)}, bf16[128,256]{1,0:T(8,128)(2,1)S(1)}, u32[]{:S(2)}, u32[]{:S(2)}) collective-permute-start(bf16[128,256]{1,0:T(8,128)(2,1)S(1)} %get-tuple-element.79), channel_id=1, source_target_pairs={{0,32},{4,36},{8,40},{12,44},{16,48},{20,52},{24,56},{28,60},{32,6... | collective-permute-start | bytes 196616 | tf_op jit(solution)/shard_map/ppermute | solution.py:81
  56.6 4.7 %collective-permute-start.12 = (bf16[64,4352]{1,0:T(8,128)(2,1)S(1)}, bf16[64,4352]{1,0:T(8,128)(2,1)S(1)}, u32[]{:S(2)}, u32[]{:S(2)}) collective-permute-start(bf16[64,4352]{1,0:T(8,128)(2,1)S(1)} %get-tuple-element.69), channel_id=1, source_target_pairs={{0,4},{4,0},{8,12},{12,8},{16,20},{20,16},{24,28},{28,24},{32,36},... | collective-permute-start | bytes 1671176 | tf_op jit(solution)/shard_map/ppermute | solution.py:76
  59.1 3.3 %collective-permute-start.22 = (bf16[64,256]{1,0:T(8,128)(2,1)S(1)}, bf16[64,256]{1,0:T(8,128)(2,1)S(1)}, u32[]{:S(2)}, u32[]{:S(2)}) collective-permute-start(bf16[64,256]{1,0:T(8,128)(2,1)S(1)} %get-tuple-element.83), channel_id=1, source_target_pairs={{0,4},{4,0},{8,12},{12,8},{16,20},{20,16},{24,28},{28,24},{32,36},... | collective-permute-start | bytes 98312 | tf_op jit(solution)/shard_map/ppermute | solution.py:76

commit v6 on v5

--- a/solution.py
+++ b/solution.py
@@ -129,25 +129,38 @@
     ]
 
 
-def pack_kernel(prompt_kv, resp_kv, pq, rq, pg, rg, own, send, send_q, sems):
+def pack_kv_kernel(prompt_kv, resp_kv, own, send, sems):
     core = here()[0]
     pairs = []
     for side, out in ((core, own), (1 - core, send)):
         cols = columns(side, KV_COLS)
         pairs.append((prompt_kv.at[:, cols], out.at[pl.ds(0, TOKENS)]))
         pairs.append((resp_kv.at[0, :, cols], out.at[pl.ds(TOKENS, TOKENS)]))
-    pairs += half_copies(1 - core, pq, rq, pg, rg, send_q)
     waited(started(pairs, sems))
 
 
-def pack(*operands):
-    return call(
-        pack_kernel,
-        "pack",
-        [HBM] * 6,
-        [shape(BLOCK, KV_COLS)] * 2 + [shape(4, TOKENS, Q_COLS)],
-        [pltpu.SemaphoreType.DMA((8,))],
-    )(*operands)
+def pack_kv(prompt_kv, resp_kv):
+    return call(
+        pack_kv_kernel,
+        "pack_kv",
+        [HBM] * 2,
+        [shape(BLOCK, KV_COLS)] * 2,
+        [pltpu.SemaphoreType.DMA((4,))],
+    )(prompt_kv, resp_kv)
+
+
+def pack_q_kernel(pq, rq, pg, rg, after, send, sems):
+    waited(started(half_copies(1 - here()[0], pq, rq, pg, rg, send), sems))
+
+
+def pack_q(prompt_q, resp_q, prompt_grad, resp_grad, after):
+    return call(
+        pack_q_kernel,
+        "pack_q",
+        [HBM] * 4 + [AFTER],
+        shape(4, TOKENS, Q_COLS),
+        [pltpu.SemaphoreType.DMA((4,))],
+    )(prompt_q, resp_q, prompt_grad, resp_grad, after)
 
 
 def note_of(core, first, values):
@@ -173,6 +186,7 @@
         "join_cores",
         [SMEM] + [VMEM] * 2 + [AFTER],
         shape(PIECE, KV_COLS),
+        flops=2 * 10**10,
     )(logratio, own, recv, after)
 
 
@@ -306,9 +320,9 @@
     return (info[1] + 4 - p) % 4, (info[2] + offsets[i]) % 4
 
 
-def forward_kernel(part, *refs):
+def forward_kernel(part, has_top, *refs):
     kvs = refs[: len(part)]
-    q_aug, after, raised, packed, key_aug, value_rows, scores = refs[len(part) :]
+    q_aug, given, raised, packed, key_aug, value_rows, tops = refs[len(part) :]
     info = here()
     core, z_own, x_own = info
     row = iota((BLOCK, HEAD_DIM), 1)
@@ -330,21 +344,43 @@
             key_aug[rows, HEAD_DIM:] = hidden.astype(bf16)
             number += 1
     value_rows[...] = with_ones(part_rows(kvs, part, value_cols))
-    scores[0] = dot(key_aug[...], q_aug[:, lanes_of(0)])
-    for j in range(SUBS):
-        if j + 1 < SUBS:
-            scores[(j + 1) % 2] = dot(key_aug[...], q_aug[:, lanes_of(j + 1)])
-        one, info_rows = softmax_part(scores[j % 2], value_rows[...])
-        raised[:, lanes_of(j)] = one
-        packed[:, lanes_of(j)] = info_rows
-
-
-def forward(kvs, q_aug, after, part):
+
+    def find_tops():
+        for j in range(SUBS):
+            lanes = lanes_of(j)
+            top = jnp.max(dot(key_aug[...], q_aug[:, lanes]), axis=0, keepdims=True)
+            tops[:, lanes] = jnp.broadcast_to(top, (8, TILE))
+
+    def weigh():
+        for j in range(SUBS):
+            lanes = lanes_of(j)
+            scores = dot(key_aug[...], q_aug[:, lanes])
+            raised[:, lanes] = jnp.exp2((scores - tops[0:1, lanes]) * exp2_scale).astype(bf16)
+        total = dot(value_rows[...], raised[...])
+        packed[: HEAD_DIM + 8] = total[: HEAD_DIM + 8]
+        packed[HEAD_DIM + 8 :] = tops[...]
+
+    if not has_top:
+        find_tops()
+        weigh()
+        return
+    tops[...] = given[HEAD_DIM + 8 :]
+    weigh()
+    largest = jnp.max(packed[HEAD_DIM : HEAD_DIM + 1, :])
+
+    @pl.when(jnp.logical_not(largest < 2.0**40))
+    def _():
+        find_tops()
+        weigh()
+
+
+def forward(kvs, q_aug, given, part):
     keys = keys_in(part)
-    return call(
-        functools.partial(forward_kernel, part),
+    has_top = part is not early_part
+    return call(
+        functools.partial(forward_kernel, part, has_top),
         "forward",
-        [VMEM] * (len(part) + 1) + [AFTER],
+        [VMEM] * (len(part) + 1) + [VMEM if has_top else AFTER],
         [
             shape(keys, LANES),
             shape(HEAD_DIM + 16, LANES, dtype=f32),
@@ -352,10 +388,10 @@
         [
             pltpu.VMEM((keys, 2 * HEAD_DIM), bf16),
             pltpu.VMEM((HEAD_DIM + 16, keys), bf16),
-            pltpu.VMEM((2, keys, TILE), f32),
+            pltpu.VMEM((8, LANES), f32),
         ],
         flops=4 * keys * LANES * HEAD_DIM,
-    )(*kvs, q_aug, after)
+    )(*kvs, q_aug, given)
 
 
 def collect_kernel(*refs):
@@ -680,12 +716,11 @@
         pltpu.with_memory_space_constraint(array, pltpu.HBM)
         for array in (prompt_q, prompt_kv, resp_q, resp_kv, prompt_grad, resp_grad)
     ]
-    kv_own, kv_send, q_send = pack(
-        prompt_kv, resp_kv, prompt_q, resp_q, prompt_grad, resp_grad
-    )
+    kv_own, kv_send = pack_kv(prompt_kv, resp_kv)
     kv_recv = swap_core(kv_send)
+    q_send = pack_q(prompt_q, resp_q, prompt_grad, resp_grad, kv_send)
     q_recv = swap_core(q_send)
-    block = join_cores(logratio, kv_own, kv_recv, q_recv)
+    block = join_cores(logratio, kv_own, kv_recv, q_send)
 
     from_x = [shift_x(block, 4 - offset) for offset in offsets[1:3]]
     from_z = [shift_z(block, p) for p in (1, 2, 3)]
@@ -702,8 +737,8 @@
     kv_lists = [early_kvs, side_kvs, far_kvs]
 
     early = forward(early_kvs, q_aug, part_own, early_part)
-    far_ones = forward(far_kvs, q_aug, early[0], far_part)
-    side = forward(side_kvs, q_aug, far_ones[0], side_part)
+    far_ones = forward(far_kvs, q_aug, early[1], far_part)
+    side = forward(side_kvs, q_aug, far_ones[1], side_part)
     raised, packs = zip(early, side, far_ones)
     own_notes = collect(note, kv_lists, far_ones[0])
     out, cot_aug, gains = combine(

time: 63.3 us -> 64 us (1.011)
  starting transfers between devices: 27 us -> 29 us
  Pallas kernels: 22.2 us -> 21.1 us
    ppermute x7, starting transfers between devices: 6.42 us -> 8.18 us  [shift_z(): return lax.ppermute(value, 'resp', pairs)]
    pallas_call x4 -> x5, Pallas kernels: 8.36 us -> 7.28 us  [the longest x3 5.3 us: forward(): call(functools.partial(forward_kernel, part, has_top), 'forward', [VMEM]...]
    ppermute x5, waiting for transfers between devices: 0.89 us -> 0.01 us  [swap_core(): return lax.ppermute(value, 'resp', [(r, r ^ 1) for r in range(32)])]
    ppermute x11, waiting for transfers between devices: 6.27 us -> 7.05 us  [shift_x(): return lax.ppermute(value, 'resp', pairs)]
  transfers between devices with their start and end apart: 23 -> 23, of which waited for: 7 -> 5; matrix products, arithmetic and copies ran while one was open for 0% -> 0% of each run, Pallas kernels for 28% -> 26%
where the time goes in v6:
time: 64 us; the launch traced here: 63.8 us
  starting transfers between devices  29 us (45%)
  Pallas kernels  21.1 us (33%)
  waiting for transfers between devices  10.3 us (16%)
  between operations  3.47 us (5%)
    ppermute x11, starting transfers between devices, shift_x(): return lax.ppermute(value, 'resp', pairs)  11.8 us
    ppermute x5, starting transfers between devices, swap_core(): return lax.ppermute(value, 'resp', [(r, r ^ 1) for r in range(32)])  9.04 us
    ppermute x7, starting transfers between devices, shift_z(): return lax.ppermute(value, 'resp', pairs)  8.18 us
    ppermute x11, waiting for transfers between devices, shift_x(): return lax.ppermute(value, 'resp', pairs)  7.05 us
    pallas_call x3, Pallas kernels, backward(): call(functools.partial(backward_kernel, part, splits, chunk), 'backward',...  7 us
    pallas_call x3, Pallas kernels, forward(): call(functools.partial(forward_kernel, part, has_top), 'forward', [VMEM]...  5.3 us
    ppermute x7, waiting for transfers between devices, shift_z(): return lax.ppermute(value, 'resp', pairs)  3.22 us
    pallas_call x1, Pallas kernels, finish(): call(finish_kernel, 'finish', [VMEM] * (len(flat) + len(slopes) + 7) + [A...  1.98 us
  transfers between devices with their start and end apart: 23, of which 5 were waited for; matrix products, arithmetic and copies ran while one was open for 0% of the time, Pallas kernels for 26%

profile of v6, /device:TPU:1, one launch (start us, length us, event | category | flops | bytes accessed | tf_op | source)
XLA Modules:
  0.0 63.8 jit_solution(14622190713634997696)
XLA Ops:
  0.6 0.9 %pack_kv.1 = (bf16[128,256]{1,0:T(8,128)(2,1)S(1)}, bf16[128,256]{1,0:T(8,128)(2,1)S(1)}) custom-call(bf16[64,512]{1,0:T(8,128)(2,1)} %prompt_kv.1, bf16[1,64,512]{2,1,0:T(8,128)(2,1)} %resp_kv.1), custom_call_target="tpu_custom_call" | custom-call | bytes 1048576 | tf_op jit(solution)/shard_map/pack_kv/pallas_call | solution.py:143
  1.5 3.3 %collective-permute-start = (bf16[128,256]{1,0:T(8,128)(2,1)S(1)}, bf16[128,256]{1,0:T(8,128)(2,1)S(1)}, u32[]{:S(2)}, u32[]{:S(2)}) collective-permute-start(bf16[128,256]{1,0:T(8,128)(2,1)S(1)} %get-tuple-element.46.after), channel_id=1, source_target_pairs={{0,4},{4,0},{8,12},{12,8},{16,20},{20,16},{24,28},{28,24},{32,36},... | collective-permute-start | bytes 196616 | tf_op jit(solution)/shard_map/ppermute | solution.py:76
  4.8 1.1 %pack_q.1.after = bf16[4,64,1024]{2,1,0:T(8,128)(2,1)S(1)} custom-call(bf16[64,2048]{1,0:T(8,128)(2,1)} %pq.3, bf16[1,64,2048]{2,1,0:T(8,128)(2,1)} %rq.3, bf16[64,2048]{1,0:T(8,128)(2,1)} %pg.3, bf16[1,64,2048]{2,1,0:T(8,128)(2,1)} %rg.3, bf16[128,256]{1,0:T(8,128)(2,1)S(1)} %get-tuple-element.46.after), custom_call_target="tpu_custom_call" | custom-call | bytes 1048576 | tf_op jit(solution)/shard_map/pack_q/pallas_call | solution.py:157
  6.0 0.1 collective-permute-start.6
  6.8 0.8 %collective-permute-start.5 = (bf16[144,256]{1,0:T(8,128)(2,1)S(1)}, bf16[144,256]{1,0:T(8,128)(2,1)S(1)}, u32[]{:S(2)}, u32[]{:S(2)}) collective-permute-start(bf16[144,256]{1,0:T(8,128)(2,1)S(1)} %join_cores.1.refs_0_.refs_1_), channel_id=1, source_target_pairs={{0,24},{4,28},{8,0},{12,4},{16,8},{20,12},{24,16},{28,20},{32,56},... | collective-permute-start | bytes 221192 | tf_op jit(solution)/shard_map/ppermute | solution.py:86
  7.6 0.7 %collective-permute-start.4 = (bf16[144,256]{1,0:T(8,128)(2,1)S(1)}, bf16[144,256]{1,0:T(8,128)(2,1)S(1)}, u32[]{:S(2)}, u32[]{:S(2)}) collective-permute-start(bf16[144,256]{1,0:T(8,128)(2,1)S(1)} %join_cores.1.refs_0_.refs_1_), channel_id=1, source_target_pairs={{0,8},{4,12},{8,16},{12,20},{16,24},{20,28},{24,0},{28,4},{32,40},... | collective-permute-start | bytes 221192 | tf_op jit(solution)/shard_map/ppermute | solution.py:86
  8.3 3.6 %collective-permute-start.3 = (bf16[144,256]{1,0:T(8,128)(2,1)S(1)}, bf16[144,256]{1,0:T(8,128)(2,1)S(1)}, u32[]{:S(2)}, u32[]{:S(2)}) collective-permute-start(bf16[144,256]{1,0:T(8,128)(2,1)S(1)} %join_cores.1.refs_0_.refs_1_), channel_id=1, source_target_pairs={{0,96},{4,100},{8,104},{12,108},{16,112},{20,116},{24,120},{28,124... | collective-permute-start | bytes 221192 | tf_op jit(solution)/shard_map/ppermute | solution.py:81
  11.9 0.0 collective-permute-start.2
  11.9 0.0 collective-permute-done.6.recv
  11.9 0.3 collective-permute-start.1
  14.2 1.9 %prep.1 = (bf16[256,2048]{1,0:T(8,128)(2,1)S(1)}, bf16[128,2048]{1,0:T(8,128)(2,1)S(1)}, bf16[64,1024]{1,0:T(8,128)(2,1)S(1)}, f32[144,2048]{1,0:T(8,128)S(1)}) custom-call(bf16[64,2048]{1,0:T(8,128)(2,1)} %pq.3, bf16[1,64,2048]{2,1,0:T(8,128)(2,1)} %rq.3, bf16[64,2048]{1,0:T(8,128)(2,1)} %pg.3, bf16[1,64,2048]{2,1,0:T(8,128)(2,1)} %rg.3, ...), custom_call_target="tpu_custom_call" | custom-call | bytes 1048576 | tf_op jit(solution)/shard_map/prep/pallas_call | solution.py:276
  16.1 0.0 collective-permute-done.5.refs_1_
  16.2 0.0 collective-permute-done.3.refs_5_.refs_1_.refs_3_.refs_4_
  16.2 3.2 %collective-permute-done.2.refs_4_.refs_0_.refs_2_.refs_3_ = bf16[144,256]{1,0:T(8,128)(2,1)S(1)} collective-permute-done((bf16[144,256]{1,0:T(8,128)(2,1)S(1)}, bf16[144,256]{1,0:T(8,128)(2,1)S(1)}, u32[]{:S(2)}, u32[]{:S(2)}) %collective-permute-start.2) | collective-permute-done | bytes 73760 | tf_op jit(solution)/shard_map/ppermute | solution.py:81
  19.4 1.7 %collective-permute-start.10 = (bf16[576,256]{1,0:T(8,128)(2,1)S(1)}, bf16[576,256]{1,0:T(8,128)(2,1)S(1)}, u32[]{:S(2)}, u32[]{:S(2)}) collective-permute-start(bf16[576,256]{1,0:T(8,128)(2,1)S(1)} %join.5), channel_id=1, source_target_pairs={{0,16},{4,20},{8,24},{12,28},{16,0},{20,4},{24,8},{28,12},{32,48},... | collective-permute-start | bytes 884744 | tf_op jit(solution)/shard_map/ppermute | solution.py:86
  21.2 1.0 %collective-permute-start.9 = (bf16[288,256]{1,0:T(8,128)(2,1)S(1)}, bf16[288,256]{1,0:T(8,128)(2,1)S(1)}, u32[]{:S(2)}, u32[]{:S(2)}) collective-permute-start(bf16[288,256]{1,0:T(8,128)(2,1)S(1)} %join.4), channel_id=1, source_target_pairs={{0,24},{4,28},{8,0},{12,4},{16,8},{20,12},{24,16},{28,20},{32,56},... | collective-permute-start | bytes 442376 | tf_op jit(solution)/shard_map/ppermute | solution.py:86
  22.2 0.6 %collective-permute-start.8 = (bf16[288,256]{1,0:T(8,128)(2,1)S(1)}, bf16[288,256]{1,0:T(8,128)(2,1)S(1)}, u32[]{:S(2)}, u32[]{:S(2)}) collective-permute-start(bf16[288,256]{1,0:T(8,128)(2,1)S(1)} %join.4), channel_id=1, source_target_pairs={{0,8},{4,12},{8,16},{12,20},{16,24},{20,28},{24,0},{28,4},{32,40},... | collective-permute-start | bytes 442376 | tf_op jit(solution)/shard_map/ppermute | solution.py:86
  22.9 2.3 %forward.3 = (bf16[768,2048]{1,0:T(8,128)(2,1)S(1)}, f32[144,2048]{1,0:T(8,128)S(1)}) custom-call(bf16[144,256]{1,0:T(8,128)(2,1)S(1)} %join_cores.1.refs_0_.refs_1_, bf16[144,256]{1,0:T(8,128)(2,1)S(1)} %collective-permute-done.1.refs_3_.refs_1_.refs_2_, bf16[144,256]{1,0:T(8,128)(2,1)S(1)} %collective-permute-done.2.refs_4_.refs_0_.refs_2_.refs_3_, ...), custom_call_target="tpu_custom_call" | custom-call | flops 805306368 | bytes 1048576 | tf_op jit(solution)/shard_map/forward/pallas_call | solution.py:380
  25.2 3.9 %collective-permute-done.10.refs_0_.refs_9_.refs_8_ = bf16[576,256]{1,0:T(8,128)(2,1)S(1)} collective-permute-done((bf16[576,256]{1,0:T(8,128)(2,1)S(1)}, bf16[576,256]{1,0:T(8,128)(2,1)S(1)}, u32[]{:S(2)}, u32[]{:S(2)}) %collective-permute-start.10) | collective-permute-done | bytes 294944 | tf_op jit(solution)/shard_map/ppermute | solution.py:86
  29.1 1.4 %forward.4 = (bf16[512,2048]{1,0:T(8,128)(2,1)S(1)}, f32[144,2048]{1,0:T(8,128)S(1)}) custom-call(bf16[576,256]{1,0:T(8,128)(2,1)S(1)} %collective-permute-done.10.refs_0_.refs_9_.refs_8_, bf16[256,2048]{1,0:T(8,128)(2,1)S(1)} %get-tuple-element.48.refs_5_.refs_1_.refs_3_.refs_2_.refs_4_.refs_6_.refs_15_, f32[144,2048]{1,0:T(8,128)S(1)} %get-tuple-element.50.refs_2_.part_0), custom_call_target="tpu_custom_call" | custom-call | flops 536870912 | bytes 1048576 | tf_op jit(solution)/shard_map/forward/pallas_call | solution.py:380
  30.5 1.9 %collective-permute-done.9.refs_8_.refs_2_.refs_7_ = bf16[288,256]{1,0:T(8,128)(2,1)S(1)} collective-permute-done((bf16[288,256]{1,0:T(8,128)(2,1)S(1)}, bf16[288,256]{1,0:T(8,128)(2,1)S(1)}, u32[]{:S(2)}, u32[]{:S(2)}) %collective-permute-start.9) | collective-permute-done | bytes 147488 | tf_op jit(solution)/shard_map/ppermute | solution.py:86
  32.4 0.7 %collective-permute-done.8.refs_7_.refs_1_.refs_6_ = bf16[288,256]{1,0:T(8,128)(2,1)S(1)} collective-permute-done((bf16[288,256]{1,0:T(8,128)(2,1)S(1)}, bf16[288,256]{1,0:T(8,128)(2,1)S(1)}, u32[]{:S(2)}, u32[]{:S(2)}) %collective-permute-start.8) | collective-permute-done | bytes 147488 | tf_op jit(solution)/shard_map/ppermute | solution.py:86
  33.1 0.0 collective-permute-done.7.refs_6_.refs_0_.refs_5_
  33.1 0.8 %collective-permute-start.11 = (bf16[16,256]{1,0:T(8,128)(2,1)S(1)}, bf16[16,256]{1,0:T(8,128)(2,1)S(1)}, u32[]{:S(2)}, u32[]{:S(2)}) collective-permute-start(bf16[16,256]{1,0:T(8,128)(2,1)S(1)} %collect.1.own_notes), channel_id=1, source_target_pairs={{0,4},{4,0},{8,12},{12,8},{16,20},{20,16},{24,28},{28,24},{32,36},... | collective-permute-start | bytes 24584 | tf_op jit(solution)/shard_map/ppermute | solution.py:76
  34.0 1.6 %forward.5 = (bf16[768,2048]{1,0:T(8,128)(2,1)S(1)}, f32[144,2048]{1,0:T(8,128)S(1)}) custom-call(bf16[288,256]{1,0:T(8,128)(2,1)S(1)} %collective-permute-done.7.refs_6_.refs_0_.refs_5_, bf16[288,256]{1,0:T(8,128)(2,1)S(1)} %collective-permute-done.8.refs_7_.refs_1_.refs_6_, bf16[288,256]{1,0:T(8,128)(2,1)S(1)} %collective-permute-done.9.refs_8_.refs_2_.refs_7_, ...), custom_call_target="tpu_custom_call" | custom-call | flops 805306368 | bytes 1048576 | tf_op jit(solution)/shard_map/forward/pallas_call | solution.py:380
  35.6 0.9 %combine.1 = (bf16[128,2048]{1,0:T(8,128)(2,1)S(1)}, bf16[256,2048]{1,0:T(8,128)(2,1)S(1)}, f32[8,2048]{1,0:T(8,128)S(1)}) custom-call(bf16[16,256]{1,0:T(8,128)(2,1)S(1)} %collect.1.own_notes, bf16[16,256]{1,0:T(8,128)(2,1)S(1)} %collective-permute-done.11.sib_notes, bf16[128,2048]{1,0:T(8,128)(2,1)S(1)} %get-tuple-element.52.grads, ...), custom_call_target="tpu_custom_call" | custom-call | bytes 1048576 | tf_op jit(solution)/shard_map/combine/pallas_call | solution.py:485
  36.5 1.8 %backward.3 = (bf16[512,2048]{1,0:T(8,128)(2,1)S(1)}, bf16[384,256]{1,0:T(8,128)(2,1)S(1)}, bf16[128,256]{1,0:T(8,128)(2,1)S(1)}) custom-call(bf16[576,256]{1,0:T(8,128)(2,1)S(1)} %collective-permute-done.10.refs_0_.refs_9_.refs_8_, bf16[512,2048]{1,0:T(8,128)(2,1)S(1)} %get-tuple-element.51.refs_10_.refs_1_, ...), custom_call_target="tpu_custom_call" | custom-call | flops 805306368 | bytes 1048576 | tf_op jit(solution)/shard_map/backward/pallas_call | solution.py:529
  38.3 2.4 %collective-permute-start.13 = (bf16[384,256]{1,0:T(8,128)(2,1)S(1)}, bf16[384,256]{1,0:T(8,128)(2,1)S(1)}, u32[]{:S(2)}, u32[]{:S(2)}) collective-permute-start(bf16[384,256]{1,0:T(8,128)(2,1)S(1)} %get-tuple-element.58.refs_7_), channel_id=1, source_target_pairs={{0,16},{4,20},{8,24},{12,28},{16,0},{20,4},{24,8},{28,12},{32,48},... | collective-permute-start | bytes 589832 | tf_op jit(solution)/shard_map/ppermute | solution.py:86
  40.8 2.6 %backward.4 = (bf16[768,2048]{1,0:T(8,128)(2,1)S(1)}, bf16[384,256]{1,0:T(8,128)(2,1)S(1)}, bf16[384,256]{1,0:T(8,128)(2,1)S(1)}) custom-call(bf16[288,256]{1,0:T(8,128)(2,1)S(1)} %collective-permute-done.7.refs_6_.refs_0_.refs_5_, bf16[288,256]{1,0:T(8,128)(2,1)S(1)} %collective-permute-done.8.refs_7_.refs_1_.refs_6_, ...), custom_call_target="tpu_custom_call" | custom-call | flops 1207959552 | bytes 1048576 | tf_op jit(solution)/shard_map/backward/pallas_call | solution.py:529
  43.4 0.5 collective-permute-start.15
  43.9 2.3 %collective-permute-start.14 = (bf16[384,256]{1,0:T(8,128)(2,1)S(1)}, bf16[384,256]{1,0:T(8,128)(2,1)S(1)}, u32[]{:S(2)}, u32[]{:S(2)}) collective-permute-start(bf16[384,256]{1,0:T(8,128)(2,1)S(1)} %get-tuple-element.59.refs_9_), channel_id=1, source_target_pairs={{0,24},{4,28},{8,0},{12,4},{16,8},{20,12},{24,16},{28,20},{32,56},... | collective-permute-start | bytes 589832 | tf_op jit(solution)/shard_map/ppermute | solution.py:86
  46.1 2.6 %backward.5 = (bf16[768,2048]{1,0:T(8,128)(2,1)S(1)}, f32[128,256]{1,0:T(8,128)S(1)}, f32[384,256]{1,0:T(8,128)S(1)}, bf16[128,256]{1,0:T(8,128)(2,1)S(1)}, bf16[128,256]{1,0:T(8,128)(2,1)S(1)}) custom-call(bf16[144,256]{1,0:T(8,128)(2,1)S(1)} %join_cores.1.refs_0_.refs_1_, bf16[144,256]{1,0:T(8,128)(2,1)S(1)} %collective-permute-done.1.refs_3_.refs_1_.refs_2_, ...), custom_call_target="tpu_custom_call" | custom-call | flops 1207959552 | bytes 1048576 | tf_op jit(solution)/shard_map/backward/pallas_call | solution.py:529
  48.7 0.1 collective-permute-start.19
  48.8 1.5 %collective-permute-start.20 = (bf16[128,256]{1,0:T(8,128)(2,1)S(1)}, bf16[128,256]{1,0:T(8,128)(2,1)S(1)}, u32[]{:S(2)}, u32[]{:S(2)}) collective-permute-start(bf16[128,256]{1,0:T(8,128)(2,1)S(1)} %get-tuple-element.79), channel_id=1, source_target_pairs={{0,8},{4,12},{8,16},{12,20},{16,24},{20,28},{24,0},{28,4},{32,40},... | collective-permute-start | bytes 196616 | tf_op jit(solution)/shard_map/ppermute | solution.py:86
  50.3 0.0 collective-permute-done.13.after.back_far
  50.3 0.1 collective-permute-start.21
  50.4 0.5 collective-permute-done.15.back_2
  50.9 0.0 collective-permute-done.14.back_1
  50.9 0.1 sum_column.1
  51.0 1.7 %collective-permute-start.16 = (bf16[128,256]{1,0:T(8,128)(2,1)S(1)}, bf16[128,256]{1,0:T(8,128)(2,1)S(1)}, u32[]{:S(2)}, u32[]{:S(2)}) collective-permute-start(bf16[128,256]{1,0:T(8,128)(2,1)S(1)} %get-tuple-element.75), channel_id=1, source_target_pairs={{0,96},{4,100},{8,104},{12,108},{16,112},{20,116},{24,120},{28,124... | collective-permute-start | bytes 196616 | tf_op jit(solution)/shard_map/ppermute | solution.py:81
  52.6 1.2 %collective-permute-start.17 = (bf16[128,256]{1,0:T(8,128)(2,1)S(1)}, bf16[128,256]{1,0:T(8,128)(2,1)S(1)}, u32[]{:S(2)}, u32[]{:S(2)}) collective-permute-start(bf16[128,256]{1,0:T(8,128)(2,1)S(1)} %get-tuple-element.76), channel_id=1, source_target_pairs={{0,64},{4,68},{8,72},{12,76},{16,80},{20,84},{24,88},{28,92},{32,9... | collective-permute-start | bytes 196616 | tf_op jit(solution)/shard_map/ppermute | solution.py:81
  53.9 1.4 %collective-permute-start.18 = (bf16[128,256]{1,0:T(8,128)(2,1)S(1)}, bf16[128,256]{1,0:T(8,128)(2,1)S(1)}, u32[]{:S(2)}, u32[]{:S(2)}) collective-permute-start(bf16[128,256]{1,0:T(8,128)(2,1)S(1)} %get-tuple-element.77), channel_id=1, source_target_pairs={{0,32},{4,36},{8,40},{12,44},{16,48},{20,52},{24,56},{28,60},{32,6... | collective-permute-start | bytes 196616 | tf_op jit(solution)/shard_map/ppermute | solution.py:81
  55.2 2.0 %finish.1 = (bf16[64,4352]{1,0:T(8,128)(2,1)S(1)}, bf16[64,4352]{1,0:T(8,128)(2,1)S(1)}) custom-call(bf16[144,256]{1,0:T(8,128)(2,1)S(1)} %join_cores.1.refs_0_.refs_1_, bf16[144,256]{1,0:T(8,128)(2,1)S(1)} %collective-permute-done.1.refs_3_.refs_1_.refs_2_, bf16[144,256]{1,0:T(8,128)(2,1)S(1)} %collective-permute-done.2.refs_4_.refs_0_.refs_2_.refs_3_, ...), custom_call_target="tpu_custom_call" | custom-call | flops 805306368 | bytes 1048576 | tf_op jit(solution)/shard_map/finish/pallas_call | solution.py:593
  57.2 2.6 %collective-permute-start.12 = (bf16[64,4352]{1,0:T(8,128)(2,1)S(1)}, bf16[64,4352]{1,0:T(8,128)(2,1)S(1)}, u32[]{:S(2)}, u32[]{:S(2)}) collective-permute-start(bf16[64,4352]{1,0:T(8,128)(2,1)S(1)} %get-tuple-element.67), channel_id=1, source_target_pairs={{0,4},{4,0},{8,12},{12,8},{16,20},{20,16},{24,28},{28,24},{32,36},... | collective-permute-start | bytes 1671176 | tf_op jit(solution)/shard_map/ppermute | solution.py:76
  59.9 0.1 add_split.1
  60.0 2.1 %collective-permute-start.22 = (bf16[64,256]{1,0:T(8,128)(2,1)S(1)}, bf16[64,256]{1,0:T(8,128)(2,1)S(1)}, u32[]{:S(2)}, u32[]{:S(2)}) collective-permute-start(bf16[64,256]{1,0:T(8,128)(2,1)S(1)} %get-tuple-element.81), channel_id=1, source_target_pairs={{0,4},{4,0},{8,12},{12,8},{16,20},{20,16},{24,28},{28,24},{32,36},... | collective-permute-start | bytes 98312 | tf_op jit(solution)/shard_map/ppermute | solution.py:76
  62.1 1.1 %place.1 = (bf16[64,2048]{1,0:T(8,128)(2,1)}, bf16[1,64,2048]{2,1,0:T(8,128)(2,1)}, bf16[64,2048]{1,0:T(8,128)(2,1)}, bf16[1,64,2048]{2,1,0:T(8,128)(2,1)}, bf16...) custom-call(bf16[64,4352]{1,0:T(8,128)(2,1)S(1)} %get-tuple-element.66.own, bf16[64,4352]{1,0:T(8,128)(2,1)S(1)} %collective-permute-done.12.recv), custom_call_target="tpu_custom_call" | custom-call | bytes 1048576 | tf_op jit(solution)/shard_map/place/pallas_call | solution.py:628
  63.2 0.7 %last.1 = bf16[64,512]{1,0:T(8,128)(2,1)} custom-call(bf16[64,256]{1,0:T(8,128)(2,1)S(1)} %get-tuple-element.80.kept, bf16[64,256]{1,0:T(8,128)(2,1)S(1)} %collective-permute-done.22.recv, f32[8,128]{1,0:T(8,128)S(1)} %get-tuple-element.82.after), custom_call_target="tpu_custom_call" | custom-call | bytes 1048576 | tf_op jit(solution)/shard_map/last/pallas_call | solution.py:698
  (20 shorter events, 0.1 us)
Async XLA Ops:
  1.5 5.2 %collective-permute-start = (bf16[128,256]{1,0:T(8,128)(2,1)S(1)}, bf16[128,256]{1,0:T(8,128)(2,1)S(1)}, u32[]{:S(2)}, u32[]{:S(2)}) collective-permute-start(bf16[128,256]{1,0:T(8,128)(2,1)S(1)} %get-tuple-element.46.after), channel_id=1, source_target_pairs={{0,4},{4,0},{8,12},{12,8},{16,20},{20,16},{24,28},{28,24},{32,36},... | collective-permute-start | bytes 196616 | tf_op jit(solution)/shard_map/ppermute | solution.py:76
  6.0 6.0 %collective-permute-start.6 = (bf16[4,64,1024]{2,1,0:T(8,128)(2,1)S(1)}, bf16[4,64,1024]{2,1,0:T(8,128)(2,1)S(1)}, u32[]{:S(2)}, u32[]{:S(2)}) collective-permute-start(bf16[4,64,1024]{2,1,0:T(8,128)(2,1)S(1)} %pack_q.1.after), channel_id=1, source_target_pairs={{0,4},{4,0},{8,12},{12,8},{16,20},{20,16},{24,28},{28,24},{32,36},... | collective-permute-start | bytes 1572872 | tf_op jit(solution)/shard_map/ppermute | solution.py:76
  6.8 9.4 %collective-permute-start.5 = (bf16[144,256]{1,0:T(8,128)(2,1)S(1)}, bf16[144,256]{1,0:T(8,128)(2,1)S(1)}, u32[]{:S(2)}, u32[]{:S(2)}) collective-permute-start(bf16[144,256]{1,0:T(8,128)(2,1)S(1)} %join_cores.1.refs_0_.refs_1_), channel_id=1, source_target_pairs={{0,24},{4,28},{8,0},{12,4},{16,8},{20,12},{24,16},{28,20},{32,56},... | collective-permute-start | bytes 221192 | tf_op jit(solution)/shard_map/ppermute | solution.py:86
  7.6 8.6 %collective-permute-start.4 = (bf16[144,256]{1,0:T(8,128)(2,1)S(1)}, bf16[144,256]{1,0:T(8,128)(2,1)S(1)}, u32[]{:S(2)}, u32[]{:S(2)}) collective-permute-start(bf16[144,256]{1,0:T(8,128)(2,1)S(1)} %join_cores.1.refs_0_.refs_1_), channel_id=1, source_target_pairs={{0,8},{4,12},{8,16},{12,20},{16,24},{20,28},{24,0},{28,4},{32,40},... | collective-permute-start | bytes 221192 | tf_op jit(solution)/shard_map/ppermute | solution.py:86
  8.3 7.8 %collective-permute-start.3 = (bf16[144,256]{1,0:T(8,128)(2,1)S(1)}, bf16[144,256]{1,0:T(8,128)(2,1)S(1)}, u32[]{:S(2)}, u32[]{:S(2)}) collective-permute-start(bf16[144,256]{1,0:T(8,128)(2,1)S(1)} %join_cores.1.refs_0_.refs_1_), channel_id=1, source_target_pairs={{0,96},{4,100},{8,104},{12,108},{16,112},{20,116},{24,120},{28,124... | collective-permute-start | bytes 221192 | tf_op jit(solution)/shard_map/ppermute | solution.py:81
  11.9 7.4 %collective-permute-start.2 = (bf16[144,256]{1,0:T(8,128)(2,1)S(1)}, bf16[144,256]{1,0:T(8,128)(2,1)S(1)}, u32[]{:S(2)}, u32[]{:S(2)}) collective-permute-start(bf16[144,256]{1,0:T(8,128)(2,1)S(1)} %join_cores.1.refs_0_.refs_1_), channel_id=1, source_target_pairs={{0,64},{4,68},{8,72},{12,76},{16,80},{20,84},{24,88},{28,92},{32,9... | collective-permute-start | bytes 221192 | tf_op jit(solution)/shard_map/ppermute | solution.py:81
  11.9 7.4 %collective-permute-start.1 = (bf16[144,256]{1,0:T(8,128)(2,1)S(1)}, bf16[144,256]{1,0:T(8,128)(2,1)S(1)}, u32[]{:S(2)}, u32[]{:S(2)}) collective-permute-start(bf16[144,256]{1,0:T(8,128)(2,1)S(1)} %join_cores.1.refs_0_.refs_1_), channel_id=1, source_target_pairs={{0,32},{4,36},{8,40},{12,44},{16,48},{20,52},{24,56},{28,60},{32,6... | collective-permute-start | bytes 221192 | tf_op jit(solution)/shard_map/ppermute | solution.py:81
  19.4 9.7 %collective-permute-start.10 = (bf16[576,256]{1,0:T(8,128)(2,1)S(1)}, bf16[576,256]{1,0:T(8,128)(2,1)S(1)}, u32[]{:S(2)}, u32[]{:S(2)}) collective-permute-start(bf16[576,256]{1,0:T(8,128)(2,1)S(1)} %join.5), channel_id=1, source_target_pairs={{0,16},{4,20},{8,24},{12,28},{16,0},{20,4},{24,8},{28,12},{32,48},... | collective-permute-start | bytes 884744 | tf_op jit(solution)/shard_map/ppermute | solution.py:86
  21.2 11.3 %collective-permute-start.9 = (bf16[288,256]{1,0:T(8,128)(2,1)S(1)}, bf16[288,256]{1,0:T(8,128)(2,1)S(1)}, u32[]{:S(2)}, u32[]{:S(2)}) collective-permute-start(bf16[288,256]{1,0:T(8,128)(2,1)S(1)} %join.4), channel_id=1, source_target_pairs={{0,24},{4,28},{8,0},{12,4},{16,8},{20,12},{24,16},{28,20},{32,56},... | collective-permute-start | bytes 442376 | tf_op jit(solution)/shard_map/ppermute | solution.py:86
  22.2 10.9 %collective-permute-start.8 = (bf16[288,256]{1,0:T(8,128)(2,1)S(1)}, bf16[288,256]{1,0:T(8,128)(2,1)S(1)}, u32[]{:S(2)}, u32[]{:S(2)}) collective-permute-start(bf16[288,256]{1,0:T(8,128)(2,1)S(1)} %join.4), channel_id=1, source_target_pairs={{0,8},{4,12},{8,16},{12,20},{16,24},{20,28},{24,0},{28,4},{32,40},... | collective-permute-start | bytes 442376 | tf_op jit(solution)/shard_map/ppermute | solution.py:86
  22.9 10.2 %collective-permute-start.7 = (bf16[288,256]{1,0:T(8,128)(2,1)S(1)}, bf16[288,256]{1,0:T(8,128)(2,1)S(1)}, u32[]{:S(2)}, u32[]{:S(2)}) collective-permute-start(bf16[288,256]{1,0:T(8,128)(2,1)S(1)} %join.3.refs_4_.refs_5_), channel_id=1, source_target_pairs={{0,32},{4,36},{8,40},{12,44},{16,48},{20,52},{24,56},{28,60},{32,6... | collective-permute-start | bytes 442376 | tf_op jit(solution)/shard_map/ppermute | solution.py:81
  33.1 2.5 %collective-permute-start.11 = (bf16[16,256]{1,0:T(8,128)(2,1)S(1)}, bf16[16,256]{1,0:T(8,128)(2,1)S(1)}, u32[]{:S(2)}, u32[]{:S(2)}) collective-permute-start(bf16[16,256]{1,0:T(8,128)(2,1)S(1)} %collect.1.own_notes), channel_id=1, source_target_pairs={{0,4},{4,0},{8,12},{12,8},{16,20},{20,16},{24,28},{28,24},{32,36},... | collective-permute-start | bytes 24584 | tf_op jit(solution)/shard_map/ppermute | solution.py:76
  38.3 11.9 %collective-permute-start.13 = (bf16[384,256]{1,0:T(8,128)(2,1)S(1)}, bf16[384,256]{1,0:T(8,128)(2,1)S(1)}, u32[]{:S(2)}, u32[]{:S(2)}) collective-permute-start(bf16[384,256]{1,0:T(8,128)(2,1)S(1)} %get-tuple-element.58.refs_7_), channel_id=1, source_target_pairs={{0,16},{4,20},{8,24},{12,28},{16,0},{20,4},{24,8},{28,12},{32,48},... | collective-permute-start | bytes 589832 | tf_op jit(solution)/shard_map/ppermute | solution.py:86
  43.4 7.5 %collective-permute-start.15 = (bf16[384,256]{1,0:T(8,128)(2,1)S(1)}, bf16[384,256]{1,0:T(8,128)(2,1)S(1)}, u32[]{:S(2)}, u32[]{:S(2)}) collective-permute-start(bf16[384,256]{1,0:T(8,128)(2,1)S(1)} %get-tuple-element.73), channel_id=1, source_target_pairs={{0,8},{4,12},{8,16},{12,20},{16,24},{20,28},{24,0},{28,4},{32,40},... | collective-permute-start | bytes 589832 | tf_op jit(solution)/shard_map/ppermute | solution.py:86
  43.9 7.0 %collective-permute-start.14 = (bf16[384,256]{1,0:T(8,128)(2,1)S(1)}, bf16[384,256]{1,0:T(8,128)(2,1)S(1)}, u32[]{:S(2)}, u32[]{:S(2)}) collective-permute-start(bf16[384,256]{1,0:T(8,128)(2,1)S(1)} %get-tuple-element.59.refs_9_), channel_id=1, source_target_pairs={{0,24},{4,28},{8,0},{12,4},{16,8},{20,12},{24,16},{28,20},{32,56},... | collective-permute-start | bytes 589832 | tf_op jit(solution)/shard_map/ppermute | solution.py:86
  48.7 5.1 %collective-permute-start.19 = (bf16[128,256]{1,0:T(8,128)(2,1)S(1)}, bf16[128,256]{1,0:T(8,128)(2,1)S(1)}, u32[]{:S(2)}, u32[]{:S(2)}) collective-permute-start(bf16[128,256]{1,0:T(8,128)(2,1)S(1)} %get-tuple-element.78), channel_id=1, source_target_pairs={{0,24},{4,28},{8,0},{12,4},{16,8},{20,12},{24,16},{28,20},{32,56},... | collective-permute-start | bytes 196616 | tf_op jit(solution)/shard_map/ppermute | solution.py:86
  48.8 8.4 %collective-permute-start.20 = (bf16[128,256]{1,0:T(8,128)(2,1)S(1)}, bf16[128,256]{1,0:T(8,128)(2,1)S(1)}, u32[]{:S(2)}, u32[]{:S(2)}) collective-permute-start(bf16[128,256]{1,0:T(8,128)(2,1)S(1)} %get-tuple-element.79), channel_id=1, source_target_pairs={{0,8},{4,12},{8,16},{12,20},{16,24},{20,28},{24,0},{28,4},{32,40},... | collective-permute-start | bytes 196616 | tf_op jit(solution)/shard_map/ppermute | solution.py:86
  50.3 9.6 %collective-permute-start.21 = (bf16[128,256]{1,0:T(8,128)(2,1)S(1)}, bf16[128,256]{1,0:T(8,128)(2,1)S(1)}, u32[]{:S(2)}, u32[]{:S(2)}) collective-permute-start(bf16[128,256]{1,0:T(8,128)(2,1)S(1)} %gate.1.after), channel_id=1, source_target_pairs={{0,16},{4,20},{8,24},{12,28},{16,0},{20,4},{24,8},{28,12},{32,48},... | collective-permute-start | bytes 196616 | tf_op jit(solution)/shard_map/ppermute | solution.py:86
  51.0 8.9 %collective-permute-start.16 = (bf16[128,256]{1,0:T(8,128)(2,1)S(1)}, bf16[128,256]{1,0:T(8,128)(2,1)S(1)}, u32[]{:S(2)}, u32[]{:S(2)}) collective-permute-start(bf16[128,256]{1,0:T(8,128)(2,1)S(1)} %get-tuple-element.75), channel_id=1, source_target_pairs={{0,96},{4,100},{8,104},{12,108},{16,112},{20,116},{24,120},{28,124... | collective-permute-start | bytes 196616 | tf_op jit(solution)/shard_map/ppermute | solution.py:81
  52.6 7.2 %collective-permute-start.17 = (bf16[128,256]{1,0:T(8,128)(2,1)S(1)}, bf16[128,256]{1,0:T(8,128)(2,1)S(1)}, u32[]{:S(2)}, u32[]{:S(2)}) collective-permute-start(bf16[128,256]{1,0:T(8,128)(2,1)S(1)} %get-tuple-element.76), channel_id=1, source_target_pairs={{0,64},{4,68},{8,72},{12,76},{16,80},{20,84},{24,88},{28,92},{32,9... | collective-permute-start | bytes 196616 | tf_op jit(solution)/shard_map/ppermute | solution.py:81
  53.9 6.0 %collective-permute-start.18 = (bf16[128,256]{1,0:T(8,128)(2,1)S(1)}, bf16[128,256]{1,0:T(8,128)(2,1)S(1)}, u32[]{:S(2)}, u32[]{:S(2)}) collective-permute-start(bf16[128,256]{1,0:T(8,128)(2,1)S(1)} %get-tuple-element.77), channel_id=1, source_target_pairs={{0,32},{4,36},{8,40},{12,44},{16,48},{20,52},{24,56},{28,60},{32,6... | collective-permute-start | bytes 196616 | tf_op jit(solution)/shard_map/ppermute | solution.py:81
  57.2 4.9 %collective-permute-start.12 = (bf16[64,4352]{1,0:T(8,128)(2,1)S(1)}, bf16[64,4352]{1,0:T(8,128)(2,1)S(1)}, u32[]{:S(2)}, u32[]{:S(2)}) collective-permute-start(bf16[64,4352]{1,0:T(8,128)(2,1)S(1)} %get-tuple-element.67), channel_id=1, source_target_pairs={{0,4},{4,0},{8,12},{12,8},{16,20},{20,16},{24,28},{28,24},{32,36},... | collective-permute-start | bytes 1671176 | tf_op jit(solution)/shard_map/ppermute | solution.py:76
  60.0 3.2 %collective-permute-start.22 = (bf16[64,256]{1,0:T(8,128)(2,1)S(1)}, bf16[64,256]{1,0:T(8,128)(2,1)S(1)}, u32[]{:S(2)}, u32[]{:S(2)}) collective-permute-start(bf16[64,256]{1,0:T(8,128)(2,1)S(1)} %get-tuple-element.81), channel_id=1, source_target_pairs={{0,4},{4,0},{8,12},{12,8},{16,20},{20,16},{24,28},{28,24},{32,36},... | collective-permute-start | bytes 98312 | tf_op jit(solution)/shard_map/ppermute | solution.py:76

commit v7 on v6

--- a/solution.py
+++ b/solution.py
@@ -499,19 +499,17 @@
     kvs = refs[: len(part)]
     raised, q_aug, cot_aug, gains, after, slopes = refs[len(part) : len(part) + 6]
     grads = refs[len(part) + 6 : len(part) + 6 + len(splits)]
-    value_aug, moved, scaled_q, scaled_cot = refs[len(part) + 6 + len(splits) :]
+    value_aug, scaled_q, scaled_cot = refs[len(part) + 6 + len(splits) :]
     value_aug[...] = value_aug_of(part_rows(kvs, part, value_cols))
-    moved[0] = dot(value_aug[...], cot_aug[:, lanes_of(0)])
     for j in range(SUBS):
         lanes = lanes_of(j)
-        if j + 1 < SUBS:
-            moved[(j + 1) % 2] = dot(value_aug[...], cot_aug[:, lanes_of(j + 1)])
         gain = gains[chunk : chunk + 1, lanes]
         scaled_cot[:, lanes] = (cot_aug[:HEAD_DIM, lanes].astype(f32) * gain).astype(bf16)
         scaled_q[:, lanes] = (
             q_aug[:HEAD_DIM, lanes].astype(f32) * (gain * score_scale)
         ).astype(bf16)
-        slopes[:, lanes] = (raised[:, lanes].astype(f32) * moved[j % 2]).astype(bf16)
+        moved = dot(value_aug[...], cot_aug[:, lanes])
+        slopes[:, lanes] = (raised[:, lanes].astype(f32) * moved).astype(bf16)
     for columns_here, left, right in (
         (value_cols, raised, scaled_cot),
         (key_cols, slopes, scaled_q),
@@ -534,7 +532,6 @@
         + [shape(len(numbers) * BLOCK, KV_COLS, dtype=kind) for numbers, kind in splits],
         [
             pltpu.VMEM((keys, 2 * HEAD_DIM), bf16),
-            pltpu.VMEM((2, keys, TILE), f32),
             pltpu.VMEM((HEAD_DIM, LANES), bf16),
             pltpu.VMEM((HEAD_DIM, LANES), bf16),
         ],
@@ -722,7 +719,8 @@
     q_recv = swap_core(q_send)
     block = join_cores(logratio, kv_own, kv_recv, q_send)
 
-    from_x = [shift_x(block, 4 - offset) for offset in offsets[1:3]]
+    block_again = gate(block, q_recv)
+    from_x = [shift_x(block_again, 4 - offset) for offset in offsets[1:3]]
     from_z = [shift_z(block, p) for p in (1, 2, 3)]
     q_aug, grads, raised_own, part_own = prep(
         prompt_q, resp_q, prompt_grad, resp_grad, q_recv, kv_own, kv_recv

time: 64 us -> 63.8 us (level)
  waiting for transfers between devices: 10.3 us -> 5.93 us
  starting transfers between devices: 29 us -> 32.9 us
    ppermute x11, starting transfers between devices: 11.8 us -> 14.8 us  [shift_x(): return lax.ppermute(value, 'resp', pairs)]
    ppermute x11, waiting for transfers between devices: 7.05 us -> 4.62 us  [shift_x(): return lax.ppermute(value, 'resp', pairs)]
    ppermute x7, waiting for transfers between devices: 3.22 us -> 1.3 us  [shift_z(): return lax.ppermute(value, 'resp', pairs)]
    ppermute x5, starting transfers between devices: 9.04 us -> 9.84 us  [swap_core(): return lax.ppermute(value, 'resp', [(r, r ^ 1) for r in range(32)])]
  transfers between devices with their start and end apart: 23 -> 23, of which waited for: 5 -> 6; matrix products, arithmetic and copies ran while one was open for 0% -> 0% of each run, Pallas kernels for 26% -> 26%
where the time goes in v7:
time: 63.8 us; the launch traced here: 63.4 us
  starting transfers between devices  32.9 us (52%)
  Pallas kernels  21 us (33%)
  waiting for transfers between devices  5.93 us (9%)
  between operations  3.45 us (5%)
    ppermute x11, starting transfers between devices, shift_x(): return lax.ppermute(value, 'resp', pairs)  14.8 us
    ppermute x5, starting transfers between devices, swap_core(): return lax.ppermute(value, 'resp', [(r, r ^ 1) for r in range(32)])  9.84 us
    ppermute x7, starting transfers between devices, shift_z(): return lax.ppermute(value, 'resp', pairs)  8.29 us
    pallas_call x3, Pallas kernels, backward(): call(functools.partial(backward_kernel, part, splits, chunk), 'backward',...  7 us
    pallas_call x3, Pallas kernels, forward(): call(functools.partial(forward_kernel, part, has_top), 'forward', [VMEM]...  5.28 us
    ppermute x11, waiting for transfers between devices, shift_x(): return lax.ppermute(value, 'resp', pairs)  4.62 us
    pallas_call x1, Pallas kernels, finish(): call(finish_kernel, 'finish', [VMEM] * (len(flat) + len(slopes) + 7) + [A...  1.98 us
    pallas_call x1, Pallas kernels, prep(): call(prep_kernel, 'prep', [HBM] * 4 + [VMEM] * 3, [shape(2 * HEAD_DIM, LA...  1.93 us
  transfers between devices with their start and end apart: 23, of which 6 were waited for; matrix products, arithmetic and copies ran while one was open for 0% of the time, Pallas kernels for 26%

profile of v7, /device:TPU:1, one launch (start us, length us, event | category | flops | bytes accessed | tf_op | source)
XLA Modules:
  0.0 63.4 jit_solution(2940123677397822141)
XLA Ops:
  0.6 0.9 %pack_kv.1 = (bf16[128,256]{1,0:T(8,128)(2,1)S(1)}, bf16[128,256]{1,0:T(8,128)(2,1)S(1)}) custom-call(bf16[64,512]{1,0:T(8,128)(2,1)} %prompt_kv.1, bf16[1,64,512]{2,1,0:T(8,128)(2,1)} %resp_kv.1), custom_call_target="tpu_custom_call" | custom-call | bytes 1048576 | tf_op jit(solution)/shard_map/pack_kv/pallas_call | solution.py:143
  1.5 3.3 %collective-permute-start = (bf16[128,256]{1,0:T(8,128)(2,1)S(1)}, bf16[128,256]{1,0:T(8,128)(2,1)S(1)}, u32[]{:S(2)}, u32[]{:S(2)}) collective-permute-start(bf16[128,256]{1,0:T(8,128)(2,1)S(1)} %get-tuple-element.46.after), channel_id=1, source_target_pairs={{0,4},{4,0},{8,12},{12,8},{16,20},{20,16},{24,28},{28,24},{32,36},... | collective-permute-start | bytes 196616 | tf_op jit(solution)/shard_map/ppermute | solution.py:76
  4.8 1.1 %pack_q.1.after = bf16[4,64,1024]{2,1,0:T(8,128)(2,1)S(1)} custom-call(bf16[64,2048]{1,0:T(8,128)(2,1)} %pq.3, bf16[1,64,2048]{2,1,0:T(8,128)(2,1)} %rq.3, bf16[64,2048]{1,0:T(8,128)(2,1)} %pg.3, bf16[1,64,2048]{2,1,0:T(8,128)(2,1)} %rg.3, bf16[128,256]{1,0:T(8,128)(2,1)S(1)} %get-tuple-element.46.after), custom_call_target="tpu_custom_call" | custom-call | bytes 1048576 | tf_op jit(solution)/shard_map/pack_q/pallas_call | solution.py:157
  6.0 0.1 collective-permute-start.4
  6.7 0.0 collective-permute-done.recv.kv_recv.refs_13_
  6.8 2.7 %collective-permute-start.3 = (bf16[144,256]{1,0:T(8,128)(2,1)S(1)}, bf16[144,256]{1,0:T(8,128)(2,1)S(1)}, u32[]{:S(2)}, u32[]{:S(2)}) collective-permute-start(bf16[144,256]{1,0:T(8,128)(2,1)S(1)} %join_cores.1.value.refs_0_.refs_1_), channel_id=1, source_target_pairs={{0,96},{4,100},{8,104},{12,108},{16,112},{20,116},{24,120},{28,124... | collective-permute-start | bytes 221192 | tf_op jit(solution)/shard_map/ppermute | solution.py:81
  9.5 0.4 collective-permute-start.1
  9.8 0.0 collective-permute-done.4.after.recv
  9.8 2.6 %collective-permute-start.6 = (bf16[144,256]{1,0:T(8,128)(2,1)S(1)}, bf16[144,256]{1,0:T(8,128)(2,1)S(1)}, u32[]{:S(2)}, u32[]{:S(2)}) collective-permute-start(bf16[144,256]{1,0:T(8,128)(2,1)S(1)} %gate.2), channel_id=1, source_target_pairs={{0,24},{4,28},{8,0},{12,4},{16,8},{20,12},{24,16},{28,20},{32,56},... | collective-permute-start | bytes 221192 | tf_op jit(solution)/shard_map/ppermute | solution.py:86
  12.4 0.0 collective-permute-start.5
  14.4 1.9 %prep.1 = (bf16[256,2048]{1,0:T(8,128)(2,1)S(1)}, bf16[128,2048]{1,0:T(8,128)(2,1)S(1)}, bf16[64,1024]{1,0:T(8,128)(2,1)S(1)}, f32[144,2048]{1,0:T(8,128)S(1)}) custom-call(bf16[64,2048]{1,0:T(8,128)(2,1)} %pq.3, bf16[1,64,2048]{2,1,0:T(8,128)(2,1)} %rq.3, bf16[64,2048]{1,0:T(8,128)(2,1)} %pg.3, bf16[1,64,2048]{2,1,0:T(8,128)(2,1)} %rg.3, ...), custom_call_target="tpu_custom_call" | custom-call | bytes 1048576 | tf_op jit(solution)/shard_map/prep/pallas_call | solution.py:276
  16.3 0.6 collective-permute-done.2.refs_4_.refs_0_.refs_2_.refs_3_
  16.9 0.0 collective-permute-done.1.refs_3_.refs_1_.refs_2_
  16.9 0.0 collective-permute-done.6.refs_1_
  16.9 0.0 collective-permute-done.5.refs_0_
  17.0 2.8 %collective-permute-start.10 = (bf16[576,256]{1,0:T(8,128)(2,1)S(1)}, bf16[576,256]{1,0:T(8,128)(2,1)S(1)}, u32[]{:S(2)}, u32[]{:S(2)}) collective-permute-start(bf16[576,256]{1,0:T(8,128)(2,1)S(1)} %join.5), channel_id=1, source_target_pairs={{0,16},{4,20},{8,24},{12,28},{16,0},{20,4},{24,8},{28,12},{32,48},... | collective-permute-start | bytes 884744 | tf_op jit(solution)/shard_map/ppermute | solution.py:86
  19.8 0.9 %collective-permute-start.9 = (bf16[288,256]{1,0:T(8,128)(2,1)S(1)}, bf16[288,256]{1,0:T(8,128)(2,1)S(1)}, u32[]{:S(2)}, u32[]{:S(2)}) collective-permute-start(bf16[288,256]{1,0:T(8,128)(2,1)S(1)} %join.4), channel_id=1, source_target_pairs={{0,24},{4,28},{8,0},{12,4},{16,8},{20,12},{24,16},{28,20},{32,56},... | collective-permute-start | bytes 442376 | tf_op jit(solution)/shard_map/ppermute | solution.py:86
  20.8 0.6 collective-permute-start.8
  21.4 0.8 %collective-permute-start.7 = (bf16[288,256]{1,0:T(8,128)(2,1)S(1)}, bf16[288,256]{1,0:T(8,128)(2,1)S(1)}, u32[]{:S(2)}, u32[]{:S(2)}) collective-permute-start(bf16[288,256]{1,0:T(8,128)(2,1)S(1)} %join.3.refs_4_.refs_5_), channel_id=1, source_target_pairs={{0,32},{4,36},{8,40},{12,44},{16,48},{20,52},{24,56},{28,60},{32,6... | collective-permute-start | bytes 442376 | tf_op jit(solution)/shard_map/ppermute | solution.py:81
  22.2 2.3 %forward.3 = (bf16[768,2048]{1,0:T(8,128)(2,1)S(1)}, f32[144,2048]{1,0:T(8,128)S(1)}) custom-call(bf16[144,256]{1,0:T(8,128)(2,1)S(1)} %join_cores.1.value.refs_0_.refs_1_, bf16[144,256]{1,0:T(8,128)(2,1)S(1)} %collective-permute-done.1.refs_3_.refs_1_.refs_2_, bf16[144,256]{1,0:T(8,128)(2,1)S(1)} %collective-permute-done.2.refs_4_.refs_0_.refs_2_.refs_3_, ...), custom_call_target="tpu_custom_call" | custom-call | flops 805306368 | bytes 1048576 | tf_op jit(solution)/shard_map/forward/pallas_call | solution.py:380
  24.5 1.2 %collective-permute-done.10.refs_0_.refs_9_.refs_8_ = bf16[576,256]{1,0:T(8,128)(2,1)S(1)} collective-permute-done((bf16[576,256]{1,0:T(8,128)(2,1)S(1)}, bf16[576,256]{1,0:T(8,128)(2,1)S(1)}, u32[]{:S(2)}, u32[]{:S(2)}) %collective-permute-start.10) | collective-permute-done | bytes 294944 | tf_op jit(solution)/shard_map/ppermute | solution.py:86
  25.7 1.4 %forward.4 = (bf16[512,2048]{1,0:T(8,128)(2,1)S(1)}, f32[144,2048]{1,0:T(8,128)S(1)}) custom-call(bf16[576,256]{1,0:T(8,128)(2,1)S(1)} %collective-permute-done.10.refs_0_.refs_9_.refs_8_, bf16[256,2048]{1,0:T(8,128)(2,1)S(1)} %get-tuple-element.48.refs_5_.refs_1_.refs_3_.refs_2_.refs_4_.refs_6_.refs_15_, f32[144,2048]{1,0:T(8,128)S(1)} %get-tuple-element.50.refs_2_.part_0), custom_call_target="tpu_custom_call" | custom-call | flops 536870912 | bytes 1048576 | tf_op jit(solution)/shard_map/forward/pallas_call | solution.py:380
  27.1 2.6 %collective-permute-done.9.refs_8_.refs_2_.refs_7_ = bf16[288,256]{1,0:T(8,128)(2,1)S(1)} collective-permute-done((bf16[288,256]{1,0:T(8,128)(2,1)S(1)}, bf16[288,256]{1,0:T(8,128)(2,1)S(1)}, u32[]{:S(2)}, u32[]{:S(2)}) %collective-permute-start.9) | collective-permute-done | bytes 147488 | tf_op jit(solution)/shard_map/ppermute | solution.py:86
  29.7 0.3 collective-permute-done.8.refs_7_.refs_1_.refs_6_
  30.0 1.4 %collective-permute-start.11 = (bf16[16,256]{1,0:T(8,128)(2,1)S(1)}, bf16[16,256]{1,0:T(8,128)(2,1)S(1)}, u32[]{:S(2)}, u32[]{:S(2)}) collective-permute-start(bf16[16,256]{1,0:T(8,128)(2,1)S(1)} %collect.1.own_notes), channel_id=1, source_target_pairs={{0,4},{4,0},{8,12},{12,8},{16,20},{20,16},{24,28},{28,24},{32,36},... | collective-permute-start | bytes 24584 | tf_op jit(solution)/shard_map/ppermute | solution.py:76
  31.4 1.6 %forward.5 = (bf16[768,2048]{1,0:T(8,128)(2,1)S(1)}, f32[144,2048]{1,0:T(8,128)S(1)}) custom-call(bf16[288,256]{1,0:T(8,128)(2,1)S(1)} %collective-permute-done.7.refs_6_.refs_0_.refs_5_, bf16[288,256]{1,0:T(8,128)(2,1)S(1)} %collective-permute-done.8.refs_7_.refs_1_.refs_6_, bf16[288,256]{1,0:T(8,128)(2,1)S(1)} %collective-permute-done.9.refs_8_.refs_2_.refs_7_, ...), custom_call_target="tpu_custom_call" | custom-call | flops 805306368 | bytes 1048576 | tf_op jit(solution)/shard_map/forward/pallas_call | solution.py:380
  33.0 0.9 %combine.1 = (bf16[128,2048]{1,0:T(8,128)(2,1)S(1)}, bf16[256,2048]{1,0:T(8,128)(2,1)S(1)}, f32[8,2048]{1,0:T(8,128)S(1)}) custom-call(bf16[16,256]{1,0:T(8,128)(2,1)S(1)} %collect.1.own_notes, bf16[16,256]{1,0:T(8,128)(2,1)S(1)} %collective-permute-done.11.sib_notes, bf16[128,2048]{1,0:T(8,128)(2,1)S(1)} %get-tuple-element.52.grads, ...), custom_call_target="tpu_custom_call" | custom-call | bytes 1048576 | tf_op jit(solution)/shard_map/combine/pallas_call | solution.py:485
  33.9 1.8 %backward.3 = (bf16[512,2048]{1,0:T(8,128)(2,1)S(1)}, bf16[384,256]{1,0:T(8,128)(2,1)S(1)}, bf16[128,256]{1,0:T(8,128)(2,1)S(1)}) custom-call(bf16[576,256]{1,0:T(8,128)(2,1)S(1)} %collective-permute-done.10.refs_0_.refs_9_.refs_8_, bf16[512,2048]{1,0:T(8,128)(2,1)S(1)} %get-tuple-element.51.refs_10_.refs_1_, ...), custom_call_target="tpu_custom_call" | custom-call | flops 805306368 | bytes 1048576 | tf_op jit(solution)/shard_map/backward/pallas_call | solution.py:527
  35.8 3.5 %collective-permute-start.13 = (bf16[384,256]{1,0:T(8,128)(2,1)S(1)}, bf16[384,256]{1,0:T(8,128)(2,1)S(1)}, u32[]{:S(2)}, u32[]{:S(2)}) collective-permute-start(bf16[384,256]{1,0:T(8,128)(2,1)S(1)} %get-tuple-element.58.refs_7_), channel_id=1, source_target_pairs={{0,16},{4,20},{8,24},{12,28},{16,0},{20,4},{24,8},{28,12},{32,48},... | collective-permute-start | bytes 589832 | tf_op jit(solution)/shard_map/ppermute | solution.py:86
  39.3 2.6 %backward.4 = (bf16[768,2048]{1,0:T(8,128)(2,1)S(1)}, bf16[384,256]{1,0:T(8,128)(2,1)S(1)}, bf16[384,256]{1,0:T(8,128)(2,1)S(1)}) custom-call(bf16[288,256]{1,0:T(8,128)(2,1)S(1)} %collective-permute-done.7.refs_6_.refs_0_.refs_5_, bf16[288,256]{1,0:T(8,128)(2,1)S(1)} %collective-permute-done.8.refs_7_.refs_1_.refs_6_, ...), custom_call_target="tpu_custom_call" | custom-call | flops 1207959552 | bytes 1048576 | tf_op jit(solution)/shard_map/backward/pallas_call | solution.py:527
  41.9 0.1 collective-permute-start.15
  42.0 2.7 %collective-permute-start.14 = (bf16[384,256]{1,0:T(8,128)(2,1)S(1)}, bf16[384,256]{1,0:T(8,128)(2,1)S(1)}, u32[]{:S(2)}, u32[]{:S(2)}) collective-permute-start(bf16[384,256]{1,0:T(8,128)(2,1)S(1)} %get-tuple-element.59.refs_9_), channel_id=1, source_target_pairs={{0,24},{4,28},{8,0},{12,4},{16,8},{20,12},{24,16},{28,20},{32,56},... | collective-permute-start | bytes 589832 | tf_op jit(solution)/shard_map/ppermute | solution.py:86
  44.6 2.6 %backward.5 = (bf16[768,2048]{1,0:T(8,128)(2,1)S(1)}, f32[128,256]{1,0:T(8,128)S(1)}, f32[384,256]{1,0:T(8,128)S(1)}, bf16[128,256]{1,0:T(8,128)(2,1)S(1)}, bf16[128,256]{1,0:T(8,128)(2,1)S(1)}) custom-call(bf16[144,256]{1,0:T(8,128)(2,1)S(1)} %join_cores.1.value.refs_0_.refs_1_, bf16[144,256]{1,0:T(8,128)(2,1)S(1)} %collective-permute-done.1.refs_3_.refs_1_.refs_2_, ...), custom_call_target="tpu_custom_call" | custom-call | flops 1207959552 | bytes 1048576 | tf_op jit(solution)/shard_map/backward/pallas_call | solution.py:527
  47.2 0.1 collective-permute-start.19
  47.3 1.5 %collective-permute-start.20 = (bf16[128,256]{1,0:T(8,128)(2,1)S(1)}, bf16[128,256]{1,0:T(8,128)(2,1)S(1)}, u32[]{:S(2)}, u32[]{:S(2)}) collective-permute-start(bf16[128,256]{1,0:T(8,128)(2,1)S(1)} %get-tuple-element.79), channel_id=1, source_target_pairs={{0,8},{4,12},{8,16},{12,20},{16,24},{20,28},{24,0},{28,4},{32,40},... | collective-permute-start | bytes 196616 | tf_op jit(solution)/shard_map/ppermute | solution.py:86
  48.8 0.1 collective-permute-start.21
  48.9 0.5 collective-permute-done.15.back_2
  49.4 0.1 sum_column.1
  49.5 3.4 %collective-permute-start.16 = (bf16[128,256]{1,0:T(8,128)(2,1)S(1)}, bf16[128,256]{1,0:T(8,128)(2,1)S(1)}, u32[]{:S(2)}, u32[]{:S(2)}) collective-permute-start(bf16[128,256]{1,0:T(8,128)(2,1)S(1)} %get-tuple-element.75), channel_id=1, source_target_pairs={{0,96},{4,100},{8,104},{12,108},{16,112},{20,116},{24,120},{28,124... | collective-permute-start | bytes 196616 | tf_op jit(solution)/shard_map/ppermute | solution.py:81
  52.9 0.6 collective-permute-start.17
  53.4 0.4 collective-permute-start.18
  53.8 2.0 %finish.1 = (bf16[64,4352]{1,0:T(8,128)(2,1)S(1)}, bf16[64,4352]{1,0:T(8,128)(2,1)S(1)}) custom-call(bf16[144,256]{1,0:T(8,128)(2,1)S(1)} %join_cores.1.value.refs_0_.refs_1_, bf16[144,256]{1,0:T(8,128)(2,1)S(1)} %collective-permute-done.1.refs_3_.refs_1_.refs_2_, bf16[144,256]{1,0:T(8,128)(2,1)S(1)} %collective-permute-done.2.refs_4_.refs_0_.refs_2_.refs_3_, ...), custom_call_target="tpu_custom_call" | custom-call | flops 805306368 | bytes 1048576 | tf_op jit(solution)/shard_map/finish/pallas_call | solution.py:590
  55.8 2.3 %collective-permute-start.12 = (bf16[64,4352]{1,0:T(8,128)(2,1)S(1)}, bf16[64,4352]{1,0:T(8,128)(2,1)S(1)}, u32[]{:S(2)}, u32[]{:S(2)}) collective-permute-start(bf16[64,4352]{1,0:T(8,128)(2,1)S(1)} %get-tuple-element.67), channel_id=1, source_target_pairs={{0,4},{4,0},{8,12},{12,8},{16,20},{20,16},{24,28},{28,24},{32,36},... | collective-permute-start | bytes 1671176 | tf_op jit(solution)/shard_map/ppermute | solution.py:76
  58.2 0.7 %collective-permute-done.17.refs_2_ = bf16[128,256]{1,0:T(8,128)(2,1)S(1)} collective-permute-done((bf16[128,256]{1,0:T(8,128)(2,1)S(1)}, bf16[128,256]{1,0:T(8,128)(2,1)S(1)}, u32[]{:S(2)}, u32[]{:S(2)}) %collective-permute-start.17) | collective-permute-done | bytes 65568 | tf_op jit(solution)/shard_map/ppermute | solution.py:81
  58.9 0.1 add_split.1
  59.0 2.7 %collective-permute-start.22 = (bf16[64,256]{1,0:T(8,128)(2,1)S(1)}, bf16[64,256]{1,0:T(8,128)(2,1)S(1)}, u32[]{:S(2)}, u32[]{:S(2)}) collective-permute-start(bf16[64,256]{1,0:T(8,128)(2,1)S(1)} %get-tuple-element.81), channel_id=1, source_target_pairs={{0,4},{4,0},{8,12},{12,8},{16,20},{20,16},{24,28},{28,24},{32,36},... | collective-permute-start | bytes 98312 | tf_op jit(solution)/shard_map/ppermute | solution.py:76
  61.6 1.1 %place.1 = (bf16[64,2048]{1,0:T(8,128)(2,1)}, bf16[1,64,2048]{2,1,0:T(8,128)(2,1)}, bf16[64,2048]{1,0:T(8,128)(2,1)}, bf16[1,64,2048]{2,1,0:T(8,128)(2,1)}, bf16...) custom-call(bf16[64,4352]{1,0:T(8,128)(2,1)S(1)} %get-tuple-element.66.own, bf16[64,4352]{1,0:T(8,128)(2,1)S(1)} %collective-permute-done.12.recv), custom_call_target="tpu_custom_call" | custom-call | bytes 1048576 | tf_op jit(solution)/shard_map/place/pallas_call | solution.py:625
  62.7 0.7 %last.1 = bf16[64,512]{1,0:T(8,128)(2,1)} custom-call(bf16[64,256]{1,0:T(8,128)(2,1)S(1)} %get-tuple-element.80.kept, bf16[64,256]{1,0:T(8,128)(2,1)S(1)} %collective-permute-done.22.recv, f32[8,128]{1,0:T(8,128)S(1)} %get-tuple-element.82.after), custom_call_target="tpu_custom_call" | custom-call | bytes 1048576 | tf_op jit(solution)/shard_map/last/pallas_call | solution.py:695
  (21 shorter events, 0.1 us)
Async XLA Ops:
  1.5 5.2 %collective-permute-start = (bf16[128,256]{1,0:T(8,128)(2,1)S(1)}, bf16[128,256]{1,0:T(8,128)(2,1)S(1)}, u32[]{:S(2)}, u32[]{:S(2)}) collective-permute-start(bf16[128,256]{1,0:T(8,128)(2,1)S(1)} %get-tuple-element.46.after), channel_id=1, source_target_pairs={{0,4},{4,0},{8,12},{12,8},{16,20},{20,16},{24,28},{28,24},{32,36},... | collective-permute-start | bytes 196616 | tf_op jit(solution)/shard_map/ppermute | solution.py:76
  6.0 3.9 %collective-permute-start.4 = (bf16[4,64,1024]{2,1,0:T(8,128)(2,1)S(1)}, bf16[4,64,1024]{2,1,0:T(8,128)(2,1)S(1)}, u32[]{:S(2)}, u32[]{:S(2)}) collective-permute-start(bf16[4,64,1024]{2,1,0:T(8,128)(2,1)S(1)} %pack_q.1.after), channel_id=1, source_target_pairs={{0,4},{4,0},{8,12},{12,8},{16,20},{20,16},{24,28},{28,24},{32,36},... | collective-permute-start | bytes 1572872 | tf_op jit(solution)/shard_map/ppermute | solution.py:76
  6.8 9.6 %collective-permute-start.3 = (bf16[144,256]{1,0:T(8,128)(2,1)S(1)}, bf16[144,256]{1,0:T(8,128)(2,1)S(1)}, u32[]{:S(2)}, u32[]{:S(2)}) collective-permute-start(bf16[144,256]{1,0:T(8,128)(2,1)S(1)} %join_cores.1.value.refs_0_.refs_1_), channel_id=1, source_target_pairs={{0,96},{4,100},{8,104},{12,108},{16,112},{20,116},{24,120},{28,124... | collective-permute-start | bytes 221192 | tf_op jit(solution)/shard_map/ppermute | solution.py:81
  9.4 7.5 %collective-permute-start.2 = (bf16[144,256]{1,0:T(8,128)(2,1)S(1)}, bf16[144,256]{1,0:T(8,128)(2,1)S(1)}, u32[]{:S(2)}, u32[]{:S(2)}) collective-permute-start(bf16[144,256]{1,0:T(8,128)(2,1)S(1)} %join_cores.1.value.refs_0_.refs_1_), channel_id=1, source_target_pairs={{0,64},{4,68},{8,72},{12,76},{16,80},{20,84},{24,88},{28,92},{32,9... | collective-permute-start | bytes 221192 | tf_op jit(solution)/shard_map/ppermute | solution.py:81
  9.5 7.5 %collective-permute-start.1 = (bf16[144,256]{1,0:T(8,128)(2,1)S(1)}, bf16[144,256]{1,0:T(8,128)(2,1)S(1)}, u32[]{:S(2)}, u32[]{:S(2)}) collective-permute-start(bf16[144,256]{1,0:T(8,128)(2,1)S(1)} %join_cores.1.value.refs_0_.refs_1_), channel_id=1, source_target_pairs={{0,32},{4,36},{8,40},{12,44},{16,48},{20,52},{24,56},{28,60},{32,6... | collective-permute-start | bytes 221192 | tf_op jit(solution)/shard_map/ppermute | solution.py:81
  9.8 7.1 %collective-permute-start.6 = (bf16[144,256]{1,0:T(8,128)(2,1)S(1)}, bf16[144,256]{1,0:T(8,128)(2,1)S(1)}, u32[]{:S(2)}, u32[]{:S(2)}) collective-permute-start(bf16[144,256]{1,0:T(8,128)(2,1)S(1)} %gate.2), channel_id=1, source_target_pairs={{0,24},{4,28},{8,0},{12,4},{16,8},{20,12},{24,16},{28,20},{32,56},... | collective-permute-start | bytes 221192 | tf_op jit(solution)/shard_map/ppermute | solution.py:86
  12.4 4.6 %collective-permute-start.5 = (bf16[144,256]{1,0:T(8,128)(2,1)S(1)}, bf16[144,256]{1,0:T(8,128)(2,1)S(1)}, u32[]{:S(2)}, u32[]{:S(2)}) collective-permute-start(bf16[144,256]{1,0:T(8,128)(2,1)S(1)} %gate.2), channel_id=1, source_target_pairs={{0,8},{4,12},{8,16},{12,20},{16,24},{20,28},{24,0},{28,4},{32,40},... | collective-permute-start | bytes 221192 | tf_op jit(solution)/shard_map/ppermute | solution.py:86
  17.0 8.7 %collective-permute-start.10 = (bf16[576,256]{1,0:T(8,128)(2,1)S(1)}, bf16[576,256]{1,0:T(8,128)(2,1)S(1)}, u32[]{:S(2)}, u32[]{:S(2)}) collective-permute-start(bf16[576,256]{1,0:T(8,128)(2,1)S(1)} %join.5), channel_id=1, source_target_pairs={{0,16},{4,20},{8,24},{12,28},{16,0},{20,4},{24,8},{28,12},{32,48},... | collective-permute-start | bytes 884744 | tf_op jit(solution)/shard_map/ppermute | solution.py:86
  19.8 9.9 %collective-permute-start.9 = (bf16[288,256]{1,0:T(8,128)(2,1)S(1)}, bf16[288,256]{1,0:T(8,128)(2,1)S(1)}, u32[]{:S(2)}, u32[]{:S(2)}) collective-permute-start(bf16[288,256]{1,0:T(8,128)(2,1)S(1)} %join.4), channel_id=1, source_target_pairs={{0,24},{4,28},{8,0},{12,4},{16,8},{20,12},{24,16},{28,20},{32,56},... | collective-permute-start | bytes 442376 | tf_op jit(solution)/shard_map/ppermute | solution.py:86
  20.8 9.2 %collective-permute-start.8 = (bf16[288,256]{1,0:T(8,128)(2,1)S(1)}, bf16[288,256]{1,0:T(8,128)(2,1)S(1)}, u32[]{:S(2)}, u32[]{:S(2)}) collective-permute-start(bf16[288,256]{1,0:T(8,128)(2,1)S(1)} %join.4), channel_id=1, source_target_pairs={{0,8},{4,12},{8,16},{12,20},{16,24},{20,28},{24,0},{28,4},{32,40},... | collective-permute-start | bytes 442376 | tf_op jit(solution)/shard_map/ppermute | solution.py:86
  21.4 8.6 %collective-permute-start.7 = (bf16[288,256]{1,0:T(8,128)(2,1)S(1)}, bf16[288,256]{1,0:T(8,128)(2,1)S(1)}, u32[]{:S(2)}, u32[]{:S(2)}) collective-permute-start(bf16[288,256]{1,0:T(8,128)(2,1)S(1)} %join.3.refs_4_.refs_5_), channel_id=1, source_target_pairs={{0,32},{4,36},{8,40},{12,44},{16,48},{20,52},{24,56},{28,60},{32,6... | collective-permute-start | bytes 442376 | tf_op jit(solution)/shard_map/ppermute | solution.py:81
  30.0 3.0 %collective-permute-start.11 = (bf16[16,256]{1,0:T(8,128)(2,1)S(1)}, bf16[16,256]{1,0:T(8,128)(2,1)S(1)}, u32[]{:S(2)}, u32[]{:S(2)}) collective-permute-start(bf16[16,256]{1,0:T(8,128)(2,1)S(1)} %collect.1.own_notes), channel_id=1, source_target_pairs={{0,4},{4,0},{8,12},{12,8},{16,20},{20,16},{24,28},{28,24},{32,36},... | collective-permute-start | bytes 24584 | tf_op jit(solution)/shard_map/ppermute | solution.py:76
  35.8 13.0 %collective-permute-start.13 = (bf16[384,256]{1,0:T(8,128)(2,1)S(1)}, bf16[384,256]{1,0:T(8,128)(2,1)S(1)}, u32[]{:S(2)}, u32[]{:S(2)}) collective-permute-start(bf16[384,256]{1,0:T(8,128)(2,1)S(1)} %get-tuple-element.58.refs_7_), channel_id=1, source_target_pairs={{0,16},{4,20},{8,24},{12,28},{16,0},{20,4},{24,8},{28,12},{32,48},... | collective-permute-start | bytes 589832 | tf_op jit(solution)/shard_map/ppermute | solution.py:86
  41.9 7.5 %collective-permute-start.15 = (bf16[384,256]{1,0:T(8,128)(2,1)S(1)}, bf16[384,256]{1,0:T(8,128)(2,1)S(1)}, u32[]{:S(2)}, u32[]{:S(2)}) collective-permute-start(bf16[384,256]{1,0:T(8,128)(2,1)S(1)} %get-tuple-element.73), channel_id=1, source_target_pairs={{0,8},{4,12},{8,16},{12,20},{16,24},{20,28},{24,0},{28,4},{32,40},... | collective-permute-start | bytes 589832 | tf_op jit(solution)/shard_map/ppermute | solution.py:86
  42.0 7.4 %collective-permute-start.14 = (bf16[384,256]{1,0:T(8,128)(2,1)S(1)}, bf16[384,256]{1,0:T(8,128)(2,1)S(1)}, u32[]{:S(2)}, u32[]{:S(2)}) collective-permute-start(bf16[384,256]{1,0:T(8,128)(2,1)S(1)} %get-tuple-element.59.refs_9_), channel_id=1, source_target_pairs={{0,24},{4,28},{8,0},{12,4},{16,8},{20,12},{24,16},{28,20},{32,56},... | collective-permute-start | bytes 589832 | tf_op jit(solution)/shard_map/ppermute | solution.py:86
  47.2 6.2 %collective-permute-start.19 = (bf16[128,256]{1,0:T(8,128)(2,1)S(1)}, bf16[128,256]{1,0:T(8,128)(2,1)S(1)}, u32[]{:S(2)}, u32[]{:S(2)}) collective-permute-start(bf16[128,256]{1,0:T(8,128)(2,1)S(1)} %get-tuple-element.78), channel_id=1, source_target_pairs={{0,24},{4,28},{8,0},{12,4},{16,8},{20,12},{24,16},{28,20},{32,56},... | collective-permute-start | bytes 196616 | tf_op jit(solution)/shard_map/ppermute | solution.py:86
  47.3 8.5 %collective-permute-start.20 = (bf16[128,256]{1,0:T(8,128)(2,1)S(1)}, bf16[128,256]{1,0:T(8,128)(2,1)S(1)}, u32[]{:S(2)}, u32[]{:S(2)}) collective-permute-start(bf16[128,256]{1,0:T(8,128)(2,1)S(1)} %get-tuple-element.79), channel_id=1, source_target_pairs={{0,8},{4,12},{8,16},{12,20},{16,24},{20,28},{24,0},{28,4},{32,40},... | collective-permute-start | bytes 196616 | tf_op jit(solution)/shard_map/ppermute | solution.py:86
  48.8 9.4 %collective-permute-start.21 = (bf16[128,256]{1,0:T(8,128)(2,1)S(1)}, bf16[128,256]{1,0:T(8,128)(2,1)S(1)}, u32[]{:S(2)}, u32[]{:S(2)}) collective-permute-start(bf16[128,256]{1,0:T(8,128)(2,1)S(1)} %gate.3.after), channel_id=1, source_target_pairs={{0,16},{4,20},{8,24},{12,28},{16,0},{20,4},{24,8},{28,12},{32,48},... | collective-permute-start | bytes 196616 | tf_op jit(solution)/shard_map/ppermute | solution.py:86
  49.5 8.7 %collective-permute-start.16 = (bf16[128,256]{1,0:T(8,128)(2,1)S(1)}, bf16[128,256]{1,0:T(8,128)(2,1)S(1)}, u32[]{:S(2)}, u32[]{:S(2)}) collective-permute-start(bf16[128,256]{1,0:T(8,128)(2,1)S(1)} %get-tuple-element.75), channel_id=1, source_target_pairs={{0,96},{4,100},{8,104},{12,108},{16,112},{20,116},{24,120},{28,124... | collective-permute-start | bytes 196616 | tf_op jit(solution)/shard_map/ppermute | solution.py:81
  52.9 6.0 %collective-permute-start.17 = (bf16[128,256]{1,0:T(8,128)(2,1)S(1)}, bf16[128,256]{1,0:T(8,128)(2,1)S(1)}, u32[]{:S(2)}, u32[]{:S(2)}) collective-permute-start(bf16[128,256]{1,0:T(8,128)(2,1)S(1)} %get-tuple-element.76), channel_id=1, source_target_pairs={{0,64},{4,68},{8,72},{12,76},{16,80},{20,84},{24,88},{28,92},{32,9... | collective-permute-start | bytes 196616 | tf_op jit(solution)/shard_map/ppermute | solution.py:81
  53.4 5.5 %collective-permute-start.18 = (bf16[128,256]{1,0:T(8,128)(2,1)S(1)}, bf16[128,256]{1,0:T(8,128)(2,1)S(1)}, u32[]{:S(2)}, u32[]{:S(2)}) collective-permute-start(bf16[128,256]{1,0:T(8,128)(2,1)S(1)} %get-tuple-element.77), channel_id=1, source_target_pairs={{0,32},{4,36},{8,40},{12,44},{16,48},{20,52},{24,56},{28,60},{32,6... | collective-permute-start | bytes 196616 | tf_op jit(solution)/shard_map/ppermute | solution.py:81
  55.8 5.8 %collective-permute-start.12 = (bf16[64,4352]{1,0:T(8,128)(2,1)S(1)}, bf16[64,4352]{1,0:T(8,128)(2,1)S(1)}, u32[]{:S(2)}, u32[]{:S(2)}) collective-permute-start(bf16[64,4352]{1,0:T(8,128)(2,1)S(1)} %get-tuple-element.67), channel_id=1, source_target_pairs={{0,4},{4,0},{8,12},{12,8},{16,20},{20,16},{24,28},{28,24},{32,36},... | collective-permute-start | bytes 1671176 | tf_op jit(solution)/shard_map/ppermute | solution.py:76
  59.0 3.7 %collective-permute-start.22 = (bf16[64,256]{1,0:T(8,128)(2,1)S(1)}, bf16[64,256]{1,0:T(8,128)(2,1)S(1)}, u32[]{:S(2)}, u32[]{:S(2)}) collective-permute-start(bf16[64,256]{1,0:T(8,128)(2,1)S(1)} %get-tuple-element.81), channel_id=1, source_target_pairs={{0,4},{4,0},{8,12},{12,8},{16,20},{20,16},{24,28},{28,24},{32,36},... | collective-permute-start | bytes 98312 | tf_op jit(solution)/shard_map/ppermute | solution.py:76

commit v8 on v7

--- a/solution.py
+++ b/solution.py
@@ -725,16 +725,16 @@
     q_aug, grads, raised_own, part_own = prep(
         prompt_q, resp_q, prompt_grad, resp_grad, q_recv, kv_own, kv_recv
     )
-    note = facts(partner, chosen, resp_len, part_own)
-    near = join(from_x, note, *from_z)
-    far = join(from_z[1:], note, from_z[0], near)
-    column = join([block] + from_z, note, near)
+    near = join(from_x, part_own, *from_z)
+    far = join(from_z[1:], part_own, from_z[0], near)
+    column = join([block] + from_z, part_own, near)
     early_kvs = [block] + from_z + [near]
     side_kvs = [shift_z(near, 1)] + [shift_x(far, 4 - offset) for offset in offsets[1:3]]
     far_kvs = [shift_x(column, 2)]
     kv_lists = [early_kvs, side_kvs, far_kvs]
 
     early = forward(early_kvs, q_aug, part_own, early_part)
+    note = facts(partner, chosen, resp_len, early[0])
     far_ones = forward(far_kvs, q_aug, early[1], far_part)
     side = forward(side_kvs, q_aug, far_ones[1], side_part)
     raised, packs = zip(early, side, far_ones)

time: 63.8 us -> 61.9 us (0.970)
  starting transfers between devices: 32.9 us -> 30.6 us
  waiting for transfers between devices: 5.93 us -> 6.59 us
    ppermute x7, starting transfers between devices: 8.29 us -> 6.1 us  [shift_z(): return lax.ppermute(value, 'resp', pairs)]
    ppermute x7, waiting for transfers between devices: 1.3 us -> 3.09 us  [shift_z(): return lax.ppermute(value, 'resp', pairs)]
    ppermute x11, waiting for transfers between devices: 4.62 us -> 3.48 us  [shift_x(): return lax.ppermute(value, 'resp', pairs)]
  transfers between devices with their start and end apart: 23 -> 23, of which waited for: 6 -> 6; matrix products, arithmetic and copies ran while one was open for 0% -> 0% of each run, Pallas kernels for 26% -> 27%
where the time goes in v8:
time: 61.9 us; the launch traced here: 61.7 us
  starting transfers between devices  30.6 us (49%)
  Pallas kernels  21 us (34%)
  waiting for transfers between devices  6.59 us (11%)
  between operations  3.45 us (6%)
    ppermute x11, starting transfers between devices, shift_x(): return lax.ppermute(value, 'resp', pairs)  15 us
    ppermute x5, starting transfers between devices, swap_core(): return lax.ppermute(value, 'resp', [(r, r ^ 1) for r in range(32)])  9.51 us
    pallas_call x3, Pallas kernels, backward(): call(functools.partial(backward_kernel, part, splits, chunk), 'backward',...  7 us
    ppermute x7, starting transfers between devices, shift_z(): return lax.ppermute(value, 'resp', pairs)  6.1 us
    pallas_call x3, Pallas kernels, forward(): call(functools.partial(forward_kernel, part, has_top), 'forward', [VMEM]...  5.29 us
    ppermute x11, waiting for transfers between devices, shift_x(): return lax.ppermute(value, 'resp', pairs)  3.48 us
    ppermute x7, waiting for transfers between devices, shift_z(): return lax.ppermute(value, 'resp', pairs)  3.09 us
    pallas_call x1, Pallas kernels, finish(): call(finish_kernel, 'finish', [VMEM] * (len(flat) + len(slopes) + 7) + [A...  1.95 us
  transfers between devices with their start and end apart: 23, of which 6 were waited for; matrix products, arithmetic and copies ran while one was open for 0% of the time, Pallas kernels for 27%

profile of v8, /device:TPU:1, one launch (start us, length us, event | category | flops | bytes accessed | tf_op | source)
XLA Modules:
  0.0 61.7 jit_solution(5470774480873963166)
XLA Ops:
  0.6 0.9 %pack_kv.1 = (bf16[128,256]{1,0:T(8,128)(2,1)S(1)}, bf16[128,256]{1,0:T(8,128)(2,1)S(1)}) custom-call(bf16[64,512]{1,0:T(8,128)(2,1)} %prompt_kv.1, bf16[1,64,512]{2,1,0:T(8,128)(2,1)} %resp_kv.1), custom_call_target="tpu_custom_call" | custom-call | bytes 1048576 | tf_op jit(solution)/shard_map/pack_kv/pallas_call | solution.py:143
  1.5 3.3 %collective-permute-start = (bf16[128,256]{1,0:T(8,128)(2,1)S(1)}, bf16[128,256]{1,0:T(8,128)(2,1)S(1)}, u32[]{:S(2)}, u32[]{:S(2)}) collective-permute-start(bf16[128,256]{1,0:T(8,128)(2,1)S(1)} %get-tuple-element.46.after), channel_id=1, source_target_pairs={{0,4},{4,0},{8,12},{12,8},{16,20},{20,16},{24,28},{28,24},{32,36},... | collective-permute-start | bytes 196616 | tf_op jit(solution)/shard_map/ppermute | solution.py:76
  4.8 1.1 %pack_q.1.after = bf16[4,64,1024]{2,1,0:T(8,128)(2,1)S(1)} custom-call(bf16[64,2048]{1,0:T(8,128)(2,1)} %pq.3, bf16[1,64,2048]{2,1,0:T(8,128)(2,1)} %rq.3, bf16[64,2048]{1,0:T(8,128)(2,1)} %pg.3, bf16[1,64,2048]{2,1,0:T(8,128)(2,1)} %rg.3, bf16[128,256]{1,0:T(8,128)(2,1)S(1)} %get-tuple-element.46.after), custom_call_target="tpu_custom_call" | custom-call | bytes 1048576 | tf_op jit(solution)/shard_map/pack_q/pallas_call | solution.py:157
  6.0 0.1 collective-permute-start.4
  6.8 2.7 %collective-permute-start.3 = (bf16[144,256]{1,0:T(8,128)(2,1)S(1)}, bf16[144,256]{1,0:T(8,128)(2,1)S(1)}, u32[]{:S(2)}, u32[]{:S(2)}) collective-permute-start(bf16[144,256]{1,0:T(8,128)(2,1)S(1)} %join_cores.1.value.refs_0_.refs_1_), channel_id=1, source_target_pairs={{0,96},{4,100},{8,104},{12,108},{16,112},{20,116},{24,120},{28,124... | collective-permute-start | bytes 221192 | tf_op jit(solution)/shard_map/ppermute | solution.py:81
  9.5 0.4 collective-permute-start.1
  9.8 0.0 collective-permute-done.4.after.recv
  9.8 2.6 %collective-permute-start.6 = (bf16[144,256]{1,0:T(8,128)(2,1)S(1)}, bf16[144,256]{1,0:T(8,128)(2,1)S(1)}, u32[]{:S(2)}, u32[]{:S(2)}) collective-permute-start(bf16[144,256]{1,0:T(8,128)(2,1)S(1)} %gate.2), channel_id=1, source_target_pairs={{0,24},{4,28},{8,0},{12,4},{16,8},{20,12},{24,16},{28,20},{32,56},... | collective-permute-start | bytes 221192 | tf_op jit(solution)/shard_map/ppermute | solution.py:86
  12.4 0.0 collective-permute-start.5
  12.4 1.9 %prep.1 = (bf16[256,2048]{1,0:T(8,128)(2,1)S(1)}, bf16[128,2048]{1,0:T(8,128)(2,1)S(1)}, bf16[64,1024]{1,0:T(8,128)(2,1)S(1)}, f32[144,2048]{1,0:T(8,128)S(1)}) custom-call(bf16[64,2048]{1,0:T(8,128)(2,1)} %pq.3, bf16[1,64,2048]{2,1,0:T(8,128)(2,1)} %rq.3, bf16[64,2048]{1,0:T(8,128)(2,1)} %pg.3, bf16[1,64,2048]{2,1,0:T(8,128)(2,1)} %rg.3, ...), custom_call_target="tpu_custom_call" | custom-call | bytes 1048576 | tf_op jit(solution)/shard_map/prep/pallas_call | solution.py:276
  14.3 2.6 %collective-permute-done.2.refs_4_.refs_0_.refs_2_.refs_3_ = bf16[144,256]{1,0:T(8,128)(2,1)S(1)} collective-permute-done((bf16[144,256]{1,0:T(8,128)(2,1)S(1)}, bf16[144,256]{1,0:T(8,128)(2,1)S(1)}, u32[]{:S(2)}, u32[]{:S(2)}) %collective-permute-start.2) | collective-permute-done | bytes 73760 | tf_op jit(solution)/shard_map/ppermute | solution.py:81
  16.9 0.0 collective-permute-done.1.refs_3_.refs_1_.refs_2_
  16.9 0.0 collective-permute-done.6.refs_1_
  16.9 0.0 collective-permute-done.5.refs_0_
  17.0 2.8 %collective-permute-start.10 = (bf16[576,256]{1,0:T(8,128)(2,1)S(1)}, bf16[576,256]{1,0:T(8,128)(2,1)S(1)}, u32[]{:S(2)}, u32[]{:S(2)}) collective-permute-start(bf16[576,256]{1,0:T(8,128)(2,1)S(1)} %join.5), channel_id=1, source_target_pairs={{0,16},{4,20},{8,24},{12,28},{16,0},{20,4},{24,8},{28,12},{32,48},... | collective-permute-start | bytes 884744 | tf_op jit(solution)/shard_map/ppermute | solution.py:86
  19.8 0.9 %collective-permute-start.9 = (bf16[288,256]{1,0:T(8,128)(2,1)S(1)}, bf16[288,256]{1,0:T(8,128)(2,1)S(1)}, u32[]{:S(2)}, u32[]{:S(2)}) collective-permute-start(bf16[288,256]{1,0:T(8,128)(2,1)S(1)} %join.4), channel_id=1, source_target_pairs={{0,24},{4,28},{8,0},{12,4},{16,8},{20,12},{24,16},{28,20},{32,56},... | collective-permute-start | bytes 442376 | tf_op jit(solution)/shard_map/ppermute | solution.py:86
  20.8 0.6 collective-permute-start.8
  21.4 0.0 collective-permute-start.7
  23.3 2.3 %forward.3 = (bf16[768,2048]{1,0:T(8,128)(2,1)S(1)}, f32[144,2048]{1,0:T(8,128)S(1)}) custom-call(bf16[144,256]{1,0:T(8,128)(2,1)S(1)} %join_cores.1.value.refs_0_.refs_1_, bf16[144,256]{1,0:T(8,128)(2,1)S(1)} %collective-permute-done.1.refs_3_.refs_1_.refs_2_, bf16[144,256]{1,0:T(8,128)(2,1)S(1)} %collective-permute-done.2.refs_4_.refs_0_.refs_2_.refs_3_, ...), custom_call_target="tpu_custom_call" | custom-call | flops 805306368 | bytes 1048576 | tf_op jit(solution)/shard_map/forward/pallas_call | solution.py:380
  25.7 0.1 collective-permute-done.10.refs_0_.refs_9_.refs_8_
  25.7 1.4 %forward.4 = (bf16[512,2048]{1,0:T(8,128)(2,1)S(1)}, f32[144,2048]{1,0:T(8,128)S(1)}) custom-call(bf16[576,256]{1,0:T(8,128)(2,1)S(1)} %collective-permute-done.10.refs_0_.refs_9_.refs_8_, bf16[256,2048]{1,0:T(8,128)(2,1)S(1)} %get-tuple-element.48.refs_5_.refs_1_.refs_3_.refs_2_.refs_4_.refs_6_.refs_15_, f32[144,2048]{1,0:T(8,128)S(1)} %get-tuple-element.50.refs_2_.part_0), custom_call_target="tpu_custom_call" | custom-call | flops 536870912 | bytes 1048576 | tf_op jit(solution)/shard_map/forward/pallas_call | solution.py:380
  27.1 2.8 %collective-permute-done.9.refs_8_.refs_2_.refs_7_ = bf16[288,256]{1,0:T(8,128)(2,1)S(1)} collective-permute-done((bf16[288,256]{1,0:T(8,128)(2,1)S(1)}, bf16[288,256]{1,0:T(8,128)(2,1)S(1)}, u32[]{:S(2)}, u32[]{:S(2)}) %collective-permute-start.9) | collective-permute-done | bytes 147488 | tf_op jit(solution)/shard_map/ppermute | solution.py:86
  29.9 0.1 collective-permute-done.8.refs_7_.refs_1_.refs_6_
  30.0 0.0 collective-permute-done.7.refs_6_.refs_0_.refs_5_
  30.0 1.4 %collective-permute-start.11 = (bf16[16,256]{1,0:T(8,128)(2,1)S(1)}, bf16[16,256]{1,0:T(8,128)(2,1)S(1)}, u32[]{:S(2)}, u32[]{:S(2)}) collective-permute-start(bf16[16,256]{1,0:T(8,128)(2,1)S(1)} %collect.1.own_notes), channel_id=1, source_target_pairs={{0,4},{4,0},{8,12},{12,8},{16,20},{20,16},{24,28},{28,24},{32,36},... | collective-permute-start | bytes 24584 | tf_op jit(solution)/shard_map/ppermute | solution.py:76
  31.4 1.6 %forward.5 = (bf16[768,2048]{1,0:T(8,128)(2,1)S(1)}, f32[144,2048]{1,0:T(8,128)S(1)}) custom-call(bf16[288,256]{1,0:T(8,128)(2,1)S(1)} %collective-permute-done.7.refs_6_.refs_0_.refs_5_, bf16[288,256]{1,0:T(8,128)(2,1)S(1)} %collective-permute-done.8.refs_7_.refs_1_.refs_6_, bf16[288,256]{1,0:T(8,128)(2,1)S(1)} %collective-permute-done.9.refs_8_.refs_2_.refs_7_, ...), custom_call_target="tpu_custom_call" | custom-call | flops 805306368 | bytes 1048576 | tf_op jit(solution)/shard_map/forward/pallas_call | solution.py:380
  33.0 0.9 %combine.1 = (bf16[128,2048]{1,0:T(8,128)(2,1)S(1)}, bf16[256,2048]{1,0:T(8,128)(2,1)S(1)}, f32[8,2048]{1,0:T(8,128)S(1)}) custom-call(bf16[16,256]{1,0:T(8,128)(2,1)S(1)} %collect.1.own_notes, bf16[16,256]{1,0:T(8,128)(2,1)S(1)} %collective-permute-done.11.sib_notes, bf16[128,2048]{1,0:T(8,128)(2,1)S(1)} %get-tuple-element.52.grads, ...), custom_call_target="tpu_custom_call" | custom-call | bytes 1048576 | tf_op jit(solution)/shard_map/combine/pallas_call | solution.py:485
  34.0 1.8 %backward.3 = (bf16[512,2048]{1,0:T(8,128)(2,1)S(1)}, bf16[384,256]{1,0:T(8,128)(2,1)S(1)}, bf16[128,256]{1,0:T(8,128)(2,1)S(1)}) custom-call(bf16[576,256]{1,0:T(8,128)(2,1)S(1)} %collective-permute-done.10.refs_0_.refs_9_.refs_8_, bf16[512,2048]{1,0:T(8,128)(2,1)S(1)} %get-tuple-element.51.refs_10_.refs_1_, ...), custom_call_target="tpu_custom_call" | custom-call | flops 805306368 | bytes 1048576 | tf_op jit(solution)/shard_map/backward/pallas_call | solution.py:527
  35.8 3.7 %collective-permute-start.13 = (bf16[384,256]{1,0:T(8,128)(2,1)S(1)}, bf16[384,256]{1,0:T(8,128)(2,1)S(1)}, u32[]{:S(2)}, u32[]{:S(2)}) collective-permute-start(bf16[384,256]{1,0:T(8,128)(2,1)S(1)} %get-tuple-element.58.refs_7_), channel_id=1, source_target_pairs={{0,16},{4,20},{8,24},{12,28},{16,0},{20,4},{24,8},{28,12},{32,48},... | collective-permute-start | bytes 589832 | tf_op jit(solution)/shard_map/ppermute | solution.py:86
  39.5 2.6 %backward.4 = (bf16[768,2048]{1,0:T(8,128)(2,1)S(1)}, bf16[384,256]{1,0:T(8,128)(2,1)S(1)}, bf16[384,256]{1,0:T(8,128)(2,1)S(1)}) custom-call(bf16[288,256]{1,0:T(8,128)(2,1)S(1)} %collective-permute-done.7.refs_6_.refs_0_.refs_5_, bf16[288,256]{1,0:T(8,128)(2,1)S(1)} %collective-permute-done.8.refs_7_.refs_1_.refs_6_, ...), custom_call_target="tpu_custom_call" | custom-call | flops 1207959552 | bytes 1048576 | tf_op jit(solution)/shard_map/backward/pallas_call | solution.py:527
  42.1 0.1 collective-permute-start.15
  42.2 2.7 %collective-permute-start.14 = (bf16[384,256]{1,0:T(8,128)(2,1)S(1)}, bf16[384,256]{1,0:T(8,128)(2,1)S(1)}, u32[]{:S(2)}, u32[]{:S(2)}) collective-permute-start(bf16[384,256]{1,0:T(8,128)(2,1)S(1)} %get-tuple-element.59.refs_9_), channel_id=1, source_target_pairs={{0,24},{4,28},{8,0},{12,4},{16,8},{20,12},{24,16},{28,20},{32,56},... | collective-permute-start | bytes 589832 | tf_op jit(solution)/shard_map/ppermute | solution.py:86
  44.8 2.6 %backward.5 = (bf16[768,2048]{1,0:T(8,128)(2,1)S(1)}, f32[128,256]{1,0:T(8,128)S(1)}, f32[384,256]{1,0:T(8,128)S(1)}, bf16[128,256]{1,0:T(8,128)(2,1)S(1)}, bf16[128,256]{1,0:T(8,128)(2,1)S(1)}) custom-call(bf16[144,256]{1,0:T(8,128)(2,1)S(1)} %join_cores.1.value.refs_0_.refs_1_, bf16[144,256]{1,0:T(8,128)(2,1)S(1)} %collective-permute-done.1.refs_3_.refs_1_.refs_2_, ...), custom_call_target="tpu_custom_call" | custom-call | flops 1207959552 | bytes 1048576 | tf_op jit(solution)/shard_map/backward/pallas_call | solution.py:527
  47.4 0.1 collective-permute-start.19
  47.5 1.5 %collective-permute-start.20 = (bf16[128,256]{1,0:T(8,128)(2,1)S(1)}, bf16[128,256]{1,0:T(8,128)(2,1)S(1)}, u32[]{:S(2)}, u32[]{:S(2)}) collective-permute-start(bf16[128,256]{1,0:T(8,128)(2,1)S(1)} %get-tuple-element.79), channel_id=1, source_target_pairs={{0,8},{4,12},{8,16},{12,20},{16,24},{20,28},{24,0},{28,4},{32,40},... | collective-permute-start | bytes 196616 | tf_op jit(solution)/shard_map/ppermute | solution.py:86
  49.0 0.1 collective-permute-start.21
  49.1 0.5 collective-permute-done.15.back_2
  49.6 0.1 sum_column.1
  49.7 1.2 %collective-permute-start.16 = (bf16[128,256]{1,0:T(8,128)(2,1)S(1)}, bf16[128,256]{1,0:T(8,128)(2,1)S(1)}, u32[]{:S(2)}, u32[]{:S(2)}) collective-permute-start(bf16[128,256]{1,0:T(8,128)(2,1)S(1)} %get-tuple-element.75), channel_id=1, source_target_pairs={{0,96},{4,100},{8,104},{12,108},{16,112},{20,116},{24,120},{28,124... | collective-permute-start | bytes 196616 | tf_op jit(solution)/shard_map/ppermute | solution.py:81
  50.9 0.6 %collective-permute-start.17 = (bf16[128,256]{1,0:T(8,128)(2,1)S(1)}, bf16[128,256]{1,0:T(8,128)(2,1)S(1)}, u32[]{:S(2)}, u32[]{:S(2)}) collective-permute-start(bf16[128,256]{1,0:T(8,128)(2,1)S(1)} %get-tuple-element.76), channel_id=1, source_target_pairs={{0,64},{4,68},{8,72},{12,76},{16,80},{20,84},{24,88},{28,92},{32,9... | collective-permute-start | bytes 196616 | tf_op jit(solution)/shard_map/ppermute | solution.py:81
  51.5 1.2 %collective-permute-start.18 = (bf16[128,256]{1,0:T(8,128)(2,1)S(1)}, bf16[128,256]{1,0:T(8,128)(2,1)S(1)}, u32[]{:S(2)}, u32[]{:S(2)}) collective-permute-start(bf16[128,256]{1,0:T(8,128)(2,1)S(1)} %get-tuple-element.77), channel_id=1, source_target_pairs={{0,32},{4,36},{8,40},{12,44},{16,48},{20,52},{24,56},{28,60},{32,6... | collective-permute-start | bytes 196616 | tf_op jit(solution)/shard_map/ppermute | solution.py:81
  52.7 2.0 %finish.1 = (bf16[64,4352]{1,0:T(8,128)(2,1)S(1)}, bf16[64,4352]{1,0:T(8,128)(2,1)S(1)}) custom-call(bf16[144,256]{1,0:T(8,128)(2,1)S(1)} %join_cores.1.value.refs_0_.refs_1_, bf16[144,256]{1,0:T(8,128)(2,1)S(1)} %collective-permute-done.1.refs_3_.refs_1_.refs_2_, bf16[144,256]{1,0:T(8,128)(2,1)S(1)} %collective-permute-done.2.refs_4_.refs_0_.refs_2_.refs_3_, ...), custom_call_target="tpu_custom_call" | custom-call | flops 805306368 | bytes 1048576 | tf_op jit(solution)/shard_map/finish/pallas_call | solution.py:590
  54.7 2.3 %collective-permute-start.12 = (bf16[64,4352]{1,0:T(8,128)(2,1)S(1)}, bf16[64,4352]{1,0:T(8,128)(2,1)S(1)}, u32[]{:S(2)}, u32[]{:S(2)}) collective-permute-start(bf16[64,4352]{1,0:T(8,128)(2,1)S(1)} %get-tuple-element.67), channel_id=1, source_target_pairs={{0,4},{4,0},{8,12},{12,8},{16,20},{20,16},{24,28},{28,24},{32,36},... | collective-permute-start | bytes 1671176 | tf_op jit(solution)/shard_map/ppermute | solution.py:76
  57.0 0.5 collective-permute-done.17.refs_2_
  57.5 0.1 add_split.1
  57.6 2.3 %collective-permute-start.22 = (bf16[64,256]{1,0:T(8,128)(2,1)S(1)}, bf16[64,256]{1,0:T(8,128)(2,1)S(1)}, u32[]{:S(2)}, u32[]{:S(2)}) collective-permute-start(bf16[64,256]{1,0:T(8,128)(2,1)S(1)} %get-tuple-element.81), channel_id=1, source_target_pairs={{0,4},{4,0},{8,12},{12,8},{16,20},{20,16},{24,28},{28,24},{32,36},... | collective-permute-start | bytes 98312 | tf_op jit(solution)/shard_map/ppermute | solution.py:76
  59.9 1.1 %place.1 = (bf16[64,2048]{1,0:T(8,128)(2,1)}, bf16[1,64,2048]{2,1,0:T(8,128)(2,1)}, bf16[64,2048]{1,0:T(8,128)(2,1)}, bf16[1,64,2048]{2,1,0:T(8,128)(2,1)}, bf16...) custom-call(bf16[64,4352]{1,0:T(8,128)(2,1)S(1)} %get-tuple-element.66.own, bf16[64,4352]{1,0:T(8,128)(2,1)S(1)} %collective-permute-done.12.recv), custom_call_target="tpu_custom_call" | custom-call | bytes 1048576 | tf_op jit(solution)/shard_map/place/pallas_call | solution.py:625
  61.0 0.7 %last.1 = bf16[64,512]{1,0:T(8,128)(2,1)} custom-call(bf16[64,256]{1,0:T(8,128)(2,1)S(1)} %get-tuple-element.80.kept, bf16[64,256]{1,0:T(8,128)(2,1)S(1)} %collective-permute-done.22.recv, f32[8,128]{1,0:T(8,128)S(1)} %get-tuple-element.82.after), custom_call_target="tpu_custom_call" | custom-call | bytes 1048576 | tf_op jit(solution)/shard_map/last/pallas_call | solution.py:695
  (21 shorter events, 0.1 us)
Async XLA Ops:
  1.5 5.2 %collective-permute-start = (bf16[128,256]{1,0:T(8,128)(2,1)S(1)}, bf16[128,256]{1,0:T(8,128)(2,1)S(1)}, u32[]{:S(2)}, u32[]{:S(2)}) collective-permute-start(bf16[128,256]{1,0:T(8,128)(2,1)S(1)} %get-tuple-element.46.after), channel_id=1, source_target_pairs={{0,4},{4,0},{8,12},{12,8},{16,20},{20,16},{24,28},{28,24},{32,36},... | collective-permute-start | bytes 196616 | tf_op jit(solution)/shard_map/ppermute | solution.py:76
  6.0 3.9 %collective-permute-start.4 = (bf16[4,64,1024]{2,1,0:T(8,128)(2,1)S(1)}, bf16[4,64,1024]{2,1,0:T(8,128)(2,1)S(1)}, u32[]{:S(2)}, u32[]{:S(2)}) collective-permute-start(bf16[4,64,1024]{2,1,0:T(8,128)(2,1)S(1)} %pack_q.1.after), channel_id=1, source_target_pairs={{0,4},{4,0},{8,12},{12,8},{16,20},{20,16},{24,28},{28,24},{32,36},... | collective-permute-start | bytes 1572872 | tf_op jit(solution)/shard_map/ppermute | solution.py:76
  6.8 7.6 %collective-permute-start.3 = (bf16[144,256]{1,0:T(8,128)(2,1)S(1)}, bf16[144,256]{1,0:T(8,128)(2,1)S(1)}, u32[]{:S(2)}, u32[]{:S(2)}) collective-permute-start(bf16[144,256]{1,0:T(8,128)(2,1)S(1)} %join_cores.1.value.refs_0_.refs_1_), channel_id=1, source_target_pairs={{0,96},{4,100},{8,104},{12,108},{16,112},{20,116},{24,120},{28,124... | collective-permute-start | bytes 221192 | tf_op jit(solution)/shard_map/ppermute | solution.py:81
  9.4 7.5 %collective-permute-start.2 = (bf16[144,256]{1,0:T(8,128)(2,1)S(1)}, bf16[144,256]{1,0:T(8,128)(2,1)S(1)}, u32[]{:S(2)}, u32[]{:S(2)}) collective-permute-start(bf16[144,256]{1,0:T(8,128)(2,1)S(1)} %join_cores.1.value.refs_0_.refs_1_), channel_id=1, source_target_pairs={{0,64},{4,68},{8,72},{12,76},{16,80},{20,84},{24,88},{28,92},{32,9... | collective-permute-start | bytes 221192 | tf_op jit(solution)/shard_map/ppermute | solution.py:81
  9.5 7.5 %collective-permute-start.1 = (bf16[144,256]{1,0:T(8,128)(2,1)S(1)}, bf16[144,256]{1,0:T(8,128)(2,1)S(1)}, u32[]{:S(2)}, u32[]{:S(2)}) collective-permute-start(bf16[144,256]{1,0:T(8,128)(2,1)S(1)} %join_cores.1.value.refs_0_.refs_1_), channel_id=1, source_target_pairs={{0,32},{4,36},{8,40},{12,44},{16,48},{20,52},{24,56},{28,60},{32,6... | collective-permute-start | bytes 221192 | tf_op jit(solution)/shard_map/ppermute | solution.py:81
  9.8 7.1 %collective-permute-start.6 = (bf16[144,256]{1,0:T(8,128)(2,1)S(1)}, bf16[144,256]{1,0:T(8,128)(2,1)S(1)}, u32[]{:S(2)}, u32[]{:S(2)}) collective-permute-start(bf16[144,256]{1,0:T(8,128)(2,1)S(1)} %gate.2), channel_id=1, source_target_pairs={{0,24},{4,28},{8,0},{12,4},{16,8},{20,12},{24,16},{28,20},{32,56},... | collective-permute-start | bytes 221192 | tf_op jit(solution)/shard_map/ppermute | solution.py:86
  12.4 4.6 %collective-permute-start.5 = (bf16[144,256]{1,0:T(8,128)(2,1)S(1)}, bf16[144,256]{1,0:T(8,128)(2,1)S(1)}, u32[]{:S(2)}, u32[]{:S(2)}) collective-permute-start(bf16[144,256]{1,0:T(8,128)(2,1)S(1)} %gate.2), channel_id=1, source_target_pairs={{0,8},{4,12},{8,16},{12,20},{16,24},{20,28},{24,0},{28,4},{32,40},... | collective-permute-start | bytes 221192 | tf_op jit(solution)/shard_map/ppermute | solution.py:86
  17.0 8.7 %collective-permute-start.10 = (bf16[576,256]{1,0:T(8,128)(2,1)S(1)}, bf16[576,256]{1,0:T(8,128)(2,1)S(1)}, u32[]{:S(2)}, u32[]{:S(2)}) collective-permute-start(bf16[576,256]{1,0:T(8,128)(2,1)S(1)} %join.5), channel_id=1, source_target_pairs={{0,16},{4,20},{8,24},{12,28},{16,0},{20,4},{24,8},{28,12},{32,48},... | collective-permute-start | bytes 884744 | tf_op jit(solution)/shard_map/ppermute | solution.py:86
  19.8 10.1 %collective-permute-start.9 = (bf16[288,256]{1,0:T(8,128)(2,1)S(1)}, bf16[288,256]{1,0:T(8,128)(2,1)S(1)}, u32[]{:S(2)}, u32[]{:S(2)}) collective-permute-start(bf16[288,256]{1,0:T(8,128)(2,1)S(1)} %join.4), channel_id=1, source_target_pairs={{0,24},{4,28},{8,0},{12,4},{16,8},{20,12},{24,16},{28,20},{32,56},... | collective-permute-start | bytes 442376 | tf_op jit(solution)/shard_map/ppermute | solution.py:86
  20.8 9.2 %collective-permute-start.8 = (bf16[288,256]{1,0:T(8,128)(2,1)S(1)}, bf16[288,256]{1,0:T(8,128)(2,1)S(1)}, u32[]{:S(2)}, u32[]{:S(2)}) collective-permute-start(bf16[288,256]{1,0:T(8,128)(2,1)S(1)} %join.4), channel_id=1, source_target_pairs={{0,8},{4,12},{8,16},{12,20},{16,24},{20,28},{24,0},{28,4},{32,40},... | collective-permute-start | bytes 442376 | tf_op jit(solution)/shard_map/ppermute | solution.py:86
  21.4 8.6 %collective-permute-start.7 = (bf16[288,256]{1,0:T(8,128)(2,1)S(1)}, bf16[288,256]{1,0:T(8,128)(2,1)S(1)}, u32[]{:S(2)}, u32[]{:S(2)}) collective-permute-start(bf16[288,256]{1,0:T(8,128)(2,1)S(1)} %join.3.refs_4_.refs_5_), channel_id=1, source_target_pairs={{0,32},{4,36},{8,40},{12,44},{16,48},{20,52},{24,56},{28,60},{32,6... | collective-permute-start | bytes 442376 | tf_op jit(solution)/shard_map/ppermute | solution.py:81
  30.0 3.0 %collective-permute-start.11 = (bf16[16,256]{1,0:T(8,128)(2,1)S(1)}, bf16[16,256]{1,0:T(8,128)(2,1)S(1)}, u32[]{:S(2)}, u32[]{:S(2)}) collective-permute-start(bf16[16,256]{1,0:T(8,128)(2,1)S(1)} %collect.1.own_notes), channel_id=1, source_target_pairs={{0,4},{4,0},{8,12},{12,8},{16,20},{20,16},{24,28},{28,24},{32,36},... | collective-permute-start | bytes 24584 | tf_op jit(solution)/shard_map/ppermute | solution.py:76
  35.8 13.2 %collective-permute-start.13 = (bf16[384,256]{1,0:T(8,128)(2,1)S(1)}, bf16[384,256]{1,0:T(8,128)(2,1)S(1)}, u32[]{:S(2)}, u32[]{:S(2)}) collective-permute-start(bf16[384,256]{1,0:T(8,128)(2,1)S(1)} %get-tuple-element.58.refs_7_), channel_id=1, source_target_pairs={{0,16},{4,20},{8,24},{12,28},{16,0},{20,4},{24,8},{28,12},{32,48},... | collective-permute-start | bytes 589832 | tf_op jit(solution)/shard_map/ppermute | solution.py:86
  42.1 7.5 %collective-permute-start.15 = (bf16[384,256]{1,0:T(8,128)(2,1)S(1)}, bf16[384,256]{1,0:T(8,128)(2,1)S(1)}, u32[]{:S(2)}, u32[]{:S(2)}) collective-permute-start(bf16[384,256]{1,0:T(8,128)(2,1)S(1)} %get-tuple-element.73), channel_id=1, source_target_pairs={{0,8},{4,12},{8,16},{12,20},{16,24},{20,28},{24,0},{28,4},{32,40},... | collective-permute-start | bytes 589832 | tf_op jit(solution)/shard_map/ppermute | solution.py:86
  42.2 7.4 %collective-permute-start.14 = (bf16[384,256]{1,0:T(8,128)(2,1)S(1)}, bf16[384,256]{1,0:T(8,128)(2,1)S(1)}, u32[]{:S(2)}, u32[]{:S(2)}) collective-permute-start(bf16[384,256]{1,0:T(8,128)(2,1)S(1)} %get-tuple-element.59.refs_9_), channel_id=1, source_target_pairs={{0,24},{4,28},{8,0},{12,4},{16,8},{20,12},{24,16},{28,20},{32,56},... | collective-permute-start | bytes 589832 | tf_op jit(solution)/shard_map/ppermute | solution.py:86
  47.4 4.0 %collective-permute-start.19 = (bf16[128,256]{1,0:T(8,128)(2,1)S(1)}, bf16[128,256]{1,0:T(8,128)(2,1)S(1)}, u32[]{:S(2)}, u32[]{:S(2)}) collective-permute-start(bf16[128,256]{1,0:T(8,128)(2,1)S(1)} %get-tuple-element.78), channel_id=1, source_target_pairs={{0,24},{4,28},{8,0},{12,4},{16,8},{20,12},{24,16},{28,20},{32,56},... | collective-permute-start | bytes 196616 | tf_op jit(solution)/shard_map/ppermute | solution.py:86
  47.5 7.1 %collective-permute-start.20 = (bf16[128,256]{1,0:T(8,128)(2,1)S(1)}, bf16[128,256]{1,0:T(8,128)(2,1)S(1)}, u32[]{:S(2)}, u32[]{:S(2)}) collective-permute-start(bf16[128,256]{1,0:T(8,128)(2,1)S(1)} %get-tuple-element.79), channel_id=1, source_target_pairs={{0,8},{4,12},{8,16},{12,20},{16,24},{20,28},{24,0},{28,4},{32,40},... | collective-permute-start | bytes 196616 | tf_op jit(solution)/shard_map/ppermute | solution.py:86
  49.0 8.0 %collective-permute-start.21 = (bf16[128,256]{1,0:T(8,128)(2,1)S(1)}, bf16[128,256]{1,0:T(8,128)(2,1)S(1)}, u32[]{:S(2)}, u32[]{:S(2)}) collective-permute-start(bf16[128,256]{1,0:T(8,128)(2,1)S(1)} %gate.3.after), channel_id=1, source_target_pairs={{0,16},{4,20},{8,24},{12,28},{16,0},{20,4},{24,8},{28,12},{32,48},... | collective-permute-start | bytes 196616 | tf_op jit(solution)/shard_map/ppermute | solution.py:86
  49.7 7.3 %collective-permute-start.16 = (bf16[128,256]{1,0:T(8,128)(2,1)S(1)}, bf16[128,256]{1,0:T(8,128)(2,1)S(1)}, u32[]{:S(2)}, u32[]{:S(2)}) collective-permute-start(bf16[128,256]{1,0:T(8,128)(2,1)S(1)} %get-tuple-element.75), channel_id=1, source_target_pairs={{0,96},{4,100},{8,104},{12,108},{16,112},{20,116},{24,120},{28,124... | collective-permute-start | bytes 196616 | tf_op jit(solution)/shard_map/ppermute | solution.py:81
  50.9 6.7 %collective-permute-start.17 = (bf16[128,256]{1,0:T(8,128)(2,1)S(1)}, bf16[128,256]{1,0:T(8,128)(2,1)S(1)}, u32[]{:S(2)}, u32[]{:S(2)}) collective-permute-start(bf16[128,256]{1,0:T(8,128)(2,1)S(1)} %get-tuple-element.76), channel_id=1, source_target_pairs={{0,64},{4,68},{8,72},{12,76},{16,80},{20,84},{24,88},{28,92},{32,9... | collective-permute-start | bytes 196616 | tf_op jit(solution)/shard_map/ppermute | solution.py:81
  51.5 6.0 %collective-permute-start.18 = (bf16[128,256]{1,0:T(8,128)(2,1)S(1)}, bf16[128,256]{1,0:T(8,128)(2,1)S(1)}, u32[]{:S(2)}, u32[]{:S(2)}) collective-permute-start(bf16[128,256]{1,0:T(8,128)(2,1)S(1)} %get-tuple-element.77), channel_id=1, source_target_pairs={{0,32},{4,36},{8,40},{12,44},{16,48},{20,52},{24,56},{28,60},{32,6... | collective-permute-start | bytes 196616 | tf_op jit(solution)/shard_map/ppermute | solution.py:81
  54.7 5.3 %collective-permute-start.12 = (bf16[64,4352]{1,0:T(8,128)(2,1)S(1)}, bf16[64,4352]{1,0:T(8,128)(2,1)S(1)}, u32[]{:S(2)}, u32[]{:S(2)}) collective-permute-start(bf16[64,4352]{1,0:T(8,128)(2,1)S(1)} %get-tuple-element.67), channel_id=1, source_target_pairs={{0,4},{4,0},{8,12},{12,8},{16,20},{20,16},{24,28},{28,24},{32,36},... | collective-permute-start | bytes 1671176 | tf_op jit(solution)/shard_map/ppermute | solution.py:76
  57.6 3.4 %collective-permute-start.22 = (bf16[64,256]{1,0:T(8,128)(2,1)S(1)}, bf16[64,256]{1,0:T(8,128)(2,1)S(1)}, u32[]{:S(2)}, u32[]{:S(2)}) collective-permute-start(bf16[64,256]{1,0:T(8,128)(2,1)S(1)} %get-tuple-element.81), channel_id=1, source_target_pairs={{0,4},{4,0},{8,12},{12,8},{16,20},{20,16},{24,28},{28,24},{32,36},... | collective-permute-start | bytes 98312 | tf_op jit(solution)/shard_map/ppermute | solution.py:76
